TPU v7x, 256 devices: a whole 4x4x8 slice. The times are simulated.
256 devices in a mesh: lat: 16 (over y_hi, z), lon: 16 (over y_lo, x, core).
Axes of the slice: x: 4, y: 4 (y_hi: 2, y_lo: 2; y = y_hi * 2 + y_lo), z: 8, core: 2. Of those that a mesh axis runs over, the one named last changes fastest.
Arguments:
- tokens: bfloat16 [192, 768, 512], P('lat', 'lon'), may hold values from -6 to 6
- gain_attn: float32 [512], replicated, may hold values from 0.1 to 1.9
- w_qkv: bfloat16 [512, 1536], replicated, may hold values from -4 to 4
- w_proj: bfloat16 [512, 512], replicated, may hold values from -0.25 to 0.25
- gain_merge: float32 [2048], replicated, may hold values from 0.1 to 1.9
- w_merge: bfloat16 [2048, 1024], replicated, may hold values from -0.125 to 0.125
- g_merged: bfloat16 [96, 384, 1024], P('lat', 'lon'), may hold values from -60 to 60
Outputs:
- merged: bfloat16 [96, 384, 1024], P('lat', 'lon')
- grad_tokens: bfloat16 [192, 768, 512], P('lat', 'lon')
- grad_weights: float32 [512, 2048], P('lat', 'lon')
All inputs are finite; a program needn't handle non-finite values.
Results may differ from a plain program's by a relative error of at most 0.03.
Values may be sent and summed in bfloat16 or wider, within the bound.
No kernel may reach another device: no remote copies, remote signals or barrier semaphores. Data moves between devices by JAX's collectives and lax.ppermute only.
A program may use at most 64 MiB of HBM per device.

v0:
```python
import jax
import jax.numpy as jnp
import numpy as np
from jax import lax
from jax.experimental import pallas as pl
from jax.experimental.pallas import tpu as pltpu
from jax.sharding import PartitionSpec as P

D = 512
HEADS = 8
HEAD = D // HEADS
WIN_LAT = 6
WIN_LON = 12
SHIFT_LAT = 3
SHIFT_LON = 6
EPS = 1e-05

ROWS, COLS = 12, 48
BORDER = 8
TOKENS = ROWS * COLS
LEN = WIN_LAT * WIN_LON
PAD = 80
PER_BAND = COLS // WIN_LON
BAND = PER_BAND * PAD
WINDOWS = 2 * PER_BAND
TOP = SHIFT_LAT * COLS
EDGE = ROWS * BORDER
CORNER = SHIFT_LAT * BORDER
SIDE = WIN_LAT * BORDER
BAND_CELLS = WIN_LAT * COLS
GROUP = HEADS // 2
GROUP_WIDTH = GROUP * HEAD
LOCAL = PER_BAND - 1
INNER = LOCAL * PAD
REST = WINDOWS - LOCAL
OUTER = REST * PAD
HELD = 8
WIDTH = WINDOWS * PAD
NEG = -1e30

f32 = jnp.float32
bf16 = jnp.bfloat16


def window_selector():
    pick = np.zeros((BAND, BAND_CELLS + SIDE), np.float32)
    for win in range(PER_BAND):
        for i in range(WIN_LAT):
            for j in range(WIN_LON):
                col = win * WIN_LON + j + SHIFT_LON
                at = i * COLS + col if col < COLS else BAND_CELLS + i * BORDER + col - COLS
                pick[win * PAD + i * WIN_LON + j, at] = 1.0
    return pick


def pair_selector():
    pick = np.zeros((4 * COLS, 4 * COLS), np.float32)
    quarter = COLS
    for a in range(2):
        for b in range(COLS // 2):
            for k, (i, j) in enumerate(((0, 0), (1, 0), (0, 1), (1, 1))):
                pick[k * quarter + a * (COLS // 2) + b, (2 * a + i) * COLS + 2 * b + j] = 1.0
    return pick


def dot(a, b):
    return lax.dot_general(a, b, (((1,), (0,)), ((), ())), preferred_element_type=f32)


def dot_nt(a, b):
    return lax.dot_general(a, b, (((1,), (1,)), ((), ())), preferred_element_type=f32)


def dot_tn(a, b):
    return lax.dot_general(a, b, (((0,), (0,)), ((), ())), preferred_element_type=f32)


def norm_parts(values):
    centred = values - jnp.mean(values, axis=-1, keepdims=True)
    scale = lax.rsqrt(jnp.mean(centred * centred, axis=-1, keepdims=True) + EPS)
    return centred * scale, scale


def outer_windows(pick_ref, cells, lat, lon, diag):
    first = jnp.concatenate([cells[:BAND_CELLS], lon[CORNER : CORNER + SIDE].astype(bf16)], axis=0)
    beside = jnp.concatenate([lon[CORNER + SIDE :], diag[:CORNER]], axis=0).astype(bf16)
    second = jnp.concatenate([cells[BAND_CELLS:], lat, beside], axis=0)
    return dot(pick_ref[INNER:], first).astype(bf16), dot(pick_ref[...], second).astype(bf16)


def head_masks(dtype):
    lane = lax.broadcasted_iota(jnp.int32, (1, GROUP_WIDTH), 1) // HEAD
    return [(lane == h).astype(f32).astype(dtype) for h in range(GROUP)]


def spread_heads(block, masks):
    return jnp.concatenate([block * m for m in masks], axis=0)


def collect_heads(stacked, masks):
    total = stacked[:PAD] * masks[0]
    for h in range(1, GROUP):
        total = total + stacked[h * PAD : (h + 1) * PAD] * masks[h]
    return total


def last_band():
    at_end = lax.axis_index("lat") == lax.axis_size("lat") - 1
    return jnp.where(at_end, f32(1), f32(0))


def score_masks():
    shape = (PAD, GROUP * PAD)
    key = lax.broadcasted_iota(jnp.int32, shape, 0)
    query = lax.rem(lax.broadcasted_iota(jnp.int32, shape, 1), PAD)
    base = jnp.where(key >= LEN, f32(NEG), f32(0))
    apart = jnp.where((key < LEN // 2) != (query < LEN // 2), f32(NEG), f32(0))
    return base, jnp.minimum(base, apart * last_band())


def attend(windows, qkv_ref, mixed_ref, probs_ref):
    low, wide = head_masks(bf16), head_masks(f32)
    masks = score_masks()
    for win, wraps in enumerate(windows):
        rows = pl.ds(win * PAD, PAD)
        mask = masks[1] if wraps else masks[0]
        for g in range(2):
            at = g * GROUP_WIDTH
            queries = spread_heads(qkv_ref[rows, at : at + GROUP_WIDTH], low)
            keys = qkv_ref[rows, D + at : D + at + GROUP_WIDTH]
            values = qkv_ref[rows, 2 * D + at : 2 * D + at + GROUP_WIDTH]
            scores = dot_nt(keys, queries) * HEAD ** (-0.5) + mask
            weights = jnp.exp(scores - jnp.max(scores, axis=0, keepdims=True))
            probs = weights * (1.0 / jnp.sum(weights, axis=0, keepdims=True))
            probs_ref[win, g] = probs
            mixed = collect_heads(dot_tn(probs.astype(bf16), values), wide)
            mixed_ref[rows, at : at + GROUP_WIDTH] = mixed.astype(bf16)


def attend_back(count, offset, qkv_ref, probs_ref, dmix_ref, dqkv_ref):
    low, wide = head_masks(bf16), head_masks(f32)
    for win in range(count):
        rows = pl.ds(win * PAD, PAD)
        out = pl.ds(offset + win * PAD, PAD)
        for g in range(2):
            at = g * GROUP_WIDTH
            queries = spread_heads(qkv_ref[rows, at : at + GROUP_WIDTH], low)
            keys = qkv_ref[rows, D + at : D + at + GROUP_WIDTH]
            values = qkv_ref[rows, 2 * D + at : 2 * D + at + GROUP_WIDTH]
            above = spread_heads(dmix_ref[rows, at : at + GROUP_WIDTH], low)
            probs = probs_ref[win, g]
            d_probs = dot_nt(values, above).astype(bf16).astype(f32)
            along = probs * d_probs
            d_scores = along - probs * jnp.sum(along, axis=0, keepdims=True)
            d_scores = (d_scores * HEAD ** (-0.5)).astype(bf16)
            d_queries = collect_heads(dot_tn(d_scores, keys), wide)
            d_keys = dot(d_scores, queries)
            d_values = dot(probs.astype(bf16), above)
            dqkv_ref[out, at : at + GROUP_WIDTH] = d_queries.astype(bf16)
            dqkv_ref[out, D + at : D + at + GROUP_WIDTH] = d_keys.astype(bf16)
            dqkv_ref[out, 2 * D + at : 2 * D + at + GROUP_WIDTH] = d_values.astype(bf16)


def put_back(result, back_ref, main_ref, lat_ref, lon_ref):
    for band in range(2):
        cells = dot(back_ref[...], result(band)).astype(bf16)
        if band == 0:
            main_ref[:BAND_CELLS] = cells[:BAND_CELLS]
        else:
            main_ref[BAND_CELLS:] = cells[: BAND_CELLS - TOP]
            lat_ref[...] = cells[BAND_CELLS - TOP : BAND_CELLS]
        lon_ref[band * SIDE : (band + 1) * SIDE] = cells[BAND_CELLS:]


def assemble(main_ref, lat_ref, lon_ref, diag_ref, out_ref):
    out_ref[:SHIFT_LAT] = lat_ref[...].astype(f32).reshape(SHIFT_LAT, COLS, D)
    out_ref[SHIFT_LAT:] = main_ref[...].astype(f32).reshape(ROWS - SHIFT_LAT, COLS, D)
    corner = diag_ref[...].astype(f32)[SIDE - CORNER :].reshape(SHIFT_LAT, BORDER, D)
    beside = lon_ref[...].astype(f32)[: EDGE - CORNER].reshape(ROWS - SHIFT_LAT, BORDER, D)
    out_ref[:SHIFT_LAT, :BORDER] += corner
    out_ref[SHIFT_LAT:, :BORDER] += beside


def border_kernel(tok_ref, own_ref, top_ref, edge_ref, corner_ref, sem):
    copy = pltpu.make_async_copy(tok_ref, own_ref, sem)
    copy.start()
    copy.wait()
    top_ref[...] = own_ref[:TOP]
    edge = [own_ref[row * COLS : row * COLS + 16].astype(f32)[:BORDER] for row in range(ROWS)]
    edge_ref[...] = jnp.concatenate(edge, axis=0).astype(bf16)
    corner_ref[...] = jnp.concatenate(edge[:WIN_LAT], axis=0).astype(bf16)


def inner_kernel(tok_ref, *refs):
    held, got = refs[:HELD], refs[HELD : 2 * HELD]
    cells_ref, xs_ref, qkv_ref, mixed_ref, probs_ref, att_ref, sem = refs[2 * HELD :]
    copies = [pltpu.make_async_copy(a, b, sem.at[i]) for i, (a, b) in enumerate(zip(held, got))]
    for copy in copies:
        copy.start()
    gain_ref, pick_ref, wqkv_ref, wproj_ref = got[:4]
    normed = norm_parts(tok_ref[TOP:].astype(f32))[0]
    for copy in copies:
        copy.wait()
    cells_ref[...] = (normed * gain_ref[...]).astype(bf16)
    xs_ref[...] = dot(pick_ref[:INNER, :BAND_CELLS], cells_ref[:BAND_CELLS]).astype(bf16)
    qkv_ref[...] = dot(xs_ref[...], wqkv_ref[...]).astype(bf16)
    attend([False] * LOCAL, qkv_ref, mixed_ref, probs_ref)
    att_ref[...] = dot(mixed_ref[...], wproj_ref[...]).astype(bf16)


def outer_kernel(
    cells_ref, lat_ref, lon_ref, diag_ref, gain_ref, wqkv_ref, wproj_ref, pick_ref, back_ref, att0_ref,
    xs_ref, qkv_ref, mixed_ref, probs_ref, main_ref, out_lat_ref, out_lon_ref,
    att_ref,
):
    def normed(ref):
        return norm_parts(ref[...].astype(f32))[0] * gain_ref[...]

    first, second = outer_windows(
        pick_ref, cells_ref[...], normed(lat_ref).astype(bf16), normed(lon_ref), normed(diag_ref)
    )
    xs_ref[:PAD] = first
    xs_ref[PAD:] = second
    qkv_ref[...] = dot(xs_ref[...], wqkv_ref[...]).astype(bf16)
    attend([False] + [True] * PER_BAND, qkv_ref, mixed_ref, probs_ref)
    att_ref[:INNER] = att0_ref[...]
    att_ref[INNER:] = dot(mixed_ref[...], wproj_ref[...]).astype(bf16)
    put_back(lambda band: att_ref[pl.ds(band * BAND, BAND)], back_ref, main_ref, out_lat_ref, out_lon_ref)


def cotangent_kernel(g_ref, gain_ref, wmerge_ref, out_ref, weights_ref, held_ref, sem):
    copies = [
        pltpu.make_async_copy(g_ref, held_ref, sem.at[0]),
        pltpu.make_async_copy(wmerge_ref, weights_ref, sem.at[1]),
    ]
    for copy in copies:
        copy.start()
    for copy in copies:
        copy.wait()
    for k in range(4):
        out_ref[k] = dot_nt(held_ref[...], weights_ref[k * D : (k + 1) * D]) * gain_ref[k]


def pair_kernel(
    tok_ref, main_ref, lat_ref, lon_ref, diag_ref, gain_ref, cot_ref, pair_ref, unpair_ref,
    dsum_ref, edge_ref, normed_ref,
    added_ref, members_ref,
):
    assemble(main_ref, lat_ref, lon_ref, diag_ref, added_ref)
    quarter = COLS
    for part in range(3):
        rows = pl.ds(part * 4 * COLS, 4 * COLS)
        added = added_ref[pl.ds(part * 4, 4)].reshape(4 * COLS, D)
        summed = (tok_ref[rows].astype(f32) + added).astype(bf16)
        paired = dot(pair_ref[...], summed)
        for k in range(4):
            members_ref[k, pl.ds(part * quarter, quarter)] = paired[k * quarter : (k + 1) * quarter]
    width = 4 * D
    total = sum(jnp.sum(members_ref[k], axis=-1, keepdims=True) for k in range(4))
    center = total / width
    for k in range(4):
        members_ref[k] = members_ref[k] - center
    spread = sum(jnp.sum(members_ref[k] * members_ref[k], axis=-1, keepdims=True) for k in range(4)) / width
    scale = lax.rsqrt(spread + EPS)
    for k in range(4):
        members_ref[k] = members_ref[k] * scale
        normed_ref[k] = (members_ref[k] * gain_ref[k]).astype(bf16)
    flat = sum(jnp.sum(cot_ref[k], axis=-1, keepdims=True) for k in range(4)) / width
    along = sum(jnp.sum(cot_ref[k] * members_ref[k], axis=-1, keepdims=True) for k in range(4)) / width
    for k in range(4):
        members_ref[k] = (cot_ref[k] - flat - members_ref[k] * along) * scale
    for part in range(3):
        rows = pl.ds(part * quarter, quarter)
        block = jnp.concatenate([members_ref[k, rows].astype(bf16) for k in range(4)], axis=0)
        cells = dot(unpair_ref[...], block)
        dsum_ref[pl.ds(part * 4 * COLS, 4 * COLS)] = cells.astype(bf16)
        added_ref[pl.ds(part * 4, 4)] = cells.reshape(4, COLS, D)
    edge_ref[...] = added_ref[:, :BORDER].reshape(EDGE, D).astype(bf16)


def merge_kernel(normed_ref, wmerge_ref, out_ref):
    total = dot(normed_ref[0], wmerge_ref[:D])
    for k in range(1, 4):
        total = total + dot(normed_ref[k], wmerge_ref[k * D : (k + 1) * D])
    out_ref[...] = total.astype(bf16)


def inner_back_kernel(
    dsum_ref, qkv_ref, probs_ref, wproj_ref, pick_ref, xs0_ref, xs_ref, mixed0_ref, mixed_ref,
    up_ref, dqkv_ref, xst_ref, mixt_ref,
    dmix_ref,
):
    xst_ref[...] = jnp.concatenate([xs0_ref[...], xs_ref[...]], axis=0).T
    mixt_ref[...] = jnp.concatenate([mixed0_ref[...], mixed_ref[...]], axis=0).T
    up_ref[...] = dot(pick_ref[:INNER, :BAND_CELLS], dsum_ref[TOP : TOP + BAND_CELLS]).astype(bf16)
    dmix_ref[...] = dot_nt(up_ref[...], wproj_ref[...]).astype(bf16)
    attend_back(LOCAL, 0, qkv_ref, probs_ref, dmix_ref, dqkv_ref)


def outer_back_kernel(
    dsum_ref, lat_ref, lon_ref, diag_ref, xst_ref, mixt_ref, up0_ref, dqkv0_ref,
    qkv_ref, probs_ref, wproj_ref, pick_ref,
    dqkv_ref, keep_ref, send_ref,
    up_ref, dmix_ref,
):
    first, second = outer_windows(
        pick_ref, dsum_ref[TOP:], lat_ref[...], lon_ref[...].astype(f32), diag_ref[...].astype(f32)
    )
    up_ref[:INNER] = up0_ref[...]
    up_ref[INNER:BAND] = first
    up_ref[BAND:] = second
    dqkv_ref[:INNER] = dqkv0_ref[...]
    dmix_ref[...] = dot_nt(up_ref[INNER:], wproj_ref[...]).astype(bf16)
    attend_back(REST, INNER, qkv_ref, probs_ref, dmix_ref, dqkv_ref)
    lat_at, lon_at = lax.axis_index("lat"), lax.axis_index("lon")
    even_core = lax.rem(lon_at, 2) == 0
    my_x = lax.rem(lax.div(lon_at, 2), 4)
    my_y = lax.div(lat_at, 8) * 2 + lax.div(lon_at, 8)
    x_steps = [lax.bitwise_xor(my_x, jnp.int32(i)) for i in range(4)]
    y_steps = [lax.bitwise_xor(my_y, jnp.int32(i)) for i in range(4)]
    for col in range(8):
        if col < 6:
            grad = dot(xst_ref[...], dqkv_ref[:, col * 256 : (col + 1) * 256])
        else:
            grad = dot(mixt_ref[...], up_ref[:, (col - 6) * 256 : (col - 5) * 256])
        even, odd = grad[:, :128], grad[:, 128:]
        kept = jnp.where(even_core, even, odd).astype(bf16)
        sent = jnp.where(even_core, odd, even).astype(bf16)
        low, x = divmod(col, 4)
        for lat in range(16):
            high, z = divmod(lat, 8)
            y = high * 2 + low
            rows = slice(lat * 32, (lat + 1) * 32)
            on_even = x_steps[x], lat * 2 + low
            on_odd = y_steps[y], z * 4 + x
            mine = [jnp.where(even_core, a, b) for a, b in zip(on_even, on_odd)]
            other = [jnp.where(even_core, b, a) for a, b in zip(on_even, on_odd)]
            keep_ref[mine[0], mine[1]] = kept[rows]
            send_ref[other[0], other[1]] = sent[rows]


def cells_back_kernel(dqkv_ref, wqkv_ref, back_ref, main_ref, out_lat_ref, out_lon_ref, dx_ref):
    dx_ref[...] = dot_nt(dqkv_ref[...], wqkv_ref[...]).astype(bf16)
    put_back(lambda band: dx_ref[pl.ds(band * BAND, BAND)], back_ref, main_ref, out_lat_ref, out_lon_ref)


def add_kernel(a_ref, b_ref, *out_refs):
    for k, out_ref in enumerate(out_refs):
        out_ref[...] = (a_ref[k].astype(f32) + b_ref[k].astype(f32)).astype(bf16)


def join_kernel(a_ref, b_ref, c_ref, d_ref, out_ref):
    total = a_ref[...].astype(f32) + b_ref[...].astype(f32) + c_ref[...].astype(f32) + d_ref[...].astype(f32)
    out_ref[...] = total.astype(bf16)


def sum_kernel(parts_ref, out_ref):
    total = parts_ref[0].astype(f32)
    for i in range(1, parts_ref.shape[0]):
        total = total + parts_ref[i].astype(f32)
    out_ref[...] = total.astype(out_ref.dtype)


def tokens_kernel(tok_ref, dsum_ref, main_ref, lat_ref, lon_ref, diag_ref, gain_ref, out_ref, field_ref):
    assemble(main_ref, lat_ref, lon_ref, diag_ref, field_ref)
    for part in range(3):
        rows = pl.ds(part * 4 * COLS, 4 * COLS)
        cot = field_ref[pl.ds(part * 4, 4)].reshape(4 * COLS, D) * gain_ref[...]
        normed, scale = norm_parts(tok_ref[rows].astype(f32))
        flat = jnp.mean(cot, axis=-1, keepdims=True)
        along = jnp.mean(cot * normed, axis=-1, keepdims=True)
        d_tokens = (cot - flat - normed * along) * scale
        out_ref[rows] = (dsum_ref[rows].astype(f32) + d_tokens).astype(bf16)


def call(kernel, outs, scratch=(), places=None, limit=20):
    spaces = {} if places is None else {
        "in_specs": [pl.BlockSpec(memory_space=pl.ANY if p else pltpu.VMEM) for p in places]
    }
    return pl.pallas_call(
        kernel,
        out_shape=[jax.ShapeDtypeStruct(s, t) for s, t in outs],
        scratch_shapes=[pltpu.VMEM(*s) if isinstance(s, tuple) else s for s in scratch],
        cost_estimate=pl.CostEstimate(flops=10**9, bytes_accessed=2 * 10**6, transcendentals=0),
        compiler_params=pltpu.CompilerParams(vmem_limit_bytes=limit * 1024 * 1024),
        **spaces,
    )


SCATTERED = [((TOKENS - TOP, D), bf16), ((TOP, D), bf16), ((EDGE, D), bf16)]


def saved(count):
    rows = count * PAD
    return [((rows, D), bf16), ((rows, 3 * D), bf16), ((rows, D), bf16), ((count, 2, PAD, GROUP * PAD), f32)]


def after(value, *others):
    return lax.optimization_barrier((value, *others))[0]


def chain(tok, gain, w_qkv, w_proj, gain_merge, w_merge, g_merged, fetch, hand_on):
    tok, top, edge, corner = call(
        border_kernel,
        [((TOKENS, D), bf16), ((TOP, D), bf16), ((EDGE, D), bf16), ((SIDE, D), bf16)],
        [pltpu.SemaphoreType.DMA],
        [1],
    )(tok)
    beside = fetch(top, edge, corner)
    pick, pair = window_selector(), pair_selector()
    selectors = [jnp.asarray(c, bf16) for c in (pick.T, pair, pair.T)]
    held = [gain, jnp.asarray(pick, bf16), w_qkv, w_proj, gain_merge] + selectors
    got = call(
        inner_kernel,
        [(h.shape, h.dtype) for h in held] + [((TOKENS - TOP, D), bf16)] + saved(LOCAL) + [((INNER, D), bf16)],
        [pltpu.SemaphoreType.DMA((HELD,))],
        [0] + [1] * HELD,
    )(tok, *held)
    gain, pick, w_qkv, w_proj, gain_merge, back, pair, unpair = got[:HELD]
    cells, xs0, qkv0, mixed0, probs0, att0 = got[HELD:]
    xs1, qkv1, mixed1, probs1, main, to_lat, to_lon = call(
        outer_kernel, saved(REST) + SCATTERED, [((WIDTH, D), bf16)]
    )(cells, *beside, gain, w_qkv, w_proj, pick, back, att0)
    beside = hand_on(to_lat, to_lon)
    cots, w_merge = call(
        cotangent_kernel,
        [((4, TOKENS // 4, D), f32), ((4 * D, 2 * D), bf16)],
        [((TOKENS // 4, 2 * D), bf16), pltpu.SemaphoreType.DMA((2,))],
        [1, 0, 1],
    )(after(g_merged, to_lat), gain_merge, w_merge)
    d_summed, edge, merge_normed = call(
        pair_kernel,
        [((TOKENS, D), bf16), ((EDGE, D), bf16), ((4, TOKENS // 4, D), bf16)],
        [((ROWS, COLS, D), f32), ((4, TOKENS // 4, D), f32)],
    )(tok, main, *beside, gain_merge, cots, pair, unpair)
    beside = fetch(d_summed[:TOP], edge, edge[:SIDE])
    (merged,) = call(merge_kernel, [((TOKENS // 4, 2 * D), bf16)])(merge_normed, w_merge)
    up0, dqkv0, xst, mixt = call(
        inner_back_kernel,
        [((INNER, D), bf16), ((INNER, 3 * D), bf16), ((D, WIDTH), bf16), ((D, WIDTH), bf16)],
        [((INNER, D), bf16)],
    )(d_summed, qkv0, probs0, w_proj, pick, xs0, xs1, mixed0, mixed1)
    dqkv, keep, sent = call(
        outer_back_kernel,
        [((WIDTH, 3 * D), bf16), ((4, 32, 32, 128), bf16), ((4, 32, 32, 128), bf16)],
        [((WIDTH, D), bf16), ((OUTER, D), bf16)],
    )(d_summed, *beside, xst, mixt, after(up0, merged), dqkv0, qkv1, probs1, w_proj, pick)
    main, to_lat, to_lon = call(cells_back_kernel, SCATTERED, [((WIDTH, D), bf16)])(dqkv, w_qkv, back)

    def finish(ready):
        beside = hand_on(after(to_lat, ready), after(to_lon, ready))
        (grad_tokens,) = call(tokens_kernel, [((TOKENS, D), bf16)], [((ROWS, COLS, D), f32)])(
            tok, d_summed, main, *beside, gain
        )
        return merged, grad_tokens

    return finish, keep, sent, to_lat


def solution(mesh):
    lats, lons = mesh.shape["lat"], mesh.shape["lon"]
    count = lats * lons

    def send(block, down, right):
        route = [
            (i, (i // lons + down) % lats * lons + (i % lons + right) % lons) for i in range(count)
        ]
        return lax.ppermute(block, ("lat", "lon"), route)

    def fetch(top, edge, corner):
        return send(top, -1, 0), send(edge, 0, -1), send(corner, -1, -1)

    def hand_on(lat, lon):
        return send(lat, 1, 0), send(lon, 0, 1), send(lon[SIDE:], 1, 1)

    def place(i):
        lat, lon = divmod(i, lons)
        return lat // 8, lat % 8, lon // 8, lon // 2 % 4, lon % 2

    def across(i, step):
        high, z, low, x, core = place(i)
        if core:
            high, low = divmod((high * 2 + low) ^ step, 2)
        else:
            x = x ^ step
        return (high * 8 + z) * lons + low * 8 + x * 2 + core

    rest = {}
    for i in range(count):
        high, z, low, x, core = place(i)
        rest.setdefault((core, high * 2 + low if core else x), []).append(i)
    rest = list(rest.values())

    def reduce_across(keep, sent, ready):
        other = lax.ppermute(sent, ("lat", "lon"), [(i, i ^ 1) for i in range(count)])
        own, *others = call(add_kernel, [((32, 32, 128), bf16)] * 4)(keep, after(other, ready))
        got = [
            lax.ppermute(block, ("lat", "lon"), [(i, across(i, step)) for i in range(count)])
            for step, block in enumerate(others, 1)
        ]
        return call(join_kernel, [((32, 32, 128), bf16)])(own, *got)[0]

    def reduce_rest(sums):
        parts = lax.all_to_all(sums, ("lat", "lon"), 0, 0, axis_index_groups=rest, tiled=True)
        return call(sum_kernel, [((32, 128), f32)])(parts)[0]

    def body(tokens, gain_attn, w_qkv, w_proj, gain_merge, w_merge, g_merged):
        finish, keep, sent, ready = chain(
            tokens.reshape(TOKENS, D), gain_attn.reshape(1, D), w_qkv, w_proj, gain_merge.reshape(4, 1, D),
            w_merge, g_merged.reshape(TOKENS // 4, 2 * D), fetch, hand_on,
        )
        sums = reduce_across(keep, sent, ready)
        grad_weights = reduce_rest(sums)
        merged, grad_tokens = finish(sums)
        return (
            merged.reshape(ROWS // 2, COLS // 2, 2 * D),
            grad_tokens.reshape(ROWS, COLS, D),
            grad_weights,
        )

    return jax.shard_map(
        body,
        mesh=mesh,
        in_specs=(P("lat", "lon", None), P(), P(), P(), P(), P(), P("lat", "lon", None)),
        out_specs=(P("lat", "lon", None), P("lat", "lon", None), P("lat", "lon")),
        check_vma=False,
    )
```

profile of v0, /device:TPU:1, one launch (start us, length us, event | category | flops | bytes accessed | tf_op | source)
XLA Modules:
  0.0 87.9 jit_solution(4668314749926872437)
XLA Ops:
  0.6 1.1 %copy-done.3 = bf16[12,48,512]{2,1,0:T(8,128)(2,1)S(1)} copy-done((bf16[12,48,512]{2,1,0:T(8,128)(2,1)S(1)}, bf16[12,48,512]{2,1,0:T(8,128)(2,1)}, u32[]{:S(2)}) %copy-start.3) | copy-done | bytes 589848
  1.7 0.0 copy-start.7
  1.7 0.0 copy-start.8
  1.7 0.0 copy-start.9
  1.7 0.0 copy-start.10
  1.8 0.2 shard_map.130
  1.9 9.1 %collective-permute-start = (bf16[144,512]{1,0:T(8,128)(2,1)S(1)}, bf16[144,512]{1,0:T(8,128)(2,1)S(1)}, u32[]{:S(2)}, u32[]{:S(2)}) collective-permute-start(bf16[144,512]{1,0:T(8,128)(2,1)S(1)} %get-tuple-element.54), channel_id=1, source_target_pairs={{0,240},{1,241},{2,242},{3,243},{4,244},{5,245},{6,246},{7,247},{8... | collective-permute-start | bytes 442376 | tf_op jit(solution)/shard_map/ppermute | solution.py:468
  11.0 1.0 %collective-permute-start.1 = (bf16[96,512]{1,0:T(8,128)(2,1)S(1)}, bf16[96,512]{1,0:T(8,128)(2,1)S(1)}, u32[]{:S(2)}, u32[]{:S(2)}) collective-permute-start(bf16[96,512]{1,0:T(8,128)(2,1)S(1)} %get-tuple-element.55), channel_id=1, source_target_pairs={{0,15},{1,0},{2,1},{3,2},{4,3},{5,4},{6,5},{7,6},{8,7},{9,8},{10,9... | collective-permute-start | bytes 294920 | tf_op jit(solution)/shard_map/ppermute | solution.py:468
  12.0 3.2 %collective-permute-start.2 = (bf16[48,512]{1,0:T(8,128)(2,1)S(1)}, bf16[48,512]{1,0:T(8,128)(2,1)S(1)}, u32[]{:S(2)}, u32[]{:S(2)}) collective-permute-start(bf16[48,512]{1,0:T(8,128)(2,1)S(1)} %get-tuple-element.56), channel_id=1, source_target_pairs={{0,255},{1,240},{2,241},{3,242},{4,243},{5,244},{6,245},{7,246},{8... | collective-permute-start | bytes 147464 | tf_op jit(solution)/shard_map/ppermute | solution.py:468
  15.3 0.0 copy-start
  15.3 3.7 %shard_map.131 = (f32[1,512]{1,0:T(1,128)S(1)}, bf16[320,336]{1,0:T(8,128)(2,1)S(1)}, bf16[512,1536]{1,0:T(8,128)(2,1)S(1)}, bf16[512,512]{1,0:T(8,128)(2,1)S(1)...) custom-call(bf16[576,512]{1,0:T(8,128)(2,1)S(1)} %get-tuple-element., ...), custom_call_target="tpu_custom_call" | custom-call | flops 1000000000 | bytes 2000000 | tf_op jit(solution)/shard_map/pallas_call | solution.py:413
  19.0 0.0 collective-permute-done.2.diag_ref
  19.0 0.0 collective-permute-done.lat_ref
  19.0 0.0 copy-start.1
  19.0 3.8 %shard_map.132 = (bf16[400,512]{1,0:T(8,128)(2,1)S(1)}, bf16[400,1536]{1,0:T(8,128)(2,1)S(1)}, bf16[400,512]{1,0:T(8,128)(2,1)S(1)}, f32[5,2,80,320]{3,2,1,0:T(8...) custom-call(bf16[432,512]{1,0:T(8,128)(2,1)S(1)} %get-tuple-element.53.cells_ref,, ...), custom_call_target="tpu_custom_call" | custom-call | flops 1000000000 | bytes 2000000 | tf_op jit(solution)/shard_map/pallas_call | solution.py:421
  22.9 0.2 collective-permute-start.3
  23.1 0.0 collective-permute-start.4
  23.1 0.3 collective-permute-start.5
  23.4 1.9 %shard_map.133 = (f32[4,144,512]{2,1,0:T(8,128)S(1)}, bf16[2048,1024]{1,0:T(8,128)(2,1)S(1)}) custom-call(bf16[144,1024]{1,0:T(8,128)(2,1)S(1)} %bitcast.6, f32[4,1,512]{2,1,0:T(1,128)S(1)} %get-tuple-element.66.gain_ref, bf16[2048,1024]{1,0:T(8,128)(2,1)S(1)} %copy-done), custom_call_target="tpu_custom_call" | custom-call | flops 1000000000 | bytes 2000000 | tf_op jit(solution)/shard_map/pallas_call | solution.py:425
  25.3 8.5 %collective-permute-done.5.diag_ref = bf16[48,512]{1,0:T(8,128)(2,1)S(1)} collective-permute-done((bf16[48,512]{1,0:T(8,128)(2,1)S(1)}, bf16[48,512]{1,0:T(8,128)(2,1)S(1)}, u32[]{:S(2)}, u32[]{:S(2)}) %collective-permute-start.5) | collective-permute-done | bytes 49184 | tf_op jit(solution)/shard_map/ppermute | solution.py:468
  33.8 0.0 collective-permute-done.4.lon_ref
  33.8 0.0 collective-permute-done.3.lat_ref
  33.8 1.3 %shard_map.134 = (bf16[576,512]{1,0:T(8,128)(2,1)S(1)}, bf16[96,512]{1,0:T(8,128)(2,1)S(1)}, bf16[4,144,512]{2,1,0:T(8,128)(2,1)S(1)}) custom-call(bf16[576,512]{1,0:T(8,128)(2,1)S(1)} %get-tuple-element.52.tok_ref, bf16[432,512]{1,0:T(8,128)(2,1)S(1)} %get-tuple-element.63.main_ref, bf16[144,512]{1,0:T(8,128)(2,1)S(1)} %collective-permute-done.3.lat_ref, ...), custom_call_target="tpu_custom_call" | custom-call | flops 1000000000 | bytes 2000000 | tf_op jit(solution)/shard_map/pallas_call | solution.py:431
  35.0 0.6 collective-permute-start.7
  35.7 1.7 %collective-permute-start.6 = (bf16[144,512]{1,0:T(8,128)(2,1)S(1)}, bf16[144,512]{1,0:T(8,128)(2,1)S(1)}, u32[]{:S(2)}, u32[]{:S(2)}) collective-permute-start(bf16[144,512]{1,0:T(8,128)(2,1)S(1)} %slice.13), channel_id=1, source_target_pairs={{0,240},{1,241},{2,242},{3,243},{4,244},{5,245},{6,246},{7,247},{8... | collective-permute-start | bytes 442376 | tf_op jit(solution)/shard_map/ppermute | solution.py:468
  37.4 0.6 collective-permute-start.8
  38.0 1.5 %shard_map.135 = bf16[144,1024]{1,0:T(8,128)(2,1)} custom-call(bf16[4,144,512]{2,1,0:T(8,128)(2,1)S(1)} %get-tuple-element.71.normed_ref, bf16[2048,1024]{1,0:T(8,128)(2,1)S(1)} %get-tuple-element.72.wmerge_ref), custom_call_target="tpu_custom_call" | custom-call | flops 1000000000 | bytes 2000000 | tf_op jit(solution)/shard_map/pallas_call | solution.py:437
  39.5 2.5 %shard_map.136 = (bf16[240,512]{1,0:T(8,128)(2,1)S(1)}, bf16[240,1536]{1,0:T(8,128)(2,1)S(1)}, bf16[512,640]{1,0:T(8,128)(2,1)S(1)}, bf16[512,640]{1,0:T(8,128)(2,1)S(1)}) custom-call(bf16[576,512]{1,0:T(8,128)(2,1)S(1)} %get-tuple-element.73.dsum_ref, bf16[240,1536]{1,0:T(8,128)(2,1)S(1)} %get-tuple-element.75.qkv_ref, ...), custom_call_target="tpu_custom_call" | custom-call | flops 1000000000 | bytes 2000000 | tf_op jit(solution)/shard_map/pallas_call | solution.py:438
  42.0 0.9 collective-permute-done.8.diag_ref
  42.9 5.5 %shard_map.137 = (bf16[640,1536]{1,0:T(8,128)(2,1)S(1)}, bf16[4,32,32,128]{3,2,1,0:T(8,128)(2,1)S(1)}, bf16[4,32,32,128]{3,2,1,0:T(8,128)(2,1)S(1)}) custom-call(bf16[576,512]{1,0:T(8,128)(2,1)S(1)} %get-tuple-element.73.dsum_ref, bf16[144,512]{1,0:T(8,128)(2,1)S(1)} %collective-permute-done.6.lat_ref, bf16[96,512]{1,0:T(8,128)(2,1)S(1)} %collective-permute-done.7.lon_ref, ...), custom_call_target="tpu_custom_call" | custom-call | flops 1000000000 | bytes 2000000 | tf_op jit(solution)/shard_map/pallas_call | solution.py:443
  48.4 0.3 collective-permute-start.9
  48.7 1.6 %shard_map.138 = (bf16[432,512]{1,0:T(8,128)(2,1)S(1)}, bf16[144,512]{1,0:T(8,128)(2,1)S(1)}, bf16[96,512]{1,0:T(8,128)(2,1)S(1)}) custom-call(bf16[640,1536]{1,0:T(8,128)(2,1)S(1)} %get-tuple-element.88.dqkv_ref, bf16[512,1536]{1,0:T(8,128)(2,1)S(1)} %get-tuple-element.58.wqkv_ref, bf16[336,320]{1,0:T(8,128)(2,1)S(1)} %get-tuple-element.61.back_ref), custom_call_target="tpu_custom_call" | custom-call | flops 1000000000 | bytes 2000000 | tf_op jit(solution)/shard_map/pallas_call | solution.py:448
  50.3 1.0 %collective-permute-done.9.b_ref = bf16[4,32,32,128]{3,2,1,0:T(8,128)(2,1)S(1)} collective-permute-done((bf16[4,32,32,128]{3,2,1,0:T(8,128)(2,1)S(1)}, bf16[4,32,32,128]{3,2,1,0:T(8,128)(2,1)S(1)}, u32[]{:S(2)}, u32[]{:S(2)}) %collective-permute-start.9) | collective-permute-done | bytes 1048608 | tf_op jit(solution)/shard_map/ppermute | solution.py:495
  51.3 0.2 shard_map.139
  51.6 0.1 collective-permute-start.10
  51.7 0.9 collective-permute-start.11
  52.5 3.0 %collective-permute-start.12 = (bf16[32,32,128]{2,1,0:T(8,128)(2,1)S(1)}, bf16[32,32,128]{2,1,0:T(8,128)(2,1)S(1)}, u32[]{:S(2)}, u32[]{:S(2)}) collective-permute-start(bf16[32,32,128]{2,1,0:T(8,128)(2,1)S(1)} %get-tuple-element.97), channel_id=1, source_target_pairs={{0,6},{1,137},{2,4},{3,139},{4,2},{5,141},{6,0},{7,143},{8,14},{9,... | collective-permute-start | bytes 786440 | tf_op jit(solution)/shard_map/ppermute | solution.py:498
  55.5 1.7 %collective-permute-done.10.b_ref = bf16[32,32,128]{2,1,0:T(8,128)(2,1)S(1)} collective-permute-done((bf16[32,32,128]{2,1,0:T(8,128)(2,1)S(1)}, bf16[32,32,128]{2,1,0:T(8,128)(2,1)S(1)}, u32[]{:S(2)}, u32[]{:S(2)}) %collective-permute-start.10) | collective-permute-done | bytes 262176 | tf_op jit(solution)/shard_map/ppermute | solution.py:498
  57.2 2.0 %collective-permute-done.11.c_ref = bf16[32,32,128]{2,1,0:T(8,128)(2,1)S(1)} collective-permute-done((bf16[32,32,128]{2,1,0:T(8,128)(2,1)S(1)}, bf16[32,32,128]{2,1,0:T(8,128)(2,1)S(1)}, u32[]{:S(2)}, u32[]{:S(2)}) %collective-permute-start.11) | collective-permute-done | bytes 262176 | tf_op jit(solution)/shard_map/ppermute | solution.py:498
  59.2 3.0 %collective-permute-done.12.d_ref = bf16[32,32,128]{2,1,0:T(8,128)(2,1)S(1)} collective-permute-done((bf16[32,32,128]{2,1,0:T(8,128)(2,1)S(1)}, bf16[32,32,128]{2,1,0:T(8,128)(2,1)S(1)}, u32[]{:S(2)}, u32[]{:S(2)}) %collective-permute-start.12) | collective-permute-done | bytes 262176 | tf_op jit(solution)/shard_map/ppermute | solution.py:498
  62.2 0.8 shard_map.140
  63.0 8.4 %all-to-all-start = ((bf16[32,32,128]{2,1,0:T(8,128)(2,1)}), bf16[32,32,128]{2,1,0:T(8,128)(2,1)S(1)}, u32[]{:S(2)}, u32[]{:S(2)}) async-start(bf16[32,32,128]{2,1,0:T(8,128)(2,1)} %shard_map.140), calls=%async_computation | async-start | bytes 524288 | tf_op jit(solution)/shard_map/all_to_all | solution.py:504
  71.5 1.3 %collective-permute-start.13 = (bf16[144,512]{1,0:T(8,128)(2,1)S(1)}, bf16[144,512]{1,0:T(8,128)(2,1)S(1)}, u32[]{:S(2)}, u32[]{:S(2)}) collective-permute-start(bf16[144,512]{1,0:T(8,128)(2,1)S(1)} %get-tuple-element.98), channel_id=1, source_target_pairs={{0,16},{1,17},{2,18},{3,19},{4,20},{5,21},{6,22},{7,23},{8,24},{9,... | collective-permute-start | bytes 442376 | tf_op jit(solution)/shard_map/ppermute | solution.py:468
  72.8 0.6 collective-permute-start.14
  73.4 1.9 %collective-permute-start.15 = (bf16[48,512]{1,0:T(8,128)(2,1)S(1)}, bf16[48,512]{1,0:T(8,128)(2,1)S(1)}, u32[]{:S(2)}, u32[]{:S(2)}) collective-permute-start(bf16[48,512]{1,0:T(8,128)(2,1)S(1)} %slice.15), channel_id=1, source_target_pairs={{0,17},{1,18},{2,19},{3,20},{4,21},{5,22},{6,23},{7,24},{8,25},{9,... | collective-permute-start | bytes 147464 | tf_op jit(solution)/shard_map/ppermute | solution.py:468
  75.3 10.3 %collective-permute-done.15.diag_ref = bf16[48,512]{1,0:T(8,128)(2,1)S(1)} collective-permute-done((bf16[48,512]{1,0:T(8,128)(2,1)S(1)}, bf16[48,512]{1,0:T(8,128)(2,1)S(1)}, u32[]{:S(2)}, u32[]{:S(2)}) %collective-permute-start.15) | collective-permute-done | bytes 49184 | tf_op jit(solution)/shard_map/ppermute | solution.py:468
  85.6 1.6 %shard_map.141 = bf16[576,512]{1,0:T(8,128)(2,1)} custom-call(bf16[576,512]{1,0:T(8,128)(2,1)S(1)} %get-tuple-element.52.tok_ref, bf16[576,512]{1,0:T(8,128)(2,1)S(1)} %get-tuple-element.73.dsum_ref, bf16[432,512]{1,0:T(8,128)(2,1)S(1)} %get-tuple-element.89.main_ref, bf16[144,512]{1,0:T(8,128)(2,1)S(1)} %collective-permute-done.13.lat_ref, ...), custom_call_target="tpu_custom_call" | custom-call | flops 1000000000 | bytes 2000000 | tf_op jit(solution)/shard_map/pallas_call | solution.py:452
  87.2 0.7 shard_map.142
  (25 shorter events, 0.1 us)
Async XLA Ops:
  0.6 1.1 %copy-start.3 = (bf16[12,48,512]{2,1,0:T(8,128)(2,1)S(1)}, bf16[12,48,512]{2,1,0:T(8,128)(2,1)}, u32[]{:S(2)}) copy-start(bf16[12,48,512]{2,1,0:T(8,128)(2,1)} %param.11) | copy-start | bytes 1769476
  1.7 13.5 %copy-start.2 = (bf16[512,1536]{1,0:T(8,128)(2,1)S(1)}, bf16[512,1536]{1,0:T(8,128)(2,1)}, u32[]{:S(2)}) copy-start(bf16[512,1536]{1,0:T(8,128)(2,1)} %refs_2_.1) | copy-start | bytes 4718596
  1.7 13.5 %copy-start.4 = (bf16[512,512]{1,0:T(8,128)(2,1)S(1)}, bf16[512,512]{1,0:T(8,128)(2,1)}, u32[]{:S(2)}) copy-start(bf16[512,512]{1,0:T(8,128)(2,1)} %refs_3_.1) | copy-start | bytes 1572868
  1.7 13.5 %copy-start.5 = (f32[2048]{0:T(1024)S(1)}, f32[2048]{0:T(1024)}, u32[]{:S(2)}) copy-start(f32[2048]{0:T(1024)} %param.15) | copy-start | bytes 24580
  1.7 13.5 %copy-start.6 = (f32[512]{0:T(512)S(1)}, f32[512]{0:T(512)}, u32[]{:S(2)}) copy-start(f32[512]{0:T(512)} %param.12) | copy-start | bytes 6148
  1.7 13.5 %copy-start.7 = (bf16[336,320]{1,0:T(8,128)(2,1)S(1)}, bf16[336,320]{1,0:T(8,128)(2,1)}, u32[]{:S(2)}) copy-start(bf16[336,320]{1,0:T(8,128)(2,1)} %constant.8.clone.refs_5_) | copy-start | bytes 645124
  1.7 13.5 %copy-start.8 = (bf16[320,336]{1,0:T(8,128)(2,1)S(1)}, bf16[320,336]{1,0:T(8,128)(2,1)}, u32[]{:S(2)}) copy-start(bf16[320,336]{1,0:T(8,128)(2,1)} %constant.11.clone.refs_1_) | copy-start | bytes 645124
  1.7 13.5 %copy-start.9 = (bf16[192,192]{1,0:T(8,128)(2,1)S(1)}, bf16[192,192]{1,0:T(8,128)(2,1)}, u32[]{:S(2)}) copy-start(bf16[192,192]{1,0:T(8,128)(2,1)} %constant.9.clone.refs_6_) | copy-start | bytes 221188
  1.7 13.5 %copy-start.10 = (bf16[192,192]{1,0:T(8,128)(2,1)S(1)}, bf16[192,192]{1,0:T(8,128)(2,1)}, u32[]{:S(2)}) copy-start(bf16[192,192]{1,0:T(8,128)(2,1)} %constant.10.clone.refs_7_) | copy-start | bytes 221188
  1.9 17.1 %collective-permute-start = (bf16[144,512]{1,0:T(8,128)(2,1)S(1)}, bf16[144,512]{1,0:T(8,128)(2,1)S(1)}, u32[]{:S(2)}, u32[]{:S(2)}) collective-permute-start(bf16[144,512]{1,0:T(8,128)(2,1)S(1)} %get-tuple-element.54), channel_id=1, source_target_pairs={{0,240},{1,241},{2,242},{3,243},{4,244},{5,245},{6,246},{7,247},{8... | collective-permute-start | bytes 442376 | tf_op jit(solution)/shard_map/ppermute | solution.py:468
  11.0 8.0 %collective-permute-start.1 = (bf16[96,512]{1,0:T(8,128)(2,1)S(1)}, bf16[96,512]{1,0:T(8,128)(2,1)S(1)}, u32[]{:S(2)}, u32[]{:S(2)}) collective-permute-start(bf16[96,512]{1,0:T(8,128)(2,1)S(1)} %get-tuple-element.55), channel_id=1, source_target_pairs={{0,15},{1,0},{2,1},{3,2},{4,3},{5,4},{6,5},{7,6},{8,7},{9,8},{10,9... | collective-permute-start | bytes 294920 | tf_op jit(solution)/shard_map/ppermute | solution.py:468
  12.0 7.0 %collective-permute-start.2 = (bf16[48,512]{1,0:T(8,128)(2,1)S(1)}, bf16[48,512]{1,0:T(8,128)(2,1)S(1)}, u32[]{:S(2)}, u32[]{:S(2)}) collective-permute-start(bf16[48,512]{1,0:T(8,128)(2,1)S(1)} %get-tuple-element.56), channel_id=1, source_target_pairs={{0,255},{1,240},{2,241},{3,242},{4,243},{5,244},{6,245},{7,246},{8... | collective-permute-start | bytes 147464 | tf_op jit(solution)/shard_map/ppermute | solution.py:468
  15.3 8.1 %copy-start = (bf16[2048,1024]{1,0:T(8,128)(2,1)S(1)}, bf16[2048,1024]{1,0:T(8,128)(2,1)}, u32[]{:S(2)}) copy-start(bf16[2048,1024]{1,0:T(8,128)(2,1)} %wmerge_ref.1) | copy-start | bytes 12582916
  19.0 4.4 %copy-start.1 = (bf16[6,24,1024]{2,1,0:T(8,128)(2,1)S(1)}, bf16[6,24,1024]{2,1,0:T(8,128)(2,1)}, u32[]{:S(2)}) copy-start(bf16[6,24,1024]{2,1,0:T(8,128)(2,1)} %param.17) | copy-start | bytes 884740
  22.9 10.9 %collective-permute-start.3 = (bf16[144,512]{1,0:T(8,128)(2,1)S(1)}, bf16[144,512]{1,0:T(8,128)(2,1)S(1)}, u32[]{:S(2)}, u32[]{:S(2)}) collective-permute-start(bf16[144,512]{1,0:T(8,128)(2,1)S(1)} %get-tuple-element.64), channel_id=1, source_target_pairs={{0,16},{1,17},{2,18},{3,19},{4,20},{5,21},{6,22},{7,23},{8,24},{9,... | collective-permute-start | bytes 442376 | tf_op jit(solution)/shard_map/ppermute | solution.py:468
  23.1 10.7 %collective-permute-start.4 = (bf16[96,512]{1,0:T(8,128)(2,1)S(1)}, bf16[96,512]{1,0:T(8,128)(2,1)S(1)}, u32[]{:S(2)}, u32[]{:S(2)}) collective-permute-start(bf16[96,512]{1,0:T(8,128)(2,1)S(1)} %get-tuple-element.65), channel_id=1, source_target_pairs={{0,1},{1,2},{2,3},{3,4},{4,5},{5,6},{6,7},{7,8},{8,9},{9,10},{10,1... | collective-permute-start | bytes 294920 | tf_op jit(solution)/shard_map/ppermute | solution.py:468
  23.1 10.6 %collective-permute-start.5 = (bf16[48,512]{1,0:T(8,128)(2,1)S(1)}, bf16[48,512]{1,0:T(8,128)(2,1)S(1)}, u32[]{:S(2)}, u32[]{:S(2)}) collective-permute-start(bf16[48,512]{1,0:T(8,128)(2,1)S(1)} %slice.12), channel_id=1, source_target_pairs={{0,17},{1,18},{2,19},{3,20},{4,21},{5,22},{6,23},{7,24},{8,25},{9,... | collective-permute-start | bytes 147464 | tf_op jit(solution)/shard_map/ppermute | solution.py:468
  35.0 7.8 %collective-permute-start.7 = (bf16[96,512]{1,0:T(8,128)(2,1)S(1)}, bf16[96,512]{1,0:T(8,128)(2,1)S(1)}, u32[]{:S(2)}, u32[]{:S(2)}) collective-permute-start(bf16[96,512]{1,0:T(8,128)(2,1)S(1)} %get-tuple-element.74), channel_id=1, source_target_pairs={{0,15},{1,0},{2,1},{3,2},{4,3},{5,4},{6,5},{7,6},{8,7},{9,8},{10,9... | collective-permute-start | bytes 294920 | tf_op jit(solution)/shard_map/ppermute | solution.py:468
  35.7 7.2 %collective-permute-start.6 = (bf16[144,512]{1,0:T(8,128)(2,1)S(1)}, bf16[144,512]{1,0:T(8,128)(2,1)S(1)}, u32[]{:S(2)}, u32[]{:S(2)}) collective-permute-start(bf16[144,512]{1,0:T(8,128)(2,1)S(1)} %slice.13), channel_id=1, source_target_pairs={{0,240},{1,241},{2,242},{3,243},{4,244},{5,245},{6,246},{7,247},{8... | collective-permute-start | bytes 442376 | tf_op jit(solution)/shard_map/ppermute | solution.py:468
  37.4 5.4 %collective-permute-start.8 = (bf16[48,512]{1,0:T(8,128)(2,1)S(1)}, bf16[48,512]{1,0:T(8,128)(2,1)S(1)}, u32[]{:S(2)}, u32[]{:S(2)}) collective-permute-start(bf16[48,512]{1,0:T(8,128)(2,1)S(1)} %slice.14), channel_id=1, source_target_pairs={{0,255},{1,240},{2,241},{3,242},{4,243},{5,244},{6,245},{7,246},{8... | collective-permute-start | bytes 147464 | tf_op jit(solution)/shard_map/ppermute | solution.py:468
  48.4 3.0 %collective-permute-start.9 = (bf16[4,32,32,128]{3,2,1,0:T(8,128)(2,1)S(1)}, bf16[4,32,32,128]{3,2,1,0:T(8,128)(2,1)S(1)}, u32[]{:S(2)}, u32[]{:S(2)}) collective-permute-start(bf16[4,32,32,128]{3,2,1,0:T(8,128)(2,1)S(1)} %get-tuple-element.92), channel_id=1, source_target_pairs={{0,1},{1,0},{2,3},{3,2},{4,5},{5,4},{6,7},{7,6},{8,9},{9,8},{10,11... | collective-permute-start | bytes 3145736 | tf_op jit(solution)/shard_map/ppermute | solution.py:495
  51.6 5.6 %collective-permute-start.10 = (bf16[32,32,128]{2,1,0:T(8,128)(2,1)S(1)}, bf16[32,32,128]{2,1,0:T(8,128)(2,1)S(1)}, u32[]{:S(2)}, u32[]{:S(2)}) collective-permute-start(bf16[32,32,128]{2,1,0:T(8,128)(2,1)S(1)} %get-tuple-element.95), channel_id=1, source_target_pairs={{0,2},{1,9},{2,0},{3,11},{4,6},{5,13},{6,4},{7,15},{8,10},{9,1},{1... | collective-permute-start | bytes 786440 | tf_op jit(solution)/shard_map/ppermute | solution.py:498
  51.7 7.5 %collective-permute-start.11 = (bf16[32,32,128]{2,1,0:T(8,128)(2,1)S(1)}, bf16[32,32,128]{2,1,0:T(8,128)(2,1)S(1)}, u32[]{:S(2)}, u32[]{:S(2)}) collective-permute-start(bf16[32,32,128]{2,1,0:T(8,128)(2,1)S(1)} %get-tuple-element.96), channel_id=1, source_target_pairs={{0,4},{1,129},{2,6},{3,131},{4,0},{5,133},{6,2},{7,135},{8,12},{9,... | collective-permute-start | bytes 786440 | tf_op jit(solution)/shard_map/ppermute | solution.py:498
  52.5 9.7 %collective-permute-start.12 = (bf16[32,32,128]{2,1,0:T(8,128)(2,1)S(1)}, bf16[32,32,128]{2,1,0:T(8,128)(2,1)S(1)}, u32[]{:S(2)}, u32[]{:S(2)}) collective-permute-start(bf16[32,32,128]{2,1,0:T(8,128)(2,1)S(1)} %get-tuple-element.97), channel_id=1, source_target_pairs={{0,6},{1,137},{2,4},{3,139},{4,2},{5,141},{6,0},{7,143},{8,14},{9,... | collective-permute-start | bytes 786440 | tf_op jit(solution)/shard_map/ppermute | solution.py:498
  63.0 24.2 %all-to-all-start = ((bf16[32,32,128]{2,1,0:T(8,128)(2,1)}), bf16[32,32,128]{2,1,0:T(8,128)(2,1)S(1)}, u32[]{:S(2)}, u32[]{:S(2)}) async-start(bf16[32,32,128]{2,1,0:T(8,128)(2,1)} %shard_map.140), calls=%async_computation | async-start | bytes 524288 | tf_op jit(solution)/shard_map/all_to_all | solution.py:504
  71.5 14.1 %collective-permute-start.13 = (bf16[144,512]{1,0:T(8,128)(2,1)S(1)}, bf16[144,512]{1,0:T(8,128)(2,1)S(1)}, u32[]{:S(2)}, u32[]{:S(2)}) collective-permute-start(bf16[144,512]{1,0:T(8,128)(2,1)S(1)} %get-tuple-element.98), channel_id=1, source_target_pairs={{0,16},{1,17},{2,18},{3,19},{4,20},{5,21},{6,22},{7,23},{8,24},{9,... | collective-permute-start | bytes 442376 | tf_op jit(solution)/shard_map/ppermute | solution.py:468
  72.8 12.8 %collective-permute-start.14 = (bf16[96,512]{1,0:T(8,128)(2,1)S(1)}, bf16[96,512]{1,0:T(8,128)(2,1)S(1)}, u32[]{:S(2)}, u32[]{:S(2)}) collective-permute-start(bf16[96,512]{1,0:T(8,128)(2,1)S(1)} %get-tuple-element.100), channel_id=1, source_target_pairs={{0,1},{1,2},{2,3},{3,4},{4,5},{5,6},{6,7},{7,8},{8,9},{9,10},{10,1... | collective-permute-start | bytes 294920 | tf_op jit(solution)/shard_map/ppermute | solution.py:468
  73.4 12.2 %collective-permute-start.15 = (bf16[48,512]{1,0:T(8,128)(2,1)S(1)}, bf16[48,512]{1,0:T(8,128)(2,1)S(1)}, u32[]{:S(2)}, u32[]{:S(2)}) collective-permute-start(bf16[48,512]{1,0:T(8,128)(2,1)S(1)} %slice.15), channel_id=1, source_target_pairs={{0,17},{1,18},{2,19},{3,20},{4,21},{5,22},{6,23},{7,24},{8,25},{9,... | collective-permute-start | bytes 147464 | tf_op jit(solution)/shard_map/ppermute | solution.py:468
where the time goes:
time: 88.1 us; the launch traced here: 87.9 us
  starting transfers between devices  33.2 us (38%)
  waiting for transfers between devices  27.4 us (31%)
  Pallas kernels  25.2 us (29%)
  local copies, waits for them, and re-layouts  1.14 us (1%)
    ppermute x12, starting transfers between devices, send(): return lax.ppermute(block, ('lat', 'lon'), route)  20.5 us
    ppermute x12, waiting for transfers between devices, send(): return lax.ppermute(block, ('lat', 'lon'), route)  19.7 us
    all_to_all x1, starting transfers between devices, reduce_rest(): lax.all_to_all(sums, ('lat', 'lon'), 0, 0, axis_index_groups=rest, tiled=...  8.43 us
    ppermute x3, waiting for transfers between devices, reduce_across(): lax.ppermute(block, ('lat', 'lon'), [(i, across(i, step)) for i in range(...  6.7 us
    pallas_call x1, Pallas kernels, chain(): call(outer_back_kernel, [((WIDTH, 3 * D), bf16), ((4, 32, 32, 128), bf16)...  5.5 us
    ppermute x3, starting transfers between devices, reduce_across(): lax.ppermute(block, ('lat', 'lon'), [(i, across(i, step)) for i in range(...  3.94 us
    pallas_call x1, Pallas kernels, chain(): call(outer_kernel, saved(REST) + SCATTERED, [((WIDTH, D), bf16)])  3.83 us
    pallas_call x1, Pallas kernels, chain(): call(inner_kernel, [(h.shape, h.dtype) for h in held] + [((TOKENS - TOP,...  3.69 us
  transfers between devices with their start and end apart: 17, of which 7 were waited for; matrix products, arithmetic and copies ran while one was open for 0% of the time, Pallas kernels for 15%

commit v1 on v0

--- a/solution.py
+++ b/solution.py
@@ -344,14 +344,35 @@
     put_back(lambda band: dx_ref[pl.ds(band * BAND, BAND)], back_ref, main_ref, out_lat_ref, out_lon_ref)
 
 
-def add_kernel(a_ref, b_ref, *out_refs):
-    for k, out_ref in enumerate(out_refs):
-        out_ref[...] = (a_ref[k].astype(f32) + b_ref[k].astype(f32)).astype(bf16)
-
-
-def join_kernel(a_ref, b_ref, c_ref, d_ref, out_ref):
-    total = a_ref[...].astype(f32) + b_ref[...].astype(f32) + c_ref[...].astype(f32) + d_ref[...].astype(f32)
-    out_ref[...] = total.astype(bf16)
+def add_kernel(a_ref, b_ref, own_ref, later_ref, first_ref, second_ref):
+    half = own_ref.shape[0] // 2
+
+    def both(k, rows):
+        return (a_ref[k, rows].astype(f32) + b_ref[k, rows].astype(f32)).astype(bf16)
+
+    upper, lower = pl.ds(0, half), pl.ds(half, half)
+    own_ref[...] = both(0, pl.ds(0, 2 * half))
+    first_ref[0], first_ref[1] = both(1, upper), both(2, upper)
+    second_ref[0], second_ref[1] = both(3, lower), both(2, lower)
+    later_ref[0], later_ref[1] = both(3, upper), both(1, lower)
+
+
+def relay_kernel(own_ref, later_ref, first_ref, second_ref, out_ref, to_third_ref, to_first_ref):
+    half = own_ref.shape[0] // 2
+
+    def both(a, b):
+        return (a.astype(f32) + b.astype(f32)).astype(bf16)
+
+    out_ref[:half] = both(own_ref[:half], first_ref[0])
+    out_ref[half:] = both(own_ref[half:], second_ref[0])
+    to_third_ref[...] = both(later_ref[0], first_ref[1])
+    to_first_ref[...] = both(later_ref[1], second_ref[1])
+
+
+def join_kernel(own_ref, upper_ref, lower_ref, out_ref):
+    half = own_ref.shape[0] // 2
+    out_ref[:half] = (own_ref[:half].astype(f32) + upper_ref[...].astype(f32)).astype(bf16)
+    out_ref[half:] = (own_ref[half:].astype(f32) + lower_ref[...].astype(f32)).astype(bf16)
 
 
 def sum_kernel(parts_ref, out_ref):
@@ -452,7 +473,7 @@
         (grad_tokens,) = call(tokens_kernel, [((TOKENS, D), bf16)], [((ROWS, COLS, D), f32)])(
             tok, d_summed, main, *beside, gain
         )
-        return merged, grad_tokens
+        return merged, grad_tokens, beside
 
     return finish, keep, sent, to_lat
 
@@ -491,14 +512,17 @@
         rest.setdefault((core, high * 2 + low if core else x), []).append(i)
     rest = list(rest.values())
 
+    def swap(block, step):
+        return lax.ppermute(block, ("lat", "lon"), [(i, across(i, step)) for i in range(count)])
+
     def reduce_across(keep, sent, ready):
         other = lax.ppermute(sent, ("lat", "lon"), [(i, i ^ 1) for i in range(count)])
-        own, *others = call(add_kernel, [((32, 32, 128), bf16)] * 4)(keep, after(other, ready))
-        got = [
-            lax.ppermute(block, ("lat", "lon"), [(i, across(i, step)) for i in range(count)])
-            for step, block in enumerate(others, 1)
-        ]
-        return call(join_kernel, [((32, 32, 128), bf16)])(own, *got)[0]
+        whole, pair, half = ((32, 32, 128), bf16), ((2, 16, 32, 128), bf16), ((16, 32, 128), bf16)
+        own, later, first, second = call(add_kernel, [whole, pair, pair, pair])(keep, after(other, ready))
+        own, to_third, to_first = call(relay_kernel, [whole, half, half])(
+            own, later, swap(first, 1), swap(second, 3)
+        )
+        return call(join_kernel, [whole])(own, swap(to_third, 3), swap(to_first, 1))[0], later
 
     def reduce_rest(sums):
         parts = lax.all_to_all(sums, ("lat", "lon"), 0, 0, axis_index_groups=rest, tiled=True)
@@ -509,9 +533,9 @@
             tokens.reshape(TOKENS, D), gain_attn.reshape(1, D), w_qkv, w_proj, gain_merge.reshape(4, 1, D),
             w_merge, g_merged.reshape(TOKENS // 4, 2 * D), fetch, hand_on,
         )
-        sums = reduce_across(keep, sent, ready)
-        grad_weights = reduce_rest(sums)
-        merged, grad_tokens = finish(sums)
+        sums, sending = reduce_across(keep, sent, ready)
+        merged, grad_tokens, beside = finish(sending)
+        grad_weights = reduce_rest(after(sums, *beside))
         return (
             merged.reshape(ROWS // 2, COLS // 2, 2 * D),
             grad_tokens.reshape(ROWS, COLS, D),

time: 88.1 us -> 89.9 us (1.020)
  waiting for transfers between devices: 27.4 us -> 34.6 us
  starting transfers between devices: 33.2 us -> 27.8 us
    all_to_all x1, waiting for transfers between devices: 0.01 us -> 11.6 us  [reduce_rest(): lax.all_to_all(sums, ('lat', 'lon'), 0, 0, axis_index_groups=rest, tiled=...]
    all_to_all x1, starting transfers between devices: 8.43 us -> 4.17 us  [reduce_rest(): lax.all_to_all(sums, ('lat', 'lon'), 0, 0, axis_index_groups=rest, tiled=...]
    ppermute x12, waiting for transfers between devices: 19.7 us -> 15.6 us  [send(): return lax.ppermute(block, ('lat', 'lon'), route)]
    ppermute x3 -> x4, starting transfers between devices: 3.94 us -> 1.25 us  [swap(): lax.ppermute(block, ('lat', 'lon'), [(i, across(i, step)) for i in range(...]
    ppermute x12, starting transfers between devices: 20.5 us -> 22 us  [send(): return lax.ppermute(block, ('lat', 'lon'), route)]
    ppermute x3 -> x4, waiting for transfers between devices: 6.7 us -> 6.24 us  [swap(): lax.ppermute(block, ('lat', 'lon'), [(i, across(i, step)) for i in range(...]
  transfers between devices with their start and end apart: 17 -> 18, of which waited for: 7 -> 7; matrix products, arithmetic and copies ran while one was open for 0% -> 0% of each run, Pallas kernels for 15% -> 15%
where the time goes in v1:
time: 89.9 us; the launch traced here: 89.7 us
  waiting for transfers between devices  34.6 us (38%)
  starting transfers between devices  27.8 us (31%)
  Pallas kernels  25.3 us (28%)
  local copies, waits for them, and re-layouts  1.14 us (1%)
    ppermute x12, starting transfers between devices, send(): return lax.ppermute(block, ('lat', 'lon'), route)  22 us
    ppermute x12, waiting for transfers between devices, send(): return lax.ppermute(block, ('lat', 'lon'), route)  15.6 us
    all_to_all x1, waiting for transfers between devices, reduce_rest(): lax.all_to_all(sums, ('lat', 'lon'), 0, 0, axis_index_groups=rest, tiled=...  11.6 us
    ppermute x4, waiting for transfers between devices, swap(): lax.ppermute(block, ('lat', 'lon'), [(i, across(i, step)) for i in range(...  6.24 us
    pallas_call x1, Pallas kernels, chain(): call(outer_back_kernel, [((WIDTH, 3 * D), bf16), ((4, 32, 32, 128), bf16)...  5.5 us
    all_to_all x1, starting transfers between devices, reduce_rest(): lax.all_to_all(sums, ('lat', 'lon'), 0, 0, axis_index_groups=rest, tiled=...  4.17 us
    pallas_call x1, Pallas kernels, chain(): call(outer_kernel, saved(REST) + SCATTERED, [((WIDTH, D), bf16)])  3.83 us
    pallas_call x1, Pallas kernels, chain(): call(inner_kernel, [(h.shape, h.dtype) for h in held] + [((TOKENS - TOP,...  3.69 us
  transfers between devices with their start and end apart: 18, of which 7 were waited for; matrix products, arithmetic and copies ran while one was open for 0% of the time, Pallas kernels for 15%

profile of v1, /device:TPU:1, one launch (start us, length us, event | category | flops | bytes accessed | tf_op | source)
XLA Modules:
  0.0 89.7 jit_solution(16923601041004984023)
XLA Ops:
  0.6 1.1 %copy-done.3 = bf16[12,48,512]{2,1,0:T(8,128)(2,1)S(1)} copy-done((bf16[12,48,512]{2,1,0:T(8,128)(2,1)S(1)}, bf16[12,48,512]{2,1,0:T(8,128)(2,1)}, u32[]{:S(2)}) %copy-start.3) | copy-done | bytes 589848
  1.7 0.0 copy-start.7
  1.7 0.0 copy-start.8
  1.7 0.0 copy-start.9
  1.7 0.0 copy-start.10
  1.8 0.2 shard_map.130
  1.9 9.1 %collective-permute-start = (bf16[144,512]{1,0:T(8,128)(2,1)S(1)}, bf16[144,512]{1,0:T(8,128)(2,1)S(1)}, u32[]{:S(2)}, u32[]{:S(2)}) collective-permute-start(bf16[144,512]{1,0:T(8,128)(2,1)S(1)} %get-tuple-element.58), channel_id=1, source_target_pairs={{0,240},{1,241},{2,242},{3,243},{4,244},{5,245},{6,246},{7,247},{8... | collective-permute-start | bytes 442376 | tf_op jit(solution)/shard_map/ppermute | solution.py:489
  11.0 1.0 %collective-permute-start.1 = (bf16[96,512]{1,0:T(8,128)(2,1)S(1)}, bf16[96,512]{1,0:T(8,128)(2,1)S(1)}, u32[]{:S(2)}, u32[]{:S(2)}) collective-permute-start(bf16[96,512]{1,0:T(8,128)(2,1)S(1)} %get-tuple-element.59), channel_id=1, source_target_pairs={{0,15},{1,0},{2,1},{3,2},{4,3},{5,4},{6,5},{7,6},{8,7},{9,8},{10,9... | collective-permute-start | bytes 294920 | tf_op jit(solution)/shard_map/ppermute | solution.py:489
  12.0 3.2 %collective-permute-start.2 = (bf16[48,512]{1,0:T(8,128)(2,1)S(1)}, bf16[48,512]{1,0:T(8,128)(2,1)S(1)}, u32[]{:S(2)}, u32[]{:S(2)}) collective-permute-start(bf16[48,512]{1,0:T(8,128)(2,1)S(1)} %get-tuple-element.60), channel_id=1, source_target_pairs={{0,255},{1,240},{2,241},{3,242},{4,243},{5,244},{6,245},{7,246},{8... | collective-permute-start | bytes 147464 | tf_op jit(solution)/shard_map/ppermute | solution.py:489
  15.3 0.0 copy-start
  15.3 3.7 %shard_map.131 = (f32[1,512]{1,0:T(1,128)S(1)}, bf16[320,336]{1,0:T(8,128)(2,1)S(1)}, bf16[512,1536]{1,0:T(8,128)(2,1)S(1)}, bf16[512,512]{1,0:T(8,128)(2,1)S(1)...) custom-call(bf16[576,512]{1,0:T(8,128)(2,1)S(1)} %get-tuple-element., ...), custom_call_target="tpu_custom_call" | custom-call | flops 1000000000 | bytes 2000000 | tf_op jit(solution)/shard_map/pallas_call | solution.py:434
  19.0 0.0 collective-permute-done.2.diag_ref
  19.0 0.0 collective-permute-done.lat_ref
  19.0 0.0 copy-start.1
  19.0 3.8 %shard_map.132 = (bf16[400,512]{1,0:T(8,128)(2,1)S(1)}, bf16[400,1536]{1,0:T(8,128)(2,1)S(1)}, bf16[400,512]{1,0:T(8,128)(2,1)S(1)}, f32[5,2,80,320]{3,2,1,0:T(8...) custom-call(bf16[432,512]{1,0:T(8,128)(2,1)S(1)} %get-tuple-element.57.cells_ref,, ...), custom_call_target="tpu_custom_call" | custom-call | flops 1000000000 | bytes 2000000 | tf_op jit(solution)/shard_map/pallas_call | solution.py:442
  22.9 0.2 collective-permute-start.3
  23.1 0.0 collective-permute-start.4
  23.1 0.3 collective-permute-start.5
  23.4 1.9 %shard_map.133 = (f32[4,144,512]{2,1,0:T(8,128)S(1)}, bf16[2048,1024]{1,0:T(8,128)(2,1)S(1)}) custom-call(bf16[144,1024]{1,0:T(8,128)(2,1)S(1)} %bitcast.6, f32[4,1,512]{2,1,0:T(1,128)S(1)} %get-tuple-element.70.gain_ref, bf16[2048,1024]{1,0:T(8,128)(2,1)S(1)} %copy-done), custom_call_target="tpu_custom_call" | custom-call | flops 1000000000 | bytes 2000000 | tf_op jit(solution)/shard_map/pallas_call | solution.py:446
  25.3 8.5 %collective-permute-done.5.diag_ref = bf16[48,512]{1,0:T(8,128)(2,1)S(1)} collective-permute-done((bf16[48,512]{1,0:T(8,128)(2,1)S(1)}, bf16[48,512]{1,0:T(8,128)(2,1)S(1)}, u32[]{:S(2)}, u32[]{:S(2)}) %collective-permute-start.5) | collective-permute-done | bytes 49184 | tf_op jit(solution)/shard_map/ppermute | solution.py:489
  33.8 0.0 collective-permute-done.4.lon_ref
  33.8 1.3 %shard_map.134 = (bf16[576,512]{1,0:T(8,128)(2,1)S(1)}, bf16[96,512]{1,0:T(8,128)(2,1)S(1)}, bf16[4,144,512]{2,1,0:T(8,128)(2,1)S(1)}) custom-call(bf16[576,512]{1,0:T(8,128)(2,1)S(1)} %get-tuple-element.56.tok_ref, bf16[432,512]{1,0:T(8,128)(2,1)S(1)} %get-tuple-element.67.main_ref, bf16[144,512]{1,0:T(8,128)(2,1)S(1)} %collective-permute-done.3.lat_ref, ...), custom_call_target="tpu_custom_call" | custom-call | flops 1000000000 | bytes 2000000 | tf_op jit(solution)/shard_map/pallas_call | solution.py:452
  35.0 0.6 collective-permute-start.7
  35.7 1.7 %collective-permute-start.6 = (bf16[144,512]{1,0:T(8,128)(2,1)S(1)}, bf16[144,512]{1,0:T(8,128)(2,1)S(1)}, u32[]{:S(2)}, u32[]{:S(2)}) collective-permute-start(bf16[144,512]{1,0:T(8,128)(2,1)S(1)} %slice.13), channel_id=1, source_target_pairs={{0,240},{1,241},{2,242},{3,243},{4,244},{5,245},{6,246},{7,247},{8... | collective-permute-start | bytes 442376 | tf_op jit(solution)/shard_map/ppermute | solution.py:489
  37.4 0.6 collective-permute-start.8
  38.0 1.5 %shard_map.135 = bf16[144,1024]{1,0:T(8,128)(2,1)} custom-call(bf16[4,144,512]{2,1,0:T(8,128)(2,1)S(1)} %get-tuple-element.75.normed_ref, bf16[2048,1024]{1,0:T(8,128)(2,1)S(1)} %get-tuple-element.76.wmerge_ref), custom_call_target="tpu_custom_call" | custom-call | flops 1000000000 | bytes 2000000 | tf_op jit(solution)/shard_map/pallas_call | solution.py:458
  39.5 2.5 %shard_map.136 = (bf16[240,512]{1,0:T(8,128)(2,1)S(1)}, bf16[240,1536]{1,0:T(8,128)(2,1)S(1)}, bf16[512,640]{1,0:T(8,128)(2,1)S(1)}, bf16[512,640]{1,0:T(8,128)(2,1)S(1)}) custom-call(bf16[576,512]{1,0:T(8,128)(2,1)S(1)} %get-tuple-element.77.dsum_ref, bf16[240,1536]{1,0:T(8,128)(2,1)S(1)} %get-tuple-element.79.qkv_ref, ...), custom_call_target="tpu_custom_call" | custom-call | flops 1000000000 | bytes 2000000 | tf_op jit(solution)/shard_map/pallas_call | solution.py:459
  42.0 0.9 collective-permute-done.8.diag_ref
  42.9 5.5 %shard_map.137 = (bf16[640,1536]{1,0:T(8,128)(2,1)S(1)}, bf16[4,32,32,128]{3,2,1,0:T(8,128)(2,1)S(1)}, bf16[4,32,32,128]{3,2,1,0:T(8,128)(2,1)S(1)}) custom-call(bf16[576,512]{1,0:T(8,128)(2,1)S(1)} %get-tuple-element.77.dsum_ref, bf16[144,512]{1,0:T(8,128)(2,1)S(1)} %collective-permute-done.6.lat_ref, bf16[96,512]{1,0:T(8,128)(2,1)S(1)} %collective-permute-done.7.lon_ref, ...), custom_call_target="tpu_custom_call" | custom-call | flops 1000000000 | bytes 2000000 | tf_op jit(solution)/shard_map/pallas_call | solution.py:464
  48.4 0.3 collective-permute-start.9
  48.7 1.6 %shard_map.138 = (bf16[432,512]{1,0:T(8,128)(2,1)S(1)}, bf16[144,512]{1,0:T(8,128)(2,1)S(1)}, bf16[96,512]{1,0:T(8,128)(2,1)S(1)}) custom-call(bf16[640,1536]{1,0:T(8,128)(2,1)S(1)} %get-tuple-element.92.dqkv_ref, bf16[512,1536]{1,0:T(8,128)(2,1)S(1)} %get-tuple-element.62.wqkv_ref, bf16[336,320]{1,0:T(8,128)(2,1)S(1)} %get-tuple-element.65.back_ref), custom_call_target="tpu_custom_call" | custom-call | flops 1000000000 | bytes 2000000 | tf_op jit(solution)/shard_map/pallas_call | solution.py:469
  50.3 1.0 %collective-permute-done.9.b_ref = bf16[4,32,32,128]{3,2,1,0:T(8,128)(2,1)S(1)} collective-permute-done((bf16[4,32,32,128]{3,2,1,0:T(8,128)(2,1)S(1)}, bf16[4,32,32,128]{3,2,1,0:T(8,128)(2,1)S(1)}, u32[]{:S(2)}, u32[]{:S(2)}) %collective-permute-start.9) | collective-permute-done | bytes 1048608 | tf_op jit(solution)/shard_map/ppermute | solution.py:519
  51.3 0.2 shard_map.139
  51.6 0.1 collective-permute-start.13
  51.7 0.6 collective-permute-start.14
  52.2 4.9 %collective-permute-done.13.first_ref = bf16[2,16,32,128]{3,2,1,0:T(8,128)(2,1)S(1)} collective-permute-done((bf16[2,16,32,128]{3,2,1,0:T(8,128)(2,1)S(1)}, bf16[2,16,32,128]{3,2,1,0:T(8,128)(2,1)S(1)}, u32[]{:S(2)}, u32[]{:S(2)}) %collective-permute-start.13) | collective-permute-done | bytes 262176 | tf_op jit(solution)/shard_map/ppermute | solution.py:516
  57.2 1.3 %collective-permute-done.14.second_ref = bf16[2,16,32,128]{3,2,1,0:T(8,128)(2,1)S(1)} collective-permute-done((bf16[2,16,32,128]{3,2,1,0:T(8,128)(2,1)S(1)}, bf16[2,16,32,128]{3,2,1,0:T(8,128)(2,1)S(1)}, u32[]{:S(2)}, u32[]{:S(2)}) %collective-permute-start.14) | collective-permute-done | bytes 262176 | tf_op jit(solution)/shard_map/ppermute | solution.py:516
  58.5 0.1 shard_map.141
  58.6 0.6 collective-permute-start.15
  59.2 1.1 %collective-permute-start.10 = (bf16[144,512]{1,0:T(8,128)(2,1)S(1)}, bf16[144,512]{1,0:T(8,128)(2,1)S(1)}, u32[]{:S(2)}, u32[]{:S(2)}) collective-permute-start(bf16[144,512]{1,0:T(8,128)(2,1)S(1)} %get-tuple-element.99), channel_id=1, source_target_pairs={{0,16},{1,17},{2,18},{3,19},{4,20},{5,21},{6,22},{7,23},{8,24},{9,... | collective-permute-start | bytes 442376 | tf_op jit(solution)/shard_map/ppermute | solution.py:489
  60.3 3.8 %collective-permute-start.11 = (bf16[96,512]{1,0:T(8,128)(2,1)S(1)}, bf16[96,512]{1,0:T(8,128)(2,1)S(1)}, u32[]{:S(2)}, u32[]{:S(2)}) collective-permute-start(bf16[96,512]{1,0:T(8,128)(2,1)S(1)} %get-tuple-element.101), channel_id=1, source_target_pairs={{0,1},{1,2},{2,3},{3,4},{4,5},{5,6},{6,7},{7,8},{8,9},{9,10},{10,1... | collective-permute-start | bytes 294920 | tf_op jit(solution)/shard_map/ppermute | solution.py:489
  64.0 0.5 collective-permute-start.12
  64.5 0.8 shard_map.142
  65.3 6.3 %collective-permute-done.12.diag_ref = bf16[48,512]{1,0:T(8,128)(2,1)S(1)} collective-permute-done((bf16[48,512]{1,0:T(8,128)(2,1)S(1)}, bf16[48,512]{1,0:T(8,128)(2,1)S(1)}, u32[]{:S(2)}, u32[]{:S(2)}) %collective-permute-start.12) | collective-permute-done | bytes 49184 | tf_op jit(solution)/shard_map/ppermute | solution.py:489
  71.6 4.2 %all-to-all-start = ((bf16[32,32,128]{2,1,0:T(8,128)(2,1)}), bf16[32,32,128]{2,1,0:T(8,128)(2,1)S(1)}, u32[]{:S(2)}, u32[]{:S(2)}) async-start(bf16[32,32,128]{2,1,0:T(8,128)(2,1)} %shard_map.142), calls=%async_computation | async-start | bytes 524288 | tf_op jit(solution)/shard_map/all_to_all | solution.py:528
  75.8 1.6 %shard_map.140 = bf16[576,512]{1,0:T(8,128)(2,1)} custom-call(bf16[576,512]{1,0:T(8,128)(2,1)S(1)} %get-tuple-element.56.tok_ref, bf16[576,512]{1,0:T(8,128)(2,1)S(1)} %get-tuple-element.77.dsum_ref, bf16[432,512]{1,0:T(8,128)(2,1)S(1)} %get-tuple-element.93.main_ref, bf16[144,512]{1,0:T(8,128)(2,1)S(1)} %collective-permute-done.10.lat_ref, ...), custom_call_target="tpu_custom_call" | custom-call | flops 1000000000 | bytes 2000000 | tf_op jit(solution)/shard_map/pallas_call | solution.py:473
  77.4 11.6 %all-to-all-done.parts_ref = bf16[32,32,128]{2,1,0:T(8,128)(2,1)S(1)} async-done(((bf16[32,32,128]{2,1,0:T(8,128)(2,1)}), bf16[32,32,128]{2,1,0:T(8,128)(2,1)S(1)}, u32[]{:S(2)}, u32[]{:S(2)}) %all-to-all-start) | async-done | bytes 262176 | tf_op jit(solution)/shard_map/all_to_all | solution.py:528
  89.0 0.7 shard_map.143
  (28 shorter events, 0.1 us)
Async XLA Ops:
  0.6 1.1 %copy-start.3 = (bf16[12,48,512]{2,1,0:T(8,128)(2,1)S(1)}, bf16[12,48,512]{2,1,0:T(8,128)(2,1)}, u32[]{:S(2)}) copy-start(bf16[12,48,512]{2,1,0:T(8,128)(2,1)} %param.11) | copy-start | bytes 1769476
  1.7 13.5 %copy-start.2 = (bf16[512,1536]{1,0:T(8,128)(2,1)S(1)}, bf16[512,1536]{1,0:T(8,128)(2,1)}, u32[]{:S(2)}) copy-start(bf16[512,1536]{1,0:T(8,128)(2,1)} %refs_2_.1) | copy-start | bytes 4718596
  1.7 13.5 %copy-start.4 = (bf16[512,512]{1,0:T(8,128)(2,1)S(1)}, bf16[512,512]{1,0:T(8,128)(2,1)}, u32[]{:S(2)}) copy-start(bf16[512,512]{1,0:T(8,128)(2,1)} %refs_3_.1) | copy-start | bytes 1572868
  1.7 13.5 %copy-start.5 = (f32[2048]{0:T(1024)S(1)}, f32[2048]{0:T(1024)}, u32[]{:S(2)}) copy-start(f32[2048]{0:T(1024)} %param.15) | copy-start | bytes 24580
  1.7 13.5 %copy-start.6 = (f32[512]{0:T(512)S(1)}, f32[512]{0:T(512)}, u32[]{:S(2)}) copy-start(f32[512]{0:T(512)} %param.12) | copy-start | bytes 6148
  1.7 13.5 %copy-start.7 = (bf16[336,320]{1,0:T(8,128)(2,1)S(1)}, bf16[336,320]{1,0:T(8,128)(2,1)}, u32[]{:S(2)}) copy-start(bf16[336,320]{1,0:T(8,128)(2,1)} %constant.8.clone.refs_5_) | copy-start | bytes 645124
  1.7 13.5 %copy-start.8 = (bf16[320,336]{1,0:T(8,128)(2,1)S(1)}, bf16[320,336]{1,0:T(8,128)(2,1)}, u32[]{:S(2)}) copy-start(bf16[320,336]{1,0:T(8,128)(2,1)} %constant.11.clone.refs_1_) | copy-start | bytes 645124
  1.7 13.5 %copy-start.9 = (bf16[192,192]{1,0:T(8,128)(2,1)S(1)}, bf16[192,192]{1,0:T(8,128)(2,1)}, u32[]{:S(2)}) copy-start(bf16[192,192]{1,0:T(8,128)(2,1)} %constant.9.clone.refs_6_) | copy-start | bytes 221188
  1.7 13.5 %copy-start.10 = (bf16[192,192]{1,0:T(8,128)(2,1)S(1)}, bf16[192,192]{1,0:T(8,128)(2,1)}, u32[]{:S(2)}) copy-start(bf16[192,192]{1,0:T(8,128)(2,1)} %constant.10.clone.refs_7_) | copy-start | bytes 221188
  1.9 17.1 %collective-permute-start = (bf16[144,512]{1,0:T(8,128)(2,1)S(1)}, bf16[144,512]{1,0:T(8,128)(2,1)S(1)}, u32[]{:S(2)}, u32[]{:S(2)}) collective-permute-start(bf16[144,512]{1,0:T(8,128)(2,1)S(1)} %get-tuple-element.58), channel_id=1, source_target_pairs={{0,240},{1,241},{2,242},{3,243},{4,244},{5,245},{6,246},{7,247},{8... | collective-permute-start | bytes 442376 | tf_op jit(solution)/shard_map/ppermute | solution.py:489
  11.0 8.0 %collective-permute-start.1 = (bf16[96,512]{1,0:T(8,128)(2,1)S(1)}, bf16[96,512]{1,0:T(8,128)(2,1)S(1)}, u32[]{:S(2)}, u32[]{:S(2)}) collective-permute-start(bf16[96,512]{1,0:T(8,128)(2,1)S(1)} %get-tuple-element.59), channel_id=1, source_target_pairs={{0,15},{1,0},{2,1},{3,2},{4,3},{5,4},{6,5},{7,6},{8,7},{9,8},{10,9... | collective-permute-start | bytes 294920 | tf_op jit(solution)/shard_map/ppermute | solution.py:489
  12.0 7.0 %collective-permute-start.2 = (bf16[48,512]{1,0:T(8,128)(2,1)S(1)}, bf16[48,512]{1,0:T(8,128)(2,1)S(1)}, u32[]{:S(2)}, u32[]{:S(2)}) collective-permute-start(bf16[48,512]{1,0:T(8,128)(2,1)S(1)} %get-tuple-element.60), channel_id=1, source_target_pairs={{0,255},{1,240},{2,241},{3,242},{4,243},{5,244},{6,245},{7,246},{8... | collective-permute-start | bytes 147464 | tf_op jit(solution)/shard_map/ppermute | solution.py:489
  15.3 8.1 %copy-start = (bf16[2048,1024]{1,0:T(8,128)(2,1)S(1)}, bf16[2048,1024]{1,0:T(8,128)(2,1)}, u32[]{:S(2)}) copy-start(bf16[2048,1024]{1,0:T(8,128)(2,1)} %wmerge_ref.1) | copy-start | bytes 12582916
  19.0 4.4 %copy-start.1 = (bf16[6,24,1024]{2,1,0:T(8,128)(2,1)S(1)}, bf16[6,24,1024]{2,1,0:T(8,128)(2,1)}, u32[]{:S(2)}) copy-start(bf16[6,24,1024]{2,1,0:T(8,128)(2,1)} %param.17) | copy-start | bytes 884740
  22.9 10.9 %collective-permute-start.3 = (bf16[144,512]{1,0:T(8,128)(2,1)S(1)}, bf16[144,512]{1,0:T(8,128)(2,1)S(1)}, u32[]{:S(2)}, u32[]{:S(2)}) collective-permute-start(bf16[144,512]{1,0:T(8,128)(2,1)S(1)} %get-tuple-element.68), channel_id=1, source_target_pairs={{0,16},{1,17},{2,18},{3,19},{4,20},{5,21},{6,22},{7,23},{8,24},{9,... | collective-permute-start | bytes 442376 | tf_op jit(solution)/shard_map/ppermute | solution.py:489
  23.1 10.7 %collective-permute-start.4 = (bf16[96,512]{1,0:T(8,128)(2,1)S(1)}, bf16[96,512]{1,0:T(8,128)(2,1)S(1)}, u32[]{:S(2)}, u32[]{:S(2)}) collective-permute-start(bf16[96,512]{1,0:T(8,128)(2,1)S(1)} %get-tuple-element.69), channel_id=1, source_target_pairs={{0,1},{1,2},{2,3},{3,4},{4,5},{5,6},{6,7},{7,8},{8,9},{9,10},{10,1... | collective-permute-start | bytes 294920 | tf_op jit(solution)/shard_map/ppermute | solution.py:489
  23.1 10.6 %collective-permute-start.5 = (bf16[48,512]{1,0:T(8,128)(2,1)S(1)}, bf16[48,512]{1,0:T(8,128)(2,1)S(1)}, u32[]{:S(2)}, u32[]{:S(2)}) collective-permute-start(bf16[48,512]{1,0:T(8,128)(2,1)S(1)} %slice.12), channel_id=1, source_target_pairs={{0,17},{1,18},{2,19},{3,20},{4,21},{5,22},{6,23},{7,24},{8,25},{9,... | collective-permute-start | bytes 147464 | tf_op jit(solution)/shard_map/ppermute | solution.py:489
  35.0 7.8 %collective-permute-start.7 = (bf16[96,512]{1,0:T(8,128)(2,1)S(1)}, bf16[96,512]{1,0:T(8,128)(2,1)S(1)}, u32[]{:S(2)}, u32[]{:S(2)}) collective-permute-start(bf16[96,512]{1,0:T(8,128)(2,1)S(1)} %get-tuple-element.78), channel_id=1, source_target_pairs={{0,15},{1,0},{2,1},{3,2},{4,3},{5,4},{6,5},{7,6},{8,7},{9,8},{10,9... | collective-permute-start | bytes 294920 | tf_op jit(solution)/shard_map/ppermute | solution.py:489
  35.7 7.2 %collective-permute-start.6 = (bf16[144,512]{1,0:T(8,128)(2,1)S(1)}, bf16[144,512]{1,0:T(8,128)(2,1)S(1)}, u32[]{:S(2)}, u32[]{:S(2)}) collective-permute-start(bf16[144,512]{1,0:T(8,128)(2,1)S(1)} %slice.13), channel_id=1, source_target_pairs={{0,240},{1,241},{2,242},{3,243},{4,244},{5,245},{6,246},{7,247},{8... | collective-permute-start | bytes 442376 | tf_op jit(solution)/shard_map/ppermute | solution.py:489
  37.4 5.4 %collective-permute-start.8 = (bf16[48,512]{1,0:T(8,128)(2,1)S(1)}, bf16[48,512]{1,0:T(8,128)(2,1)S(1)}, u32[]{:S(2)}, u32[]{:S(2)}) collective-permute-start(bf16[48,512]{1,0:T(8,128)(2,1)S(1)} %slice.14), channel_id=1, source_target_pairs={{0,255},{1,240},{2,241},{3,242},{4,243},{5,244},{6,245},{7,246},{8... | collective-permute-start | bytes 147464 | tf_op jit(solution)/shard_map/ppermute | solution.py:489
  48.4 3.0 %collective-permute-start.9 = (bf16[4,32,32,128]{3,2,1,0:T(8,128)(2,1)S(1)}, bf16[4,32,32,128]{3,2,1,0:T(8,128)(2,1)S(1)}, u32[]{:S(2)}, u32[]{:S(2)}) collective-permute-start(bf16[4,32,32,128]{3,2,1,0:T(8,128)(2,1)S(1)} %get-tuple-element.96), channel_id=1, source_target_pairs={{0,1},{1,0},{2,3},{3,2},{4,5},{5,4},{6,7},{7,6},{8,9},{9,8},{10,11... | collective-permute-start | bytes 3145736 | tf_op jit(solution)/shard_map/ppermute | solution.py:519
  51.6 5.6 %collective-permute-start.13 = (bf16[2,16,32,128]{3,2,1,0:T(8,128)(2,1)S(1)}, bf16[2,16,32,128]{3,2,1,0:T(8,128)(2,1)S(1)}, u32[]{:S(2)}, u32[]{:S(2)}) collective-permute-start(bf16[2,16,32,128]{3,2,1,0:T(8,128)(2,1)S(1)} %get-tuple-element.103), channel_id=1, source_target_pairs={{0,2},{1,9},{2,0},{3,11},{4,6},{5,13},{6,4},{7,15},{8,10},{9,1},{1... | collective-permute-start | bytes 786440 | tf_op jit(solution)/shard_map/ppermute | solution.py:516
  51.7 6.8 %collective-permute-start.14 = (bf16[2,16,32,128]{3,2,1,0:T(8,128)(2,1)S(1)}, bf16[2,16,32,128]{3,2,1,0:T(8,128)(2,1)S(1)}, u32[]{:S(2)}, u32[]{:S(2)}) collective-permute-start(bf16[2,16,32,128]{3,2,1,0:T(8,128)(2,1)S(1)} %get-tuple-element.104), channel_id=1, source_target_pairs={{0,6},{1,137},{2,4},{3,139},{4,2},{5,141},{6,0},{7,143},{8,14},{9,... | collective-permute-start | bytes 786440 | tf_op jit(solution)/shard_map/ppermute | solution.py:516
  58.6 5.9 %collective-permute-start.15 = (bf16[16,32,128]{2,1,0:T(8,128)(2,1)S(1)}, bf16[16,32,128]{2,1,0:T(8,128)(2,1)S(1)}, u32[]{:S(2)}, u32[]{:S(2)}) collective-permute-start(bf16[16,32,128]{2,1,0:T(8,128)(2,1)S(1)} %get-tuple-element.106), channel_id=1, source_target_pairs={{0,6},{1,137},{2,4},{3,139},{4,2},{5,141},{6,0},{7,143},{8,14},{9,... | collective-permute-start | bytes 393224 | tf_op jit(solution)/shard_map/ppermute | solution.py:516
  59.2 5.3 %collective-permute-start.16 = (bf16[16,32,128]{2,1,0:T(8,128)(2,1)S(1)}, bf16[16,32,128]{2,1,0:T(8,128)(2,1)S(1)}, u32[]{:S(2)}, u32[]{:S(2)}) collective-permute-start(bf16[16,32,128]{2,1,0:T(8,128)(2,1)S(1)} %get-tuple-element.107), channel_id=1, source_target_pairs={{0,2},{1,9},{2,0},{3,11},{4,6},{5,13},{6,4},{7,15},{8,10},{9,1},{1... | collective-permute-start | bytes 393224 | tf_op jit(solution)/shard_map/ppermute | solution.py:516
  59.2 12.4 %collective-permute-start.10 = (bf16[144,512]{1,0:T(8,128)(2,1)S(1)}, bf16[144,512]{1,0:T(8,128)(2,1)S(1)}, u32[]{:S(2)}, u32[]{:S(2)}) collective-permute-start(bf16[144,512]{1,0:T(8,128)(2,1)S(1)} %get-tuple-element.99), channel_id=1, source_target_pairs={{0,16},{1,17},{2,18},{3,19},{4,20},{5,21},{6,22},{7,23},{8,24},{9,... | collective-permute-start | bytes 442376 | tf_op jit(solution)/shard_map/ppermute | solution.py:489
  60.3 11.3 %collective-permute-start.11 = (bf16[96,512]{1,0:T(8,128)(2,1)S(1)}, bf16[96,512]{1,0:T(8,128)(2,1)S(1)}, u32[]{:S(2)}, u32[]{:S(2)}) collective-permute-start(bf16[96,512]{1,0:T(8,128)(2,1)S(1)} %get-tuple-element.101), channel_id=1, source_target_pairs={{0,1},{1,2},{2,3},{3,4},{4,5},{5,6},{6,7},{7,8},{8,9},{9,10},{10,1... | collective-permute-start | bytes 294920 | tf_op jit(solution)/shard_map/ppermute | solution.py:489
  64.0 7.5 %collective-permute-start.12 = (bf16[48,512]{1,0:T(8,128)(2,1)S(1)}, bf16[48,512]{1,0:T(8,128)(2,1)S(1)}, u32[]{:S(2)}, u32[]{:S(2)}) collective-permute-start(bf16[48,512]{1,0:T(8,128)(2,1)S(1)} %slice.15), channel_id=1, source_target_pairs={{0,17},{1,18},{2,19},{3,20},{4,21},{5,22},{6,23},{7,24},{8,25},{9,... | collective-permute-start | bytes 147464 | tf_op jit(solution)/shard_map/ppermute | solution.py:489
  71.6 17.4 %all-to-all-start = ((bf16[32,32,128]{2,1,0:T(8,128)(2,1)}), bf16[32,32,128]{2,1,0:T(8,128)(2,1)S(1)}, u32[]{:S(2)}, u32[]{:S(2)}) async-start(bf16[32,32,128]{2,1,0:T(8,128)(2,1)} %shard_map.142), calls=%async_computation | async-start | bytes 524288 | tf_op jit(solution)/shard_map/all_to_all | solution.py:528

commit v2 on v1

v2 whole, which is shorter than its diff:
```python
import jax
import jax.numpy as jnp
import numpy as np
from jax import lax
from jax.experimental import pallas as pl
from jax.experimental.pallas import tpu as pltpu
from jax.sharding import PartitionSpec as P

D = 512
HEADS = 8
HEAD = D // HEADS
WIN_LAT = 6
WIN_LON = 12
SHIFT_LAT = 3
SHIFT_LON = 6
EPS = 1e-05

ROWS, COLS = 12, 48
BORDER = 8
TOKENS = ROWS * COLS
LEN = WIN_LAT * WIN_LON
PAD = 80
PER_BAND = COLS // WIN_LON
BAND = PER_BAND * PAD
WINDOWS = 2 * PER_BAND
TOP = SHIFT_LAT * COLS
EDGE = ROWS * BORDER
CORNER = SHIFT_LAT * BORDER
SIDE = WIN_LAT * BORDER
BAND_CELLS = WIN_LAT * COLS
GROUP = HEADS // 2
GROUP_WIDTH = GROUP * HEAD
LOCAL = PER_BAND - 1
INNER = LOCAL * PAD
REST = WINDOWS - LOCAL
OUTER = REST * PAD
PAIR_ROWS, PAIR_COLS = ROWS // 2, COLS // 2
PAIRS = PAIR_ROWS * PAIR_COLS
PAIR_TOP = 2 * PAIR_COLS
PAIR_SIDE = PAIR_ROWS * BORDER
PAIR_CORNER = 2 * BORDER
HELD = 10
WIDTH = WINDOWS * PAD
NEG = -1e30

f32 = jnp.float32
bf16 = jnp.bfloat16


def band_selector():
    pick = np.zeros((BAND, BAND_CELLS), np.float32)
    for win in range(PER_BAND):
        for i in range(WIN_LAT):
            for j in range(WIN_LON):
                pick[win * PAD + i * WIN_LON + j, i * COLS + win * WIN_LON + j] = 1.0
    return pick


def shift_selector(rows, cols, shift):
    pick = np.zeros((rows * cols, rows * (cols + BORDER)), np.float32)
    for i in range(rows):
        for j in range(cols):
            col = j + shift
            pick[i * cols + j, i * cols + col if col < cols else rows * cols + i * BORDER + col - cols] = 1.0
    return pick


def pair_selector():
    pick = np.zeros((4 * COLS, 4 * COLS), np.float32)
    quarter = COLS
    for a in range(2):
        for b in range(COLS // 2):
            for k, (i, j) in enumerate(((0, 0), (1, 0), (0, 1), (1, 1))):
                pick[k * quarter + a * (COLS // 2) + b, (2 * a + i) * COLS + 2 * b + j] = 1.0
    return pick


def dot(a, b):
    return lax.dot_general(a, b, (((1,), (0,)), ((), ())), preferred_element_type=f32)


def dot_nt(a, b):
    return lax.dot_general(a, b, (((1,), (1,)), ((), ())), preferred_element_type=f32)


def dot_tn(a, b):
    return lax.dot_general(a, b, (((0,), (0,)), ((), ())), preferred_element_type=f32)


def norm_parts(values):
    centred = values - jnp.mean(values, axis=-1, keepdims=True)
    scale = lax.rsqrt(jnp.mean(centred * centred, axis=-1, keepdims=True) + EPS)
    return centred * scale, scale


def band_sources(cells, lat, lon, diag):
    first = jnp.concatenate([cells[:BAND_CELLS], lon[CORNER : CORNER + SIDE].astype(bf16)], axis=0)
    beside = jnp.concatenate([lon[CORNER + SIDE : EDGE], diag[:CORNER]], axis=0).astype(bf16)
    second = jnp.concatenate([cells[BAND_CELLS:], lat, beside], axis=0)
    return first, second


def halves(block):
    return jnp.concatenate([block[:, :D], block[:, D:]], axis=0)


def head_masks():
    lane = lax.broadcasted_iota(jnp.int32, (1, GROUP_WIDTH), 1) // HEAD
    return [(lane == h).astype(f32).astype(bf16) for h in range(GROUP)]


def spread_heads(block, masks):
    return jnp.concatenate([block * m for m in masks], axis=0)


def per_head(stacked, block):
    first = lax.broadcasted_iota(jnp.int32, (1, 2 * HEAD), 1) < HEAD
    all_heads = dot_tn(stacked, block)
    out = []
    for pair in range(GROUP // 2):
        part = all_heads[:, pair * 2 * HEAD : (pair + 1) * 2 * HEAD]
        at = pair * 2 * PAD
        out.append(jnp.where(first, part[at : at + PAD], part[at + PAD : at + 2 * PAD]))
    return jnp.concatenate(out, axis=1)


def last_band():
    at_end = lax.axis_index("lat") == lax.axis_size("lat") - 1
    return jnp.where(at_end, f32(1), f32(0))


def halves_apart():
    shape = (LEN, GROUP * PAD)
    key = lax.broadcasted_iota(jnp.int32, shape, 0)
    query = lax.rem(lax.broadcasted_iota(jnp.int32, shape, 1), PAD)
    return jnp.where((key < LEN // 2) != (query < LEN // 2), f32(NEG), f32(0)) * last_band()


def attend(windows, qkv_ref, mixed_ref, probs_ref):
    masks = [m * HEAD ** (-0.5) for m in head_masks()]
    apart = halves_apart() if any(windows) else None
    for win, wraps in enumerate(windows):
        rows = pl.ds(win * PAD, PAD)
        for g in range(2):
            at = g * GROUP_WIDTH
            queries = spread_heads(qkv_ref[rows, at : at + GROUP_WIDTH], masks)
            keys = qkv_ref[rows, D + at : D + at + GROUP_WIDTH]
            values = qkv_ref[rows, 2 * D + at : 2 * D + at + GROUP_WIDTH]
            scores = dot_nt(keys, queries)[:LEN]
            if wraps:
                scores = scores + apart
            weights = jnp.exp(scores - jnp.max(scores, axis=0, keepdims=True))
            probs = weights * (1.0 / jnp.sum(weights, axis=0, keepdims=True))
            probs = jnp.concatenate([probs, jnp.zeros((PAD - LEN, GROUP * PAD), f32)], axis=0)
            probs_ref[win, g] = probs
            mixed_ref[rows, at : at + GROUP_WIDTH] = per_head(probs.astype(bf16), values).astype(bf16)


def attend_back(windows, dmix_ref, dqkv_ref, offset):
    masks = head_masks()
    scaled = [m * HEAD ** (-0.5) for m in masks]
    for win, (qkv_ref, probs_ref, place) in enumerate(windows):
        rows = pl.ds(place * PAD, PAD)
        out = pl.ds(offset + win * PAD, PAD)
        for g in range(2):
            at = g * GROUP_WIDTH
            queries = spread_heads(qkv_ref[rows, at : at + GROUP_WIDTH], scaled)
            keys = qkv_ref[rows, D + at : D + at + GROUP_WIDTH]
            values = qkv_ref[rows, 2 * D + at : 2 * D + at + GROUP_WIDTH]
            above = spread_heads(dmix_ref[pl.ds(win * PAD, PAD), at : at + GROUP_WIDTH], masks)
            probs = probs_ref[place, g]
            d_probs = dot_nt(values, above)
            along = jnp.sum(probs * d_probs, axis=0, keepdims=True)
            d_scores = (probs * (d_probs - along)).astype(bf16)
            d_queries = per_head(d_scores, keys) * HEAD ** (-0.5)
            d_keys = dot(d_scores, queries)
            d_values = dot(probs.astype(bf16), above)
            dqkv_ref[out, at : at + GROUP_WIDTH] = d_queries.astype(bf16)
            dqkv_ref[out, D + at : D + at + GROUP_WIDTH] = d_keys.astype(bf16)
            dqkv_ref[out, 2 * D + at : 2 * D + at + GROUP_WIDTH] = d_values.astype(bf16)


def border_kernel(tok_ref, g_ref, own_ref, own_g_ref, top_ref, edge_ref, corner_ref, sem):
    copies = [
        pltpu.make_async_copy(tok_ref, own_ref, sem.at[0]),
        pltpu.make_async_copy(g_ref, own_g_ref, sem.at[1]),
    ]
    for copy in copies:
        copy.start()
    for copy in copies:
        copy.wait()
    edge = [own_ref[row * COLS : row * COLS + 16].astype(f32)[:BORDER] for row in range(ROWS)]
    cots = own_g_ref[...].astype(f32)
    side = [cots[row * PAIR_COLS : row * PAIR_COLS + BORDER] for row in range(PAIR_ROWS)]
    top_ref[:TOP] = own_ref[:TOP]
    top_ref[TOP:] = halves(own_g_ref[:PAIR_TOP])
    edge_ref[:EDGE] = jnp.concatenate(edge, axis=0).astype(bf16)
    edge_ref[EDGE:] = halves(jnp.concatenate(side, axis=0).astype(bf16))
    corner_ref[:SIDE] = jnp.concatenate(edge[:WIN_LAT], axis=0).astype(bf16)
    corner_ref[SIDE:] = halves(jnp.concatenate(side[:2], axis=0).astype(bf16))


def inner_kernel(tok_ref, *refs):
    held, got = refs[:HELD], refs[HELD : 2 * HELD]
    cells_ref, xs_ref, qkv_ref, mixed_ref, probs_ref, att_ref, sem = refs[2 * HELD :]
    copies = [pltpu.make_async_copy(a, b, sem.at[i]) for i, (a, b) in enumerate(zip(held, got))]
    for copy in copies:
        copy.start()
    gain_ref, pick_ref, wqkv_ref, wproj_ref = got[:4]
    normed = norm_parts(tok_ref[TOP:].astype(f32))[0]
    for copy in copies:
        copy.wait()
    cells_ref[...] = (normed * gain_ref[...]).astype(bf16)
    xs_ref[...] = dot(pick_ref[:INNER, :BAND_CELLS], cells_ref[:BAND_CELLS]).astype(bf16)
    qkv_ref[...] = dot(xs_ref[...], wqkv_ref[...]).astype(bf16)
    attend([False] * LOCAL, qkv_ref, mixed_ref, probs_ref)
    att_ref[...] = dot(mixed_ref[...], wproj_ref[...]).astype(bf16)


def outer_kernel(
    tok_ref, cells_ref, lat_ref, lon_ref, diag_ref, gain_ref, wqkv_ref, wproj_ref, pick_ref, shift_ref, cells_pick_ref,
    att0_ref,
    xs_ref, qkv_ref, mixed_ref, probs_ref, tok_out_ref, summed_ref, row_ref,
    att_ref,
):
    def normed(values):
        return norm_parts(values)[0] * gain_ref[...]

    lat, lon, diag = lat_ref[:TOP], lon_ref[:EDGE].astype(f32), diag_ref[:SIDE].astype(f32)
    first, second = band_sources(cells_ref[...], normed(lat.astype(f32)).astype(bf16), normed(lon), normed(diag))
    xs_ref[:PAD] = dot(pick_ref[INNER:], first).astype(bf16)
    xs_ref[PAD:] = dot(pick_ref[...], second).astype(bf16)
    qkv_ref[...] = dot(xs_ref[...], wqkv_ref[...]).astype(bf16)
    attend([False] + [True] * PER_BAND, qkv_ref, mixed_ref, probs_ref)
    att_ref[:INNER] = att0_ref[...]
    att_ref[INNER:] = dot(mixed_ref[...], wproj_ref[...]).astype(bf16)
    for band, source in enumerate(band_sources(tok_ref[TOP:], lat, lon, diag)):
        rows = pl.ds(band * BAND_CELLS, BAND_CELLS)
        tokens = dot(shift_ref[...], source)
        added = dot(cells_pick_ref[...], att_ref[pl.ds(band * BAND, BAND)])
        tok_out_ref[rows] = tokens.astype(bf16)
        summed_ref[rows] = (tokens + added).astype(bf16)
    row_ref[...] = summed_ref[:COLS]


def cotangent_kernel(
    g_ref, lat_ref, lon_ref, diag_ref, gain_ref, shift_ref, wmerge_ref, out_ref, weights_ref, sem
):
    copy = pltpu.make_async_copy(wmerge_ref, weights_ref, sem)
    copy.start()
    parts = []
    for half in range(2):
        lat = lat_ref[TOP + half * PAIR_TOP : TOP + (half + 1) * PAIR_TOP]
        at = EDGE + half * PAIR_SIDE
        lon = lon_ref[at + PAIR_CORNER : at + PAIR_SIDE]
        diag = diag_ref[SIDE + half * PAIR_CORNER : SIDE + (half + 1) * PAIR_CORNER]
        own = g_ref[PAIR_TOP:, half * D : (half + 1) * D]
        parts.append(dot(shift_ref[...], jnp.concatenate([own, lat, lon, diag], axis=0)).astype(bf16))
    cots = jnp.concatenate(parts, axis=1)
    copy.wait()
    for k in range(4):
        out_ref[k] = dot_nt(cots, weights_ref[k * D : (k + 1) * D]) * gain_ref[k]


def pair_kernel(
    summed_ref, row_ref, gain_ref, cot_ref, pair_ref, unpair_ref,
    dsum_ref, out_row_ref, normed_ref,
    members_ref,
):
    quarter = COLS
    for part in range(3):
        first = COLS + part * 4 * COLS
        if part < 2:
            summed = summed_ref[first : first + 4 * COLS]
        else:
            summed = jnp.concatenate([summed_ref[first:], row_ref[...]], axis=0)
        paired = dot(pair_ref[...], summed)
        for k in range(4):
            members_ref[k, pl.ds(part * quarter, quarter)] = paired[k * quarter : (k + 1) * quarter]
    width = 4 * D
    total = sum(jnp.sum(members_ref[k], axis=-1, keepdims=True) for k in range(4))
    center = total / width
    for k in range(4):
        members_ref[k] = members_ref[k] - center
    spread = sum(jnp.sum(members_ref[k] * members_ref[k], axis=-1, keepdims=True) for k in range(4)) / width
    scale = lax.rsqrt(spread + EPS)
    for k in range(4):
        members_ref[k] = members_ref[k] * scale
        normed_ref[k] = (members_ref[k] * gain_ref[k]).astype(bf16)
    flat = sum(jnp.sum(cot_ref[k], axis=-1, keepdims=True) for k in range(4)) / width
    along = sum(jnp.sum(cot_ref[k] * members_ref[k], axis=-1, keepdims=True) for k in range(4)) / width
    for k in range(4):
        members_ref[k] = (cot_ref[k] - flat - members_ref[k] * along) * scale
    for part in range(3):
        rows = pl.ds(part * quarter, quarter)
        block = jnp.concatenate([members_ref[k, rows].astype(bf16) for k in range(4)], axis=0)
        dsum_ref[pl.ds(part * 4 * COLS, 4 * COLS)] = dot(unpair_ref[...], block).astype(bf16)
    out_row_ref[...] = dsum_ref[TOKENS - COLS :]


def merge_kernel(normed_ref, wmerge_ref, unshift_ref, main_ref, lat_ref, lon_ref, diag_ref):
    total = dot(normed_ref[0], wmerge_ref[:D])
    for k in range(1, 4):
        total = total + dot(normed_ref[k], wmerge_ref[k * D : (k + 1) * D])
    pairs = dot(unshift_ref[...], total.astype(bf16)).astype(bf16)
    main_ref[...] = pairs[: PAIRS - PAIR_TOP]
    lat_ref[...] = halves(pairs[PAIRS - PAIR_TOP : PAIRS])
    lon_ref[...] = halves(pairs[PAIRS : PAIRS + PAIR_SIDE - PAIR_CORNER])
    diag_ref[...] = halves(pairs[PAIRS + PAIR_SIDE - PAIR_CORNER :])


def inner_back_kernel(
    dsum_ref, qkv_ref, probs_ref, wproj_ref, pick_ref, xs0_ref, xs_ref, mixed0_ref, mixed_ref,
    up_ref, dqkv_ref, xst_ref, mixt_ref,
    dmix_ref,
):
    xst_ref[...] = jnp.concatenate([xs0_ref[...], xs_ref[...]], axis=0).T
    mixt_ref[...] = jnp.concatenate([mixed0_ref[...], mixed_ref[...]], axis=0).T
    up_ref[...] = dot(pick_ref[...], dsum_ref[BAND_CELLS - COLS : TOKENS - COLS]).astype(bf16)
    dmix_ref[...] = dot_nt(up_ref[...], wproj_ref[...]).astype(bf16)
    attend_back([(qkv_ref, probs_ref, win) for win in range(1, REST)], dmix_ref, dqkv_ref, 0)


def outer_back_kernel(
    dsum_ref, row_ref, xst_ref, mixt_ref, up1_ref, dqkv1_ref, qkv0_ref, probs0_ref, qkv_ref, probs_ref,
    wproj_ref, pick_ref,
    dqkv_ref, keep_ref, send_ref,
    up_ref, dmix_ref,
):
    cells = jnp.concatenate([row_ref[...], dsum_ref[: BAND_CELLS - COLS]], axis=0)
    up_ref[:BAND] = dot(pick_ref[...], cells).astype(bf16)
    up_ref[BAND:] = up1_ref[...]
    dqkv_ref[BAND:] = dqkv1_ref[...]
    dmix_ref[...] = dot_nt(up_ref[:BAND], wproj_ref[...]).astype(bf16)
    windows = [(qkv0_ref, probs0_ref, win) for win in range(LOCAL)] + [(qkv_ref, probs_ref, 0)]
    attend_back(windows, dmix_ref, dqkv_ref, 0)
    lat_at, lon_at = lax.axis_index("lat"), lax.axis_index("lon")
    even_core = lax.rem(lon_at, 2) == 0
    my_x = lax.rem(lax.div(lon_at, 2), 4)
    my_y = lax.div(lat_at, 8) * 2 + lax.div(lon_at, 8)
    x_steps = [lax.bitwise_xor(my_x, jnp.int32(i)) for i in range(4)]
    y_steps = [lax.bitwise_xor(my_y, jnp.int32(i)) for i in range(4)]
    for col in range(8):
        if col < 6:
            grad = dot(xst_ref[...], dqkv_ref[:, col * 256 : (col + 1) * 256])
        else:
            grad = dot(mixt_ref[...], up_ref[:, (col - 6) * 256 : (col - 5) * 256])
        even, odd = grad[:, :128], grad[:, 128:]
        kept = jnp.where(even_core, even, odd).astype(bf16)
        sent = jnp.where(even_core, odd, even).astype(bf16)
        low, x = divmod(col, 4)
        for lat in range(16):
            high, z = divmod(lat, 8)
            y = high * 2 + low
            rows = slice(lat * 32, (lat + 1) * 32)
            on_even = x_steps[x], lat * 2 + low
            on_odd = y_steps[y], z * 4 + x
            mine = [jnp.where(even_core, a, b) for a, b in zip(on_even, on_odd)]
            other = [jnp.where(even_core, b, a) for a, b in zip(on_even, on_odd)]
            keep_ref[mine[0], mine[1]] = kept[rows]
            send_ref[other[0], other[1]] = sent[rows]


def cells_back_kernel(
    dqkv_ref, wqkv_ref, cells_pick_ref, unshift_ref, tok_ref, dsum_ref, row_ref, gain_ref, m_lat_ref, m_lon_ref, m_diag_ref,
    main_ref, lat_ref, lon_ref, diag_ref,
    dx_ref,
):
    dx_ref[...] = dot_nt(dqkv_ref[...], wqkv_ref[...]).astype(bf16)
    for band in range(2):
        if band == 0:
            above = jnp.concatenate([row_ref[...], dsum_ref[: BAND_CELLS - COLS]], axis=0)
        else:
            above = dsum_ref[BAND_CELLS - COLS : TOKENS - COLS]
        cot = dot(cells_pick_ref[...], dx_ref[pl.ds(band * BAND, BAND)]) * gain_ref[...]
        normed, scale = norm_parts(tok_ref[pl.ds(band * BAND_CELLS, BAND_CELLS)].astype(f32))
        flat = jnp.mean(cot, axis=-1, keepdims=True)
        along = jnp.mean(cot * normed, axis=-1, keepdims=True)
        grads = (above.astype(f32) + (cot - flat - normed * along) * scale).astype(bf16)
        cells = dot(unshift_ref[...], grads).astype(bf16)
        if band == 0:
            main_ref[:BAND_CELLS] = cells[:BAND_CELLS]
        else:
            main_ref[BAND_CELLS:] = cells[: BAND_CELLS - TOP]
            lat_ref[:TOP] = cells[BAND_CELLS - TOP : BAND_CELLS]
            diag_ref[:SIDE] = cells[BAND_CELLS:]
        lon_ref[band * SIDE : (band + 1) * SIDE] = cells[BAND_CELLS:]
    lat_ref[TOP:] = m_lat_ref[...]
    lon_ref[EDGE:] = m_lon_ref[...]
    diag_ref[SIDE:] = m_diag_ref[...]


def fill_edge(field, side, rows, cols):
    width = field.shape[-1]
    field, side = field.astype(f32).reshape(rows, cols, width), side.astype(f32).reshape(rows, BORDER, width)
    first = field[:, :BORDER] + side
    return jnp.concatenate([first, field[:, BORDER:]], axis=1).reshape(rows * cols, width).astype(bf16)


def own_cells_kernel(main_ref, lat_ref, lon_ref, diag_ref, m_main_ref, tokens_ref, merged_ref):
    corner = diag_ref[:SIDE].astype(f32)[SIDE - CORNER :]
    beside = lon_ref[:EDGE].astype(f32)[: EDGE - CORNER]
    tokens_ref[:TOP] = fill_edge(lat_ref[:TOP], corner, SHIFT_LAT, COLS)
    tokens_ref[TOP:] = fill_edge(main_ref[...], beside, ROWS - SHIFT_LAT, COLS)
    side_rows = PAIR_SIDE - PAIR_CORNER
    for half in range(2):
        cols = pl.ds(half * D, D)
        lat = lat_ref[TOP + half * PAIR_TOP : TOP + (half + 1) * PAIR_TOP]
        lon = lon_ref[EDGE + half * side_rows : EDGE + (half + 1) * side_rows]
        diag = diag_ref[SIDE + half * PAIR_CORNER : SIDE + (half + 1) * PAIR_CORNER]
        merged_ref[:PAIR_TOP, cols] = fill_edge(lat, diag, 2, PAIR_COLS)
        merged_ref[PAIR_TOP:, cols] = fill_edge(m_main_ref[:, cols], lon, PAIR_ROWS - 2, PAIR_COLS)


def add_kernel(a_ref, b_ref, own_ref, later_ref, first_ref, second_ref):
    half = own_ref.shape[0] // 2

    def both(k, rows):
        return (a_ref[k, rows].astype(f32) + b_ref[k, rows].astype(f32)).astype(bf16)

    upper, lower = pl.ds(0, half), pl.ds(half, half)
    own_ref[...] = both(0, pl.ds(0, 2 * half))
    first_ref[0], first_ref[1] = both(1, upper), both(2, upper)
    second_ref[0], second_ref[1] = both(3, lower), both(2, lower)
    later_ref[0], later_ref[1] = both(3, upper), both(1, lower)


def relay_kernel(own_ref, later_ref, first_ref, second_ref, out_ref, to_third_ref, to_first_ref):
    half = own_ref.shape[0] // 2

    def both(a, b):
        return (a.astype(f32) + b.astype(f32)).astype(bf16)

    out_ref[:half] = both(own_ref[:half], first_ref[0])
    out_ref[half:] = both(own_ref[half:], second_ref[0])
    to_third_ref[...] = both(later_ref[0], first_ref[1])
    to_first_ref[...] = both(later_ref[1], second_ref[1])


def join_kernel(own_ref, upper_ref, lower_ref, out_ref):
    half = own_ref.shape[0] // 2
    out_ref[:half] = (own_ref[:half].astype(f32) + upper_ref[...].astype(f32)).astype(bf16)
    out_ref[half:] = (own_ref[half:].astype(f32) + lower_ref[...].astype(f32)).astype(bf16)


def sum_kernel(parts_ref, out_ref):
    total = parts_ref[0].astype(f32)
    for i in range(1, parts_ref.shape[0]):
        total = total + parts_ref[i].astype(f32)
    out_ref[...] = total.astype(out_ref.dtype)


def call(kernel, outs, scratch=(), places=None, limit=20):
    spaces = {} if places is None else {
        "in_specs": [pl.BlockSpec(memory_space=(pltpu.VMEM, pl.ANY, pltpu.HBM)[p]) for p in places]
    }
    return pl.pallas_call(
        kernel,
        out_shape=[jax.ShapeDtypeStruct(s, t) for s, t in outs],
        scratch_shapes=[pltpu.VMEM(*s) if isinstance(s, tuple) else s for s in scratch],
        cost_estimate=pl.CostEstimate(flops=10**9, bytes_accessed=2 * 10**6, transcendentals=0),
        compiler_params=pltpu.CompilerParams(vmem_limit_bytes=limit * 1024 * 1024),
        **spaces,
    )


def saved(count):
    rows = count * PAD
    return [((rows, D), bf16), ((rows, 3 * D), bf16), ((rows, D), bf16), ((count, 2, PAD, GROUP * PAD), f32)]


def after(value, *others):
    return lax.optimization_barrier((value, *others))[0]


def chain(tok, gain, w_qkv, w_proj, gain_merge, w_merge, g_merged, fetch, hand_on, up, down):
    tok, g_merged, top, edge, corner = call(
        border_kernel,
        [
            ((TOKENS, D), bf16), ((PAIRS, 2 * D), bf16),
            ((TOP + 2 * PAIR_TOP, D), bf16), ((EDGE + 2 * PAIR_SIDE, D), bf16), ((SIDE + 2 * PAIR_CORNER, D), bf16),
        ],
        [pltpu.SemaphoreType.DMA((2,))],
        [2, 2],
    )(tok, g_merged)
    beside = fetch(top, edge, corner)
    pair, band = pair_selector(), band_selector()
    shift = shift_selector(WIN_LAT, COLS, SHIFT_LON)
    pair_shift = shift_selector(PAIR_ROWS, PAIR_COLS, SHIFT_LON // 2)
    held = [gain, jnp.asarray(band @ shift, bf16), w_qkv, w_proj, gain_merge]
    held += [jnp.asarray(c, bf16) for c in (shift, band.T, pair, pair.T, pair_shift)]
    got = call(
        inner_kernel,
        [(h.shape, h.dtype) for h in held] + [((TOKENS - TOP, D), bf16)] + saved(LOCAL) + [((INNER, D), bf16)],
        [pltpu.SemaphoreType.DMA((HELD,))],
        [0] + [1] * HELD,
    )(tok, *held)
    gain, pick, w_qkv, w_proj, gain_merge, shift, cells_pick, pair, unpair, pair_shift = got[:HELD]
    cells, xs0, qkv0, mixed0, probs0, att0 = got[HELD:]
    xs1, qkv1, mixed1, probs1, tok, summed, row = call(
        outer_kernel,
        saved(REST) + [((TOKENS, D), bf16), ((TOKENS, D), bf16), ((COLS, D), bf16)],
        [((WIDTH, D), bf16)],
    )(tok, cells, *beside, gain, w_qkv, w_proj, pick, shift, cells_pick, att0)
    last = up(row)
    cots, w_merge = call(
        cotangent_kernel,
        [((4, PAIRS, D), f32), ((4 * D, 2 * D), bf16)],
        [pltpu.SemaphoreType.DMA],
        [0] * 6 + [1],
    )(after(g_merged, row), *beside, gain_merge, pair_shift, w_merge)
    d_summed, row, merge_normed = call(
        pair_kernel,
        [((TOKENS, D), bf16), ((COLS, D), bf16), ((4, PAIRS, D), bf16)],
        [((4, PAIRS, D), f32)],
    )(summed, last, gain_merge, cots, pair, unpair)
    first = down(row)
    band = jnp.asarray(band_selector(), bf16)
    unshift = jnp.asarray(shift_selector(WIN_LAT, COLS, SHIFT_LON).T, bf16)
    pair_unshift = jnp.asarray(shift_selector(PAIR_ROWS, PAIR_COLS, SHIFT_LON // 2).T, bf16)
    up1, dqkv1, xst, mixt = call(
        inner_back_kernel,
        [((BAND, D), bf16), ((BAND, 3 * D), bf16), ((D, WIDTH), bf16), ((D, WIDTH), bf16)],
        [((BAND, D), bf16)],
    )(d_summed, qkv1, probs1, w_proj, band, xs0, xs1, mixed0, mixed1)
    m_main, m_lat, m_lon, m_diag = call(
        merge_kernel,
        [
            ((PAIRS - PAIR_TOP, 2 * D), bf16), ((2 * PAIR_TOP, D), bf16),
            ((2 * (PAIR_SIDE - PAIR_CORNER), D), bf16), ((2 * PAIR_CORNER, D), bf16),
        ],
    )(merge_normed, w_merge, pair_unshift)
    dqkv, keep, sent = call(
        outer_back_kernel,
        [((WIDTH, 3 * D), bf16), ((4, 32, 32, 128), bf16), ((4, 32, 32, 128), bf16)],
        [((WIDTH, D), bf16), ((BAND, D), bf16)],
    )(d_summed, first, xst, mixt, up1, dqkv1, qkv0, probs0, qkv1, probs1, w_proj, band)

    def cells_back(ready):
        return call(
            cells_back_kernel,
            [
                ((TOKENS - TOP, D), bf16), ((TOP + 2 * PAIR_TOP, D), bf16),
                ((EDGE + 2 * (PAIR_SIDE - PAIR_CORNER), D), bf16), ((SIDE + 2 * PAIR_CORNER, D), bf16),
            ],
            [((WIDTH, D), bf16)],
        )(after(dqkv, ready), w_qkv, cells_pick, unshift, tok, d_summed, first, gain, m_lat, m_lon, m_diag)

    def finish(main, *pieces):
        grad_tokens, merged = call(own_cells_kernel, [((TOKENS, D), bf16), ((PAIRS, 2 * D), bf16)])(
            main, *hand_on(*pieces), m_main
        )
        return merged, grad_tokens

    return cells_back, finish, keep, sent, m_lat


def solution(mesh):
    lats, lons = mesh.shape["lat"], mesh.shape["lon"]
    count = lats * lons

    def send(block, down, right):
        route = [
            (i, (i // lons + down) % lats * lons + (i % lons + right) % lons) for i in range(count)
        ]
        return lax.ppermute(block, ("lat", "lon"), route)

    def fetch(top, edge, corner):
        return send(top, -1, 0), send(edge, 0, -1), send(corner, -1, -1)

    def hand_on(lat, lon, diag):
        return send(lat, 1, 0), send(lon, 0, 1), send(diag, 1, 1)

    def place(i):
        lat, lon = divmod(i, lons)
        return lat // 8, lat % 8, lon // 8, lon // 2 % 4, lon % 2

    def across(i, step):
        high, z, low, x, core = place(i)
        if core:
            high, low = divmod((high * 2 + low) ^ step, 2)
        else:
            x = x ^ step
        return (high * 8 + z) * lons + low * 8 + x * 2 + core

    rest = {}
    for i in range(count):
        high, z, low, x, core = place(i)
        rest.setdefault((core, high * 2 + low if core else x), []).append(i)
    rest = list(rest.values())

    def swap(block, step):
        return lax.ppermute(block, ("lat", "lon"), [(i, across(i, step)) for i in range(count)])

    def reduce_across(keep, sent, ready, cells_back):
        other = lax.ppermute(sent, ("lat", "lon"), [(i, i ^ 1) for i in range(count)])
        whole, pair, half = ((32, 32, 128), bf16), ((2, 16, 32, 128), bf16), ((16, 32, 128), bf16)
        own, later, first, second = call(add_kernel, [whole, pair, pair, pair])(keep, after(other, ready))
        first, second = swap(first, 1), swap(second, 3)
        pieces = cells_back(later)
        own, to_third, to_first = call(relay_kernel, [whole, half, half])(own, after(later, *pieces), first, second)
        sums = call(join_kernel, [whole])(own, swap(to_third, 3), swap(to_first, 1))[0]
        return sums, [after(piece, sums) for piece in pieces]

    def reduce_rest(sums):
        parts = lax.all_to_all(sums, ("lat", "lon"), 0, 0, axis_index_groups=rest, tiled=True)
        return call(sum_kernel, [((32, 128), f32)])(parts)[0]

    def body(tokens, gain_attn, w_qkv, w_proj, gain_merge, w_merge, g_merged):
        cells_back, finish, keep, sent, ready = chain(
            tokens.reshape(TOKENS, D), gain_attn.reshape(1, D), w_qkv, w_proj, gain_merge.reshape(4, 1, D),
            w_merge, g_merged.reshape(PAIRS, 2 * D), fetch, hand_on,
            lambda row: send(row, -1, 0), lambda row: send(row, 1, 0),
        )
        sums, pieces = reduce_across(keep, sent, ready, cells_back)
        grad_weights = reduce_rest(sums)
        merged, grad_tokens = finish(*pieces)
        return (
            merged.reshape(ROWS // 2, COLS // 2, 2 * D),
            grad_tokens.reshape(ROWS, COLS, D),
            grad_weights,
        )

    return jax.shard_map(
        body,
        mesh=mesh,
        in_specs=(P("lat", "lon", None), P(), P(), P(), P(), P(), P("lat", "lon", None)),
        out_specs=(P("lat", "lon", None), P("lat", "lon", None), P("lat", "lon")),
        check_vma=False,
    )
```

time: 89.9 us -> 88.4 us (0.983)
  waiting for transfers between devices: 34.6 us -> 25.4 us
  starting transfers between devices: 27.8 us -> 33.9 us
  local copies, waits for them, and re-layouts: 1.14 us -> 2.09 us
    all_to_all x1, waiting for transfers between devices: 11.6 us -> 0.01 us  [reduce_rest(): lax.all_to_all(sums, ('lat', 'lon'), 0, 0, axis_index_groups=rest, tiled=...]
    all_to_all x1, starting transfers between devices: 4.17 us -> 7.8 us  [reduce_rest(): lax.all_to_all(sums, ('lat', 'lon'), 0, 0, axis_index_groups=rest, tiled=...]
    ppermute x4, waiting for transfers between devices: 6.24 us -> 8.34 us  [swap(): lax.ppermute(block, ('lat', 'lon'), [(i, across(i, step)) for i in range(...]
    ppermute x12 -> x8, starting transfers between devices: 22 us -> 24.1 us  [send(): return lax.ppermute(block, ('lat', 'lon'), route)]
    unnamed x22 -> x32, local copies, waits for them, and re-layouts: 1.11 us -> 2.09 us
    ppermute x12 -> x8, waiting for transfers between devices: 15.6 us -> 15.7 us  [send(): return lax.ppermute(block, ('lat', 'lon'), route)]
  transfers between devices with their start and end apart: 18 -> 14, of which waited for: 7 -> 6; matrix products, arithmetic and copies ran while one was open for 0% -> 0% of each run, Pallas kernels for 15% -> 16%
where the time goes in v2:
time: 88.4 us; the launch traced here: 88.1 us
  starting transfers between devices  33.9 us (38%)
  Pallas kernels  25.9 us (29%)
  waiting for transfers between devices  25.4 us (29%)
  local copies, waits for them, and re-layouts  2.09 us (2%)
  between operations  0.9 us (1%)
    ppermute x8, starting transfers between devices, send(): return lax.ppermute(block, ('lat', 'lon'), route)  24.1 us
    ppermute x8, waiting for transfers between devices, send(): return lax.ppermute(block, ('lat', 'lon'), route)  15.7 us
    ppermute x4, waiting for transfers between devices, swap(): lax.ppermute(block, ('lat', 'lon'), [(i, across(i, step)) for i in range(...  8.34 us
    all_to_all x1, starting transfers between devices, reduce_rest(): lax.all_to_all(sums, ('lat', 'lon'), 0, 0, axis_index_groups=rest, tiled=...  7.8 us
    pallas_call x1, Pallas kernels, chain(): call(outer_back_kernel, [((WIDTH, 3 * D), bf16), ((4, 32, 32, 128), bf16)...  4.89 us
    pallas_call x1, Pallas kernels, chain(): call(inner_kernel, [(h.shape, h.dtype) for h in held] + [((TOKENS - TOP,...  4.15 us
    pallas_call x1, Pallas kernels, chain(): call(outer_kernel, saved(REST) + [((TOKENS, D), bf16), ((TOKENS, D), bf16...  4.05 us
    pallas_call x1, Pallas kernels, chain(): call(inner_back_kernel, [((BAND, D), bf16), ((BAND, 3 * D), bf16), ((D, W...  3.1 us
  transfers between devices with their start and end apart: 14, of which 6 were waited for; matrix products, arithmetic and copies ran while one was open for 0% of the time, Pallas kernels for 16%

profile of v2, /device:TPU:1, one launch (start us, length us, event | category | flops | bytes accessed | tf_op | source)
XLA Modules:
  0.0 88.1 jit_solution(4953568417326652491)
XLA Ops:
  0.6 1.1 %copy-done.5 = bf16[12,48,512]{2,1,0:T(8,128)(2,1)S(1)} copy-done((bf16[12,48,512]{2,1,0:T(8,128)(2,1)S(1)}, bf16[12,48,512]{2,1,0:T(8,128)(2,1)}, u32[]{:S(2)}) %copy-start.5) | copy-done | bytes 589848
  1.7 1.0 %copy-done.7 = bf16[6,24,1024]{2,1,0:T(8,128)(2,1)S(1)} copy-done((bf16[6,24,1024]{2,1,0:T(8,128)(2,1)S(1)}, bf16[6,24,1024]{2,1,0:T(8,128)(2,1)}, u32[]{:S(2)}) %copy-start.7) | copy-done | bytes 294936
  2.7 0.0 copy-start.10
  2.7 0.0 copy-start.11
  2.7 0.0 copy-start.12
  2.7 0.0 copy-start.13
  2.7 0.0 copy-start.14
  2.7 0.0 copy-start.15
  2.7 0.2 shard_map.175
  3.0 9.1 %collective-permute-start = (bf16[240,512]{1,0:T(8,128)(2,1)S(1)}, bf16[240,512]{1,0:T(8,128)(2,1)S(1)}, u32[]{:S(2)}, u32[]{:S(2)}) collective-permute-start(bf16[240,512]{1,0:T(8,128)(2,1)S(1)} %get-tuple-element.70), channel_id=1, source_target_pairs={{0,240},{1,241},{2,242},{3,243},{4,244},{5,245},{6,246},{7,247},{8... | collective-permute-start | bytes 737288 | tf_op jit(solution)/shard_map/ppermute | solution.py:566
  12.1 1.0 %collective-permute-start.1 = (bf16[192,512]{1,0:T(8,128)(2,1)S(1)}, bf16[192,512]{1,0:T(8,128)(2,1)S(1)}, u32[]{:S(2)}, u32[]{:S(2)}) collective-permute-start(bf16[192,512]{1,0:T(8,128)(2,1)S(1)} %get-tuple-element.71), channel_id=1, source_target_pairs={{0,15},{1,0},{2,1},{3,2},{4,3},{5,4},{6,5},{7,6},{8,7},{9,8},{10,9... | collective-permute-start | bytes 589832 | tf_op jit(solution)/shard_map/ppermute | solution.py:566
  13.1 3.2 %collective-permute-start.2 = (bf16[80,512]{1,0:T(8,128)(2,1)S(1)}, bf16[80,512]{1,0:T(8,128)(2,1)S(1)}, u32[]{:S(2)}, u32[]{:S(2)}) collective-permute-start(bf16[80,512]{1,0:T(8,128)(2,1)S(1)} %get-tuple-element.72), channel_id=1, source_target_pairs={{0,255},{1,240},{2,241},{3,242},{4,243},{5,244},{6,245},{7,246},{8... | collective-permute-start | bytes 245768 | tf_op jit(solution)/shard_map/ppermute | solution.py:566
  16.4 4.2 %shard_map.176 = (f32[1,512]{1,0:T(1,128)S(1)}, bf16[320,336]{1,0:T(8,128)(2,1)S(1)}, bf16[512,1536]{1,0:T(8,128)(2,1)S(1)}, bf16[512,512]{1,0:T(8,128)(2,1)S(1)...) custom-call(bf16[576,512]{1,0:T(8,128)(2,1)S(1)} %get-tuple-element., ...), custom_call_target="tpu_custom_call" | custom-call | flops 1000000000 | bytes 2000000 | tf_op jit(solution)/shard_map/pallas_call | solution.py:492
  20.6 0.0 collective-permute-done.1.lon_ref
  20.6 0.0 collective-permute-done.lat_ref
  20.6 0.0 copy-start
  20.6 4.0 %shard_map.177 = (bf16[400,512]{1,0:T(8,128)(2,1)S(1)}, bf16[400,1536]{1,0:T(8,128)(2,1)S(1)}, bf16[400,512]{1,0:T(8,128)(2,1)S(1)}, f32[5,2,80,320]{3,2,1,0:T(8...) custom-call(bf16[576,512]{1,0:T(8,128)(2,1)S(1)} %get-tuple-element.68.tok_ref, ...), custom_call_target="tpu_custom_call" | custom-call | flops 1000000000 | bytes 2000000 | tf_op jit(solution)/shard_map/pallas_call | solution.py:500
  24.6 5.6 %collective-permute-start.3 = (bf16[48,512]{1,0:T(8,128)(2,1)S(1)}, bf16[48,512]{1,0:T(8,128)(2,1)S(1)}, u32[]{:S(2)}, u32[]{:S(2)}) collective-permute-start(bf16[48,512]{1,0:T(8,128)(2,1)S(1)} %get-tuple-element.81), channel_id=1, source_target_pairs={{0,240},{1,241},{2,242},{3,243},{4,244},{5,245},{6,246},{7,247},{8... | collective-permute-start | bytes 147464 | tf_op jit(solution)/shard_map/ppermute | solution.py:566
  30.2 2.0 %shard_map.178 = (f32[4,144,512]{2,1,0:T(8,128)S(1)}, bf16[2048,1024]{1,0:T(8,128)(2,1)S(1)}) custom-call(bf16[144,1024]{1,0:T(8,128)(2,1)S(1)} %get-tuple-element.84.g_ref, bf16[240,512]{1,0:T(8,128)(2,1)S(1)} %collective-permute-done.lat_ref, bf16[192,512]{1,0:T(8,128)(2,1)S(1)} %collective-permute-done.1.lon_ref, ...), custom_call_target="tpu_custom_call" | custom-call | flops 1000000000 | bytes 2000000 | tf_op jit(solution)/shard_map/pallas_call | solution.py:506
  32.3 0.0 collective-permute-done.3.row_ref
  32.3 0.0 copy-start.1
  32.3 1.2 %shard_map.179 = (bf16[576,512]{1,0:T(8,128)(2,1)S(1)}, bf16[48,512]{1,0:T(8,128)(2,1)S(1)}, bf16[4,144,512]{2,1,0:T(8,128)(2,1)S(1)}) custom-call(bf16[576,512]{1,0:T(8,128)(2,1)S(1)} %get-tuple-element.80.summed_ref, bf16[48,512]{1,0:T(8,128)(2,1)S(1)} %collective-permute-done.3.row_ref, f32[4,1,512]{2,1,0:T(1,128)S(1)} %get-tuple-element.82.gain_ref, ...), custom_call_target="tpu_custom_call" | custom-call | flops 1000000000 | bytes 2000000 | tf_op jit(solution)/shard_map/pallas_call | solution.py:512
  33.5 0.3 collective-permute-start.4
  33.8 3.1 %shard_map.180 = (bf16[320,512]{1,0:T(8,128)(2,1)S(1)}, bf16[320,1536]{1,0:T(8,128)(2,1)S(1)}, bf16[512,640]{1,0:T(8,128)(2,1)S(1)}, bf16[512,640]{1,0:T(8,128)(2,1)S(1)}) custom-call(bf16[576,512]{1,0:T(8,128)(2,1)S(1)} %get-tuple-element.89.dsum_ref, bf16[400,1536]{1,0:T(8,128)(2,1)S(1)} %get-tuple-element.91.qkv_ref, ...), custom_call_target="tpu_custom_call" | custom-call | flops 1000000000 | bytes 2000000 | tf_op jit(solution)/shard_map/pallas_call | solution.py:521
  36.9 3.6 %collective-permute-done.4.row_ref = bf16[48,512]{1,0:T(8,128)(2,1)S(1)} collective-permute-done((bf16[48,512]{1,0:T(8,128)(2,1)S(1)}, bf16[48,512]{1,0:T(8,128)(2,1)S(1)}, u32[]{:S(2)}, u32[]{:S(2)}) %collective-permute-start.4) | collective-permute-done | bytes 49184 | tf_op jit(solution)/shard_map/ppermute | solution.py:566
  40.5 4.9 %shard_map.181 = (bf16[640,1536]{1,0:T(8,128)(2,1)S(1)}, bf16[4,32,32,128]{3,2,1,0:T(8,128)(2,1)S(1)}, bf16[4,32,32,128]{3,2,1,0:T(8,128)(2,1)S(1)}) custom-call(bf16[576,512]{1,0:T(8,128)(2,1)S(1)} %get-tuple-element.89.dsum_ref, bf16[48,512]{1,0:T(8,128)(2,1)S(1)} %collective-permute-done.4.row_ref, bf16[512,640]{1,0:T(8,128)(2,1)S(1)} %get-tuple-element.97.xst_ref, ...), custom_call_target="tpu_custom_call" | custom-call | flops 1000000000 | bytes 2000000 | tf_op jit(solution)/shard_map/pallas_call | solution.py:533
  45.4 0.5 collective-permute-start.5
  45.8 1.0 %shard_map.182 = (bf16[96,1024]{1,0:T(8,128)(2,1)S(1)}, bf16[96,512]{1,0:T(8,128)(2,1)S(1)}, bf16[64,512]{1,0:T(8,128)(2,1)S(1)}, bf16[32,512]{1,0:T(8,128)(2,1)S(1)}) custom-call(bf16[4,144,512]{2,1,0:T(8,128)(2,1)S(1)} %get-tuple-element.106.normed_ref, bf16[2048,1024]{1,0:T(8,128)(2,1)S(1)} %get-tuple-element.107.wmerge_ref, bf16[192,144]{1,0:T(8,128)(2,1)S(1)} %copy-done.3), custom_call_target="tpu_custom_call" | custom-call | flops 1000000000 | bytes 2000000 | tf_op jit(solution)/shard_map/pallas_call | solution.py:526
  46.8 1.3 %collective-permute-done.5.b_ref = bf16[4,32,32,128]{3,2,1,0:T(8,128)(2,1)S(1)} collective-permute-done((bf16[4,32,32,128]{3,2,1,0:T(8,128)(2,1)S(1)}, bf16[4,32,32,128]{3,2,1,0:T(8,128)(2,1)S(1)}, u32[]{:S(2)}, u32[]{:S(2)}) %collective-permute-start.5) | collective-permute-done | bytes 1048608 | tf_op jit(solution)/shard_map/ppermute | solution.py:596
  48.1 0.2 shard_map.183
  48.4 0.5 collective-permute-start.6
  48.9 0.5 collective-permute-start.7
  49.3 2.5 %shard_map.184 = (bf16[432,512]{1,0:T(8,128)(2,1)S(1)}, bf16[240,512]{1,0:T(8,128)(2,1)S(1)}, bf16[160,512]{1,0:T(8,128)(2,1)S(1)}, bf16[80,512]{1,0:T(8,128)(2,1)S(1)}) custom-call(bf16[640,1536]{1,0:T(8,128)(2,1)S(1)} %get-tuple-element.111.dqkv_ref, bf16[512,1536]{1,0:T(8,128)(2,1)S(1)} %get-tuple-element.74.wqkv_ref, ...), custom_call_target="tpu_custom_call" | custom-call | flops 1000000000 | bytes 2000000 | tf_op jit(solution)/shard_map/pallas_call | solution.py:540
  51.8 2.2 %collective-permute-done.6.first_ref = bf16[2,16,32,128]{3,2,1,0:T(8,128)(2,1)S(1)} collective-permute-done((bf16[2,16,32,128]{3,2,1,0:T(8,128)(2,1)S(1)}, bf16[2,16,32,128]{3,2,1,0:T(8,128)(2,1)S(1)}, u32[]{:S(2)}, u32[]{:S(2)}) %collective-permute-start.6) | collective-permute-done | bytes 262176 | tf_op jit(solution)/shard_map/ppermute | solution.py:593
  54.0 1.6 %collective-permute-done.7.second_ref = bf16[2,16,32,128]{3,2,1,0:T(8,128)(2,1)S(1)} collective-permute-done((bf16[2,16,32,128]{3,2,1,0:T(8,128)(2,1)S(1)}, bf16[2,16,32,128]{3,2,1,0:T(8,128)(2,1)S(1)}, u32[]{:S(2)}, u32[]{:S(2)}) %collective-permute-start.7) | collective-permute-done | bytes 262176 | tf_op jit(solution)/shard_map/ppermute | solution.py:593
  55.6 0.1 shard_map.185
  55.7 0.6 collective-permute-start.8
  56.3 0.0 collective-permute-start.9
  56.3 4.6 %collective-permute-done.8.upper_ref = bf16[16,32,128]{2,1,0:T(8,128)(2,1)S(1)} collective-permute-done((bf16[16,32,128]{2,1,0:T(8,128)(2,1)S(1)}, bf16[16,32,128]{2,1,0:T(8,128)(2,1)S(1)}, u32[]{:S(2)}, u32[]{:S(2)}) %collective-permute-start.8) | collective-permute-done | bytes 131104 | tf_op jit(solution)/shard_map/ppermute | solution.py:593
  60.8 0.0 collective-permute-done.9.lower_ref
  60.8 0.8 shard_map.186
  61.6 7.8 %all-to-all-start = ((bf16[32,32,128]{2,1,0:T(8,128)(2,1)}), bf16[32,32,128]{2,1,0:T(8,128)(2,1)S(1)}, u32[]{:S(2)}, u32[]{:S(2)}) async-start(bf16[32,32,128]{2,1,0:T(8,128)(2,1)} %shard_map.186), calls=%async_computation | async-start | bytes 524288 | tf_op jit(solution)/shard_map/all_to_all | solution.py:606
  69.4 1.3 %collective-permute-start.10 = (bf16[240,512]{1,0:T(8,128)(2,1)S(1)}, bf16[240,512]{1,0:T(8,128)(2,1)S(1)}, u32[]{:S(2)}, u32[]{:S(2)}) collective-permute-start(bf16[240,512]{1,0:T(8,128)(2,1)S(1)} %get-tuple-element.127), channel_id=1, source_target_pairs={{0,16},{1,17},{2,18},{3,19},{4,20},{5,21},{6,22},{7,23},{8,24},{9,... | collective-permute-start | bytes 737288 | tf_op jit(solution)/shard_map/ppermute | solution.py:566
  70.7 2.7 %collective-permute-start.11 = (bf16[160,512]{1,0:T(8,128)(2,1)S(1)}, bf16[160,512]{1,0:T(8,128)(2,1)S(1)}, u32[]{:S(2)}, u32[]{:S(2)}) collective-permute-start(bf16[160,512]{1,0:T(8,128)(2,1)S(1)} %get-tuple-element.128), channel_id=1, source_target_pairs={{0,1},{1,2},{2,3},{3,4},{4,5},{5,6},{6,7},{7,8},{8,9},{9,10},{10,1... | collective-permute-start | bytes 491528 | tf_op jit(solution)/shard_map/ppermute | solution.py:566
  73.4 0.9 %collective-permute-start.12 = (bf16[80,512]{1,0:T(8,128)(2,1)S(1)}, bf16[80,512]{1,0:T(8,128)(2,1)S(1)}, u32[]{:S(2)}, u32[]{:S(2)}) collective-permute-start(bf16[80,512]{1,0:T(8,128)(2,1)S(1)} %get-tuple-element.129), channel_id=1, source_target_pairs={{0,17},{1,18},{2,19},{3,20},{4,21},{5,22},{6,23},{7,24},{8,25},{9,... | collective-permute-start | bytes 245768 | tf_op jit(solution)/shard_map/ppermute | solution.py:566
  74.3 12.1 %collective-permute-done.12.diag_ref = bf16[80,512]{1,0:T(8,128)(2,1)S(1)} collective-permute-done((bf16[80,512]{1,0:T(8,128)(2,1)S(1)}, bf16[80,512]{1,0:T(8,128)(2,1)S(1)}, u32[]{:S(2)}, u32[]{:S(2)}) %collective-permute-start.12) | collective-permute-done | bytes 81952 | tf_op jit(solution)/shard_map/ppermute | solution.py:566
  86.5 1.0 %shard_map.187 = (bf16[576,512]{1,0:T(8,128)(2,1)}, bf16[144,1024]{1,0:T(8,128)(2,1)}) custom-call(bf16[432,512]{1,0:T(8,128)(2,1)S(1)} %get-tuple-element.126.main_ref, bf16[240,512]{1,0:T(8,128)(2,1)S(1)} %collective-permute-done.10.lat_ref, bf16[160,512]{1,0:T(8,128)(2,1)S(1)} %collective-permute-done.11.lon_ref, ...), custom_call_target="tpu_custom_call" | custom-call | flops 1000000000 | bytes 2000000 | tf_op jit(solution)/shard_map/pallas_call | solution.py:550
  87.5 0.7 shard_map.188
  (26 shorter events, 0.1 us)
Async XLA Ops:
  0.6 1.1 %copy-start.5 = (bf16[12,48,512]{2,1,0:T(8,128)(2,1)S(1)}, bf16[12,48,512]{2,1,0:T(8,128)(2,1)}, u32[]{:S(2)}) copy-start(bf16[12,48,512]{2,1,0:T(8,128)(2,1)} %param.16) | copy-start | bytes 1769476
  1.7 1.0 %copy-start.7 = (bf16[6,24,1024]{2,1,0:T(8,128)(2,1)S(1)}, bf16[6,24,1024]{2,1,0:T(8,128)(2,1)}, u32[]{:S(2)}) copy-start(bf16[6,24,1024]{2,1,0:T(8,128)(2,1)} %param.22) | copy-start | bytes 884740
  2.7 13.7 %copy-start.4 = (bf16[512,1536]{1,0:T(8,128)(2,1)S(1)}, bf16[512,1536]{1,0:T(8,128)(2,1)}, u32[]{:S(2)}) copy-start(bf16[512,1536]{1,0:T(8,128)(2,1)} %refs_2_.1) | copy-start | bytes 4718596
  2.7 13.7 %copy-start.6 = (bf16[512,512]{1,0:T(8,128)(2,1)S(1)}, bf16[512,512]{1,0:T(8,128)(2,1)}, u32[]{:S(2)}) copy-start(bf16[512,512]{1,0:T(8,128)(2,1)} %refs_3_.1) | copy-start | bytes 1572868
  2.7 13.7 %copy-start.8 = (f32[2048]{0:T(1024)S(1)}, f32[2048]{0:T(1024)}, u32[]{:S(2)}) copy-start(f32[2048]{0:T(1024)} %param.20) | copy-start | bytes 24580
  2.7 13.7 %copy-start.9 = (f32[512]{0:T(512)S(1)}, f32[512]{0:T(512)}, u32[]{:S(2)}) copy-start(f32[512]{0:T(512)} %param.17) | copy-start | bytes 6148
  2.7 13.7 %copy-start.10 = (bf16[320,336]{1,0:T(8,128)(2,1)S(1)}, bf16[320,336]{1,0:T(8,128)(2,1)}, u32[]{:S(2)}) copy-start(bf16[320,336]{1,0:T(8,128)(2,1)} %constant.18.clone.refs_1_) | copy-start | bytes 645124
  2.7 13.7 %copy-start.11 = (bf16[288,320]{1,0:T(8,128)(2,1)S(1)}, bf16[288,320]{1,0:T(8,128)(2,1)}, u32[]{:S(2)}) copy-start(bf16[288,320]{1,0:T(8,128)(2,1)} %constant.20.clone.refs_6_) | copy-start | bytes 552964
  2.7 13.7 %copy-start.12 = (bf16[288,336]{1,0:T(8,128)(2,1)S(1)}, bf16[288,336]{1,0:T(8,128)(2,1)}, u32[]{:S(2)}) copy-start(bf16[288,336]{1,0:T(8,128)(2,1)} %constant.19.clone.refs_5_) | copy-start | bytes 580612
  2.7 13.6 %copy-start.13 = (bf16[192,192]{1,0:T(8,128)(2,1)S(1)}, bf16[192,192]{1,0:T(8,128)(2,1)}, u32[]{:S(2)}) copy-start(bf16[192,192]{1,0:T(8,128)(2,1)} %constant.22.clone.refs_8_) | copy-start | bytes 221188
  2.7 13.6 %copy-start.14 = (bf16[192,192]{1,0:T(8,128)(2,1)S(1)}, bf16[192,192]{1,0:T(8,128)(2,1)}, u32[]{:S(2)}) copy-start(bf16[192,192]{1,0:T(8,128)(2,1)} %constant.21.clone.refs_7_) | copy-start | bytes 221188
  2.7 13.6 %copy-start.15 = (bf16[144,192]{1,0:T(8,128)(2,1)S(1)}, bf16[144,192]{1,0:T(8,128)(2,1)}, u32[]{:S(2)}) copy-start(bf16[144,192]{1,0:T(8,128)(2,1)} %constant.23.clone.refs_9_) | copy-start | bytes 165892
  3.0 17.6 %collective-permute-start = (bf16[240,512]{1,0:T(8,128)(2,1)S(1)}, bf16[240,512]{1,0:T(8,128)(2,1)S(1)}, u32[]{:S(2)}, u32[]{:S(2)}) collective-permute-start(bf16[240,512]{1,0:T(8,128)(2,1)S(1)} %get-tuple-element.70), channel_id=1, source_target_pairs={{0,240},{1,241},{2,242},{3,243},{4,244},{5,245},{6,246},{7,247},{8... | collective-permute-start | bytes 737288 | tf_op jit(solution)/shard_map/ppermute | solution.py:566
  12.1 8.5 %collective-permute-start.1 = (bf16[192,512]{1,0:T(8,128)(2,1)S(1)}, bf16[192,512]{1,0:T(8,128)(2,1)S(1)}, u32[]{:S(2)}, u32[]{:S(2)}) collective-permute-start(bf16[192,512]{1,0:T(8,128)(2,1)S(1)} %get-tuple-element.71), channel_id=1, source_target_pairs={{0,15},{1,0},{2,1},{3,2},{4,3},{5,4},{6,5},{7,6},{8,7},{9,8},{10,9... | collective-permute-start | bytes 589832 | tf_op jit(solution)/shard_map/ppermute | solution.py:566
  13.1 7.5 %collective-permute-start.2 = (bf16[80,512]{1,0:T(8,128)(2,1)S(1)}, bf16[80,512]{1,0:T(8,128)(2,1)S(1)}, u32[]{:S(2)}, u32[]{:S(2)}) collective-permute-start(bf16[80,512]{1,0:T(8,128)(2,1)S(1)} %get-tuple-element.72), channel_id=1, source_target_pairs={{0,255},{1,240},{2,241},{3,242},{4,243},{5,244},{6,245},{7,246},{8... | collective-permute-start | bytes 245768 | tf_op jit(solution)/shard_map/ppermute | solution.py:566
  20.6 9.7 %copy-start = (bf16[2048,1024]{1,0:T(8,128)(2,1)S(1)}, bf16[2048,1024]{1,0:T(8,128)(2,1)}, u32[]{:S(2)}) copy-start(bf16[2048,1024]{1,0:T(8,128)(2,1)} %wmerge_ref.1) | copy-start | bytes 12582916
  24.6 7.6 %collective-permute-start.3 = (bf16[48,512]{1,0:T(8,128)(2,1)S(1)}, bf16[48,512]{1,0:T(8,128)(2,1)S(1)}, u32[]{:S(2)}, u32[]{:S(2)}) collective-permute-start(bf16[48,512]{1,0:T(8,128)(2,1)S(1)} %get-tuple-element.81), channel_id=1, source_target_pairs={{0,240},{1,241},{2,242},{3,243},{4,244},{5,245},{6,246},{7,247},{8... | collective-permute-start | bytes 147464 | tf_op jit(solution)/shard_map/ppermute | solution.py:566
  32.3 1.5 %copy-start.1 = (bf16[320,288]{1,0:T(8,128)(2,1)S(1)}, bf16[320,288]{1,0:T(8,128)(2,1)}, u32[]{:S(2)}) copy-start(bf16[320,288]{1,0:T(8,128)(2,1)} %constant.24.clone.pick_ref) | copy-start | bytes 552964
  33.5 6.9 %collective-permute-start.4 = (bf16[48,512]{1,0:T(8,128)(2,1)S(1)}, bf16[48,512]{1,0:T(8,128)(2,1)S(1)}, u32[]{:S(2)}, u32[]{:S(2)}) collective-permute-start(bf16[48,512]{1,0:T(8,128)(2,1)S(1)} %get-tuple-element.90), channel_id=1, source_target_pairs={{0,16},{1,17},{2,18},{3,19},{4,20},{5,21},{6,22},{7,23},{8,24},{9,... | collective-permute-start | bytes 147464 | tf_op jit(solution)/shard_map/ppermute | solution.py:566
  40.5 5.3 %copy-start.3 = (bf16[192,144]{1,0:T(8,128)(2,1)S(1)}, bf16[192,144]{1,0:T(8,128)(2,1)}, u32[]{:S(2)}) copy-start(bf16[192,144]{1,0:T(8,128)(2,1)} %constant.26.clone.unshift_ref) | copy-start | bytes 165892
  45.4 2.7 %collective-permute-start.5 = (bf16[4,32,32,128]{3,2,1,0:T(8,128)(2,1)S(1)}, bf16[4,32,32,128]{3,2,1,0:T(8,128)(2,1)S(1)}, u32[]{:S(2)}, u32[]{:S(2)}) collective-permute-start(bf16[4,32,32,128]{3,2,1,0:T(8,128)(2,1)S(1)} %get-tuple-element.105), channel_id=1, source_target_pairs={{0,1},{1,0},{2,3},{3,2},{4,5},{5,4},{6,7},{7,6},{8,9},{9,8},{10,11... | collective-permute-start | bytes 3145736 | tf_op jit(solution)/shard_map/ppermute | solution.py:596
  48.1 1.2 %copy-start.2 = (bf16[336,288]{1,0:T(8,128)(2,1)S(1)}, bf16[336,288]{1,0:T(8,128)(2,1)}, u32[]{:S(2)}) copy-start(bf16[336,288]{1,0:T(8,128)(2,1)} %constant.25.clone.unshift_ref) | copy-start | bytes 580612
  48.4 5.6 %collective-permute-start.6 = (bf16[2,16,32,128]{3,2,1,0:T(8,128)(2,1)S(1)}, bf16[2,16,32,128]{3,2,1,0:T(8,128)(2,1)S(1)}, u32[]{:S(2)}, u32[]{:S(2)}) collective-permute-start(bf16[2,16,32,128]{3,2,1,0:T(8,128)(2,1)S(1)} %get-tuple-element.121), channel_id=1, source_target_pairs={{0,2},{1,9},{2,0},{3,11},{4,6},{5,13},{6,4},{7,15},{8,10},{9,1},{1... | collective-permute-start | bytes 786440 | tf_op jit(solution)/shard_map/ppermute | solution.py:593
  48.9 6.7 %collective-permute-start.7 = (bf16[2,16,32,128]{3,2,1,0:T(8,128)(2,1)S(1)}, bf16[2,16,32,128]{3,2,1,0:T(8,128)(2,1)S(1)}, u32[]{:S(2)}, u32[]{:S(2)}) collective-permute-start(bf16[2,16,32,128]{3,2,1,0:T(8,128)(2,1)S(1)} %get-tuple-element.122), channel_id=1, source_target_pairs={{0,6},{1,137},{2,4},{3,139},{4,2},{5,141},{6,0},{7,143},{8,14},{9,... | collective-permute-start | bytes 786440 | tf_op jit(solution)/shard_map/ppermute | solution.py:593
  55.7 5.1 %collective-permute-start.8 = (bf16[16,32,128]{2,1,0:T(8,128)(2,1)S(1)}, bf16[16,32,128]{2,1,0:T(8,128)(2,1)S(1)}, u32[]{:S(2)}, u32[]{:S(2)}) collective-permute-start(bf16[16,32,128]{2,1,0:T(8,128)(2,1)S(1)} %get-tuple-element.124), channel_id=1, source_target_pairs={{0,6},{1,137},{2,4},{3,139},{4,2},{5,141},{6,0},{7,143},{8,14},{9,... | collective-permute-start | bytes 393224 | tf_op jit(solution)/shard_map/ppermute | solution.py:593
  56.3 4.6 %collective-permute-start.9 = (bf16[16,32,128]{2,1,0:T(8,128)(2,1)S(1)}, bf16[16,32,128]{2,1,0:T(8,128)(2,1)S(1)}, u32[]{:S(2)}, u32[]{:S(2)}) collective-permute-start(bf16[16,32,128]{2,1,0:T(8,128)(2,1)S(1)} %get-tuple-element.125), channel_id=1, source_target_pairs={{0,2},{1,9},{2,0},{3,11},{4,6},{5,13},{6,4},{7,15},{8,10},{9,1},{1... | collective-permute-start | bytes 393224 | tf_op jit(solution)/shard_map/ppermute | solution.py:593
  61.6 25.9 %all-to-all-start = ((bf16[32,32,128]{2,1,0:T(8,128)(2,1)}), bf16[32,32,128]{2,1,0:T(8,128)(2,1)S(1)}, u32[]{:S(2)}, u32[]{:S(2)}) async-start(bf16[32,32,128]{2,1,0:T(8,128)(2,1)} %shard_map.186), calls=%async_computation | async-start | bytes 524288 | tf_op jit(solution)/shard_map/all_to_all | solution.py:606
  69.4 17.1 %collective-permute-start.10 = (bf16[240,512]{1,0:T(8,128)(2,1)S(1)}, bf16[240,512]{1,0:T(8,128)(2,1)S(1)}, u32[]{:S(2)}, u32[]{:S(2)}) collective-permute-start(bf16[240,512]{1,0:T(8,128)(2,1)S(1)} %get-tuple-element.127), channel_id=1, source_target_pairs={{0,16},{1,17},{2,18},{3,19},{4,20},{5,21},{6,22},{7,23},{8,24},{9,... | collective-permute-start | bytes 737288 | tf_op jit(solution)/shard_map/ppermute | solution.py:566
  70.7 15.8 %collective-permute-start.11 = (bf16[160,512]{1,0:T(8,128)(2,1)S(1)}, bf16[160,512]{1,0:T(8,128)(2,1)S(1)}, u32[]{:S(2)}, u32[]{:S(2)}) collective-permute-start(bf16[160,512]{1,0:T(8,128)(2,1)S(1)} %get-tuple-element.128), channel_id=1, source_target_pairs={{0,1},{1,2},{2,3},{3,4},{4,5},{5,6},{6,7},{7,8},{8,9},{9,10},{10,1... | collective-permute-start | bytes 491528 | tf_op jit(solution)/shard_map/ppermute | solution.py:566
  73.4 13.0 %collective-permute-start.12 = (bf16[80,512]{1,0:T(8,128)(2,1)S(1)}, bf16[80,512]{1,0:T(8,128)(2,1)S(1)}, u32[]{:S(2)}, u32[]{:S(2)}) collective-permute-start(bf16[80,512]{1,0:T(8,128)(2,1)S(1)} %get-tuple-element.129), channel_id=1, source_target_pairs={{0,17},{1,18},{2,19},{3,20},{4,21},{5,22},{6,23},{7,24},{8,25},{9,... | collective-permute-start | bytes 245768 | tf_op jit(solution)/shard_map/ppermute | solution.py:566

commit v3 on v2

--- a/solution.py
+++ b/solution.py
@@ -412,35 +412,14 @@
         merged_ref[PAIR_TOP:, cols] = fill_edge(m_main_ref[:, cols], lon, PAIR_ROWS - 2, PAIR_COLS)
 
 
-def add_kernel(a_ref, b_ref, own_ref, later_ref, first_ref, second_ref):
-    half = own_ref.shape[0] // 2
-
-    def both(k, rows):
-        return (a_ref[k, rows].astype(f32) + b_ref[k, rows].astype(f32)).astype(bf16)
-
-    upper, lower = pl.ds(0, half), pl.ds(half, half)
-    own_ref[...] = both(0, pl.ds(0, 2 * half))
-    first_ref[0], first_ref[1] = both(1, upper), both(2, upper)
-    second_ref[0], second_ref[1] = both(3, lower), both(2, lower)
-    later_ref[0], later_ref[1] = both(3, upper), both(1, lower)
-
-
-def relay_kernel(own_ref, later_ref, first_ref, second_ref, out_ref, to_third_ref, to_first_ref):
-    half = own_ref.shape[0] // 2
-
-    def both(a, b):
-        return (a.astype(f32) + b.astype(f32)).astype(bf16)
-
-    out_ref[:half] = both(own_ref[:half], first_ref[0])
-    out_ref[half:] = both(own_ref[half:], second_ref[0])
-    to_third_ref[...] = both(later_ref[0], first_ref[1])
-    to_first_ref[...] = both(later_ref[1], second_ref[1])
-
-
-def join_kernel(own_ref, upper_ref, lower_ref, out_ref):
-    half = own_ref.shape[0] // 2
-    out_ref[:half] = (own_ref[:half].astype(f32) + upper_ref[...].astype(f32)).astype(bf16)
-    out_ref[half:] = (own_ref[half:].astype(f32) + lower_ref[...].astype(f32)).astype(bf16)
+def add_kernel(a_ref, b_ref, *out_refs):
+    for k, out_ref in enumerate(out_refs):
+        out_ref[...] = (a_ref[k].astype(f32) + b_ref[k].astype(f32)).astype(bf16)
+
+
+def join_kernel(a_ref, b_ref, c_ref, d_ref, out_ref):
+    total = a_ref[...].astype(f32) + b_ref[...].astype(f32) + c_ref[...].astype(f32) + d_ref[...].astype(f32)
+    out_ref[...] = total.astype(bf16)
 
 
 def sum_kernel(parts_ref, out_ref):
@@ -473,7 +452,7 @@
     return lax.optimization_barrier((value, *others))[0]
 
 
-def chain(tok, gain, w_qkv, w_proj, gain_merge, w_merge, g_merged, fetch, hand_on, up, down):
+def chain(tok, gain, w_qkv, w_proj, gain_merge, w_merge, g_merged, fetch, up, down):
     tok, g_merged, top, edge, corner = call(
         border_kernel,
         [
@@ -534,25 +513,23 @@
         outer_back_kernel,
         [((WIDTH, 3 * D), bf16), ((4, 32, 32, 128), bf16), ((4, 32, 32, 128), bf16)],
         [((WIDTH, D), bf16), ((BAND, D), bf16)],
-    )(d_summed, first, xst, mixt, up1, dqkv1, qkv0, probs0, qkv1, probs1, w_proj, band)
-
-    def cells_back(ready):
-        return call(
-            cells_back_kernel,
-            [
-                ((TOKENS - TOP, D), bf16), ((TOP + 2 * PAIR_TOP, D), bf16),
-                ((EDGE + 2 * (PAIR_SIDE - PAIR_CORNER), D), bf16), ((SIDE + 2 * PAIR_CORNER, D), bf16),
-            ],
-            [((WIDTH, D), bf16)],
-        )(after(dqkv, ready), w_qkv, cells_pick, unshift, tok, d_summed, first, gain, m_lat, m_lon, m_diag)
-
-    def finish(main, *pieces):
+    )(d_summed, first, xst, mixt, after(up1, m_lat), dqkv1, qkv0, probs0, qkv1, probs1, w_proj, band)
+    main, to_lat, to_lon, to_diag = call(
+        cells_back_kernel,
+        [
+            ((TOKENS - TOP, D), bf16), ((TOP + 2 * PAIR_TOP, D), bf16),
+            ((EDGE + 2 * (PAIR_SIDE - PAIR_CORNER), D), bf16), ((SIDE + 2 * PAIR_CORNER, D), bf16),
+        ],
+        [((WIDTH, D), bf16)],
+    )(dqkv, w_qkv, cells_pick, unshift, tok, d_summed, first, gain, m_lat, m_lon, m_diag)
+
+    def finish(lat, lon, diag):
         grad_tokens, merged = call(own_cells_kernel, [((TOKENS, D), bf16), ((PAIRS, 2 * D), bf16)])(
-            main, *hand_on(*pieces), m_main
+            main, lat, lon, diag, m_main
         )
         return merged, grad_tokens
 
-    return cells_back, finish, keep, sent, m_lat
+    return finish, keep, sent, (to_lat, to_lon, to_diag)
 
 
 def solution(mesh):
@@ -567,9 +544,6 @@
 
     def fetch(top, edge, corner):
         return send(top, -1, 0), send(edge, 0, -1), send(corner, -1, -1)
-
-    def hand_on(lat, lon, diag):
-        return send(lat, 1, 0), send(lon, 0, 1), send(diag, 1, 1)
 
     def place(i):
         lat, lon = divmod(i, lons)
@@ -592,29 +566,27 @@
     def swap(block, step):
         return lax.ppermute(block, ("lat", "lon"), [(i, across(i, step)) for i in range(count)])
 
-    def reduce_across(keep, sent, ready, cells_back):
+    def reduce_across(keep, sent, to_lat):
         other = lax.ppermute(sent, ("lat", "lon"), [(i, i ^ 1) for i in range(count)])
-        whole, pair, half = ((32, 32, 128), bf16), ((2, 16, 32, 128), bf16), ((16, 32, 128), bf16)
-        own, later, first, second = call(add_kernel, [whole, pair, pair, pair])(keep, after(other, ready))
-        first, second = swap(first, 1), swap(second, 3)
-        pieces = cells_back(later)
-        own, to_third, to_first = call(relay_kernel, [whole, half, half])(own, after(later, *pieces), first, second)
-        sums = call(join_kernel, [whole])(own, swap(to_third, 3), swap(to_first, 1))[0]
-        return sums, [after(piece, sums) for piece in pieces]
+        own, *others = call(add_kernel, [((32, 32, 128), bf16)] * 4)(keep, after(other, to_lat))
+        got = [swap(block, step) for step, block in enumerate(others, 1)]
+        lat = send(to_lat, 1, 0)
+        return call(join_kernel, [((32, 32, 128), bf16)])(after(own, lat), *got)[0], lat
 
     def reduce_rest(sums):
         parts = lax.all_to_all(sums, ("lat", "lon"), 0, 0, axis_index_groups=rest, tiled=True)
         return call(sum_kernel, [((32, 128), f32)])(parts)[0]
 
     def body(tokens, gain_attn, w_qkv, w_proj, gain_merge, w_merge, g_merged):
-        cells_back, finish, keep, sent, ready = chain(
+        finish, keep, sent, (to_lat, to_lon, to_diag) = chain(
             tokens.reshape(TOKENS, D), gain_attn.reshape(1, D), w_qkv, w_proj, gain_merge.reshape(4, 1, D),
-            w_merge, g_merged.reshape(PAIRS, 2 * D), fetch, hand_on,
+            w_merge, g_merged.reshape(PAIRS, 2 * D), fetch,
             lambda row: send(row, -1, 0), lambda row: send(row, 1, 0),
         )
-        sums, pieces = reduce_across(keep, sent, ready, cells_back)
+        sums, lat = reduce_across(keep, sent, to_lat)
         grad_weights = reduce_rest(sums)
-        merged, grad_tokens = finish(*pieces)
+        lon, diag = send(after(to_lon, sums), 0, 1), send(after(to_diag, sums), 1, 1)
+        merged, grad_tokens = finish(lat, lon, diag)
         return (
             merged.reshape(ROWS // 2, COLS // 2, 2 * D),
             grad_tokens.reshape(ROWS, COLS, D),

time: 88.4 us -> 86.5 us (0.979)
  starting transfers between devices: 33.9 us -> 32.7 us
    ppermute x4 -> x3, waiting for transfers between devices: 8.34 us -> 3.83 us  [swap(): lax.ppermute(block, ('lat', 'lon'), [(i, across(i, step)) for i in range(...]
    ppermute x8, waiting for transfers between devices: 15.7 us -> 19.8 us  [send(): return lax.ppermute(block, ('lat', 'lon'), route)]
    ppermute x4 -> x3, starting transfers between devices: 1.52 us -> 3.95 us  [swap(): lax.ppermute(block, ('lat', 'lon'), [(i, across(i, step)) for i in range(...]
    ppermute x8, starting transfers between devices: 24.1 us -> 21.8 us  [send(): return lax.ppermute(block, ('lat', 'lon'), route)]
    ppermute x1, waiting for transfers between devices: 1.31 us -> 0.01 us  [reduce_across(): lax.ppermute(sent, ('lat', 'lon'), [(i, i ^ 1) for i in range(count)])]
    all_to_all x1, starting transfers between devices: 7.8 us -> 6.54 us  [reduce_rest(): lax.all_to_all(sums, ('lat', 'lon'), 0, 0, axis_index_groups=rest, tiled=...]
    all_to_all x1, waiting for transfers between devices: 0.01 us -> 0.94 us  [reduce_rest(): lax.all_to_all(sums, ('lat', 'lon'), 0, 0, axis_index_groups=rest, tiled=...]
    pallas_call x4 -> x3, Pallas kernels: 3.58 us -> 3.56 us  [the longest x1 2.48 us: chain(): call(cells_back_kernel, [((TOKENS - TOP, D), bf16), ((TOP + 2 * PAIR_TOP,...]
  transfers between devices with their start and end apart: 14 -> 13, of which waited for: 6 -> 5; matrix products, arithmetic and copies ran while one was open for 0% -> 0% of each run, Pallas kernels for 16% -> 16%
where the time goes in v3:
time: 86.5 us; the launch traced here: 86.2 us
  starting transfers between devices  32.7 us (38%)
  Pallas kernels  25.8 us (30%)
  waiting for transfers between devices  24.6 us (28%)
  local copies, waits for them, and re-layouts  2.1 us (2%)
  between operations  0.93 us (1%)
    ppermute x8, starting transfers between devices, send(): return lax.ppermute(block, ('lat', 'lon'), route)  21.8 us
    ppermute x8, waiting for transfers between devices, send(): return lax.ppermute(block, ('lat', 'lon'), route)  19.8 us
    all_to_all x1, starting transfers between devices, reduce_rest(): lax.all_to_all(sums, ('lat', 'lon'), 0, 0, axis_index_groups=rest, tiled=...  6.54 us
    pallas_call x1, Pallas kernels, chain(): call(outer_back_kernel, [((WIDTH, 3 * D), bf16), ((4, 32, 32, 128), bf16)...  4.88 us
    pallas_call x1, Pallas kernels, chain(): call(inner_kernel, [(h.shape, h.dtype) for h in held] + [((TOKENS - TOP,...  4.15 us
    pallas_call x1, Pallas kernels, chain(): call(outer_kernel, saved(REST) + [((TOKENS, D), bf16), ((TOKENS, D), bf16...  4.05 us
    ppermute x3, starting transfers between devices, swap(): lax.ppermute(block, ('lat', 'lon'), [(i, across(i, step)) for i in range(...  3.95 us
    ppermute x3, waiting for transfers between devices, swap(): lax.ppermute(block, ('lat', 'lon'), [(i, across(i, step)) for i in range(...  3.83 us
  transfers between devices with their start and end apart: 13, of which 5 were waited for; matrix products, arithmetic and copies ran while one was open for 0% of the time, Pallas kernels for 16%

profile of v3, /device:TPU:1, one launch (start us, length us, event | category | flops | bytes accessed | tf_op | source)
XLA Modules:
  0.0 86.2 jit_solution(13395668369151966047)
XLA Ops:
  0.6 1.1 %copy-done.5 = bf16[12,48,512]{2,1,0:T(8,128)(2,1)S(1)} copy-done((bf16[12,48,512]{2,1,0:T(8,128)(2,1)S(1)}, bf16[12,48,512]{2,1,0:T(8,128)(2,1)}, u32[]{:S(2)}) %copy-start.5) | copy-done | bytes 589848
  1.7 1.0 %copy-done.7 = bf16[6,24,1024]{2,1,0:T(8,128)(2,1)S(1)} copy-done((bf16[6,24,1024]{2,1,0:T(8,128)(2,1)S(1)}, bf16[6,24,1024]{2,1,0:T(8,128)(2,1)}, u32[]{:S(2)}) %copy-start.7) | copy-done | bytes 294936
  2.7 0.0 copy-start.10
  2.7 0.0 copy-start.11
  2.7 0.0 copy-start.12
  2.7 0.0 copy-start.13
  2.7 0.0 copy-start.14
  2.7 0.0 copy-start.15
  2.7 0.2 shard_map.175
  3.0 9.1 %collective-permute-start = (bf16[240,512]{1,0:T(8,128)(2,1)S(1)}, bf16[240,512]{1,0:T(8,128)(2,1)S(1)}, u32[]{:S(2)}, u32[]{:S(2)}) collective-permute-start(bf16[240,512]{1,0:T(8,128)(2,1)S(1)} %get-tuple-element.65), channel_id=1, source_target_pairs={{0,240},{1,241},{2,242},{3,243},{4,244},{5,245},{6,246},{7,247},{8... | collective-permute-start | bytes 737288 | tf_op jit(solution)/shard_map/ppermute | solution.py:543
  12.1 1.0 %collective-permute-start.1 = (bf16[192,512]{1,0:T(8,128)(2,1)S(1)}, bf16[192,512]{1,0:T(8,128)(2,1)S(1)}, u32[]{:S(2)}, u32[]{:S(2)}) collective-permute-start(bf16[192,512]{1,0:T(8,128)(2,1)S(1)} %get-tuple-element.66), channel_id=1, source_target_pairs={{0,15},{1,0},{2,1},{3,2},{4,3},{5,4},{6,5},{7,6},{8,7},{9,8},{10,9... | collective-permute-start | bytes 589832 | tf_op jit(solution)/shard_map/ppermute | solution.py:543
  13.1 3.2 %collective-permute-start.2 = (bf16[80,512]{1,0:T(8,128)(2,1)S(1)}, bf16[80,512]{1,0:T(8,128)(2,1)S(1)}, u32[]{:S(2)}, u32[]{:S(2)}) collective-permute-start(bf16[80,512]{1,0:T(8,128)(2,1)S(1)} %get-tuple-element.67), channel_id=1, source_target_pairs={{0,255},{1,240},{2,241},{3,242},{4,243},{5,244},{6,245},{7,246},{8... | collective-permute-start | bytes 245768 | tf_op jit(solution)/shard_map/ppermute | solution.py:543
  16.4 4.1 %shard_map.176 = (f32[1,512]{1,0:T(1,128)S(1)}, bf16[320,336]{1,0:T(8,128)(2,1)S(1)}, bf16[512,1536]{1,0:T(8,128)(2,1)S(1)}, bf16[512,512]{1,0:T(8,128)(2,1)S(1)...) custom-call(bf16[576,512]{1,0:T(8,128)(2,1)S(1)} %get-tuple-element., ...), custom_call_target="tpu_custom_call" | custom-call | flops 1000000000 | bytes 2000000 | tf_op jit(solution)/shard_map/pallas_call | solution.py:471
  20.5 0.0 collective-permute-done.2.diag_ref
  20.6 0.0 collective-permute-done.1.lon_ref
  20.6 0.0 collective-permute-done.lat_ref
  20.6 0.0 copy-start
  20.6 4.0 %shard_map.177 = (bf16[400,512]{1,0:T(8,128)(2,1)S(1)}, bf16[400,1536]{1,0:T(8,128)(2,1)S(1)}, bf16[400,512]{1,0:T(8,128)(2,1)S(1)}, f32[5,2,80,320]{3,2,1,0:T(8...) custom-call(bf16[576,512]{1,0:T(8,128)(2,1)S(1)} %get-tuple-element.63.tok_ref, ...), custom_call_target="tpu_custom_call" | custom-call | flops 1000000000 | bytes 2000000 | tf_op jit(solution)/shard_map/pallas_call | solution.py:479
  24.6 5.6 %collective-permute-start.3 = (bf16[48,512]{1,0:T(8,128)(2,1)S(1)}, bf16[48,512]{1,0:T(8,128)(2,1)S(1)}, u32[]{:S(2)}, u32[]{:S(2)}) collective-permute-start(bf16[48,512]{1,0:T(8,128)(2,1)S(1)} %get-tuple-element.76), channel_id=1, source_target_pairs={{0,240},{1,241},{2,242},{3,243},{4,244},{5,245},{6,246},{7,247},{8... | collective-permute-start | bytes 147464 | tf_op jit(solution)/shard_map/ppermute | solution.py:543
  30.2 2.0 %shard_map.178 = (f32[4,144,512]{2,1,0:T(8,128)S(1)}, bf16[2048,1024]{1,0:T(8,128)(2,1)S(1)}) custom-call(bf16[144,1024]{1,0:T(8,128)(2,1)S(1)} %get-tuple-element.79.g_ref, bf16[240,512]{1,0:T(8,128)(2,1)S(1)} %collective-permute-done.lat_ref, bf16[192,512]{1,0:T(8,128)(2,1)S(1)} %collective-permute-done.1.lon_ref, ...), custom_call_target="tpu_custom_call" | custom-call | flops 1000000000 | bytes 2000000 | tf_op jit(solution)/shard_map/pallas_call | solution.py:485
  32.3 0.0 collective-permute-done.3.row_ref
  32.3 0.0 copy-start.3
  32.3 1.2 %shard_map.179 = (bf16[576,512]{1,0:T(8,128)(2,1)S(1)}, bf16[48,512]{1,0:T(8,128)(2,1)S(1)}, bf16[4,144,512]{2,1,0:T(8,128)(2,1)S(1)}) custom-call(bf16[576,512]{1,0:T(8,128)(2,1)S(1)} %get-tuple-element.75.summed_ref, bf16[48,512]{1,0:T(8,128)(2,1)S(1)} %collective-permute-done.3.row_ref, f32[4,1,512]{2,1,0:T(1,128)S(1)} %get-tuple-element.77.gain_ref, ...), custom_call_target="tpu_custom_call" | custom-call | flops 1000000000 | bytes 2000000 | tf_op jit(solution)/shard_map/pallas_call | solution.py:491
  33.5 0.3 collective-permute-start.4
  33.8 0.0 copy-start.1
  33.8 1.0 %shard_map.181 = (bf16[96,1024]{1,0:T(8,128)(2,1)S(1)}, bf16[96,512]{1,0:T(8,128)(2,1)S(1)}, bf16[64,512]{1,0:T(8,128)(2,1)S(1)}, bf16[32,512]{1,0:T(8,128)(2,1)S(1)}) custom-call(bf16[4,144,512]{2,1,0:T(8,128)(2,1)S(1)} %get-tuple-element.95.normed_ref, bf16[2048,1024]{1,0:T(8,128)(2,1)S(1)} %get-tuple-element.96.wmerge_ref, bf16[192,144]{1,0:T(8,128)(2,1)S(1)} %copy-done.3), custom_call_target="tpu_custom_call" | custom-call | flops 1000000000 | bytes 2000000 | tf_op jit(solution)/shard_map/pallas_call | solution.py:505
  34.8 3.1 %shard_map.180 = (bf16[320,512]{1,0:T(8,128)(2,1)S(1)}, bf16[320,1536]{1,0:T(8,128)(2,1)S(1)}, bf16[512,640]{1,0:T(8,128)(2,1)S(1)}, bf16[512,640]{1,0:T(8,128)(2,1)S(1)}) custom-call(bf16[576,512]{1,0:T(8,128)(2,1)S(1)} %get-tuple-element.84.dsum_ref, bf16[400,1536]{1,0:T(8,128)(2,1)S(1)} %get-tuple-element.86.qkv_ref, ...), custom_call_target="tpu_custom_call" | custom-call | flops 1000000000 | bytes 2000000 | tf_op jit(solution)/shard_map/pallas_call | solution.py:500
  37.9 2.6 %collective-permute-done.4.row_ref = bf16[48,512]{1,0:T(8,128)(2,1)S(1)} collective-permute-done((bf16[48,512]{1,0:T(8,128)(2,1)S(1)}, bf16[48,512]{1,0:T(8,128)(2,1)S(1)}, u32[]{:S(2)}, u32[]{:S(2)}) %collective-permute-start.4) | collective-permute-done | bytes 49184 | tf_op jit(solution)/shard_map/ppermute | solution.py:543
  40.5 4.9 %shard_map.182 = (bf16[640,1536]{1,0:T(8,128)(2,1)S(1)}, bf16[4,32,32,128]{3,2,1,0:T(8,128)(2,1)S(1)}, bf16[4,32,32,128]{3,2,1,0:T(8,128)(2,1)S(1)}) custom-call(bf16[576,512]{1,0:T(8,128)(2,1)S(1)} %get-tuple-element.84.dsum_ref, bf16[48,512]{1,0:T(8,128)(2,1)S(1)} %collective-permute-done.4.row_ref, bf16[512,640]{1,0:T(8,128)(2,1)S(1)} %get-tuple-element.92.xst_ref, ...), custom_call_target="tpu_custom_call" | custom-call | flops 1000000000 | bytes 2000000 | tf_op jit(solution)/shard_map/pallas_call | solution.py:512
  45.4 0.5 collective-permute-start.6
  45.9 2.5 %shard_map.183 = (bf16[432,512]{1,0:T(8,128)(2,1)S(1)}, bf16[240,512]{1,0:T(8,128)(2,1)S(1)}, bf16[160,512]{1,0:T(8,128)(2,1)S(1)}, bf16[80,512]{1,0:T(8,128)(2,1)S(1)}) custom-call(bf16[640,1536]{1,0:T(8,128)(2,1)S(1)} %get-tuple-element.102.dqkv_ref, bf16[512,1536]{1,0:T(8,128)(2,1)S(1)} %get-tuple-element.69.wqkv_ref, ...), custom_call_target="tpu_custom_call" | custom-call | flops 1000000000 | bytes 2000000 | tf_op jit(solution)/shard_map/pallas_call | solution.py:517
  48.3 0.0 collective-permute-done.6.b_ref
  48.4 0.2 shard_map.184
  48.6 0.5 collective-permute-start.7
  49.1 1.6 %collective-permute-start.8 = (bf16[32,32,128]{2,1,0:T(8,128)(2,1)S(1)}, bf16[32,32,128]{2,1,0:T(8,128)(2,1)S(1)}, u32[]{:S(2)}, u32[]{:S(2)}) collective-permute-start(bf16[32,32,128]{2,1,0:T(8,128)(2,1)S(1)} %get-tuple-element.115), channel_id=1, source_target_pairs={{0,4},{1,129},{2,6},{3,131},{4,0},{5,133},{6,2},{7,135},{8,12},{9,... | collective-permute-start | bytes 786440 | tf_op jit(solution)/shard_map/ppermute | solution.py:567
  50.6 1.9 %collective-permute-start.9 = (bf16[32,32,128]{2,1,0:T(8,128)(2,1)S(1)}, bf16[32,32,128]{2,1,0:T(8,128)(2,1)S(1)}, u32[]{:S(2)}, u32[]{:S(2)}) collective-permute-start(bf16[32,32,128]{2,1,0:T(8,128)(2,1)S(1)} %get-tuple-element.116), channel_id=1, source_target_pairs={{0,6},{1,137},{2,4},{3,139},{4,2},{5,141},{6,0},{7,143},{8,14},{9,... | collective-permute-start | bytes 786440 | tf_op jit(solution)/shard_map/ppermute | solution.py:567
  52.6 0.0 collective-permute-start.5
  52.6 8.8 %collective-permute-done.5.lat_ref = bf16[240,512]{1,0:T(8,128)(2,1)S(1)} collective-permute-done((bf16[240,512]{1,0:T(8,128)(2,1)S(1)}, bf16[240,512]{1,0:T(8,128)(2,1)S(1)}, u32[]{:S(2)}, u32[]{:S(2)}) %collective-permute-start.5) | collective-permute-done | bytes 245792 | tf_op jit(solution)/shard_map/ppermute | solution.py:543
  61.3 3.8 %collective-permute-done.9.d_ref = bf16[32,32,128]{2,1,0:T(8,128)(2,1)S(1)} collective-permute-done((bf16[32,32,128]{2,1,0:T(8,128)(2,1)S(1)}, bf16[32,32,128]{2,1,0:T(8,128)(2,1)S(1)}, u32[]{:S(2)}, u32[]{:S(2)}) %collective-permute-start.9) | collective-permute-done | bytes 262176 | tf_op jit(solution)/shard_map/ppermute | solution.py:567
  65.2 0.8 shard_map.185
  66.0 6.5 %all-to-all-start = ((bf16[32,32,128]{2,1,0:T(8,128)(2,1)}), bf16[32,32,128]{2,1,0:T(8,128)(2,1)S(1)}, u32[]{:S(2)}, u32[]{:S(2)}) async-start(bf16[32,32,128]{2,1,0:T(8,128)(2,1)} %shard_map.185), calls=%async_computation | async-start | bytes 524288 | tf_op jit(solution)/shard_map/all_to_all | solution.py:577
  72.5 0.1 collective-permute-start.10
  72.6 2.5 %collective-permute-start.11 = (bf16[80,512]{1,0:T(8,128)(2,1)S(1)}, bf16[80,512]{1,0:T(8,128)(2,1)S(1)}, u32[]{:S(2)}, u32[]{:S(2)}) collective-permute-start(bf16[80,512]{1,0:T(8,128)(2,1)S(1)} %get-tuple-element.119), channel_id=1, source_target_pairs={{0,17},{1,18},{2,19},{3,20},{4,21},{5,22},{6,23},{7,24},{8,25},{9,... | collective-permute-start | bytes 245768 | tf_op jit(solution)/shard_map/ppermute | solution.py:543
  75.1 8.5 %collective-permute-done.11.diag_ref = bf16[80,512]{1,0:T(8,128)(2,1)S(1)} collective-permute-done((bf16[80,512]{1,0:T(8,128)(2,1)S(1)}, bf16[80,512]{1,0:T(8,128)(2,1)S(1)}, u32[]{:S(2)}, u32[]{:S(2)}) %collective-permute-start.11) | collective-permute-done | bytes 81952 | tf_op jit(solution)/shard_map/ppermute | solution.py:543
  83.6 0.0 collective-permute-done.10.lon_ref
  83.6 1.0 %shard_map.186 = (bf16[576,512]{1,0:T(8,128)(2,1)}, bf16[144,1024]{1,0:T(8,128)(2,1)}) custom-call(bf16[432,512]{1,0:T(8,128)(2,1)S(1)} %get-tuple-element.106.main_ref, bf16[240,512]{1,0:T(8,128)(2,1)S(1)} %collective-permute-done.5.lat_ref, bf16[160,512]{1,0:T(8,128)(2,1)S(1)} %collective-permute-done.10.lon_ref, ...), custom_call_target="tpu_custom_call" | custom-call | flops 1000000000 | bytes 2000000 | tf_op jit(solution)/shard_map/pallas_call | solution.py:527
  84.6 0.9 %all-to-all-done.parts_ref = bf16[32,32,128]{2,1,0:T(8,128)(2,1)S(1)} async-done(((bf16[32,32,128]{2,1,0:T(8,128)(2,1)}), bf16[32,32,128]{2,1,0:T(8,128)(2,1)S(1)}, u32[]{:S(2)}, u32[]{:S(2)}) %all-to-all-start) | async-done | bytes 262176 | tf_op jit(solution)/shard_map/all_to_all | solution.py:577
  85.5 0.7 shard_map.187
  (23 shorter events, 0.0 us)
Async XLA Ops:
  0.6 1.1 %copy-start.5 = (bf16[12,48,512]{2,1,0:T(8,128)(2,1)S(1)}, bf16[12,48,512]{2,1,0:T(8,128)(2,1)}, u32[]{:S(2)}) copy-start(bf16[12,48,512]{2,1,0:T(8,128)(2,1)} %param.16) | copy-start | bytes 1769476
  1.7 1.0 %copy-start.7 = (bf16[6,24,1024]{2,1,0:T(8,128)(2,1)S(1)}, bf16[6,24,1024]{2,1,0:T(8,128)(2,1)}, u32[]{:S(2)}) copy-start(bf16[6,24,1024]{2,1,0:T(8,128)(2,1)} %param.22) | copy-start | bytes 884740
  2.7 13.7 %copy-start.4 = (bf16[512,1536]{1,0:T(8,128)(2,1)S(1)}, bf16[512,1536]{1,0:T(8,128)(2,1)}, u32[]{:S(2)}) copy-start(bf16[512,1536]{1,0:T(8,128)(2,1)} %refs_2_.1) | copy-start | bytes 4718596
  2.7 13.7 %copy-start.6 = (bf16[512,512]{1,0:T(8,128)(2,1)S(1)}, bf16[512,512]{1,0:T(8,128)(2,1)}, u32[]{:S(2)}) copy-start(bf16[512,512]{1,0:T(8,128)(2,1)} %refs_3_.1) | copy-start | bytes 1572868
  2.7 13.7 %copy-start.8 = (f32[2048]{0:T(1024)S(1)}, f32[2048]{0:T(1024)}, u32[]{:S(2)}) copy-start(f32[2048]{0:T(1024)} %param.20) | copy-start | bytes 24580
  2.7 13.7 %copy-start.9 = (f32[512]{0:T(512)S(1)}, f32[512]{0:T(512)}, u32[]{:S(2)}) copy-start(f32[512]{0:T(512)} %param.17) | copy-start | bytes 6148
  2.7 13.7 %copy-start.10 = (bf16[320,336]{1,0:T(8,128)(2,1)S(1)}, bf16[320,336]{1,0:T(8,128)(2,1)}, u32[]{:S(2)}) copy-start(bf16[320,336]{1,0:T(8,128)(2,1)} %constant.18.clone.refs_1_) | copy-start | bytes 645124
  2.7 13.7 %copy-start.11 = (bf16[288,320]{1,0:T(8,128)(2,1)S(1)}, bf16[288,320]{1,0:T(8,128)(2,1)}, u32[]{:S(2)}) copy-start(bf16[288,320]{1,0:T(8,128)(2,1)} %constant.20.clone.refs_6_) | copy-start | bytes 552964
  2.7 13.7 %copy-start.12 = (bf16[288,336]{1,0:T(8,128)(2,1)S(1)}, bf16[288,336]{1,0:T(8,128)(2,1)}, u32[]{:S(2)}) copy-start(bf16[288,336]{1,0:T(8,128)(2,1)} %constant.19.clone.refs_5_) | copy-start | bytes 580612
  2.7 13.6 %copy-start.13 = (bf16[192,192]{1,0:T(8,128)(2,1)S(1)}, bf16[192,192]{1,0:T(8,128)(2,1)}, u32[]{:S(2)}) copy-start(bf16[192,192]{1,0:T(8,128)(2,1)} %constant.22.clone.refs_8_) | copy-start | bytes 221188
  2.7 13.6 %copy-start.14 = (bf16[192,192]{1,0:T(8,128)(2,1)S(1)}, bf16[192,192]{1,0:T(8,128)(2,1)}, u32[]{:S(2)}) copy-start(bf16[192,192]{1,0:T(8,128)(2,1)} %constant.21.clone.refs_7_) | copy-start | bytes 221188
  2.7 13.6 %copy-start.15 = (bf16[144,192]{1,0:T(8,128)(2,1)S(1)}, bf16[144,192]{1,0:T(8,128)(2,1)}, u32[]{:S(2)}) copy-start(bf16[144,192]{1,0:T(8,128)(2,1)} %constant.23.clone.refs_9_) | copy-start | bytes 165892
  3.0 17.6 %collective-permute-start = (bf16[240,512]{1,0:T(8,128)(2,1)S(1)}, bf16[240,512]{1,0:T(8,128)(2,1)S(1)}, u32[]{:S(2)}, u32[]{:S(2)}) collective-permute-start(bf16[240,512]{1,0:T(8,128)(2,1)S(1)} %get-tuple-element.65), channel_id=1, source_target_pairs={{0,240},{1,241},{2,242},{3,243},{4,244},{5,245},{6,246},{7,247},{8... | collective-permute-start | bytes 737288 | tf_op jit(solution)/shard_map/ppermute | solution.py:543
  12.1 8.4 %collective-permute-start.1 = (bf16[192,512]{1,0:T(8,128)(2,1)S(1)}, bf16[192,512]{1,0:T(8,128)(2,1)S(1)}, u32[]{:S(2)}, u32[]{:S(2)}) collective-permute-start(bf16[192,512]{1,0:T(8,128)(2,1)S(1)} %get-tuple-element.66), channel_id=1, source_target_pairs={{0,15},{1,0},{2,1},{3,2},{4,3},{5,4},{6,5},{7,6},{8,7},{9,8},{10,9... | collective-permute-start | bytes 589832 | tf_op jit(solution)/shard_map/ppermute | solution.py:543
  13.1 7.5 %collective-permute-start.2 = (bf16[80,512]{1,0:T(8,128)(2,1)S(1)}, bf16[80,512]{1,0:T(8,128)(2,1)S(1)}, u32[]{:S(2)}, u32[]{:S(2)}) collective-permute-start(bf16[80,512]{1,0:T(8,128)(2,1)S(1)} %get-tuple-element.67), channel_id=1, source_target_pairs={{0,255},{1,240},{2,241},{3,242},{4,243},{5,244},{6,245},{7,246},{8... | collective-permute-start | bytes 245768 | tf_op jit(solution)/shard_map/ppermute | solution.py:543
  20.6 9.7 %copy-start = (bf16[2048,1024]{1,0:T(8,128)(2,1)S(1)}, bf16[2048,1024]{1,0:T(8,128)(2,1)}, u32[]{:S(2)}) copy-start(bf16[2048,1024]{1,0:T(8,128)(2,1)} %wmerge_ref.1) | copy-start | bytes 12582916
  24.6 7.6 %collective-permute-start.3 = (bf16[48,512]{1,0:T(8,128)(2,1)S(1)}, bf16[48,512]{1,0:T(8,128)(2,1)S(1)}, u32[]{:S(2)}, u32[]{:S(2)}) collective-permute-start(bf16[48,512]{1,0:T(8,128)(2,1)S(1)} %get-tuple-element.76), channel_id=1, source_target_pairs={{0,240},{1,241},{2,242},{3,243},{4,244},{5,245},{6,246},{7,247},{8... | collective-permute-start | bytes 147464 | tf_op jit(solution)/shard_map/ppermute | solution.py:543
  32.3 1.5 %copy-start.3 = (bf16[192,144]{1,0:T(8,128)(2,1)S(1)}, bf16[192,144]{1,0:T(8,128)(2,1)}, u32[]{:S(2)}) copy-start(bf16[192,144]{1,0:T(8,128)(2,1)} %constant.26.clone.unshift_ref) | copy-start | bytes 165892
  33.5 6.9 %collective-permute-start.4 = (bf16[48,512]{1,0:T(8,128)(2,1)S(1)}, bf16[48,512]{1,0:T(8,128)(2,1)S(1)}, u32[]{:S(2)}, u32[]{:S(2)}) collective-permute-start(bf16[48,512]{1,0:T(8,128)(2,1)S(1)} %get-tuple-element.85), channel_id=1, source_target_pairs={{0,16},{1,17},{2,18},{3,19},{4,20},{5,21},{6,22},{7,23},{8,24},{9,... | collective-permute-start | bytes 147464 | tf_op jit(solution)/shard_map/ppermute | solution.py:543
  33.8 1.0 %copy-start.1 = (bf16[320,288]{1,0:T(8,128)(2,1)S(1)}, bf16[320,288]{1,0:T(8,128)(2,1)}, u32[]{:S(2)}) copy-start(bf16[320,288]{1,0:T(8,128)(2,1)} %constant.24.clone.pick_ref) | copy-start | bytes 552964
  40.5 5.4 %copy-start.2 = (bf16[336,288]{1,0:T(8,128)(2,1)S(1)}, bf16[336,288]{1,0:T(8,128)(2,1)}, u32[]{:S(2)}) copy-start(bf16[336,288]{1,0:T(8,128)(2,1)} %constant.25.clone.unshift_ref) | copy-start | bytes 580612
  45.4 3.0 %collective-permute-start.6 = (bf16[4,32,32,128]{3,2,1,0:T(8,128)(2,1)S(1)}, bf16[4,32,32,128]{3,2,1,0:T(8,128)(2,1)S(1)}, u32[]{:S(2)}, u32[]{:S(2)}) collective-permute-start(bf16[4,32,32,128]{3,2,1,0:T(8,128)(2,1)S(1)} %get-tuple-element.110), channel_id=1, source_target_pairs={{0,1},{1,0},{2,3},{3,2},{4,5},{5,4},{6,7},{7,6},{8,9},{9,8},{10,11... | collective-permute-start | bytes 3145736 | tf_op jit(solution)/shard_map/ppermute | solution.py:570
  48.6 12.7 %collective-permute-start.7 = (bf16[32,32,128]{2,1,0:T(8,128)(2,1)S(1)}, bf16[32,32,128]{2,1,0:T(8,128)(2,1)S(1)}, u32[]{:S(2)}, u32[]{:S(2)}) collective-permute-start(bf16[32,32,128]{2,1,0:T(8,128)(2,1)S(1)} %get-tuple-element.114), channel_id=1, source_target_pairs={{0,2},{1,9},{2,0},{3,11},{4,6},{5,13},{6,4},{7,15},{8,10},{9,1},{1... | collective-permute-start | bytes 786440 | tf_op jit(solution)/shard_map/ppermute | solution.py:567
  49.1 12.3 %collective-permute-start.8 = (bf16[32,32,128]{2,1,0:T(8,128)(2,1)S(1)}, bf16[32,32,128]{2,1,0:T(8,128)(2,1)S(1)}, u32[]{:S(2)}, u32[]{:S(2)}) collective-permute-start(bf16[32,32,128]{2,1,0:T(8,128)(2,1)S(1)} %get-tuple-element.115), channel_id=1, source_target_pairs={{0,4},{1,129},{2,6},{3,131},{4,0},{5,133},{6,2},{7,135},{8,12},{9,... | collective-permute-start | bytes 786440 | tf_op jit(solution)/shard_map/ppermute | solution.py:567
  50.6 14.5 %collective-permute-start.9 = (bf16[32,32,128]{2,1,0:T(8,128)(2,1)S(1)}, bf16[32,32,128]{2,1,0:T(8,128)(2,1)S(1)}, u32[]{:S(2)}, u32[]{:S(2)}) collective-permute-start(bf16[32,32,128]{2,1,0:T(8,128)(2,1)S(1)} %get-tuple-element.116), channel_id=1, source_target_pairs={{0,6},{1,137},{2,4},{3,139},{4,2},{5,141},{6,0},{7,143},{8,14},{9,... | collective-permute-start | bytes 786440 | tf_op jit(solution)/shard_map/ppermute | solution.py:567
  52.6 8.8 %collective-permute-start.5 = (bf16[240,512]{1,0:T(8,128)(2,1)S(1)}, bf16[240,512]{1,0:T(8,128)(2,1)S(1)}, u32[]{:S(2)}, u32[]{:S(2)}) collective-permute-start(bf16[240,512]{1,0:T(8,128)(2,1)S(1)} %get-tuple-element.107), channel_id=1, source_target_pairs={{0,16},{1,17},{2,18},{3,19},{4,20},{5,21},{6,22},{7,23},{8,24},{9,... | collective-permute-start | bytes 737288 | tf_op jit(solution)/shard_map/ppermute | solution.py:543
  66.0 19.6 %all-to-all-start = ((bf16[32,32,128]{2,1,0:T(8,128)(2,1)}), bf16[32,32,128]{2,1,0:T(8,128)(2,1)S(1)}, u32[]{:S(2)}, u32[]{:S(2)}) async-start(bf16[32,32,128]{2,1,0:T(8,128)(2,1)} %shard_map.185), calls=%async_computation | async-start | bytes 524288 | tf_op jit(solution)/shard_map/all_to_all | solution.py:577
  72.5 11.1 %collective-permute-start.10 = (bf16[160,512]{1,0:T(8,128)(2,1)S(1)}, bf16[160,512]{1,0:T(8,128)(2,1)S(1)}, u32[]{:S(2)}, u32[]{:S(2)}) collective-permute-start(bf16[160,512]{1,0:T(8,128)(2,1)S(1)} %get-tuple-element.117), channel_id=1, source_target_pairs={{0,1},{1,2},{2,3},{3,4},{4,5},{5,6},{6,7},{7,8},{8,9},{9,10},{10,1... | collective-permute-start | bytes 491528 | tf_op jit(solution)/shard_map/ppermute | solution.py:543
  72.6 11.0 %collective-permute-start.11 = (bf16[80,512]{1,0:T(8,128)(2,1)S(1)}, bf16[80,512]{1,0:T(8,128)(2,1)S(1)}, u32[]{:S(2)}, u32[]{:S(2)}) collective-permute-start(bf16[80,512]{1,0:T(8,128)(2,1)S(1)} %get-tuple-element.119), channel_id=1, source_target_pairs={{0,17},{1,18},{2,19},{3,20},{4,21},{5,22},{6,23},{7,24},{8,25},{9,... | collective-permute-start | bytes 245768 | tf_op jit(solution)/shard_map/ppermute | solution.py:543

commit v4 on v3

--- a/solution.py
+++ b/solution.py
@@ -180,7 +180,7 @@
             dqkv_ref[out, 2 * D + at : 2 * D + at + GROUP_WIDTH] = d_values.astype(bf16)
 
 
-def border_kernel(tok_ref, g_ref, own_ref, own_g_ref, top_ref, edge_ref, corner_ref, sem):
+def border_kernel(tok_ref, g_ref, own_ref, own_g_ref, top_ref, g_top_ref, edge_ref, corner_ref, sem):
     copies = [
         pltpu.make_async_copy(tok_ref, own_ref, sem.at[0]),
         pltpu.make_async_copy(g_ref, own_g_ref, sem.at[1]),
@@ -192,8 +192,8 @@
     edge = [own_ref[row * COLS : row * COLS + 16].astype(f32)[:BORDER] for row in range(ROWS)]
     cots = own_g_ref[...].astype(f32)
     side = [cots[row * PAIR_COLS : row * PAIR_COLS + BORDER] for row in range(PAIR_ROWS)]
-    top_ref[:TOP] = own_ref[:TOP]
-    top_ref[TOP:] = halves(own_g_ref[:PAIR_TOP])
+    top_ref[...] = own_ref[:TOP]
+    g_top_ref[...] = halves(own_g_ref[:PAIR_TOP])
     edge_ref[:EDGE] = jnp.concatenate(edge, axis=0).astype(bf16)
     edge_ref[EDGE:] = halves(jnp.concatenate(side, axis=0).astype(bf16))
     corner_ref[:SIDE] = jnp.concatenate(edge[:WIN_LAT], axis=0).astype(bf16)
@@ -226,7 +226,7 @@
     def normed(values):
         return norm_parts(values)[0] * gain_ref[...]
 
-    lat, lon, diag = lat_ref[:TOP], lon_ref[:EDGE].astype(f32), diag_ref[:SIDE].astype(f32)
+    lat, lon, diag = lat_ref[...], lon_ref[:EDGE].astype(f32), diag_ref[:SIDE].astype(f32)
     first, second = band_sources(cells_ref[...], normed(lat.astype(f32)).astype(bf16), normed(lon), normed(diag))
     xs_ref[:PAD] = dot(pick_ref[INNER:], first).astype(bf16)
     xs_ref[PAD:] = dot(pick_ref[...], second).astype(bf16)
@@ -250,7 +250,7 @@
     copy.start()
     parts = []
     for half in range(2):
-        lat = lat_ref[TOP + half * PAIR_TOP : TOP + (half + 1) * PAIR_TOP]
+        lat = lat_ref[half * PAIR_TOP : (half + 1) * PAIR_TOP]
         at = EDGE + half * PAIR_SIDE
         lon = lon_ref[at + PAIR_CORNER : at + PAIR_SIDE]
         diag = diag_ref[SIDE + half * PAIR_CORNER : SIDE + (half + 1) * PAIR_CORNER]
@@ -362,7 +362,7 @@
 
 
 def cells_back_kernel(
-    dqkv_ref, wqkv_ref, cells_pick_ref, unshift_ref, tok_ref, dsum_ref, row_ref, gain_ref, m_lat_ref, m_lon_ref, m_diag_ref,
+    dqkv_ref, wqkv_ref, cells_pick_ref, unshift_ref, tok_ref, dsum_ref, row_ref, gain_ref, m_lon_ref, m_diag_ref,
     main_ref, lat_ref, lon_ref, diag_ref,
     dx_ref,
 ):
@@ -382,10 +382,9 @@
             main_ref[:BAND_CELLS] = cells[:BAND_CELLS]
         else:
             main_ref[BAND_CELLS:] = cells[: BAND_CELLS - TOP]
-            lat_ref[:TOP] = cells[BAND_CELLS - TOP : BAND_CELLS]
+            lat_ref[...] = cells[BAND_CELLS - TOP : BAND_CELLS]
             diag_ref[:SIDE] = cells[BAND_CELLS:]
         lon_ref[band * SIDE : (band + 1) * SIDE] = cells[BAND_CELLS:]
-    lat_ref[TOP:] = m_lat_ref[...]
     lon_ref[EDGE:] = m_lon_ref[...]
     diag_ref[SIDE:] = m_diag_ref[...]
 
@@ -397,15 +396,15 @@
     return jnp.concatenate([first, field[:, BORDER:]], axis=1).reshape(rows * cols, width).astype(bf16)
 
 
-def own_cells_kernel(main_ref, lat_ref, lon_ref, diag_ref, m_main_ref, tokens_ref, merged_ref):
+def own_cells_kernel(main_ref, lat_ref, lon_ref, diag_ref, m_main_ref, m_lat_ref, tokens_ref, merged_ref):
     corner = diag_ref[:SIDE].astype(f32)[SIDE - CORNER :]
     beside = lon_ref[:EDGE].astype(f32)[: EDGE - CORNER]
-    tokens_ref[:TOP] = fill_edge(lat_ref[:TOP], corner, SHIFT_LAT, COLS)
+    tokens_ref[:TOP] = fill_edge(lat_ref[...], corner, SHIFT_LAT, COLS)
     tokens_ref[TOP:] = fill_edge(main_ref[...], beside, ROWS - SHIFT_LAT, COLS)
     side_rows = PAIR_SIDE - PAIR_CORNER
     for half in range(2):
         cols = pl.ds(half * D, D)
-        lat = lat_ref[TOP + half * PAIR_TOP : TOP + (half + 1) * PAIR_TOP]
+        lat = m_lat_ref[half * PAIR_TOP : (half + 1) * PAIR_TOP]
         lon = lon_ref[EDGE + half * side_rows : EDGE + (half + 1) * side_rows]
         diag = diag_ref[SIDE + half * PAIR_CORNER : SIDE + (half + 1) * PAIR_CORNER]
         merged_ref[:PAIR_TOP, cols] = fill_edge(lat, diag, 2, PAIR_COLS)
@@ -453,16 +452,18 @@
 
 
 def chain(tok, gain, w_qkv, w_proj, gain_merge, w_merge, g_merged, fetch, up, down):
-    tok, g_merged, top, edge, corner = call(
+    tok, g_merged, top, g_top, edge, corner = call(
         border_kernel,
         [
             ((TOKENS, D), bf16), ((PAIRS, 2 * D), bf16),
-            ((TOP + 2 * PAIR_TOP, D), bf16), ((EDGE + 2 * PAIR_SIDE, D), bf16), ((SIDE + 2 * PAIR_CORNER, D), bf16),
+            ((TOP, D), bf16), ((2 * PAIR_TOP, D), bf16),
+            ((EDGE + 2 * PAIR_SIDE, D), bf16), ((SIDE + 2 * PAIR_CORNER, D), bf16),
         ],
         [pltpu.SemaphoreType.DMA((2,))],
         [2, 2],
     )(tok, g_merged)
     beside = fetch(top, edge, corner)
+    g_lat = up(g_top)
     pair, band = pair_selector(), band_selector()
     shift = shift_selector(WIN_LAT, COLS, SHIFT_LON)
     pair_shift = shift_selector(PAIR_ROWS, PAIR_COLS, SHIFT_LON // 2)
@@ -487,7 +488,7 @@
         [((4, PAIRS, D), f32), ((4 * D, 2 * D), bf16)],
         [pltpu.SemaphoreType.DMA],
         [0] * 6 + [1],
-    )(after(g_merged, row), *beside, gain_merge, pair_shift, w_merge)
+    )(after(g_merged, row), g_lat, *beside[1:], gain_merge, pair_shift, w_merge)
     d_summed, row, merge_normed = call(
         pair_kernel,
         [((TOKENS, D), bf16), ((COLS, D), bf16), ((4, PAIRS, D), bf16)],
@@ -509,27 +510,28 @@
             ((2 * (PAIR_SIDE - PAIR_CORNER), D), bf16), ((2 * PAIR_CORNER, D), bf16),
         ],
     )(merge_normed, w_merge, pair_unshift)
+    m_lat = down(m_lat)
     dqkv, keep, sent = call(
         outer_back_kernel,
         [((WIDTH, 3 * D), bf16), ((4, 32, 32, 128), bf16), ((4, 32, 32, 128), bf16)],
         [((WIDTH, D), bf16), ((BAND, D), bf16)],
-    )(d_summed, first, xst, mixt, after(up1, m_lat), dqkv1, qkv0, probs0, qkv1, probs1, w_proj, band)
+    )(d_summed, first, xst, mixt, after(up1, m_main), dqkv1, qkv0, probs0, qkv1, probs1, w_proj, band)
     main, to_lat, to_lon, to_diag = call(
         cells_back_kernel,
         [
-            ((TOKENS - TOP, D), bf16), ((TOP + 2 * PAIR_TOP, D), bf16),
+            ((TOKENS - TOP, D), bf16), ((TOP, D), bf16),
             ((EDGE + 2 * (PAIR_SIDE - PAIR_CORNER), D), bf16), ((SIDE + 2 * PAIR_CORNER, D), bf16),
         ],
         [((WIDTH, D), bf16)],
-    )(dqkv, w_qkv, cells_pick, unshift, tok, d_summed, first, gain, m_lat, m_lon, m_diag)
+    )(dqkv, w_qkv, cells_pick, unshift, tok, d_summed, first, gain, m_lon, m_diag)
 
     def finish(lat, lon, diag):
         grad_tokens, merged = call(own_cells_kernel, [((TOKENS, D), bf16), ((PAIRS, 2 * D), bf16)])(
-            main, lat, lon, diag, m_main
+            main, lat, lon, diag, m_main, m_lat
         )
         return merged, grad_tokens
 
-    return finish, keep, sent, (to_lat, to_lon, to_diag)
+    return finish, keep, sent, (to_lat, to_lon, to_diag), m_lat
 
 
 def solution(mesh):
@@ -570,23 +572,22 @@
         other = lax.ppermute(sent, ("lat", "lon"), [(i, i ^ 1) for i in range(count)])
         own, *others = call(add_kernel, [((32, 32, 128), bf16)] * 4)(keep, after(other, to_lat))
         got = [swap(block, step) for step, block in enumerate(others, 1)]
-        lat = send(to_lat, 1, 0)
-        return call(join_kernel, [((32, 32, 128), bf16)])(after(own, lat), *got)[0], lat
+        return call(join_kernel, [((32, 32, 128), bf16)])(own, *got)[0]
 
     def reduce_rest(sums):
         parts = lax.all_to_all(sums, ("lat", "lon"), 0, 0, axis_index_groups=rest, tiled=True)
         return call(sum_kernel, [((32, 128), f32)])(parts)[0]
 
     def body(tokens, gain_attn, w_qkv, w_proj, gain_merge, w_merge, g_merged):
-        finish, keep, sent, (to_lat, to_lon, to_diag) = chain(
+        finish, keep, sent, pieces, m_lat = chain(
             tokens.reshape(TOKENS, D), gain_attn.reshape(1, D), w_qkv, w_proj, gain_merge.reshape(4, 1, D),
             w_merge, g_merged.reshape(PAIRS, 2 * D), fetch,
             lambda row: send(row, -1, 0), lambda row: send(row, 1, 0),
         )
-        sums, lat = reduce_across(keep, sent, to_lat)
+        sums = after(reduce_across(keep, sent, pieces[0]), m_lat)
         grad_weights = reduce_rest(sums)
-        lon, diag = send(after(to_lon, sums), 0, 1), send(after(to_diag, sums), 1, 1)
-        merged, grad_tokens = finish(lat, lon, diag)
+        to_lat, to_lon, to_diag = (after(piece, sums) for piece in pieces)
+        merged, grad_tokens = finish(send(to_lat, 1, 0), send(to_lon, 0, 1), send(to_diag, 1, 1))
         return (
             merged.reshape(ROWS // 2, COLS // 2, 2 * D),
             grad_tokens.reshape(ROWS, COLS, D),

time: 86.5 us -> 85.1 us (0.984)
  waiting for transfers between devices: 24.6 us -> 22.4 us
    ppermute x8 -> x10, waiting for transfers between devices: 19.8 us -> 13.5 us  [send(): return lax.ppermute(block, ('lat', 'lon'), route)]
    ppermute x3, waiting for transfers between devices: 3.83 us -> 8.83 us  [swap(): lax.ppermute(block, ('lat', 'lon'), [(i, across(i, step)) for i in range(...]
    all_to_all x1, starting transfers between devices: 6.54 us -> 4.09 us  [reduce_rest(): lax.all_to_all(sums, ('lat', 'lon'), 0, 0, axis_index_groups=rest, tiled=...]
    ppermute x1, starting transfers between devices: 0.48 us -> 2.06 us  [reduce_across(): lax.ppermute(sent, ('lat', 'lon'), [(i, i ^ 1) for i in range(count)])]
    ppermute x8 -> x10, starting transfers between devices: 21.8 us -> 23 us  [send(): return lax.ppermute(block, ('lat', 'lon'), route)]
    all_to_all x1, waiting for transfers between devices: 0.94 us -> 0.01 us  [reduce_rest(): lax.all_to_all(sums, ('lat', 'lon'), 0, 0, axis_index_groups=rest, tiled=...]
  transfers between devices with their start and end apart: 13 -> 15, of which waited for: 5 -> 5; matrix products, arithmetic and copies ran while one was open for 0% -> 0% of each run, Pallas kernels for 16% -> 22%
where the time goes in v4:
time: 85.1 us; the launch traced here: 84.3 us
  starting transfers between devices  33.1 us (39%)
  Pallas kernels  25.8 us (30%)
  waiting for transfers between devices  22.4 us (26%)
  local copies, waits for them, and re-layouts  2.1 us (2%)
  between operations  0.93 us (1%)
    ppermute x10, starting transfers between devices, send(): return lax.ppermute(block, ('lat', 'lon'), route)  23 us
    ppermute x10, waiting for transfers between devices, send(): return lax.ppermute(block, ('lat', 'lon'), route)  13.5 us
    ppermute x3, waiting for transfers between devices, swap(): lax.ppermute(block, ('lat', 'lon'), [(i, across(i, step)) for i in range(...  8.83 us
    pallas_call x1, Pallas kernels, chain(): call(outer_back_kernel, [((WIDTH, 3 * D), bf16), ((4, 32, 32, 128), bf16)...  4.88 us
    pallas_call x1, Pallas kernels, chain(): call(inner_kernel, [(h.shape, h.dtype) for h in held] + [((TOKENS - TOP,...  4.15 us
    all_to_all x1, starting transfers between devices, reduce_rest(): lax.all_to_all(sums, ('lat', 'lon'), 0, 0, axis_index_groups=rest, tiled=...  4.09 us
    pallas_call x1, Pallas kernels, chain(): call(outer_kernel, saved(REST) + [((TOKENS, D), bf16), ((TOKENS, D), bf16...  4.04 us
    ppermute x3, starting transfers between devices, swap(): lax.ppermute(block, ('lat', 'lon'), [(i, across(i, step)) for i in range(...  3.94 us
  transfers between devices with their start and end apart: 15, of which 5 were waited for; matrix products, arithmetic and copies ran while one was open for 0% of the time, Pallas kernels for 22%

profile of v4, /device:TPU:1, one launch (start us, length us, event | category | flops | bytes accessed | tf_op | source)
XLA Modules:
  0.0 84.3 jit_solution(17235159332937682128)
XLA Ops:
  0.6 1.1 %copy-done.5 = bf16[12,48,512]{2,1,0:T(8,128)(2,1)S(1)} copy-done((bf16[12,48,512]{2,1,0:T(8,128)(2,1)S(1)}, bf16[12,48,512]{2,1,0:T(8,128)(2,1)}, u32[]{:S(2)}) %copy-start.5) | copy-done | bytes 589848
  1.7 1.0 %copy-done.7 = bf16[6,24,1024]{2,1,0:T(8,128)(2,1)S(1)} copy-done((bf16[6,24,1024]{2,1,0:T(8,128)(2,1)S(1)}, bf16[6,24,1024]{2,1,0:T(8,128)(2,1)}, u32[]{:S(2)}) %copy-start.7) | copy-done | bytes 294936
  2.7 0.0 copy-start.10
  2.7 0.0 copy-start.11
  2.7 0.0 copy-start.12
  2.7 0.0 copy-start.13
  2.7 0.0 copy-start.14
  2.7 0.0 copy-start.15
  2.7 0.2 shard_map.175
  3.0 3.3 %collective-permute-start.1 = (bf16[192,512]{1,0:T(8,128)(2,1)S(1)}, bf16[192,512]{1,0:T(8,128)(2,1)S(1)}, u32[]{:S(2)}, u32[]{:S(2)}) collective-permute-start(bf16[192,512]{1,0:T(8,128)(2,1)S(1)} %get-tuple-element.68), channel_id=1, source_target_pairs={{0,15},{1,0},{2,1},{3,2},{4,3},{5,4},{6,5},{7,6},{8,7},{9,8},{10,9... | collective-permute-start | bytes 589832 | tf_op jit(solution)/shard_map/ppermute | solution.py:545
  6.3 6.5 %collective-permute-start = (bf16[144,512]{1,0:T(8,128)(2,1)S(1)}, bf16[144,512]{1,0:T(8,128)(2,1)S(1)}, u32[]{:S(2)}, u32[]{:S(2)}) collective-permute-start(bf16[144,512]{1,0:T(8,128)(2,1)S(1)} %get-tuple-element.67), channel_id=1, source_target_pairs={{0,240},{1,241},{2,242},{3,243},{4,244},{5,245},{6,246},{7,247},{8... | collective-permute-start | bytes 442376 | tf_op jit(solution)/shard_map/ppermute | solution.py:545
  12.8 3.8 %collective-permute-start.2 = (bf16[80,512]{1,0:T(8,128)(2,1)S(1)}, bf16[80,512]{1,0:T(8,128)(2,1)S(1)}, u32[]{:S(2)}, u32[]{:S(2)}) collective-permute-start(bf16[80,512]{1,0:T(8,128)(2,1)S(1)} %get-tuple-element.69), channel_id=1, source_target_pairs={{0,255},{1,240},{2,241},{3,242},{4,243},{5,244},{6,245},{7,246},{8... | collective-permute-start | bytes 245768 | tf_op jit(solution)/shard_map/ppermute | solution.py:545
  16.6 0.7 collective-permute-start.4
  17.4 4.2 %shard_map.176 = (f32[1,512]{1,0:T(1,128)S(1)}, bf16[320,336]{1,0:T(8,128)(2,1)S(1)}, bf16[512,1536]{1,0:T(8,128)(2,1)S(1)}, bf16[512,512]{1,0:T(8,128)(2,1)S(1)...) custom-call(bf16[576,512]{1,0:T(8,128)(2,1)S(1)} %get-tuple-element., ...), custom_call_target="tpu_custom_call" | custom-call | flops 1000000000 | bytes 2000000 | tf_op jit(solution)/shard_map/pallas_call | solution.py:472
  21.6 0.0 collective-permute-done.2.diag_ref
  21.6 0.0 collective-permute-done.lat_ref
  21.6 0.0 copy-start
  21.6 4.0 %shard_map.177 = (bf16[400,512]{1,0:T(8,128)(2,1)S(1)}, bf16[400,1536]{1,0:T(8,128)(2,1)S(1)}, bf16[400,512]{1,0:T(8,128)(2,1)S(1)}, f32[5,2,80,320]{3,2,1,0:T(8...) custom-call(bf16[576,512]{1,0:T(8,128)(2,1)S(1)} %get-tuple-element.65.tok_ref, ...), custom_call_target="tpu_custom_call" | custom-call | flops 1000000000 | bytes 2000000 | tf_op jit(solution)/shard_map/pallas_call | solution.py:480
  25.6 4.4 %collective-permute-start.3 = (bf16[48,512]{1,0:T(8,128)(2,1)S(1)}, bf16[48,512]{1,0:T(8,128)(2,1)S(1)}, u32[]{:S(2)}, u32[]{:S(2)}) collective-permute-start(bf16[48,512]{1,0:T(8,128)(2,1)S(1)} %get-tuple-element.78), channel_id=1, source_target_pairs={{0,240},{1,241},{2,242},{3,243},{4,244},{5,245},{6,246},{7,247},{8... | collective-permute-start | bytes 147464 | tf_op jit(solution)/shard_map/ppermute | solution.py:545
  30.1 0.0 collective-permute-done.4.lat_ref
  30.1 2.0 %shard_map.178 = (f32[4,144,512]{2,1,0:T(8,128)S(1)}, bf16[2048,1024]{1,0:T(8,128)(2,1)S(1)}) custom-call(bf16[144,1024]{1,0:T(8,128)(2,1)S(1)} %get-tuple-element.81.g_ref, bf16[96,512]{1,0:T(8,128)(2,1)S(1)} %collective-permute-done.4.lat_ref, bf16[192,512]{1,0:T(8,128)(2,1)S(1)} %collective-permute-done.1.lon_ref, ...), custom_call_target="tpu_custom_call" | custom-call | flops 1000000000 | bytes 2000000 | tf_op jit(solution)/shard_map/pallas_call | solution.py:486
  32.1 0.0 copy-start.3
  32.1 1.2 %shard_map.179 = (bf16[576,512]{1,0:T(8,128)(2,1)S(1)}, bf16[48,512]{1,0:T(8,128)(2,1)S(1)}, bf16[4,144,512]{2,1,0:T(8,128)(2,1)S(1)}) custom-call(bf16[576,512]{1,0:T(8,128)(2,1)S(1)} %get-tuple-element.77.summed_ref, bf16[48,512]{1,0:T(8,128)(2,1)S(1)} %collective-permute-done.3.row_ref, f32[4,1,512]{2,1,0:T(1,128)S(1)} %get-tuple-element.79.gain_ref, ...), custom_call_target="tpu_custom_call" | custom-call | flops 1000000000 | bytes 2000000 | tf_op jit(solution)/shard_map/pallas_call | solution.py:492
  33.4 0.3 collective-permute-start.5
  33.7 0.0 copy-start.1
  33.7 1.0 %shard_map.181 = (bf16[96,1024]{1,0:T(8,128)(2,1)S(1)}, bf16[96,512]{1,0:T(8,128)(2,1)S(1)}, bf16[64,512]{1,0:T(8,128)(2,1)S(1)}, bf16[32,512]{1,0:T(8,128)(2,1)S(1)}) custom-call(bf16[4,144,512]{2,1,0:T(8,128)(2,1)S(1)} %get-tuple-element.98.normed_ref, bf16[2048,1024]{1,0:T(8,128)(2,1)S(1)} %get-tuple-element.99.wmerge_ref, bf16[192,144]{1,0:T(8,128)(2,1)S(1)} %copy-done.3), custom_call_target="tpu_custom_call" | custom-call | flops 1000000000 | bytes 2000000 | tf_op jit(solution)/shard_map/pallas_call | solution.py:506
  34.7 3.1 %shard_map.180 = (bf16[320,512]{1,0:T(8,128)(2,1)S(1)}, bf16[320,1536]{1,0:T(8,128)(2,1)S(1)}, bf16[512,640]{1,0:T(8,128)(2,1)S(1)}, bf16[512,640]{1,0:T(8,128)(2,1)S(1)}) custom-call(bf16[576,512]{1,0:T(8,128)(2,1)S(1)} %get-tuple-element.87.dsum_ref, bf16[400,1536]{1,0:T(8,128)(2,1)S(1)} %get-tuple-element.89.qkv_ref, ...), custom_call_target="tpu_custom_call" | custom-call | flops 1000000000 | bytes 2000000 | tf_op jit(solution)/shard_map/pallas_call | solution.py:501
  37.8 2.4 %collective-permute-done.5.row_ref = bf16[48,512]{1,0:T(8,128)(2,1)S(1)} collective-permute-done((bf16[48,512]{1,0:T(8,128)(2,1)S(1)}, bf16[48,512]{1,0:T(8,128)(2,1)S(1)}, u32[]{:S(2)}, u32[]{:S(2)}) %collective-permute-start.5) | collective-permute-done | bytes 49184 | tf_op jit(solution)/shard_map/ppermute | solution.py:545
  40.2 4.9 %shard_map.182 = (bf16[640,1536]{1,0:T(8,128)(2,1)S(1)}, bf16[4,32,32,128]{3,2,1,0:T(8,128)(2,1)S(1)}, bf16[4,32,32,128]{3,2,1,0:T(8,128)(2,1)S(1)}) custom-call(bf16[576,512]{1,0:T(8,128)(2,1)S(1)} %get-tuple-element.87.dsum_ref, bf16[48,512]{1,0:T(8,128)(2,1)S(1)} %collective-permute-done.5.row_ref, bf16[512,640]{1,0:T(8,128)(2,1)S(1)} %get-tuple-element.95.xst_ref, ...), custom_call_target="tpu_custom_call" | custom-call | flops 1000000000 | bytes 2000000 | tf_op jit(solution)/shard_map/pallas_call | solution.py:514
  45.1 2.1 %collective-permute-start.6 = (bf16[4,32,32,128]{3,2,1,0:T(8,128)(2,1)S(1)}, bf16[4,32,32,128]{3,2,1,0:T(8,128)(2,1)S(1)}, u32[]{:S(2)}, u32[]{:S(2)}) collective-permute-start(bf16[4,32,32,128]{3,2,1,0:T(8,128)(2,1)S(1)} %get-tuple-element.112), channel_id=1, source_target_pairs={{0,1},{1,0},{2,3},{3,2},{4,5},{5,4},{6,7},{7,6},{8,9},{9,8},{10,11... | collective-permute-start | bytes 3145736 | tf_op jit(solution)/shard_map/ppermute | solution.py:572
  47.1 2.5 %shard_map.183 = (bf16[432,512]{1,0:T(8,128)(2,1)S(1)}, bf16[144,512]{1,0:T(8,128)(2,1)S(1)}, bf16[160,512]{1,0:T(8,128)(2,1)S(1)}, bf16[80,512]{1,0:T(8,128)(2,1)S(1)}) custom-call(bf16[640,1536]{1,0:T(8,128)(2,1)S(1)} %get-tuple-element.105.dqkv_ref, bf16[512,1536]{1,0:T(8,128)(2,1)S(1)} %get-tuple-element.71.wqkv_ref, ...), custom_call_target="tpu_custom_call" | custom-call | flops 1000000000 | bytes 2000000 | tf_op jit(solution)/shard_map/pallas_call | solution.py:519
  49.6 0.0 collective-permute-done.6.b_ref
  49.6 0.2 shard_map.184
  49.9 0.1 collective-permute-start.7
  50.0 1.1 %collective-permute-start.8 = (bf16[32,32,128]{2,1,0:T(8,128)(2,1)S(1)}, bf16[32,32,128]{2,1,0:T(8,128)(2,1)S(1)}, u32[]{:S(2)}, u32[]{:S(2)}) collective-permute-start(bf16[32,32,128]{2,1,0:T(8,128)(2,1)S(1)} %get-tuple-element.116), channel_id=1, source_target_pairs={{0,4},{1,129},{2,6},{3,131},{4,0},{5,133},{6,2},{7,135},{8,12},{9,... | collective-permute-start | bytes 786440 | tf_op jit(solution)/shard_map/ppermute | solution.py:569
  51.1 2.8 %collective-permute-start.9 = (bf16[32,32,128]{2,1,0:T(8,128)(2,1)S(1)}, bf16[32,32,128]{2,1,0:T(8,128)(2,1)S(1)}, u32[]{:S(2)}, u32[]{:S(2)}) collective-permute-start(bf16[32,32,128]{2,1,0:T(8,128)(2,1)S(1)} %get-tuple-element.117), channel_id=1, source_target_pairs={{0,6},{1,137},{2,4},{3,139},{4,2},{5,141},{6,0},{7,143},{8,14},{9,... | collective-permute-start | bytes 786440 | tf_op jit(solution)/shard_map/ppermute | solution.py:569
  53.8 1.7 %collective-permute-done.7.b_ref = bf16[32,32,128]{2,1,0:T(8,128)(2,1)S(1)} collective-permute-done((bf16[32,32,128]{2,1,0:T(8,128)(2,1)S(1)}, bf16[32,32,128]{2,1,0:T(8,128)(2,1)S(1)}, u32[]{:S(2)}, u32[]{:S(2)}) %collective-permute-start.7) | collective-permute-done | bytes 262176 | tf_op jit(solution)/shard_map/ppermute | solution.py:569
  55.5 2.5 %collective-permute-done.8.c_ref = bf16[32,32,128]{2,1,0:T(8,128)(2,1)S(1)} collective-permute-done((bf16[32,32,128]{2,1,0:T(8,128)(2,1)S(1)}, bf16[32,32,128]{2,1,0:T(8,128)(2,1)S(1)}, u32[]{:S(2)}, u32[]{:S(2)}) %collective-permute-start.8) | collective-permute-done | bytes 262176 | tf_op jit(solution)/shard_map/ppermute | solution.py:569
  58.0 4.7 %collective-permute-done.9.d_ref = bf16[32,32,128]{2,1,0:T(8,128)(2,1)S(1)} collective-permute-done((bf16[32,32,128]{2,1,0:T(8,128)(2,1)S(1)}, bf16[32,32,128]{2,1,0:T(8,128)(2,1)S(1)}, u32[]{:S(2)}, u32[]{:S(2)}) %collective-permute-start.9) | collective-permute-done | bytes 262176 | tf_op jit(solution)/shard_map/ppermute | solution.py:569
  62.7 0.8 shard_map.185
  63.5 4.1 %all-to-all-start = ((bf16[32,32,128]{2,1,0:T(8,128)(2,1)}), bf16[32,32,128]{2,1,0:T(8,128)(2,1)S(1)}, u32[]{:S(2)}, u32[]{:S(2)}) async-start(bf16[32,32,128]{2,1,0:T(8,128)(2,1)} %shard_map.185), calls=%async_computation | async-start | bytes 524288 | tf_op jit(solution)/shard_map/all_to_all | solution.py:578
  67.6 0.3 collective-permute-start.12
  67.9 1.5 %collective-permute-start.11 = (bf16[144,512]{1,0:T(8,128)(2,1)S(1)}, bf16[144,512]{1,0:T(8,128)(2,1)S(1)}, u32[]{:S(2)}, u32[]{:S(2)}) collective-permute-start(bf16[144,512]{1,0:T(8,128)(2,1)S(1)} %get-tuple-element.120), channel_id=1, source_target_pairs={{0,16},{1,17},{2,18},{3,19},{4,20},{5,21},{6,22},{7,23},{8,24},{9,... | collective-permute-start | bytes 442376 | tf_op jit(solution)/shard_map/ppermute | solution.py:545
  69.4 2.2 %collective-permute-start.13 = (bf16[80,512]{1,0:T(8,128)(2,1)S(1)}, bf16[80,512]{1,0:T(8,128)(2,1)S(1)}, u32[]{:S(2)}, u32[]{:S(2)}) collective-permute-start(bf16[80,512]{1,0:T(8,128)(2,1)S(1)} %get-tuple-element.124), channel_id=1, source_target_pairs={{0,17},{1,18},{2,19},{3,20},{4,21},{5,22},{6,23},{7,24},{8,25},{9,... | collective-permute-start | bytes 245768 | tf_op jit(solution)/shard_map/ppermute | solution.py:545
  71.6 11.1 %collective-permute-done.13.diag_ref = bf16[80,512]{1,0:T(8,128)(2,1)S(1)} collective-permute-done((bf16[80,512]{1,0:T(8,128)(2,1)S(1)}, bf16[80,512]{1,0:T(8,128)(2,1)S(1)}, u32[]{:S(2)}, u32[]{:S(2)}) %collective-permute-start.13) | collective-permute-done | bytes 81952 | tf_op jit(solution)/shard_map/ppermute | solution.py:545
  82.7 0.0 collective-permute-done.11.lat_ref
  82.7 1.0 %shard_map.186 = (bf16[576,512]{1,0:T(8,128)(2,1)}, bf16[144,1024]{1,0:T(8,128)(2,1)}) custom-call(bf16[432,512]{1,0:T(8,128)(2,1)S(1)} %get-tuple-element.109.main_ref, bf16[144,512]{1,0:T(8,128)(2,1)S(1)} %collective-permute-done.11.lat_ref, bf16[160,512]{1,0:T(8,128)(2,1)S(1)} %collective-permute-done.12.lon_ref, ...), custom_call_target="tpu_custom_call" | custom-call | flops 1000000000 | bytes 2000000 | tf_op jit(solution)/shard_map/pallas_call | solution.py:529
  83.7 0.7 shard_map.187
  (27 shorter events, 0.1 us)
Async XLA Ops:
  0.6 1.1 %copy-start.5 = (bf16[12,48,512]{2,1,0:T(8,128)(2,1)S(1)}, bf16[12,48,512]{2,1,0:T(8,128)(2,1)}, u32[]{:S(2)}) copy-start(bf16[12,48,512]{2,1,0:T(8,128)(2,1)} %param.16) | copy-start | bytes 1769476
  1.7 1.0 %copy-start.7 = (bf16[6,24,1024]{2,1,0:T(8,128)(2,1)S(1)}, bf16[6,24,1024]{2,1,0:T(8,128)(2,1)}, u32[]{:S(2)}) copy-start(bf16[6,24,1024]{2,1,0:T(8,128)(2,1)} %param.22) | copy-start | bytes 884740
  2.7 14.7 %copy-start.4 = (bf16[512,1536]{1,0:T(8,128)(2,1)S(1)}, bf16[512,1536]{1,0:T(8,128)(2,1)}, u32[]{:S(2)}) copy-start(bf16[512,1536]{1,0:T(8,128)(2,1)} %refs_2_.1) | copy-start | bytes 4718596
  2.7 14.7 %copy-start.6 = (bf16[512,512]{1,0:T(8,128)(2,1)S(1)}, bf16[512,512]{1,0:T(8,128)(2,1)}, u32[]{:S(2)}) copy-start(bf16[512,512]{1,0:T(8,128)(2,1)} %refs_3_.1) | copy-start | bytes 1572868
  2.7 14.7 %copy-start.8 = (f32[2048]{0:T(1024)S(1)}, f32[2048]{0:T(1024)}, u32[]{:S(2)}) copy-start(f32[2048]{0:T(1024)} %param.20) | copy-start | bytes 24580
  2.7 14.7 %copy-start.9 = (f32[512]{0:T(512)S(1)}, f32[512]{0:T(512)}, u32[]{:S(2)}) copy-start(f32[512]{0:T(512)} %param.17) | copy-start | bytes 6148
  2.7 14.7 %copy-start.10 = (bf16[320,336]{1,0:T(8,128)(2,1)S(1)}, bf16[320,336]{1,0:T(8,128)(2,1)}, u32[]{:S(2)}) copy-start(bf16[320,336]{1,0:T(8,128)(2,1)} %constant.18.clone.refs_1_) | copy-start | bytes 645124
  2.7 14.7 %copy-start.11 = (bf16[288,320]{1,0:T(8,128)(2,1)S(1)}, bf16[288,320]{1,0:T(8,128)(2,1)}, u32[]{:S(2)}) copy-start(bf16[288,320]{1,0:T(8,128)(2,1)} %constant.20.clone.refs_6_) | copy-start | bytes 552964
  2.7 14.7 %copy-start.12 = (bf16[288,336]{1,0:T(8,128)(2,1)S(1)}, bf16[288,336]{1,0:T(8,128)(2,1)}, u32[]{:S(2)}) copy-start(bf16[288,336]{1,0:T(8,128)(2,1)} %constant.19.clone.refs_5_) | copy-start | bytes 580612
  2.7 14.7 %copy-start.13 = (bf16[192,192]{1,0:T(8,128)(2,1)S(1)}, bf16[192,192]{1,0:T(8,128)(2,1)}, u32[]{:S(2)}) copy-start(bf16[192,192]{1,0:T(8,128)(2,1)} %constant.22.clone.refs_8_) | copy-start | bytes 221188
  2.7 14.7 %copy-start.14 = (bf16[192,192]{1,0:T(8,128)(2,1)S(1)}, bf16[192,192]{1,0:T(8,128)(2,1)}, u32[]{:S(2)}) copy-start(bf16[192,192]{1,0:T(8,128)(2,1)} %constant.21.clone.refs_7_) | copy-start | bytes 221188
  2.7 14.7 %copy-start.15 = (bf16[144,192]{1,0:T(8,128)(2,1)S(1)}, bf16[144,192]{1,0:T(8,128)(2,1)}, u32[]{:S(2)}) copy-start(bf16[144,192]{1,0:T(8,128)(2,1)} %constant.23.clone.refs_9_) | copy-start | bytes 165892
  3.0 18.6 %collective-permute-start.1 = (bf16[192,512]{1,0:T(8,128)(2,1)S(1)}, bf16[192,512]{1,0:T(8,128)(2,1)S(1)}, u32[]{:S(2)}, u32[]{:S(2)}) collective-permute-start(bf16[192,512]{1,0:T(8,128)(2,1)S(1)} %get-tuple-element.68), channel_id=1, source_target_pairs={{0,15},{1,0},{2,1},{3,2},{4,3},{5,4},{6,5},{7,6},{8,7},{9,8},{10,9... | collective-permute-start | bytes 589832 | tf_op jit(solution)/shard_map/ppermute | solution.py:545
  6.3 15.3 %collective-permute-start = (bf16[144,512]{1,0:T(8,128)(2,1)S(1)}, bf16[144,512]{1,0:T(8,128)(2,1)S(1)}, u32[]{:S(2)}, u32[]{:S(2)}) collective-permute-start(bf16[144,512]{1,0:T(8,128)(2,1)S(1)} %get-tuple-element.67), channel_id=1, source_target_pairs={{0,240},{1,241},{2,242},{3,243},{4,244},{5,245},{6,246},{7,247},{8... | collective-permute-start | bytes 442376 | tf_op jit(solution)/shard_map/ppermute | solution.py:545
  12.8 8.8 %collective-permute-start.2 = (bf16[80,512]{1,0:T(8,128)(2,1)S(1)}, bf16[80,512]{1,0:T(8,128)(2,1)S(1)}, u32[]{:S(2)}, u32[]{:S(2)}) collective-permute-start(bf16[80,512]{1,0:T(8,128)(2,1)S(1)} %get-tuple-element.69), channel_id=1, source_target_pairs={{0,255},{1,240},{2,241},{3,242},{4,243},{5,244},{6,245},{7,246},{8... | collective-permute-start | bytes 245768 | tf_op jit(solution)/shard_map/ppermute | solution.py:545
  16.6 13.5 %collective-permute-start.4 = (bf16[96,512]{1,0:T(8,128)(2,1)S(1)}, bf16[96,512]{1,0:T(8,128)(2,1)S(1)}, u32[]{:S(2)}, u32[]{:S(2)}) collective-permute-start(bf16[96,512]{1,0:T(8,128)(2,1)S(1)} %get-tuple-element.82), channel_id=1, source_target_pairs={{0,240},{1,241},{2,242},{3,243},{4,244},{5,245},{6,246},{7,247},{8... | collective-permute-start | bytes 294920 | tf_op jit(solution)/shard_map/ppermute | solution.py:545
  21.6 8.5 %copy-start = (bf16[2048,1024]{1,0:T(8,128)(2,1)S(1)}, bf16[2048,1024]{1,0:T(8,128)(2,1)}, u32[]{:S(2)}) copy-start(bf16[2048,1024]{1,0:T(8,128)(2,1)} %wmerge_ref.1) | copy-start | bytes 12582916
  25.6 6.5 %collective-permute-start.3 = (bf16[48,512]{1,0:T(8,128)(2,1)S(1)}, bf16[48,512]{1,0:T(8,128)(2,1)S(1)}, u32[]{:S(2)}, u32[]{:S(2)}) collective-permute-start(bf16[48,512]{1,0:T(8,128)(2,1)S(1)} %get-tuple-element.78), channel_id=1, source_target_pairs={{0,240},{1,241},{2,242},{3,243},{4,244},{5,245},{6,246},{7,247},{8... | collective-permute-start | bytes 147464 | tf_op jit(solution)/shard_map/ppermute | solution.py:545
  32.1 1.5 %copy-start.3 = (bf16[192,144]{1,0:T(8,128)(2,1)S(1)}, bf16[192,144]{1,0:T(8,128)(2,1)}, u32[]{:S(2)}) copy-start(bf16[192,144]{1,0:T(8,128)(2,1)} %constant.26.clone.unshift_ref) | copy-start | bytes 165892
  33.4 6.8 %collective-permute-start.5 = (bf16[48,512]{1,0:T(8,128)(2,1)S(1)}, bf16[48,512]{1,0:T(8,128)(2,1)S(1)}, u32[]{:S(2)}, u32[]{:S(2)}) collective-permute-start(bf16[48,512]{1,0:T(8,128)(2,1)S(1)} %get-tuple-element.88), channel_id=1, source_target_pairs={{0,16},{1,17},{2,18},{3,19},{4,20},{5,21},{6,22},{7,23},{8,24},{9,... | collective-permute-start | bytes 147464 | tf_op jit(solution)/shard_map/ppermute | solution.py:545
  33.7 1.0 %copy-start.1 = (bf16[320,288]{1,0:T(8,128)(2,1)S(1)}, bf16[320,288]{1,0:T(8,128)(2,1)}, u32[]{:S(2)}) copy-start(bf16[320,288]{1,0:T(8,128)(2,1)} %constant.24.clone.pick_ref) | copy-start | bytes 552964
  40.2 6.9 %copy-start.2 = (bf16[336,288]{1,0:T(8,128)(2,1)S(1)}, bf16[336,288]{1,0:T(8,128)(2,1)}, u32[]{:S(2)}) copy-start(bf16[336,288]{1,0:T(8,128)(2,1)} %constant.25.clone.unshift_ref) | copy-start | bytes 580612
  45.1 4.5 %collective-permute-start.6 = (bf16[4,32,32,128]{3,2,1,0:T(8,128)(2,1)S(1)}, bf16[4,32,32,128]{3,2,1,0:T(8,128)(2,1)S(1)}, u32[]{:S(2)}, u32[]{:S(2)}) collective-permute-start(bf16[4,32,32,128]{3,2,1,0:T(8,128)(2,1)S(1)} %get-tuple-element.112), channel_id=1, source_target_pairs={{0,1},{1,0},{2,3},{3,2},{4,5},{5,4},{6,7},{7,6},{8,9},{9,8},{10,11... | collective-permute-start | bytes 3145736 | tf_op jit(solution)/shard_map/ppermute | solution.py:572
  49.9 5.6 %collective-permute-start.7 = (bf16[32,32,128]{2,1,0:T(8,128)(2,1)S(1)}, bf16[32,32,128]{2,1,0:T(8,128)(2,1)S(1)}, u32[]{:S(2)}, u32[]{:S(2)}) collective-permute-start(bf16[32,32,128]{2,1,0:T(8,128)(2,1)S(1)} %get-tuple-element.115), channel_id=1, source_target_pairs={{0,2},{1,9},{2,0},{3,11},{4,6},{5,13},{6,4},{7,15},{8,10},{9,1},{1... | collective-permute-start | bytes 786440 | tf_op jit(solution)/shard_map/ppermute | solution.py:569
  50.0 8.0 %collective-permute-start.8 = (bf16[32,32,128]{2,1,0:T(8,128)(2,1)S(1)}, bf16[32,32,128]{2,1,0:T(8,128)(2,1)S(1)}, u32[]{:S(2)}, u32[]{:S(2)}) collective-permute-start(bf16[32,32,128]{2,1,0:T(8,128)(2,1)S(1)} %get-tuple-element.116), channel_id=1, source_target_pairs={{0,4},{1,129},{2,6},{3,131},{4,0},{5,133},{6,2},{7,135},{8,12},{9,... | collective-permute-start | bytes 786440 | tf_op jit(solution)/shard_map/ppermute | solution.py:569
  51.1 11.6 %collective-permute-start.9 = (bf16[32,32,128]{2,1,0:T(8,128)(2,1)S(1)}, bf16[32,32,128]{2,1,0:T(8,128)(2,1)S(1)}, u32[]{:S(2)}, u32[]{:S(2)}) collective-permute-start(bf16[32,32,128]{2,1,0:T(8,128)(2,1)S(1)} %get-tuple-element.117), channel_id=1, source_target_pairs={{0,6},{1,137},{2,4},{3,139},{4,2},{5,141},{6,0},{7,143},{8,14},{9,... | collective-permute-start | bytes 786440 | tf_op jit(solution)/shard_map/ppermute | solution.py:569
  53.8 9.7 %collective-permute-start.10 = (bf16[96,512]{1,0:T(8,128)(2,1)S(1)}, bf16[96,512]{1,0:T(8,128)(2,1)S(1)}, u32[]{:S(2)}, u32[]{:S(2)}) collective-permute-start(bf16[96,512]{1,0:T(8,128)(2,1)S(1)} %get-tuple-element.118), channel_id=1, source_target_pairs={{0,16},{1,17},{2,18},{3,19},{4,20},{5,21},{6,22},{7,23},{8,24},{9,... | collective-permute-start | bytes 294920 | tf_op jit(solution)/shard_map/ppermute | solution.py:545
  63.5 20.2 %all-to-all-start = ((bf16[32,32,128]{2,1,0:T(8,128)(2,1)}), bf16[32,32,128]{2,1,0:T(8,128)(2,1)S(1)}, u32[]{:S(2)}, u32[]{:S(2)}) async-start(bf16[32,32,128]{2,1,0:T(8,128)(2,1)} %shard_map.185), calls=%async_computation | async-start | bytes 524288 | tf_op jit(solution)/shard_map/all_to_all | solution.py:578
  67.6 15.1 %collective-permute-start.12 = (bf16[160,512]{1,0:T(8,128)(2,1)S(1)}, bf16[160,512]{1,0:T(8,128)(2,1)S(1)}, u32[]{:S(2)}, u32[]{:S(2)}) collective-permute-start(bf16[160,512]{1,0:T(8,128)(2,1)S(1)} %get-tuple-element.122), channel_id=1, source_target_pairs={{0,1},{1,2},{2,3},{3,4},{4,5},{5,6},{6,7},{7,8},{8,9},{9,10},{10,1... | collective-permute-start | bytes 491528 | tf_op jit(solution)/shard_map/ppermute | solution.py:545
  67.9 14.8 %collective-permute-start.11 = (bf16[144,512]{1,0:T(8,128)(2,1)S(1)}, bf16[144,512]{1,0:T(8,128)(2,1)S(1)}, u32[]{:S(2)}, u32[]{:S(2)}) collective-permute-start(bf16[144,512]{1,0:T(8,128)(2,1)S(1)} %get-tuple-element.120), channel_id=1, source_target_pairs={{0,16},{1,17},{2,18},{3,19},{4,20},{5,21},{6,22},{7,23},{8,24},{9,... | collective-permute-start | bytes 442376 | tf_op jit(solution)/shard_map/ppermute | solution.py:545
  69.4 13.3 %collective-permute-start.13 = (bf16[80,512]{1,0:T(8,128)(2,1)S(1)}, bf16[80,512]{1,0:T(8,128)(2,1)S(1)}, u32[]{:S(2)}, u32[]{:S(2)}) collective-permute-start(bf16[80,512]{1,0:T(8,128)(2,1)S(1)} %get-tuple-element.124), channel_id=1, source_target_pairs={{0,17},{1,18},{2,19},{3,20},{4,21},{5,22},{6,23},{7,24},{8,25},{9,... | collective-permute-start | bytes 245768 | tf_op jit(solution)/shard_map/ppermute | solution.py:545

commit v5 on v4

--- a/solution.py
+++ b/solution.py
@@ -27,6 +27,7 @@
 EDGE = ROWS * BORDER
 CORNER = SHIFT_LAT * BORDER
 SIDE = WIN_LAT * BORDER
+TURN = 4 * BORDER
 BAND_CELLS = WIN_LAT * COLS
 GROUP = HEADS // 2
 GROUP_WIDTH = GROUP * HEAD
@@ -196,8 +197,8 @@
     g_top_ref[...] = halves(own_g_ref[:PAIR_TOP])
     edge_ref[:EDGE] = jnp.concatenate(edge, axis=0).astype(bf16)
     edge_ref[EDGE:] = halves(jnp.concatenate(side, axis=0).astype(bf16))
-    corner_ref[:SIDE] = jnp.concatenate(edge[:WIN_LAT], axis=0).astype(bf16)
-    corner_ref[SIDE:] = halves(jnp.concatenate(side[:2], axis=0).astype(bf16))
+    corner_ref[:TURN] = jnp.concatenate(edge[:4], axis=0).astype(bf16)
+    corner_ref[TURN:] = halves(jnp.concatenate(side[:2], axis=0).astype(bf16))
 
 
 def inner_kernel(tok_ref, *refs):
@@ -226,7 +227,7 @@
     def normed(values):
         return norm_parts(values)[0] * gain_ref[...]
 
-    lat, lon, diag = lat_ref[...], lon_ref[:EDGE].astype(f32), diag_ref[:SIDE].astype(f32)
+    lat, lon, diag = lat_ref[...], lon_ref[:EDGE].astype(f32), diag_ref[:TURN].astype(f32)
     first, second = band_sources(cells_ref[...], normed(lat.astype(f32)).astype(bf16), normed(lon), normed(diag))
     xs_ref[:PAD] = dot(pick_ref[INNER:], first).astype(bf16)
     xs_ref[PAD:] = dot(pick_ref[...], second).astype(bf16)
@@ -253,7 +254,7 @@
         lat = lat_ref[half * PAIR_TOP : (half + 1) * PAIR_TOP]
         at = EDGE + half * PAIR_SIDE
         lon = lon_ref[at + PAIR_CORNER : at + PAIR_SIDE]
-        diag = diag_ref[SIDE + half * PAIR_CORNER : SIDE + (half + 1) * PAIR_CORNER]
+        diag = diag_ref[TURN + half * PAIR_CORNER : TURN + (half + 1) * PAIR_CORNER]
         own = g_ref[PAIR_TOP:, half * D : (half + 1) * D]
         parts.append(dot(shift_ref[...], jnp.concatenate([own, lat, lon, diag], axis=0)).astype(bf16))
     cots = jnp.concatenate(parts, axis=1)
@@ -383,10 +384,10 @@
         else:
             main_ref[BAND_CELLS:] = cells[: BAND_CELLS - TOP]
             lat_ref[...] = cells[BAND_CELLS - TOP : BAND_CELLS]
-            diag_ref[:SIDE] = cells[BAND_CELLS:]
+            diag_ref[:TURN] = cells[BAND_CELLS + SIDE - TURN :]
         lon_ref[band * SIDE : (band + 1) * SIDE] = cells[BAND_CELLS:]
     lon_ref[EDGE:] = m_lon_ref[...]
-    diag_ref[SIDE:] = m_diag_ref[...]
+    diag_ref[TURN:] = m_diag_ref[...]
 
 
 def fill_edge(field, side, rows, cols):
@@ -397,7 +398,7 @@
 
 
 def own_cells_kernel(main_ref, lat_ref, lon_ref, diag_ref, m_main_ref, m_lat_ref, tokens_ref, merged_ref):
-    corner = diag_ref[:SIDE].astype(f32)[SIDE - CORNER :]
+    corner = diag_ref[:TURN].astype(f32)[TURN - CORNER :]
     beside = lon_ref[:EDGE].astype(f32)[: EDGE - CORNER]
     tokens_ref[:TOP] = fill_edge(lat_ref[...], corner, SHIFT_LAT, COLS)
     tokens_ref[TOP:] = fill_edge(main_ref[...], beside, ROWS - SHIFT_LAT, COLS)
@@ -406,7 +407,7 @@
         cols = pl.ds(half * D, D)
         lat = m_lat_ref[half * PAIR_TOP : (half + 1) * PAIR_TOP]
         lon = lon_ref[EDGE + half * side_rows : EDGE + (half + 1) * side_rows]
-        diag = diag_ref[SIDE + half * PAIR_CORNER : SIDE + (half + 1) * PAIR_CORNER]
+        diag = diag_ref[TURN + half * PAIR_CORNER : TURN + (half + 1) * PAIR_CORNER]
         merged_ref[:PAIR_TOP, cols] = fill_edge(lat, diag, 2, PAIR_COLS)
         merged_ref[PAIR_TOP:, cols] = fill_edge(m_main_ref[:, cols], lon, PAIR_ROWS - 2, PAIR_COLS)
 
@@ -457,7 +458,7 @@
         [
             ((TOKENS, D), bf16), ((PAIRS, 2 * D), bf16),
             ((TOP, D), bf16), ((2 * PAIR_TOP, D), bf16),
-            ((EDGE + 2 * PAIR_SIDE, D), bf16), ((SIDE + 2 * PAIR_CORNER, D), bf16),
+            ((EDGE + 2 * PAIR_SIDE, D), bf16), ((TURN + 2 * PAIR_CORNER, D), bf16),
         ],
         [pltpu.SemaphoreType.DMA((2,))],
         [2, 2],
@@ -520,7 +521,7 @@
         cells_back_kernel,
         [
             ((TOKENS - TOP, D), bf16), ((TOP, D), bf16),
-            ((EDGE + 2 * (PAIR_SIDE - PAIR_CORNER), D), bf16), ((SIDE + 2 * PAIR_CORNER, D), bf16),
+            ((EDGE + 2 * (PAIR_SIDE - PAIR_CORNER), D), bf16), ((TURN + 2 * PAIR_CORNER, D), bf16),
         ],
         [((WIDTH, D), bf16)],
     )(dqkv, w_qkv, cells_pick, unshift, tok, d_summed, first, gain, m_lon, m_diag)
@@ -586,8 +587,9 @@
         )
         sums = after(reduce_across(keep, sent, pieces[0]), m_lat)
         grad_weights = reduce_rest(sums)
-        to_lat, to_lon, to_diag = (after(piece, sums) for piece in pieces)
-        merged, grad_tokens = finish(send(to_lat, 1, 0), send(to_lon, 0, 1), send(to_diag, 1, 1))
+        to_lat, to_lon, to_diag = pieces
+        beside = send(to_lat, 1, 0), send(to_lon, 0, 1), send(to_diag, 1, 1)
+        merged, grad_tokens = finish(*(after(piece, sums) for piece in beside))
         return (
             merged.reshape(ROWS // 2, COLS // 2, 2 * D),
             grad_tokens.reshape(ROWS, COLS, D),

time: 85.1 us -> 84.4 us (level)
  no operation moved by 1% of the time
where the time goes in v5:
time: 84.4 us; the launch traced here: 83.8 us
  starting transfers between devices  33.3 us (39%)
  Pallas kernels  25.8 us (31%)
  waiting for transfers between devices  21.6 us (26%)
  local copies, waits for them, and re-layouts  2.1 us (2%)
  between operations  0.93 us (1%)
    ppermute x10, starting transfers between devices, send(): return lax.ppermute(block, ('lat', 'lon'), route)  22.6 us
    ppermute x10, waiting for transfers between devices, send(): return lax.ppermute(block, ('lat', 'lon'), route)  13.4 us
    ppermute x3, waiting for transfers between devices, swap(): lax.ppermute(block, ('lat', 'lon'), [(i, across(i, step)) for i in range(...  8.23 us
    pallas_call x1, Pallas kernels, chain(): call(outer_back_kernel, [((WIDTH, 3 * D), bf16), ((4, 32, 32, 128), bf16)...  4.88 us
    all_to_all x1, starting transfers between devices, reduce_rest(): lax.all_to_all(sums, ('lat', 'lon'), 0, 0, axis_index_groups=rest, tiled=...  4.32 us
    pallas_call x1, Pallas kernels, chain(): call(inner_kernel, [(h.shape, h.dtype) for h in held] + [((TOKENS - TOP,...  4.15 us
    pallas_call x1, Pallas kernels, chain(): call(outer_kernel, saved(REST) + [((TOKENS, D), bf16), ((TOKENS, D), bf16...  4.05 us
    ppermute x3, starting transfers between devices, swap(): lax.ppermute(block, ('lat', 'lon'), [(i, across(i, step)) for i in range(...  3.94 us
  transfers between devices with their start and end apart: 15, of which 5 were waited for; matrix products, arithmetic and copies ran while one was open for 0% of the time, Pallas kernels for 22%

profile of v5, /device:TPU:1, one launch (start us, length us, event | category | flops | bytes accessed | tf_op | source)
XLA Modules:
  0.0 83.8 jit_solution(5805543560532418756)
XLA Ops:
  0.6 1.1 %copy-done.5 = bf16[12,48,512]{2,1,0:T(8,128)(2,1)S(1)} copy-done((bf16[12,48,512]{2,1,0:T(8,128)(2,1)S(1)}, bf16[12,48,512]{2,1,0:T(8,128)(2,1)}, u32[]{:S(2)}) %copy-start.5) | copy-done | bytes 589848
  1.7 1.0 %copy-done.7 = bf16[6,24,1024]{2,1,0:T(8,128)(2,1)S(1)} copy-done((bf16[6,24,1024]{2,1,0:T(8,128)(2,1)S(1)}, bf16[6,24,1024]{2,1,0:T(8,128)(2,1)}, u32[]{:S(2)}) %copy-start.7) | copy-done | bytes 294936
  2.7 0.0 copy-start.10
  2.7 0.0 copy-start.11
  2.7 0.0 copy-start.12
  2.7 0.0 copy-start.13
  2.7 0.0 copy-start.14
  2.7 0.0 copy-start.15
  2.7 0.2 shard_map.175
  3.0 3.3 %collective-permute-start.1 = (bf16[192,512]{1,0:T(8,128)(2,1)S(1)}, bf16[192,512]{1,0:T(8,128)(2,1)S(1)}, u32[]{:S(2)}, u32[]{:S(2)}) collective-permute-start(bf16[192,512]{1,0:T(8,128)(2,1)S(1)} %get-tuple-element.68), channel_id=1, source_target_pairs={{0,15},{1,0},{2,1},{3,2},{4,3},{5,4},{6,5},{7,6},{8,7},{9,8},{10,9... | collective-permute-start | bytes 589832 | tf_op jit(solution)/shard_map/ppermute | solution.py:546
  6.3 6.5 %collective-permute-start = (bf16[144,512]{1,0:T(8,128)(2,1)S(1)}, bf16[144,512]{1,0:T(8,128)(2,1)S(1)}, u32[]{:S(2)}, u32[]{:S(2)}) collective-permute-start(bf16[144,512]{1,0:T(8,128)(2,1)S(1)} %get-tuple-element.67), channel_id=1, source_target_pairs={{0,240},{1,241},{2,242},{3,243},{4,244},{5,245},{6,246},{7,247},{8... | collective-permute-start | bytes 442376 | tf_op jit(solution)/shard_map/ppermute | solution.py:546
  12.8 3.8 %collective-permute-start.2 = (bf16[64,512]{1,0:T(8,128)(2,1)S(1)}, bf16[64,512]{1,0:T(8,128)(2,1)S(1)}, u32[]{:S(2)}, u32[]{:S(2)}) collective-permute-start(bf16[64,512]{1,0:T(8,128)(2,1)S(1)} %get-tuple-element.69), channel_id=1, source_target_pairs={{0,255},{1,240},{2,241},{3,242},{4,243},{5,244},{6,245},{7,246},{8... | collective-permute-start | bytes 196616 | tf_op jit(solution)/shard_map/ppermute | solution.py:546
  16.6 0.7 collective-permute-start.4
  17.4 4.2 %shard_map.176 = (f32[1,512]{1,0:T(1,128)S(1)}, bf16[320,336]{1,0:T(8,128)(2,1)S(1)}, bf16[512,1536]{1,0:T(8,128)(2,1)S(1)}, bf16[512,512]{1,0:T(8,128)(2,1)S(1)...) custom-call(bf16[576,512]{1,0:T(8,128)(2,1)S(1)} %get-tuple-element., ...), custom_call_target="tpu_custom_call" | custom-call | flops 1000000000 | bytes 2000000 | tf_op jit(solution)/shard_map/pallas_call | solution.py:473
  21.6 0.0 collective-permute-done.2.diag_ref
  21.6 0.0 collective-permute-done.1.lon_ref
  21.6 0.0 copy-start
  21.6 4.0 %shard_map.177 = (bf16[400,512]{1,0:T(8,128)(2,1)S(1)}, bf16[400,1536]{1,0:T(8,128)(2,1)S(1)}, bf16[400,512]{1,0:T(8,128)(2,1)S(1)}, f32[5,2,80,320]{3,2,1,0:T(8...) custom-call(bf16[576,512]{1,0:T(8,128)(2,1)S(1)} %get-tuple-element.65.tok_ref, ...), custom_call_target="tpu_custom_call" | custom-call | flops 1000000000 | bytes 2000000 | tf_op jit(solution)/shard_map/pallas_call | solution.py:481
  25.6 4.0 %collective-permute-start.3 = (bf16[48,512]{1,0:T(8,128)(2,1)S(1)}, bf16[48,512]{1,0:T(8,128)(2,1)S(1)}, u32[]{:S(2)}, u32[]{:S(2)}) collective-permute-start(bf16[48,512]{1,0:T(8,128)(2,1)S(1)} %get-tuple-element.78), channel_id=1, source_target_pairs={{0,240},{1,241},{2,242},{3,243},{4,244},{5,245},{6,246},{7,247},{8... | collective-permute-start | bytes 147464 | tf_op jit(solution)/shard_map/ppermute | solution.py:546
  29.6 2.0 %shard_map.178 = (f32[4,144,512]{2,1,0:T(8,128)S(1)}, bf16[2048,1024]{1,0:T(8,128)(2,1)S(1)}) custom-call(bf16[144,1024]{1,0:T(8,128)(2,1)S(1)} %get-tuple-element.81.g_ref, bf16[96,512]{1,0:T(8,128)(2,1)S(1)} %collective-permute-done.4.lat_ref, bf16[192,512]{1,0:T(8,128)(2,1)S(1)} %collective-permute-done.1.lon_ref, ...), custom_call_target="tpu_custom_call" | custom-call | flops 1000000000 | bytes 2000000 | tf_op jit(solution)/shard_map/pallas_call | solution.py:487
  31.7 0.0 collective-permute-done.3.row_ref
  31.7 0.0 copy-start.3
  31.7 1.2 %shard_map.179 = (bf16[576,512]{1,0:T(8,128)(2,1)S(1)}, bf16[48,512]{1,0:T(8,128)(2,1)S(1)}, bf16[4,144,512]{2,1,0:T(8,128)(2,1)S(1)}) custom-call(bf16[576,512]{1,0:T(8,128)(2,1)S(1)} %get-tuple-element.77.summed_ref, bf16[48,512]{1,0:T(8,128)(2,1)S(1)} %collective-permute-done.3.row_ref, f32[4,1,512]{2,1,0:T(1,128)S(1)} %get-tuple-element.79.gain_ref, ...), custom_call_target="tpu_custom_call" | custom-call | flops 1000000000 | bytes 2000000 | tf_op jit(solution)/shard_map/pallas_call | solution.py:493
  32.9 0.3 collective-permute-start.5
  33.2 0.0 copy-start.1
  33.2 1.0 %shard_map.181 = (bf16[96,1024]{1,0:T(8,128)(2,1)S(1)}, bf16[96,512]{1,0:T(8,128)(2,1)S(1)}, bf16[64,512]{1,0:T(8,128)(2,1)S(1)}, bf16[32,512]{1,0:T(8,128)(2,1)S(1)}) custom-call(bf16[4,144,512]{2,1,0:T(8,128)(2,1)S(1)} %get-tuple-element.98.normed_ref, bf16[2048,1024]{1,0:T(8,128)(2,1)S(1)} %get-tuple-element.99.wmerge_ref, bf16[192,144]{1,0:T(8,128)(2,1)S(1)} %copy-done.3), custom_call_target="tpu_custom_call" | custom-call | flops 1000000000 | bytes 2000000 | tf_op jit(solution)/shard_map/pallas_call | solution.py:507
  34.2 3.1 %shard_map.180 = (bf16[320,512]{1,0:T(8,128)(2,1)S(1)}, bf16[320,1536]{1,0:T(8,128)(2,1)S(1)}, bf16[512,640]{1,0:T(8,128)(2,1)S(1)}, bf16[512,640]{1,0:T(8,128)(2,1)S(1)}) custom-call(bf16[576,512]{1,0:T(8,128)(2,1)S(1)} %get-tuple-element.87.dsum_ref, bf16[400,1536]{1,0:T(8,128)(2,1)S(1)} %get-tuple-element.89.qkv_ref, ...), custom_call_target="tpu_custom_call" | custom-call | flops 1000000000 | bytes 2000000 | tf_op jit(solution)/shard_map/pallas_call | solution.py:502
  37.3 2.4 %collective-permute-done.5.row_ref = bf16[48,512]{1,0:T(8,128)(2,1)S(1)} collective-permute-done((bf16[48,512]{1,0:T(8,128)(2,1)S(1)}, bf16[48,512]{1,0:T(8,128)(2,1)S(1)}, u32[]{:S(2)}, u32[]{:S(2)}) %collective-permute-start.5) | collective-permute-done | bytes 49184 | tf_op jit(solution)/shard_map/ppermute | solution.py:546
  39.8 4.9 %shard_map.182 = (bf16[640,1536]{1,0:T(8,128)(2,1)S(1)}, bf16[4,32,32,128]{3,2,1,0:T(8,128)(2,1)S(1)}, bf16[4,32,32,128]{3,2,1,0:T(8,128)(2,1)S(1)}) custom-call(bf16[576,512]{1,0:T(8,128)(2,1)S(1)} %get-tuple-element.87.dsum_ref, bf16[48,512]{1,0:T(8,128)(2,1)S(1)} %collective-permute-done.5.row_ref, bf16[512,640]{1,0:T(8,128)(2,1)S(1)} %get-tuple-element.95.xst_ref, ...), custom_call_target="tpu_custom_call" | custom-call | flops 1000000000 | bytes 2000000 | tf_op jit(solution)/shard_map/pallas_call | solution.py:515
  44.6 2.4 %collective-permute-start.7 = (bf16[4,32,32,128]{3,2,1,0:T(8,128)(2,1)S(1)}, bf16[4,32,32,128]{3,2,1,0:T(8,128)(2,1)S(1)}, u32[]{:S(2)}, u32[]{:S(2)}) collective-permute-start(bf16[4,32,32,128]{3,2,1,0:T(8,128)(2,1)S(1)} %get-tuple-element.112), channel_id=1, source_target_pairs={{0,1},{1,0},{2,3},{3,2},{4,5},{5,4},{6,7},{7,6},{8,9},{9,8},{10,11... | collective-permute-start | bytes 3145736 | tf_op jit(solution)/shard_map/ppermute | solution.py:573
  47.1 2.5 %shard_map.183 = (bf16[432,512]{1,0:T(8,128)(2,1)S(1)}, bf16[144,512]{1,0:T(8,128)(2,1)S(1)}, bf16[160,512]{1,0:T(8,128)(2,1)S(1)}, bf16[64,512]{1,0:T(8,128)(2,1)S(1)}) custom-call(bf16[640,1536]{1,0:T(8,128)(2,1)S(1)} %get-tuple-element.105.dqkv_ref, bf16[512,1536]{1,0:T(8,128)(2,1)S(1)} %get-tuple-element.71.wqkv_ref, ...), custom_call_target="tpu_custom_call" | custom-call | flops 1000000000 | bytes 2000000 | tf_op jit(solution)/shard_map/pallas_call | solution.py:520
  49.6 0.2 shard_map.184
  49.8 0.1 collective-permute-start.8
  49.9 0.8 collective-permute-start.9
  50.7 3.0 %collective-permute-start.10 = (bf16[32,32,128]{2,1,0:T(8,128)(2,1)S(1)}, bf16[32,32,128]{2,1,0:T(8,128)(2,1)S(1)}, u32[]{:S(2)}, u32[]{:S(2)}) collective-permute-start(bf16[32,32,128]{2,1,0:T(8,128)(2,1)S(1)} %get-tuple-element.117), channel_id=1, source_target_pairs={{0,6},{1,137},{2,4},{3,139},{4,2},{5,141},{6,0},{7,143},{8,14},{9,... | collective-permute-start | bytes 786440 | tf_op jit(solution)/shard_map/ppermute | solution.py:570
  53.7 0.0 collective-permute-start.11
  53.7 1.7 %collective-permute-done.8.b_ref = bf16[32,32,128]{2,1,0:T(8,128)(2,1)S(1)} collective-permute-done((bf16[32,32,128]{2,1,0:T(8,128)(2,1)S(1)}, bf16[32,32,128]{2,1,0:T(8,128)(2,1)S(1)}, u32[]{:S(2)}, u32[]{:S(2)}) %collective-permute-start.8) | collective-permute-done | bytes 262176 | tf_op jit(solution)/shard_map/ppermute | solution.py:570
  55.4 2.2 %collective-permute-done.9.c_ref = bf16[32,32,128]{2,1,0:T(8,128)(2,1)S(1)} collective-permute-done((bf16[32,32,128]{2,1,0:T(8,128)(2,1)S(1)}, bf16[32,32,128]{2,1,0:T(8,128)(2,1)S(1)}, u32[]{:S(2)}, u32[]{:S(2)}) %collective-permute-start.9) | collective-permute-done | bytes 262176 | tf_op jit(solution)/shard_map/ppermute | solution.py:570
  57.6 4.4 %collective-permute-done.10.d_ref = bf16[32,32,128]{2,1,0:T(8,128)(2,1)S(1)} collective-permute-done((bf16[32,32,128]{2,1,0:T(8,128)(2,1)S(1)}, bf16[32,32,128]{2,1,0:T(8,128)(2,1)S(1)}, u32[]{:S(2)}, u32[]{:S(2)}) %collective-permute-start.10) | collective-permute-done | bytes 262176 | tf_op jit(solution)/shard_map/ppermute | solution.py:570
  62.0 0.8 shard_map.185
  62.8 0.0 collective-permute-done.11.m_lat_ref
  62.8 4.3 %all-to-all-start = ((bf16[32,32,128]{2,1,0:T(8,128)(2,1)}), bf16[32,32,128]{2,1,0:T(8,128)(2,1)S(1)}, u32[]{:S(2)}, u32[]{:S(2)}) async-start(bf16[32,32,128]{2,1,0:T(8,128)(2,1)} %shard_map.185), calls=%async_computation | async-start | bytes 524288 | tf_op jit(solution)/shard_map/all_to_all | solution.py:579
  67.1 0.4 collective-permute-start.12
  67.5 1.5 %collective-permute-start.6 = (bf16[144,512]{1,0:T(8,128)(2,1)S(1)}, bf16[144,512]{1,0:T(8,128)(2,1)S(1)}, u32[]{:S(2)}, u32[]{:S(2)}) collective-permute-start(bf16[144,512]{1,0:T(8,128)(2,1)S(1)} %get-tuple-element.110), channel_id=1, source_target_pairs={{0,16},{1,17},{2,18},{3,19},{4,20},{5,21},{6,22},{7,23},{8,24},{9,... | collective-permute-start | bytes 442376 | tf_op jit(solution)/shard_map/ppermute | solution.py:546
  69.0 2.2 %collective-permute-start.13 = (bf16[64,512]{1,0:T(8,128)(2,1)S(1)}, bf16[64,512]{1,0:T(8,128)(2,1)S(1)}, u32[]{:S(2)}, u32[]{:S(2)}) collective-permute-start(bf16[64,512]{1,0:T(8,128)(2,1)S(1)} %get-tuple-element.123), channel_id=1, source_target_pairs={{0,17},{1,18},{2,19},{3,20},{4,21},{5,22},{6,23},{7,24},{8,25},{9,... | collective-permute-start | bytes 196616 | tf_op jit(solution)/shard_map/ppermute | solution.py:546
  71.2 11.0 %collective-permute-done.13.diag_ref = bf16[64,512]{1,0:T(8,128)(2,1)S(1)} collective-permute-done((bf16[64,512]{1,0:T(8,128)(2,1)S(1)}, bf16[64,512]{1,0:T(8,128)(2,1)S(1)}, u32[]{:S(2)}, u32[]{:S(2)}) %collective-permute-start.13) | collective-permute-done | bytes 65568 | tf_op jit(solution)/shard_map/ppermute | solution.py:546
  82.2 1.0 %shard_map.186 = (bf16[576,512]{1,0:T(8,128)(2,1)}, bf16[144,1024]{1,0:T(8,128)(2,1)}) custom-call(bf16[432,512]{1,0:T(8,128)(2,1)S(1)} %get-tuple-element.109.main_ref, bf16[144,512]{1,0:T(8,128)(2,1)S(1)} %collective-permute-done.6.lat_ref, bf16[160,512]{1,0:T(8,128)(2,1)S(1)} %collective-permute-done.12.lon_ref, ...), custom_call_target="tpu_custom_call" | custom-call | flops 1000000000 | bytes 2000000 | tf_op jit(solution)/shard_map/pallas_call | solution.py:530
  83.2 0.7 shard_map.187
  (27 shorter events, 0.1 us)
Async XLA Ops:
  0.6 1.1 %copy-start.5 = (bf16[12,48,512]{2,1,0:T(8,128)(2,1)S(1)}, bf16[12,48,512]{2,1,0:T(8,128)(2,1)}, u32[]{:S(2)}) copy-start(bf16[12,48,512]{2,1,0:T(8,128)(2,1)} %param.16) | copy-start | bytes 1769476
  1.7 1.0 %copy-start.7 = (bf16[6,24,1024]{2,1,0:T(8,128)(2,1)S(1)}, bf16[6,24,1024]{2,1,0:T(8,128)(2,1)}, u32[]{:S(2)}) copy-start(bf16[6,24,1024]{2,1,0:T(8,128)(2,1)} %param.22) | copy-start | bytes 884740
  2.7 14.7 %copy-start.4 = (bf16[512,1536]{1,0:T(8,128)(2,1)S(1)}, bf16[512,1536]{1,0:T(8,128)(2,1)}, u32[]{:S(2)}) copy-start(bf16[512,1536]{1,0:T(8,128)(2,1)} %refs_2_.1) | copy-start | bytes 4718596
  2.7 14.7 %copy-start.6 = (bf16[512,512]{1,0:T(8,128)(2,1)S(1)}, bf16[512,512]{1,0:T(8,128)(2,1)}, u32[]{:S(2)}) copy-start(bf16[512,512]{1,0:T(8,128)(2,1)} %refs_3_.1) | copy-start | bytes 1572868
  2.7 14.7 %copy-start.8 = (f32[2048]{0:T(1024)S(1)}, f32[2048]{0:T(1024)}, u32[]{:S(2)}) copy-start(f32[2048]{0:T(1024)} %param.20) | copy-start | bytes 24580
  2.7 14.7 %copy-start.9 = (f32[512]{0:T(512)S(1)}, f32[512]{0:T(512)}, u32[]{:S(2)}) copy-start(f32[512]{0:T(512)} %param.17) | copy-start | bytes 6148
  2.7 14.7 %copy-start.10 = (bf16[320,336]{1,0:T(8,128)(2,1)S(1)}, bf16[320,336]{1,0:T(8,128)(2,1)}, u32[]{:S(2)}) copy-start(bf16[320,336]{1,0:T(8,128)(2,1)} %constant.18.clone.refs_1_) | copy-start | bytes 645124
  2.7 14.7 %copy-start.11 = (bf16[288,320]{1,0:T(8,128)(2,1)S(1)}, bf16[288,320]{1,0:T(8,128)(2,1)}, u32[]{:S(2)}) copy-start(bf16[288,320]{1,0:T(8,128)(2,1)} %constant.20.clone.refs_6_) | copy-start | bytes 552964
  2.7 14.7 %copy-start.12 = (bf16[288,336]{1,0:T(8,128)(2,1)S(1)}, bf16[288,336]{1,0:T(8,128)(2,1)}, u32[]{:S(2)}) copy-start(bf16[288,336]{1,0:T(8,128)(2,1)} %constant.19.clone.refs_5_) | copy-start | bytes 580612
  2.7 14.7 %copy-start.13 = (bf16[192,192]{1,0:T(8,128)(2,1)S(1)}, bf16[192,192]{1,0:T(8,128)(2,1)}, u32[]{:S(2)}) copy-start(bf16[192,192]{1,0:T(8,128)(2,1)} %constant.22.clone.refs_8_) | copy-start | bytes 221188
  2.7 14.7 %copy-start.14 = (bf16[192,192]{1,0:T(8,128)(2,1)S(1)}, bf16[192,192]{1,0:T(8,128)(2,1)}, u32[]{:S(2)}) copy-start(bf16[192,192]{1,0:T(8,128)(2,1)} %constant.21.clone.refs_7_) | copy-start | bytes 221188
  2.7 14.7 %copy-start.15 = (bf16[144,192]{1,0:T(8,128)(2,1)S(1)}, bf16[144,192]{1,0:T(8,128)(2,1)}, u32[]{:S(2)}) copy-start(bf16[144,192]{1,0:T(8,128)(2,1)} %constant.23.clone.refs_9_) | copy-start | bytes 165892
  3.0 18.6 %collective-permute-start.1 = (bf16[192,512]{1,0:T(8,128)(2,1)S(1)}, bf16[192,512]{1,0:T(8,128)(2,1)S(1)}, u32[]{:S(2)}, u32[]{:S(2)}) collective-permute-start(bf16[192,512]{1,0:T(8,128)(2,1)S(1)} %get-tuple-element.68), channel_id=1, source_target_pairs={{0,15},{1,0},{2,1},{3,2},{4,3},{5,4},{6,5},{7,6},{8,7},{9,8},{10,9... | collective-permute-start | bytes 589832 | tf_op jit(solution)/shard_map/ppermute | solution.py:546
  6.3 15.3 %collective-permute-start = (bf16[144,512]{1,0:T(8,128)(2,1)S(1)}, bf16[144,512]{1,0:T(8,128)(2,1)S(1)}, u32[]{:S(2)}, u32[]{:S(2)}) collective-permute-start(bf16[144,512]{1,0:T(8,128)(2,1)S(1)} %get-tuple-element.67), channel_id=1, source_target_pairs={{0,240},{1,241},{2,242},{3,243},{4,244},{5,245},{6,246},{7,247},{8... | collective-permute-start | bytes 442376 | tf_op jit(solution)/shard_map/ppermute | solution.py:546
  12.8 8.8 %collective-permute-start.2 = (bf16[64,512]{1,0:T(8,128)(2,1)S(1)}, bf16[64,512]{1,0:T(8,128)(2,1)S(1)}, u32[]{:S(2)}, u32[]{:S(2)}) collective-permute-start(bf16[64,512]{1,0:T(8,128)(2,1)S(1)} %get-tuple-element.69), channel_id=1, source_target_pairs={{0,255},{1,240},{2,241},{3,242},{4,243},{5,244},{6,245},{7,246},{8... | collective-permute-start | bytes 196616 | tf_op jit(solution)/shard_map/ppermute | solution.py:546
  16.6 13.0 %collective-permute-start.4 = (bf16[96,512]{1,0:T(8,128)(2,1)S(1)}, bf16[96,512]{1,0:T(8,128)(2,1)S(1)}, u32[]{:S(2)}, u32[]{:S(2)}) collective-permute-start(bf16[96,512]{1,0:T(8,128)(2,1)S(1)} %get-tuple-element.82), channel_id=1, source_target_pairs={{0,240},{1,241},{2,242},{3,243},{4,244},{5,245},{6,246},{7,247},{8... | collective-permute-start | bytes 294920 | tf_op jit(solution)/shard_map/ppermute | solution.py:546
  21.6 8.0 %copy-start = (bf16[2048,1024]{1,0:T(8,128)(2,1)S(1)}, bf16[2048,1024]{1,0:T(8,128)(2,1)}, u32[]{:S(2)}) copy-start(bf16[2048,1024]{1,0:T(8,128)(2,1)} %wmerge_ref.1) | copy-start | bytes 12582916
  25.6 6.0 %collective-permute-start.3 = (bf16[48,512]{1,0:T(8,128)(2,1)S(1)}, bf16[48,512]{1,0:T(8,128)(2,1)S(1)}, u32[]{:S(2)}, u32[]{:S(2)}) collective-permute-start(bf16[48,512]{1,0:T(8,128)(2,1)S(1)} %get-tuple-element.78), channel_id=1, source_target_pairs={{0,240},{1,241},{2,242},{3,243},{4,244},{5,245},{6,246},{7,247},{8... | collective-permute-start | bytes 147464 | tf_op jit(solution)/shard_map/ppermute | solution.py:546
  31.7 1.5 %copy-start.3 = (bf16[192,144]{1,0:T(8,128)(2,1)S(1)}, bf16[192,144]{1,0:T(8,128)(2,1)}, u32[]{:S(2)}) copy-start(bf16[192,144]{1,0:T(8,128)(2,1)} %constant.26.clone.unshift_ref) | copy-start | bytes 165892
  32.9 6.8 %collective-permute-start.5 = (bf16[48,512]{1,0:T(8,128)(2,1)S(1)}, bf16[48,512]{1,0:T(8,128)(2,1)S(1)}, u32[]{:S(2)}, u32[]{:S(2)}) collective-permute-start(bf16[48,512]{1,0:T(8,128)(2,1)S(1)} %get-tuple-element.88), channel_id=1, source_target_pairs={{0,16},{1,17},{2,18},{3,19},{4,20},{5,21},{6,22},{7,23},{8,24},{9,... | collective-permute-start | bytes 147464 | tf_op jit(solution)/shard_map/ppermute | solution.py:546
  33.2 1.0 %copy-start.1 = (bf16[320,288]{1,0:T(8,128)(2,1)S(1)}, bf16[320,288]{1,0:T(8,128)(2,1)}, u32[]{:S(2)}) copy-start(bf16[320,288]{1,0:T(8,128)(2,1)} %constant.24.clone.pick_ref) | copy-start | bytes 552964
  39.8 7.3 %copy-start.2 = (bf16[336,288]{1,0:T(8,128)(2,1)S(1)}, bf16[336,288]{1,0:T(8,128)(2,1)}, u32[]{:S(2)}) copy-start(bf16[336,288]{1,0:T(8,128)(2,1)} %constant.25.clone.unshift_ref) | copy-start | bytes 580612
  44.6 4.9 %collective-permute-start.7 = (bf16[4,32,32,128]{3,2,1,0:T(8,128)(2,1)S(1)}, bf16[4,32,32,128]{3,2,1,0:T(8,128)(2,1)S(1)}, u32[]{:S(2)}, u32[]{:S(2)}) collective-permute-start(bf16[4,32,32,128]{3,2,1,0:T(8,128)(2,1)S(1)} %get-tuple-element.112), channel_id=1, source_target_pairs={{0,1},{1,0},{2,3},{3,2},{4,5},{5,4},{6,7},{7,6},{8,9},{9,8},{10,11... | collective-permute-start | bytes 3145736 | tf_op jit(solution)/shard_map/ppermute | solution.py:573
  49.8 5.6 %collective-permute-start.8 = (bf16[32,32,128]{2,1,0:T(8,128)(2,1)S(1)}, bf16[32,32,128]{2,1,0:T(8,128)(2,1)S(1)}, u32[]{:S(2)}, u32[]{:S(2)}) collective-permute-start(bf16[32,32,128]{2,1,0:T(8,128)(2,1)S(1)} %get-tuple-element.115), channel_id=1, source_target_pairs={{0,2},{1,9},{2,0},{3,11},{4,6},{5,13},{6,4},{7,15},{8,10},{9,1},{1... | collective-permute-start | bytes 786440 | tf_op jit(solution)/shard_map/ppermute | solution.py:570
  49.9 7.7 %collective-permute-start.9 = (bf16[32,32,128]{2,1,0:T(8,128)(2,1)S(1)}, bf16[32,32,128]{2,1,0:T(8,128)(2,1)S(1)}, u32[]{:S(2)}, u32[]{:S(2)}) collective-permute-start(bf16[32,32,128]{2,1,0:T(8,128)(2,1)S(1)} %get-tuple-element.116), channel_id=1, source_target_pairs={{0,4},{1,129},{2,6},{3,131},{4,0},{5,133},{6,2},{7,135},{8,12},{9,... | collective-permute-start | bytes 786440 | tf_op jit(solution)/shard_map/ppermute | solution.py:570
  50.7 11.3 %collective-permute-start.10 = (bf16[32,32,128]{2,1,0:T(8,128)(2,1)S(1)}, bf16[32,32,128]{2,1,0:T(8,128)(2,1)S(1)}, u32[]{:S(2)}, u32[]{:S(2)}) collective-permute-start(bf16[32,32,128]{2,1,0:T(8,128)(2,1)S(1)} %get-tuple-element.117), channel_id=1, source_target_pairs={{0,6},{1,137},{2,4},{3,139},{4,2},{5,141},{6,0},{7,143},{8,14},{9,... | collective-permute-start | bytes 786440 | tf_op jit(solution)/shard_map/ppermute | solution.py:570
  53.7 9.1 %collective-permute-start.11 = (bf16[96,512]{1,0:T(8,128)(2,1)S(1)}, bf16[96,512]{1,0:T(8,128)(2,1)S(1)}, u32[]{:S(2)}, u32[]{:S(2)}) collective-permute-start(bf16[96,512]{1,0:T(8,128)(2,1)S(1)} %get-tuple-element.118), channel_id=1, source_target_pairs={{0,16},{1,17},{2,18},{3,19},{4,20},{5,21},{6,22},{7,23},{8,24},{9,... | collective-permute-start | bytes 294920 | tf_op jit(solution)/shard_map/ppermute | solution.py:546
  62.8 20.3 %all-to-all-start = ((bf16[32,32,128]{2,1,0:T(8,128)(2,1)}), bf16[32,32,128]{2,1,0:T(8,128)(2,1)S(1)}, u32[]{:S(2)}, u32[]{:S(2)}) async-start(bf16[32,32,128]{2,1,0:T(8,128)(2,1)} %shard_map.185), calls=%async_computation | async-start | bytes 524288 | tf_op jit(solution)/shard_map/all_to_all | solution.py:579
  67.1 15.0 %collective-permute-start.12 = (bf16[160,512]{1,0:T(8,128)(2,1)S(1)}, bf16[160,512]{1,0:T(8,128)(2,1)S(1)}, u32[]{:S(2)}, u32[]{:S(2)}) collective-permute-start(bf16[160,512]{1,0:T(8,128)(2,1)S(1)} %get-tuple-element.121), channel_id=1, source_target_pairs={{0,1},{1,2},{2,3},{3,4},{4,5},{5,6},{6,7},{7,8},{8,9},{9,10},{10,1... | collective-permute-start | bytes 491528 | tf_op jit(solution)/shard_map/ppermute | solution.py:546
  67.5 14.7 %collective-permute-start.6 = (bf16[144,512]{1,0:T(8,128)(2,1)S(1)}, bf16[144,512]{1,0:T(8,128)(2,1)S(1)}, u32[]{:S(2)}, u32[]{:S(2)}) collective-permute-start(bf16[144,512]{1,0:T(8,128)(2,1)S(1)} %get-tuple-element.110), channel_id=1, source_target_pairs={{0,16},{1,17},{2,18},{3,19},{4,20},{5,21},{6,22},{7,23},{8,24},{9,... | collective-permute-start | bytes 442376 | tf_op jit(solution)/shard_map/ppermute | solution.py:546
  69.0 13.1 %collective-permute-start.13 = (bf16[64,512]{1,0:T(8,128)(2,1)S(1)}, bf16[64,512]{1,0:T(8,128)(2,1)S(1)}, u32[]{:S(2)}, u32[]{:S(2)}) collective-permute-start(bf16[64,512]{1,0:T(8,128)(2,1)S(1)} %get-tuple-element.123), channel_id=1, source_target_pairs={{0,17},{1,18},{2,19},{3,20},{4,21},{5,22},{6,23},{7,24},{8,25},{9,... | collective-permute-start | bytes 196616 | tf_op jit(solution)/shard_map/ppermute | solution.py:546

commit v6 on v5

--- a/solution.py
+++ b/solution.py
@@ -245,10 +245,13 @@
 
 
 def cotangent_kernel(
-    g_ref, lat_ref, lon_ref, diag_ref, gain_ref, shift_ref, wmerge_ref, out_ref, weights_ref, sem
+    g_ref, lat_ref, lon_ref, diag_ref, gain_ref, shift_ref, xs0_ref, xs_ref, mixed0_ref, mixed_ref, wmerge_ref,
+    out_ref, weights_ref, xst_ref, mixt_ref, sem
 ):
     copy = pltpu.make_async_copy(wmerge_ref, weights_ref, sem)
     copy.start()
+    xst_ref[...] = jnp.concatenate([xs0_ref[...], xs_ref[...]], axis=0).T
+    mixt_ref[...] = jnp.concatenate([mixed0_ref[...], mixed_ref[...]], axis=0).T
     parts = []
     for half in range(2):
         lat = lat_ref[half * PAIR_TOP : (half + 1) * PAIR_TOP]
@@ -299,24 +302,26 @@
     out_row_ref[...] = dsum_ref[TOKENS - COLS :]
 
 
-def merge_kernel(normed_ref, wmerge_ref, unshift_ref, main_ref, lat_ref, lon_ref, diag_ref):
+def merge_kernel(
+    normed_ref, wmerge_ref, unshift_ref, cells_lon_ref, cells_diag_ref, main_ref, lat_ref, lon_ref, diag_ref
+):
     total = dot(normed_ref[0], wmerge_ref[:D])
     for k in range(1, 4):
         total = total + dot(normed_ref[k], wmerge_ref[k * D : (k + 1) * D])
     pairs = dot(unshift_ref[...], total.astype(bf16)).astype(bf16)
     main_ref[...] = pairs[: PAIRS - PAIR_TOP]
     lat_ref[...] = halves(pairs[PAIRS - PAIR_TOP : PAIRS])
-    lon_ref[...] = halves(pairs[PAIRS : PAIRS + PAIR_SIDE - PAIR_CORNER])
-    diag_ref[...] = halves(pairs[PAIRS + PAIR_SIDE - PAIR_CORNER :])
+    lon_ref[:EDGE] = cells_lon_ref[...]
+    lon_ref[EDGE:] = halves(pairs[PAIRS : PAIRS + PAIR_SIDE - PAIR_CORNER])
+    diag_ref[:TURN] = cells_diag_ref[...]
+    diag_ref[TURN:] = halves(pairs[PAIRS + PAIR_SIDE - PAIR_CORNER :])
 
 
 def inner_back_kernel(
-    dsum_ref, qkv_ref, probs_ref, wproj_ref, pick_ref, xs0_ref, xs_ref, mixed0_ref, mixed_ref,
-    up_ref, dqkv_ref, xst_ref, mixt_ref,
+    dsum_ref, qkv_ref, probs_ref, wproj_ref, pick_ref,
+    up_ref, dqkv_ref,
     dmix_ref,
 ):
-    xst_ref[...] = jnp.concatenate([xs0_ref[...], xs_ref[...]], axis=0).T
-    mixt_ref[...] = jnp.concatenate([mixed0_ref[...], mixed_ref[...]], axis=0).T
     up_ref[...] = dot(pick_ref[...], dsum_ref[BAND_CELLS - COLS : TOKENS - COLS]).astype(bf16)
     dmix_ref[...] = dot_nt(up_ref[...], wproj_ref[...]).astype(bf16)
     attend_back([(qkv_ref, probs_ref, win) for win in range(1, REST)], dmix_ref, dqkv_ref, 0)
@@ -363,7 +368,7 @@
 
 
 def cells_back_kernel(
-    dqkv_ref, wqkv_ref, cells_pick_ref, unshift_ref, tok_ref, dsum_ref, row_ref, gain_ref, m_lon_ref, m_diag_ref,
+    dqkv_ref, wqkv_ref, cells_pick_ref, unshift_ref, tok_ref, dsum_ref, row_ref, gain_ref,
     main_ref, lat_ref, lon_ref, diag_ref,
     dx_ref,
 ):
@@ -384,10 +389,8 @@
         else:
             main_ref[BAND_CELLS:] = cells[: BAND_CELLS - TOP]
             lat_ref[...] = cells[BAND_CELLS - TOP : BAND_CELLS]
-            diag_ref[:TURN] = cells[BAND_CELLS + SIDE - TURN :]
+            diag_ref[...] = cells[BAND_CELLS + SIDE - TURN :]
         lon_ref[band * SIDE : (band + 1) * SIDE] = cells[BAND_CELLS:]
-    lon_ref[EDGE:] = m_lon_ref[...]
-    diag_ref[TURN:] = m_diag_ref[...]
 
 
 def fill_edge(field, side, rows, cols):
@@ -484,12 +487,12 @@
         [((WIDTH, D), bf16)],
     )(tok, cells, *beside, gain, w_qkv, w_proj, pick, shift, cells_pick, att0)
     last = up(row)
-    cots, w_merge = call(
+    cots, w_merge, xst, mixt = call(
         cotangent_kernel,
-        [((4, PAIRS, D), f32), ((4 * D, 2 * D), bf16)],
+        [((4, PAIRS, D), f32), ((4 * D, 2 * D), bf16), ((D, WIDTH), bf16), ((D, WIDTH), bf16)],
         [pltpu.SemaphoreType.DMA],
-        [0] * 6 + [1],
-    )(after(g_merged, row), g_lat, *beside[1:], gain_merge, pair_shift, w_merge)
+        [0] * 10 + [1],
+    )(after(g_merged, row), g_lat, *beside[1:], gain_merge, pair_shift, xs0, xs1, mixed0, mixed1, w_merge)
     d_summed, row, merge_normed = call(
         pair_kernel,
         [((TOKENS, D), bf16), ((COLS, D), bf16), ((4, PAIRS, D), bf16)],
@@ -499,40 +502,37 @@
     band = jnp.asarray(band_selector(), bf16)
     unshift = jnp.asarray(shift_selector(WIN_LAT, COLS, SHIFT_LON).T, bf16)
     pair_unshift = jnp.asarray(shift_selector(PAIR_ROWS, PAIR_COLS, SHIFT_LON // 2).T, bf16)
-    up1, dqkv1, xst, mixt = call(
-        inner_back_kernel,
-        [((BAND, D), bf16), ((BAND, 3 * D), bf16), ((D, WIDTH), bf16), ((D, WIDTH), bf16)],
-        [((BAND, D), bf16)],
-    )(d_summed, qkv1, probs1, w_proj, band, xs0, xs1, mixed0, mixed1)
-    m_main, m_lat, m_lon, m_diag = call(
-        merge_kernel,
-        [
-            ((PAIRS - PAIR_TOP, 2 * D), bf16), ((2 * PAIR_TOP, D), bf16),
-            ((2 * (PAIR_SIDE - PAIR_CORNER), D), bf16), ((2 * PAIR_CORNER, D), bf16),
-        ],
-    )(merge_normed, w_merge, pair_unshift)
-    m_lat = down(m_lat)
+    up1, dqkv1 = call(
+        inner_back_kernel, [((BAND, D), bf16), ((BAND, 3 * D), bf16)], [((BAND, D), bf16)]
+    )(d_summed, qkv1, probs1, w_proj, band)
     dqkv, keep, sent = call(
         outer_back_kernel,
         [((WIDTH, 3 * D), bf16), ((4, 32, 32, 128), bf16), ((4, 32, 32, 128), bf16)],
         [((WIDTH, D), bf16), ((BAND, D), bf16)],
-    )(d_summed, first, xst, mixt, after(up1, m_main), dqkv1, qkv0, probs0, qkv1, probs1, w_proj, band)
+    )(d_summed, first, xst, mixt, up1, dqkv1, qkv0, probs0, qkv1, probs1, w_proj, band)
     main, to_lat, to_lon, to_diag = call(
         cells_back_kernel,
-        [
-            ((TOKENS - TOP, D), bf16), ((TOP, D), bf16),
-            ((EDGE + 2 * (PAIR_SIDE - PAIR_CORNER), D), bf16), ((TURN + 2 * PAIR_CORNER, D), bf16),
-        ],
+        [((TOKENS - TOP, D), bf16), ((TOP, D), bf16), ((EDGE, D), bf16), ((TURN, D), bf16)],
         [((WIDTH, D), bf16)],
-    )(dqkv, w_qkv, cells_pick, unshift, tok, d_summed, first, gain, m_lon, m_diag)
-
-    def finish(lat, lon, diag):
+    )(dqkv, w_qkv, cells_pick, unshift, tok, d_summed, first, gain)
+
+    def merge(ready):
+        m_main, m_lat, lon, diag = call(
+            merge_kernel,
+            [
+                ((PAIRS - PAIR_TOP, 2 * D), bf16), ((2 * PAIR_TOP, D), bf16),
+                ((EDGE + 2 * (PAIR_SIDE - PAIR_CORNER), D), bf16), ((TURN + 2 * PAIR_CORNER, D), bf16),
+            ],
+        )(after(merge_normed, ready), w_merge, pair_unshift, to_lon, to_diag)
+        return m_main, down(m_lat), to_lat, lon, diag
+
+    def finish(lat, lon, diag, m_main, m_lat):
         grad_tokens, merged = call(own_cells_kernel, [((TOKENS, D), bf16), ((PAIRS, 2 * D), bf16)])(
             main, lat, lon, diag, m_main, m_lat
         )
         return merged, grad_tokens
 
-    return finish, keep, sent, (to_lat, to_lon, to_diag), m_lat
+    return merge, finish, keep, sent, to_lat
 
 
 def solution(mesh):
@@ -569,27 +569,28 @@
     def swap(block, step):
         return lax.ppermute(block, ("lat", "lon"), [(i, across(i, step)) for i in range(count)])
 
-    def reduce_across(keep, sent, to_lat):
+    def reduce_across(keep, sent, to_lat, merge):
         other = lax.ppermute(sent, ("lat", "lon"), [(i, i ^ 1) for i in range(count)])
         own, *others = call(add_kernel, [((32, 32, 128), bf16)] * 4)(keep, after(other, to_lat))
         got = [swap(block, step) for step, block in enumerate(others, 1)]
-        return call(join_kernel, [((32, 32, 128), bf16)])(own, *got)[0]
+        m_main, m_lat, *pieces = merge(own)
+        sums = call(join_kernel, [((32, 32, 128), bf16)])(after(own, m_main), *got)[0]
+        return after(sums, m_lat), m_main, m_lat, pieces
 
     def reduce_rest(sums):
         parts = lax.all_to_all(sums, ("lat", "lon"), 0, 0, axis_index_groups=rest, tiled=True)
         return call(sum_kernel, [((32, 128), f32)])(parts)[0]
 
     def body(tokens, gain_attn, w_qkv, w_proj, gain_merge, w_merge, g_merged):
-        finish, keep, sent, pieces, m_lat = chain(
+        merge, finish, keep, sent, to_lat = chain(
             tokens.reshape(TOKENS, D), gain_attn.reshape(1, D), w_qkv, w_proj, gain_merge.reshape(4, 1, D),
             w_merge, g_merged.reshape(PAIRS, 2 * D), fetch,
             lambda row: send(row, -1, 0), lambda row: send(row, 1, 0),
         )
-        sums = after(reduce_across(keep, sent, pieces[0]), m_lat)
+        sums, m_main, m_lat, (to_lat, to_lon, to_diag) = reduce_across(keep, sent, to_lat, merge)
         grad_weights = reduce_rest(sums)
-        to_lat, to_lon, to_diag = pieces
         beside = send(to_lat, 1, 0), send(to_lon, 0, 1), send(to_diag, 1, 1)
-        merged, grad_tokens = finish(*(after(piece, sums) for piece in beside))
+        merged, grad_tokens = finish(*(after(piece, sums) for piece in beside), m_main, m_lat)
         return (
             merged.reshape(ROWS // 2, COLS // 2, 2 * D),
             grad_tokens.reshape(ROWS, COLS, D),

time: 84.4 us -> 84.9 us (level)
  the two profiles are of different devices: /device:TPU:1 before, /device:TPU:0 now
where the time goes in v6:
time: 84.9 us; the launch traced here: 84.7 us
  waiting for transfers between devices  28.3 us (33%)
  starting transfers between devices  27.4 us (32%)
  Pallas kernels  26 us (31%)
  local copies, waits for them, and re-layouts  2.09 us (2%)
  between operations  0.93 us (1%)
    ppermute x10, waiting for transfers between devices, send(): return lax.ppermute(block, ('lat', 'lon'), route)  22 us
    ppermute x10, starting transfers between devices, send(): return lax.ppermute(block, ('lat', 'lon'), route)  18.4 us
    ppermute x3, waiting for transfers between devices, swap(): lax.ppermute(block, ('lat', 'lon'), [(i, across(i, step)) for i in range(...  6.08 us
    pallas_call x1, Pallas kernels, chain(): call(outer_back_kernel, [((WIDTH, 3 * D), bf16), ((4, 32, 32, 128), bf16)...  4.89 us
    ppermute x3, starting transfers between devices, swap(): lax.ppermute(block, ('lat', 'lon'), [(i, across(i, step)) for i in range(...  4.78 us
    pallas_call x1, Pallas kernels, chain(): call(inner_kernel, [(h.shape, h.dtype) for h in held] + [((TOKENS - TOP,...  4.15 us
    all_to_all x1, starting transfers between devices, reduce_rest(): lax.all_to_all(sums, ('lat', 'lon'), 0, 0, axis_index_groups=rest, tiled=...  4.09 us
    pallas_call x1, Pallas kernels, chain(): call(outer_kernel, saved(REST) + [((TOKENS, D), bf16), ((TOKENS, D), bf16...  4.05 us
  transfers between devices with their start and end apart: 15, of which 7 were waited for; matrix products, arithmetic and copies ran while one was open for 0% of the time, Pallas kernels for 22%

profile of v6, /device:TPU:0, one launch (start us, length us, event | category | flops | bytes accessed | tf_op | source)
XLA Modules:
  0.0 84.7 jit_solution(12907012800181431603)
XLA Ops:
  0.6 1.1 %copy-done.5 = bf16[12,48,512]{2,1,0:T(8,128)(2,1)S(1)} copy-done((bf16[12,48,512]{2,1,0:T(8,128)(2,1)S(1)}, bf16[12,48,512]{2,1,0:T(8,128)(2,1)}, u32[]{:S(2)}) %copy-start.5) | copy-done | bytes 589848
  1.7 1.0 %copy-done.7 = bf16[6,24,1024]{2,1,0:T(8,128)(2,1)S(1)} copy-done((bf16[6,24,1024]{2,1,0:T(8,128)(2,1)S(1)}, bf16[6,24,1024]{2,1,0:T(8,128)(2,1)}, u32[]{:S(2)}) %copy-start.7) | copy-done | bytes 294936
  2.7 0.0 copy-start.10
  2.7 0.0 copy-start.11
  2.7 0.0 copy-start.12
  2.7 0.0 copy-start.13
  2.7 0.0 copy-start.14
  2.7 0.0 copy-start.15
  2.7 0.2 shard_map.175
  3.0 1.6 %collective-permute-start.1 = (bf16[192,512]{1,0:T(8,128)(2,1)S(1)}, bf16[192,512]{1,0:T(8,128)(2,1)S(1)}, u32[]{:S(2)}, u32[]{:S(2)}) collective-permute-start(bf16[192,512]{1,0:T(8,128)(2,1)S(1)} %get-tuple-element.69), channel_id=1, source_target_pairs={{0,15},{1,0},{2,1},{3,2},{4,3},{5,4},{6,5},{7,6},{8,7},{9,8},{10,9... | collective-permute-start | bytes 589832 | tf_op jit(solution)/shard_map/ppermute | solution.py:546
  4.5 8.2 %collective-permute-start = (bf16[144,512]{1,0:T(8,128)(2,1)S(1)}, bf16[144,512]{1,0:T(8,128)(2,1)S(1)}, u32[]{:S(2)}, u32[]{:S(2)}) collective-permute-start(bf16[144,512]{1,0:T(8,128)(2,1)S(1)} %get-tuple-element.68), channel_id=1, source_target_pairs={{0,240},{1,241},{2,242},{3,243},{4,244},{5,245},{6,246},{7,247},{8... | collective-permute-start | bytes 442376 | tf_op jit(solution)/shard_map/ppermute | solution.py:546
  12.7 0.0 collective-permute-start.2
  12.7 1.8 %collective-permute-start.4 = (bf16[96,512]{1,0:T(8,128)(2,1)S(1)}, bf16[96,512]{1,0:T(8,128)(2,1)S(1)}, u32[]{:S(2)}, u32[]{:S(2)}) collective-permute-start(bf16[96,512]{1,0:T(8,128)(2,1)S(1)} %get-tuple-element.83), channel_id=1, source_target_pairs={{0,240},{1,241},{2,242},{3,243},{4,244},{5,245},{6,246},{7,247},{8... | collective-permute-start | bytes 294920 | tf_op jit(solution)/shard_map/ppermute | solution.py:546
  14.7 4.2 %shard_map.176 = (f32[1,512]{1,0:T(1,128)S(1)}, bf16[320,336]{1,0:T(8,128)(2,1)S(1)}, bf16[512,1536]{1,0:T(8,128)(2,1)S(1)}, bf16[512,512]{1,0:T(8,128)(2,1)S(1)...) custom-call(bf16[576,512]{1,0:T(8,128)(2,1)S(1)} %get-tuple-element., ...), custom_call_target="tpu_custom_call" | custom-call | flops 1000000000 | bytes 2000000 | tf_op jit(solution)/shard_map/pallas_call | solution.py:476
  18.8 0.0 collective-permute-done.2.diag_ref
  18.8 0.0 collective-permute-done.1.lon_ref
  18.8 0.0 copy-start
  18.9 4.0 %shard_map.177 = (bf16[400,512]{1,0:T(8,128)(2,1)S(1)}, bf16[400,1536]{1,0:T(8,128)(2,1)S(1)}, bf16[400,512]{1,0:T(8,128)(2,1)S(1)}, f32[5,2,80,320]{3,2,1,0:T(8...) custom-call(bf16[576,512]{1,0:T(8,128)(2,1)S(1)} %get-tuple-element.66.tok_ref, ...), custom_call_target="tpu_custom_call" | custom-call | flops 1000000000 | bytes 2000000 | tf_op jit(solution)/shard_map/pallas_call | solution.py:484
  22.9 4.6 %collective-permute-start.3 = (bf16[48,512]{1,0:T(8,128)(2,1)S(1)}, bf16[48,512]{1,0:T(8,128)(2,1)S(1)}, u32[]{:S(2)}, u32[]{:S(2)}) collective-permute-start(bf16[48,512]{1,0:T(8,128)(2,1)S(1)} %get-tuple-element.79), channel_id=1, source_target_pairs={{0,240},{1,241},{2,242},{3,243},{4,244},{5,245},{6,246},{7,247},{8... | collective-permute-start | bytes 147464 | tf_op jit(solution)/shard_map/ppermute | solution.py:546
  27.5 0.0 collective-permute-done.4.lat_ref
  27.5 2.2 %shard_map.178 = (f32[4,144,512]{2,1,0:T(8,128)S(1)}, bf16[2048,1024]{1,0:T(8,128)(2,1)S(1)}, bf16[512,640]{1,0:T(8,128)(2,1)S(1)}, bf16[512,640]{1,0:T(8,128)(2,1)S(1)}) custom-call(bf16[144,1024]{1,0:T(8,128)(2,1)S(1)} %get-tuple-element.82.g_ref, bf16[96,512]{1,0:T(8,128)(2,1)S(1)} %collective-permute-done.4.lat_ref, ...), custom_call_target="tpu_custom_call" | custom-call | flops 1000000000 | bytes 2000000 | tf_op jit(solution)/shard_map/pallas_call | solution.py:490
  29.8 0.0 collective-permute-done.3.row_ref
  29.8 0.0 copy-start.1
  29.8 1.2 %shard_map.179 = (bf16[576,512]{1,0:T(8,128)(2,1)S(1)}, bf16[48,512]{1,0:T(8,128)(2,1)S(1)}, bf16[4,144,512]{2,1,0:T(8,128)(2,1)S(1)}) custom-call(bf16[576,512]{1,0:T(8,128)(2,1)S(1)} %get-tuple-element.78.summed_ref, bf16[48,512]{1,0:T(8,128)(2,1)S(1)} %collective-permute-done.3.row_ref, f32[4,1,512]{2,1,0:T(1,128)S(1)} %get-tuple-element.80.gain_ref, ...), custom_call_target="tpu_custom_call" | custom-call | flops 1000000000 | bytes 2000000 | tf_op jit(solution)/shard_map/pallas_call | solution.py:496
  31.1 0.3 collective-permute-start.5
  31.3 3.1 %shard_map.180 = (bf16[320,512]{1,0:T(8,128)(2,1)S(1)}, bf16[320,1536]{1,0:T(8,128)(2,1)S(1)}) custom-call(bf16[576,512]{1,0:T(8,128)(2,1)S(1)} %get-tuple-element.92.dsum_ref, bf16[400,1536]{1,0:T(8,128)(2,1)S(1)} %get-tuple-element.96.qkv_ref, f32[5,2,80,320]{3,2,1,0:T(8,128)S(1)} %get-tuple-element.97.probs_ref, ...), custom_call_target="tpu_custom_call" | custom-call | flops 1000000000 | bytes 2000000 | tf_op jit(solution)/shard_map/pallas_call | solution.py:505
  34.4 4.6 %collective-permute-done.5.row_ref = bf16[48,512]{1,0:T(8,128)(2,1)S(1)} collective-permute-done((bf16[48,512]{1,0:T(8,128)(2,1)S(1)}, bf16[48,512]{1,0:T(8,128)(2,1)S(1)}, u32[]{:S(2)}, u32[]{:S(2)}) %collective-permute-start.5) | collective-permute-done | bytes 49184 | tf_op jit(solution)/shard_map/ppermute | solution.py:546
  39.0 4.9 %shard_map.181 = (bf16[640,1536]{1,0:T(8,128)(2,1)S(1)}, bf16[4,32,32,128]{3,2,1,0:T(8,128)(2,1)S(1)}, bf16[4,32,32,128]{3,2,1,0:T(8,128)(2,1)S(1)}) custom-call(bf16[576,512]{1,0:T(8,128)(2,1)S(1)} %get-tuple-element.92.dsum_ref, bf16[48,512]{1,0:T(8,128)(2,1)S(1)} %collective-permute-done.5.row_ref, bf16[512,640]{1,0:T(8,128)(2,1)S(1)} %get-tuple-element.94.xst_ref, ...), custom_call_target="tpu_custom_call" | custom-call | flops 1000000000 | bytes 2000000 | tf_op jit(solution)/shard_map/pallas_call | solution.py:508
  43.9 0.1 collective-permute-start.7
  44.0 2.5 %shard_map.182 = (bf16[432,512]{1,0:T(8,128)(2,1)S(1)}, bf16[144,512]{1,0:T(8,128)(2,1)S(1)}, bf16[96,512]{1,0:T(8,128)(2,1)S(1)}, bf16[32,512]{1,0:T(8,128)(2,1)S(1)}) custom-call(bf16[640,1536]{1,0:T(8,128)(2,1)S(1)} %get-tuple-element.102.dqkv_ref, bf16[512,1536]{1,0:T(8,128)(2,1)S(1)} %get-tuple-element.72.wqkv_ref, ...), custom_call_target="tpu_custom_call" | custom-call | flops 1000000000 | bytes 2000000 | tf_op jit(solution)/shard_map/pallas_call | solution.py:513
  46.5 0.2 collective-permute-done.7.b_ref
  46.7 0.2 shard_map.183
  46.9 0.1 collective-permute-start.8
  47.0 1.9 %collective-permute-start.9 = (bf16[32,32,128]{2,1,0:T(8,128)(2,1)S(1)}, bf16[32,32,128]{2,1,0:T(8,128)(2,1)S(1)}, u32[]{:S(2)}, u32[]{:S(2)}) collective-permute-start(bf16[32,32,128]{2,1,0:T(8,128)(2,1)S(1)} %get-tuple-element.118), channel_id=1, source_target_pairs={{0,4},{1,129},{2,6},{3,131},{4,0},{5,133},{6,2},{7,135},{8,12},{9,... | collective-permute-start | bytes 786440 | tf_op jit(solution)/shard_map/ppermute | solution.py:570
  48.9 2.8 %collective-permute-start.10 = (bf16[32,32,128]{2,1,0:T(8,128)(2,1)S(1)}, bf16[32,32,128]{2,1,0:T(8,128)(2,1)S(1)}, u32[]{:S(2)}, u32[]{:S(2)}) collective-permute-start(bf16[32,32,128]{2,1,0:T(8,128)(2,1)S(1)} %get-tuple-element.119), channel_id=1, source_target_pairs={{0,6},{1,137},{2,4},{3,139},{4,2},{5,141},{6,0},{7,143},{8,14},{9,... | collective-permute-start | bytes 786440 | tf_op jit(solution)/shard_map/ppermute | solution.py:570
  51.7 1.0 %shard_map.184 = (bf16[96,1024]{1,0:T(8,128)(2,1)S(1)}, bf16[96,512]{1,0:T(8,128)(2,1)S(1)}, bf16[160,512]{1,0:T(8,128)(2,1)S(1)}, bf16[64,512]{1,0:T(8,128)(2,1)S(1)}) custom-call(bf16[4,144,512]{2,1,0:T(8,128)(2,1)S(1)} %get-tuple-element.111.normed_ref, bf16[2048,1024]{1,0:T(8,128)(2,1)S(1)} %get-tuple-element.112.wmerge_ref, ...), custom_call_target="tpu_custom_call" | custom-call | flops 1000000000 | bytes 2000000 | tf_op jit(solution)/shard_map/pallas_call | solution.py:520
  52.7 0.1 collective-permute-start.11
  52.8 0.6 collective-permute-done.8.b_ref
  53.4 2.8 %collective-permute-done.9.c_ref = bf16[32,32,128]{2,1,0:T(8,128)(2,1)S(1)} collective-permute-done((bf16[32,32,128]{2,1,0:T(8,128)(2,1)S(1)}, bf16[32,32,128]{2,1,0:T(8,128)(2,1)S(1)}, u32[]{:S(2)}, u32[]{:S(2)}) %collective-permute-start.9) | collective-permute-done | bytes 262176 | tf_op jit(solution)/shard_map/ppermute | solution.py:570
  56.1 2.7 %collective-permute-done.10.d_ref = bf16[32,32,128]{2,1,0:T(8,128)(2,1)S(1)} collective-permute-done((bf16[32,32,128]{2,1,0:T(8,128)(2,1)S(1)}, bf16[32,32,128]{2,1,0:T(8,128)(2,1)S(1)}, u32[]{:S(2)}, u32[]{:S(2)}) %collective-permute-start.10) | collective-permute-done | bytes 262176 | tf_op jit(solution)/shard_map/ppermute | solution.py:570
  58.9 0.8 shard_map.185
  59.7 1.3 %collective-permute-done.11.m_lat_ref = bf16[96,512]{1,0:T(8,128)(2,1)S(1)} collective-permute-done((bf16[96,512]{1,0:T(8,128)(2,1)S(1)}, bf16[96,512]{1,0:T(8,128)(2,1)S(1)}, u32[]{:S(2)}, u32[]{:S(2)}) %collective-permute-start.11) | collective-permute-done | bytes 98336 | tf_op jit(solution)/shard_map/ppermute | solution.py:546
  61.0 4.1 %all-to-all-start = ((bf16[32,32,128]{2,1,0:T(8,128)(2,1)}), bf16[32,32,128]{2,1,0:T(8,128)(2,1)S(1)}, u32[]{:S(2)}, u32[]{:S(2)}) async-start(bf16[32,32,128]{2,1,0:T(8,128)(2,1)} %shard_map.185), calls=%async_computation | async-start | bytes 524288 | tf_op jit(solution)/shard_map/all_to_all | solution.py:581
  65.1 0.1 collective-permute-start.12
  65.2 1.8 %collective-permute-start.6 = (bf16[144,512]{1,0:T(8,128)(2,1)S(1)}, bf16[144,512]{1,0:T(8,128)(2,1)S(1)}, u32[]{:S(2)}, u32[]{:S(2)}) collective-permute-start(bf16[144,512]{1,0:T(8,128)(2,1)S(1)} %get-tuple-element.105), channel_id=1, source_target_pairs={{0,16},{1,17},{2,18},{3,19},{4,20},{5,21},{6,22},{7,23},{8,24},{9,... | collective-permute-start | bytes 442376 | tf_op jit(solution)/shard_map/ppermute | solution.py:546
  67.0 16.1 %collective-permute-done.13.diag_ref = bf16[64,512]{1,0:T(8,128)(2,1)S(1)} collective-permute-done((bf16[64,512]{1,0:T(8,128)(2,1)S(1)}, bf16[64,512]{1,0:T(8,128)(2,1)S(1)}, u32[]{:S(2)}, u32[]{:S(2)}) %collective-permute-start.13) | collective-permute-done | bytes 65568 | tf_op jit(solution)/shard_map/ppermute | solution.py:546
  83.0 1.0 %shard_map.186 = (bf16[576,512]{1,0:T(8,128)(2,1)}, bf16[144,1024]{1,0:T(8,128)(2,1)}) custom-call(bf16[432,512]{1,0:T(8,128)(2,1)S(1)} %get-tuple-element.104.main_ref, bf16[144,512]{1,0:T(8,128)(2,1)S(1)} %collective-permute-done.6.lat_ref, bf16[160,512]{1,0:T(8,128)(2,1)S(1)} %collective-permute-done.12.lon_ref, ...), custom_call_target="tpu_custom_call" | custom-call | flops 1000000000 | bytes 2000000 | tf_op jit(solution)/shard_map/pallas_call | solution.py:530
  84.0 0.7 shard_map.187
  (27 shorter events, 0.1 us)
Async XLA Ops:
  0.6 1.1 %copy-start.5 = (bf16[12,48,512]{2,1,0:T(8,128)(2,1)S(1)}, bf16[12,48,512]{2,1,0:T(8,128)(2,1)}, u32[]{:S(2)}) copy-start(bf16[12,48,512]{2,1,0:T(8,128)(2,1)} %param.16) | copy-start | bytes 1769476
  1.7 1.0 %copy-start.7 = (bf16[6,24,1024]{2,1,0:T(8,128)(2,1)S(1)}, bf16[6,24,1024]{2,1,0:T(8,128)(2,1)}, u32[]{:S(2)}) copy-start(bf16[6,24,1024]{2,1,0:T(8,128)(2,1)} %param.22) | copy-start | bytes 884740
  2.7 11.9 %copy-start.4 = (bf16[512,1536]{1,0:T(8,128)(2,1)S(1)}, bf16[512,1536]{1,0:T(8,128)(2,1)}, u32[]{:S(2)}) copy-start(bf16[512,1536]{1,0:T(8,128)(2,1)} %refs_2_.1) | copy-start | bytes 4718596
  2.7 11.9 %copy-start.6 = (bf16[512,512]{1,0:T(8,128)(2,1)S(1)}, bf16[512,512]{1,0:T(8,128)(2,1)}, u32[]{:S(2)}) copy-start(bf16[512,512]{1,0:T(8,128)(2,1)} %refs_3_.1) | copy-start | bytes 1572868
  2.7 11.9 %copy-start.8 = (f32[2048]{0:T(1024)S(1)}, f32[2048]{0:T(1024)}, u32[]{:S(2)}) copy-start(f32[2048]{0:T(1024)} %param.20) | copy-start | bytes 24580
  2.7 11.9 %copy-start.9 = (f32[512]{0:T(512)S(1)}, f32[512]{0:T(512)}, u32[]{:S(2)}) copy-start(f32[512]{0:T(512)} %param.17) | copy-start | bytes 6148
  2.7 11.9 %copy-start.10 = (bf16[320,336]{1,0:T(8,128)(2,1)S(1)}, bf16[320,336]{1,0:T(8,128)(2,1)}, u32[]{:S(2)}) copy-start(bf16[320,336]{1,0:T(8,128)(2,1)} %constant.18.clone.refs_1_) | copy-start | bytes 645124
  2.7 11.9 %copy-start.11 = (bf16[288,320]{1,0:T(8,128)(2,1)S(1)}, bf16[288,320]{1,0:T(8,128)(2,1)}, u32[]{:S(2)}) copy-start(bf16[288,320]{1,0:T(8,128)(2,1)} %constant.20.clone.refs_6_) | copy-start | bytes 552964
  2.7 11.9 %copy-start.12 = (bf16[288,336]{1,0:T(8,128)(2,1)S(1)}, bf16[288,336]{1,0:T(8,128)(2,1)}, u32[]{:S(2)}) copy-start(bf16[288,336]{1,0:T(8,128)(2,1)} %constant.19.clone.refs_5_) | copy-start | bytes 580612
  2.7 11.9 %copy-start.13 = (bf16[192,192]{1,0:T(8,128)(2,1)S(1)}, bf16[192,192]{1,0:T(8,128)(2,1)}, u32[]{:S(2)}) copy-start(bf16[192,192]{1,0:T(8,128)(2,1)} %constant.22.clone.refs_8_) | copy-start | bytes 221188
  2.7 11.9 %copy-start.14 = (bf16[192,192]{1,0:T(8,128)(2,1)S(1)}, bf16[192,192]{1,0:T(8,128)(2,1)}, u32[]{:S(2)}) copy-start(bf16[192,192]{1,0:T(8,128)(2,1)} %constant.21.clone.refs_7_) | copy-start | bytes 221188
  2.7 11.9 %copy-start.15 = (bf16[144,192]{1,0:T(8,128)(2,1)S(1)}, bf16[144,192]{1,0:T(8,128)(2,1)}, u32[]{:S(2)}) copy-start(bf16[144,192]{1,0:T(8,128)(2,1)} %constant.23.clone.refs_9_) | copy-start | bytes 165892
  3.0 15.8 %collective-permute-start.1 = (bf16[192,512]{1,0:T(8,128)(2,1)S(1)}, bf16[192,512]{1,0:T(8,128)(2,1)S(1)}, u32[]{:S(2)}, u32[]{:S(2)}) collective-permute-start(bf16[192,512]{1,0:T(8,128)(2,1)S(1)} %get-tuple-element.69), channel_id=1, source_target_pairs={{0,15},{1,0},{2,1},{3,2},{4,3},{5,4},{6,5},{7,6},{8,7},{9,8},{10,9... | collective-permute-start | bytes 589832 | tf_op jit(solution)/shard_map/ppermute | solution.py:546
  4.5 14.3 %collective-permute-start = (bf16[144,512]{1,0:T(8,128)(2,1)S(1)}, bf16[144,512]{1,0:T(8,128)(2,1)S(1)}, u32[]{:S(2)}, u32[]{:S(2)}) collective-permute-start(bf16[144,512]{1,0:T(8,128)(2,1)S(1)} %get-tuple-element.68), channel_id=1, source_target_pairs={{0,240},{1,241},{2,242},{3,243},{4,244},{5,245},{6,246},{7,247},{8... | collective-permute-start | bytes 442376 | tf_op jit(solution)/shard_map/ppermute | solution.py:546
  12.7 6.1 %collective-permute-start.2 = (bf16[64,512]{1,0:T(8,128)(2,1)S(1)}, bf16[64,512]{1,0:T(8,128)(2,1)S(1)}, u32[]{:S(2)}, u32[]{:S(2)}) collective-permute-start(bf16[64,512]{1,0:T(8,128)(2,1)S(1)} %get-tuple-element.70), channel_id=1, source_target_pairs={{0,255},{1,240},{2,241},{3,242},{4,243},{5,244},{6,245},{7,246},{8... | collective-permute-start | bytes 196616 | tf_op jit(solution)/shard_map/ppermute | solution.py:546
  12.7 14.8 %collective-permute-start.4 = (bf16[96,512]{1,0:T(8,128)(2,1)S(1)}, bf16[96,512]{1,0:T(8,128)(2,1)S(1)}, u32[]{:S(2)}, u32[]{:S(2)}) collective-permute-start(bf16[96,512]{1,0:T(8,128)(2,1)S(1)} %get-tuple-element.83), channel_id=1, source_target_pairs={{0,240},{1,241},{2,242},{3,243},{4,244},{5,245},{6,246},{7,247},{8... | collective-permute-start | bytes 294920 | tf_op jit(solution)/shard_map/ppermute | solution.py:546
  18.8 8.7 %copy-start = (bf16[2048,1024]{1,0:T(8,128)(2,1)S(1)}, bf16[2048,1024]{1,0:T(8,128)(2,1)}, u32[]{:S(2)}) copy-start(bf16[2048,1024]{1,0:T(8,128)(2,1)} %wmerge_ref.1) | copy-start | bytes 12582916
  22.9 6.9 %collective-permute-start.3 = (bf16[48,512]{1,0:T(8,128)(2,1)S(1)}, bf16[48,512]{1,0:T(8,128)(2,1)S(1)}, u32[]{:S(2)}, u32[]{:S(2)}) collective-permute-start(bf16[48,512]{1,0:T(8,128)(2,1)S(1)} %get-tuple-element.79), channel_id=1, source_target_pairs={{0,240},{1,241},{2,242},{3,243},{4,244},{5,245},{6,246},{7,247},{8... | collective-permute-start | bytes 147464 | tf_op jit(solution)/shard_map/ppermute | solution.py:546
  29.8 1.5 %copy-start.1 = (bf16[320,288]{1,0:T(8,128)(2,1)S(1)}, bf16[320,288]{1,0:T(8,128)(2,1)}, u32[]{:S(2)}) copy-start(bf16[320,288]{1,0:T(8,128)(2,1)} %constant.24.clone.pick_ref) | copy-start | bytes 552964
  31.1 8.0 %collective-permute-start.5 = (bf16[48,512]{1,0:T(8,128)(2,1)S(1)}, bf16[48,512]{1,0:T(8,128)(2,1)S(1)}, u32[]{:S(2)}, u32[]{:S(2)}) collective-permute-start(bf16[48,512]{1,0:T(8,128)(2,1)S(1)} %get-tuple-element.93), channel_id=1, source_target_pairs={{0,16},{1,17},{2,18},{3,19},{4,20},{5,21},{6,22},{7,23},{8,24},{9,... | collective-permute-start | bytes 147464 | tf_op jit(solution)/shard_map/ppermute | solution.py:546
  39.0 5.0 %copy-start.2 = (bf16[336,288]{1,0:T(8,128)(2,1)S(1)}, bf16[336,288]{1,0:T(8,128)(2,1)}, u32[]{:S(2)}) copy-start(bf16[336,288]{1,0:T(8,128)(2,1)} %constant.25.clone.unshift_ref) | copy-start | bytes 580612
  43.9 2.7 %collective-permute-start.7 = (bf16[4,32,32,128]{3,2,1,0:T(8,128)(2,1)S(1)}, bf16[4,32,32,128]{3,2,1,0:T(8,128)(2,1)S(1)}, u32[]{:S(2)}, u32[]{:S(2)}) collective-permute-start(bf16[4,32,32,128]{3,2,1,0:T(8,128)(2,1)S(1)} %get-tuple-element.107), channel_id=1, source_target_pairs={{0,1},{1,0},{2,3},{3,2},{4,5},{5,4},{6,7},{7,6},{8,9},{9,8},{10,11... | collective-permute-start | bytes 3145736 | tf_op jit(solution)/shard_map/ppermute | solution.py:573
  46.7 5.0 %copy-start.3 = (bf16[192,144]{1,0:T(8,128)(2,1)S(1)}, bf16[192,144]{1,0:T(8,128)(2,1)}, u32[]{:S(2)}) copy-start(bf16[192,144]{1,0:T(8,128)(2,1)} %constant.26.clone.unshift_ref) | copy-start | bytes 165892
  46.9 6.5 %collective-permute-start.8 = (bf16[32,32,128]{2,1,0:T(8,128)(2,1)S(1)}, bf16[32,32,128]{2,1,0:T(8,128)(2,1)S(1)}, u32[]{:S(2)}, u32[]{:S(2)}) collective-permute-start(bf16[32,32,128]{2,1,0:T(8,128)(2,1)S(1)} %get-tuple-element.117), channel_id=1, source_target_pairs={{0,2},{1,9},{2,0},{3,11},{4,6},{5,13},{6,4},{7,15},{8,10},{9,1},{1... | collective-permute-start | bytes 786440 | tf_op jit(solution)/shard_map/ppermute | solution.py:570
  47.0 9.1 %collective-permute-start.9 = (bf16[32,32,128]{2,1,0:T(8,128)(2,1)S(1)}, bf16[32,32,128]{2,1,0:T(8,128)(2,1)S(1)}, u32[]{:S(2)}, u32[]{:S(2)}) collective-permute-start(bf16[32,32,128]{2,1,0:T(8,128)(2,1)S(1)} %get-tuple-element.118), channel_id=1, source_target_pairs={{0,4},{1,129},{2,6},{3,131},{4,0},{5,133},{6,2},{7,135},{8,12},{9,... | collective-permute-start | bytes 786440 | tf_op jit(solution)/shard_map/ppermute | solution.py:570
  48.9 10.0 %collective-permute-start.10 = (bf16[32,32,128]{2,1,0:T(8,128)(2,1)S(1)}, bf16[32,32,128]{2,1,0:T(8,128)(2,1)S(1)}, u32[]{:S(2)}, u32[]{:S(2)}) collective-permute-start(bf16[32,32,128]{2,1,0:T(8,128)(2,1)S(1)} %get-tuple-element.119), channel_id=1, source_target_pairs={{0,6},{1,137},{2,4},{3,139},{4,2},{5,141},{6,0},{7,143},{8,14},{9,... | collective-permute-start | bytes 786440 | tf_op jit(solution)/shard_map/ppermute | solution.py:570
  52.7 8.3 %collective-permute-start.11 = (bf16[96,512]{1,0:T(8,128)(2,1)S(1)}, bf16[96,512]{1,0:T(8,128)(2,1)S(1)}, u32[]{:S(2)}, u32[]{:S(2)}) collective-permute-start(bf16[96,512]{1,0:T(8,128)(2,1)S(1)} %get-tuple-element.120), channel_id=1, source_target_pairs={{0,16},{1,17},{2,18},{3,19},{4,20},{5,21},{6,22},{7,23},{8,24},{9,... | collective-permute-start | bytes 294920 | tf_op jit(solution)/shard_map/ppermute | solution.py:546
  61.0 23.0 %all-to-all-start = ((bf16[32,32,128]{2,1,0:T(8,128)(2,1)}), bf16[32,32,128]{2,1,0:T(8,128)(2,1)S(1)}, u32[]{:S(2)}, u32[]{:S(2)}) async-start(bf16[32,32,128]{2,1,0:T(8,128)(2,1)} %shard_map.185), calls=%async_computation | async-start | bytes 524288 | tf_op jit(solution)/shard_map/all_to_all | solution.py:581
  65.1 18.0 %collective-permute-start.12 = (bf16[160,512]{1,0:T(8,128)(2,1)S(1)}, bf16[160,512]{1,0:T(8,128)(2,1)S(1)}, u32[]{:S(2)}, u32[]{:S(2)}) collective-permute-start(bf16[160,512]{1,0:T(8,128)(2,1)S(1)} %get-tuple-element.123), channel_id=1, source_target_pairs={{0,1},{1,2},{2,3},{3,4},{4,5},{5,6},{6,7},{7,8},{8,9},{9,10},{10,1... | collective-permute-start | bytes 491528 | tf_op jit(solution)/shard_map/ppermute | solution.py:546
  65.2 17.9 %collective-permute-start.6 = (bf16[144,512]{1,0:T(8,128)(2,1)S(1)}, bf16[144,512]{1,0:T(8,128)(2,1)S(1)}, u32[]{:S(2)}, u32[]{:S(2)}) collective-permute-start(bf16[144,512]{1,0:T(8,128)(2,1)S(1)} %get-tuple-element.105), channel_id=1, source_target_pairs={{0,16},{1,17},{2,18},{3,19},{4,20},{5,21},{6,22},{7,23},{8,24},{9,... | collective-permute-start | bytes 442376 | tf_op jit(solution)/shard_map/ppermute | solution.py:546
  67.0 16.1 %collective-permute-start.13 = (bf16[64,512]{1,0:T(8,128)(2,1)S(1)}, bf16[64,512]{1,0:T(8,128)(2,1)S(1)}, u32[]{:S(2)}, u32[]{:S(2)}) collective-permute-start(bf16[64,512]{1,0:T(8,128)(2,1)S(1)} %get-tuple-element.125), channel_id=1, source_target_pairs={{0,17},{1,18},{2,19},{3,20},{4,21},{5,22},{6,23},{7,24},{8,25},{9,... | collective-permute-start | bytes 196616 | tf_op jit(solution)/shard_map/ppermute | solution.py:546

commit v7 on v5

--- a/solution.py
+++ b/solution.py
@@ -37,9 +37,9 @@
 OUTER = REST * PAD
 PAIR_ROWS, PAIR_COLS = ROWS // 2, COLS // 2
 PAIRS = PAIR_ROWS * PAIR_COLS
-PAIR_TOP = 2 * PAIR_COLS
+PAIR_TOP = PAIR_COLS
 PAIR_SIDE = PAIR_ROWS * BORDER
-PAIR_CORNER = 2 * BORDER
+PAIR_CORNER = BORDER
 HELD = 10
 WIDTH = WINDOWS * PAD
 NEG = -1e30
@@ -194,11 +194,11 @@
     cots = own_g_ref[...].astype(f32)
     side = [cots[row * PAIR_COLS : row * PAIR_COLS + BORDER] for row in range(PAIR_ROWS)]
     top_ref[...] = own_ref[:TOP]
-    g_top_ref[...] = halves(own_g_ref[:PAIR_TOP])
+    g_top_ref[...] = halves(cots[:PAIR_TOP]).astype(bf16)
     edge_ref[:EDGE] = jnp.concatenate(edge, axis=0).astype(bf16)
     edge_ref[EDGE:] = halves(jnp.concatenate(side, axis=0).astype(bf16))
     corner_ref[:TURN] = jnp.concatenate(edge[:4], axis=0).astype(bf16)
-    corner_ref[TURN:] = halves(jnp.concatenate(side[:2], axis=0).astype(bf16))
+    corner_ref[TURN:] = halves(side[0]).astype(bf16)
 
 
 def inner_kernel(tok_ref, *refs):
@@ -241,7 +241,7 @@
         added = dot(cells_pick_ref[...], att_ref[pl.ds(band * BAND, BAND)])
         tok_out_ref[rows] = tokens.astype(bf16)
         summed_ref[rows] = (tokens + added).astype(bf16)
-    row_ref[...] = summed_ref[:COLS]
+    row_ref[...] = summed_ref[TOKENS - COLS :]
 
 
 def cotangent_kernel(
@@ -251,12 +251,13 @@
     copy.start()
     parts = []
     for half in range(2):
-        lat = lat_ref[half * PAIR_TOP : (half + 1) * PAIR_TOP]
+        lat = lat_ref[...].astype(f32)[half * PAIR_TOP : (half + 1) * PAIR_TOP]
         at = EDGE + half * PAIR_SIDE
-        lon = lon_ref[at + PAIR_CORNER : at + PAIR_SIDE]
-        diag = diag_ref[TURN + half * PAIR_CORNER : TURN + (half + 1) * PAIR_CORNER]
-        own = g_ref[PAIR_TOP:, half * D : (half + 1) * D]
-        parts.append(dot(shift_ref[...], jnp.concatenate([own, lat, lon, diag], axis=0)).astype(bf16))
+        lon = lon_ref[at : at + PAIR_SIDE].astype(f32)[PAIR_CORNER:]
+        diag = diag_ref[TURN:].astype(f32)[half * PAIR_CORNER : (half + 1) * PAIR_CORNER]
+        own = g_ref[:, half * D : (half + 1) * D].astype(f32)[PAIR_TOP:]
+        source = jnp.concatenate([own, lat, lon, diag], axis=0).astype(bf16)
+        parts.append(dot(shift_ref[...], source).astype(bf16))
     cots = jnp.concatenate(parts, axis=1)
     copy.wait()
     for k in range(4):
@@ -270,11 +271,11 @@
 ):
     quarter = COLS
     for part in range(3):
-        first = COLS + part * 4 * COLS
-        if part < 2:
+        first = part * 4 * COLS - COLS
+        if part:
             summed = summed_ref[first : first + 4 * COLS]
         else:
-            summed = jnp.concatenate([summed_ref[first:], row_ref[...]], axis=0)
+            summed = jnp.concatenate([row_ref[...], summed_ref[: 3 * COLS]], axis=0)
         paired = dot(pair_ref[...], summed)
         for k in range(4):
             members_ref[k, pl.ds(part * quarter, quarter)] = paired[k * quarter : (k + 1) * quarter]
@@ -296,45 +297,44 @@
         rows = pl.ds(part * quarter, quarter)
         block = jnp.concatenate([members_ref[k, rows].astype(bf16) for k in range(4)], axis=0)
         dsum_ref[pl.ds(part * 4 * COLS, 4 * COLS)] = dot(unpair_ref[...], block).astype(bf16)
-    out_row_ref[...] = dsum_ref[TOKENS - COLS :]
+    out_row_ref[...] = dsum_ref[:COLS]
 
 
 def merge_kernel(normed_ref, wmerge_ref, unshift_ref, main_ref, lat_ref, lon_ref, diag_ref):
     total = dot(normed_ref[0], wmerge_ref[:D])
     for k in range(1, 4):
         total = total + dot(normed_ref[k], wmerge_ref[k * D : (k + 1) * D])
-    pairs = dot(unshift_ref[...], total.astype(bf16)).astype(bf16)
-    main_ref[...] = pairs[: PAIRS - PAIR_TOP]
-    lat_ref[...] = halves(pairs[PAIRS - PAIR_TOP : PAIRS])
-    lon_ref[...] = halves(pairs[PAIRS : PAIRS + PAIR_SIDE - PAIR_CORNER])
-    diag_ref[...] = halves(pairs[PAIRS + PAIR_SIDE - PAIR_CORNER :])
+    pairs = dot(unshift_ref[...], total.astype(bf16))
+    main_ref[...] = pairs[:PAIRS].astype(bf16)
+    lat_ref[...] = halves(pairs[PAIRS - PAIR_TOP : PAIRS]).astype(bf16)
+    lon_ref[...] = halves(pairs[PAIRS : PAIRS + PAIR_SIDE - PAIR_CORNER]).astype(bf16)
+    diag_ref[...] = halves(pairs[PAIRS + PAIR_SIDE - PAIR_CORNER :]).astype(bf16)
 
 
 def inner_back_kernel(
-    dsum_ref, qkv_ref, probs_ref, wproj_ref, pick_ref, xs0_ref, xs_ref, mixed0_ref, mixed_ref,
+    dsum_ref, qkv0_ref, probs0_ref, qkv_ref, probs_ref, wproj_ref, pick_ref, xs0_ref, xs_ref, mixed0_ref, mixed_ref,
     up_ref, dqkv_ref, xst_ref, mixt_ref,
     dmix_ref,
 ):
     xst_ref[...] = jnp.concatenate([xs0_ref[...], xs_ref[...]], axis=0).T
     mixt_ref[...] = jnp.concatenate([mixed0_ref[...], mixed_ref[...]], axis=0).T
-    up_ref[...] = dot(pick_ref[...], dsum_ref[BAND_CELLS - COLS : TOKENS - COLS]).astype(bf16)
+    up_ref[...] = dot(pick_ref[...], dsum_ref[COLS : COLS + BAND_CELLS]).astype(bf16)
     dmix_ref[...] = dot_nt(up_ref[...], wproj_ref[...]).astype(bf16)
-    attend_back([(qkv_ref, probs_ref, win) for win in range(1, REST)], dmix_ref, dqkv_ref, 0)
+    windows = [(qkv0_ref, probs0_ref, win) for win in range(LOCAL)] + [(qkv_ref, probs_ref, 0)]
+    attend_back(windows, dmix_ref, dqkv_ref, 0)
 
 
 def outer_back_kernel(
-    dsum_ref, row_ref, xst_ref, mixt_ref, up1_ref, dqkv1_ref, qkv0_ref, probs0_ref, qkv_ref, probs_ref,
-    wproj_ref, pick_ref,
+    dsum_ref, row_ref, xst_ref, mixt_ref, up0_ref, dqkv0_ref, qkv_ref, probs_ref, wproj_ref, pick_ref,
     dqkv_ref, keep_ref, send_ref,
     up_ref, dmix_ref,
 ):
-    cells = jnp.concatenate([row_ref[...], dsum_ref[: BAND_CELLS - COLS]], axis=0)
-    up_ref[:BAND] = dot(pick_ref[...], cells).astype(bf16)
-    up_ref[BAND:] = up1_ref[...]
-    dqkv_ref[BAND:] = dqkv1_ref[...]
-    dmix_ref[...] = dot_nt(up_ref[:BAND], wproj_ref[...]).astype(bf16)
-    windows = [(qkv0_ref, probs0_ref, win) for win in range(LOCAL)] + [(qkv_ref, probs_ref, 0)]
-    attend_back(windows, dmix_ref, dqkv_ref, 0)
+    cells = jnp.concatenate([dsum_ref[COLS + BAND_CELLS :], row_ref[...]], axis=0)
+    up_ref[:BAND] = up0_ref[...]
+    up_ref[BAND:] = dot(pick_ref[...], cells).astype(bf16)
+    dqkv_ref[:BAND] = dqkv0_ref[...]
+    dmix_ref[...] = dot_nt(up_ref[BAND:], wproj_ref[...]).astype(bf16)
+    attend_back([(qkv_ref, probs_ref, win) for win in range(1, REST)], dmix_ref, dqkv_ref, BAND)
     lat_at, lon_at = lax.axis_index("lat"), lax.axis_index("lon")
     even_core = lax.rem(lon_at, 2) == 0
     my_x = lax.rem(lax.div(lon_at, 2), 4)
@@ -370,9 +370,9 @@
     dx_ref[...] = dot_nt(dqkv_ref[...], wqkv_ref[...]).astype(bf16)
     for band in range(2):
         if band == 0:
-            above = jnp.concatenate([row_ref[...], dsum_ref[: BAND_CELLS - COLS]], axis=0)
+            above = dsum_ref[COLS : COLS + BAND_CELLS]
         else:
-            above = dsum_ref[BAND_CELLS - COLS : TOKENS - COLS]
+            above = jnp.concatenate([dsum_ref[COLS + BAND_CELLS :], row_ref[...]], axis=0)
         cot = dot(cells_pick_ref[...], dx_ref[pl.ds(band * BAND, BAND)]) * gain_ref[...]
         normed, scale = norm_parts(tok_ref[pl.ds(band * BAND_CELLS, BAND_CELLS)].astype(f32))
         flat = jnp.mean(cot, axis=-1, keepdims=True)
@@ -394,22 +394,23 @@
     width = field.shape[-1]
     field, side = field.astype(f32).reshape(rows, cols, width), side.astype(f32).reshape(rows, BORDER, width)
     first = field[:, :BORDER] + side
-    return jnp.concatenate([first, field[:, BORDER:]], axis=1).reshape(rows * cols, width).astype(bf16)
+    return jnp.concatenate([first, field[:, BORDER:]], axis=1).reshape(rows * cols, width)
 
 
 def own_cells_kernel(main_ref, lat_ref, lon_ref, diag_ref, m_main_ref, m_lat_ref, tokens_ref, merged_ref):
     corner = diag_ref[:TURN].astype(f32)[TURN - CORNER :]
     beside = lon_ref[:EDGE].astype(f32)[: EDGE - CORNER]
-    tokens_ref[:TOP] = fill_edge(lat_ref[...], corner, SHIFT_LAT, COLS)
-    tokens_ref[TOP:] = fill_edge(main_ref[...], beside, ROWS - SHIFT_LAT, COLS)
+    tokens_ref[:TOP] = fill_edge(lat_ref[...], corner, SHIFT_LAT, COLS).astype(bf16)
+    tokens_ref[TOP:] = fill_edge(main_ref[...], beside, ROWS - SHIFT_LAT, COLS).astype(bf16)
     side_rows = PAIR_SIDE - PAIR_CORNER
     for half in range(2):
         cols = pl.ds(half * D, D)
-        lat = m_lat_ref[half * PAIR_TOP : (half + 1) * PAIR_TOP]
-        lon = lon_ref[EDGE + half * side_rows : EDGE + (half + 1) * side_rows]
-        diag = diag_ref[TURN + half * PAIR_CORNER : TURN + (half + 1) * PAIR_CORNER]
-        merged_ref[:PAIR_TOP, cols] = fill_edge(lat, diag, 2, PAIR_COLS)
-        merged_ref[PAIR_TOP:, cols] = fill_edge(m_main_ref[:, cols], lon, PAIR_ROWS - 2, PAIR_COLS)
+        lat = m_lat_ref[...].astype(f32)[half * PAIR_TOP : (half + 1) * PAIR_TOP]
+        lon = lon_ref[EDGE:].astype(f32)[half * side_rows : (half + 1) * side_rows]
+        diag = diag_ref[TURN:].astype(f32)[half * PAIR_CORNER : (half + 1) * PAIR_CORNER]
+        own = m_main_ref[:, cols].astype(f32)[: PAIRS - PAIR_TOP]
+        field, side = jnp.concatenate([lat, own], axis=0), jnp.concatenate([diag, lon], axis=0)
+        merged_ref[:, cols] = fill_edge(field, side, PAIR_ROWS, PAIR_COLS).astype(bf16)
 
 
 def add_kernel(a_ref, b_ref, *out_refs):
@@ -483,7 +484,7 @@
         saved(REST) + [((TOKENS, D), bf16), ((TOKENS, D), bf16), ((COLS, D), bf16)],
         [((WIDTH, D), bf16)],
     )(tok, cells, *beside, gain, w_qkv, w_proj, pick, shift, cells_pick, att0)
-    last = up(row)
+    behind = down(row)
     cots, w_merge = call(
         cotangent_kernel,
         [((4, PAIRS, D), f32), ((4 * D, 2 * D), bf16)],
@@ -494,20 +495,20 @@
         pair_kernel,
         [((TOKENS, D), bf16), ((COLS, D), bf16), ((4, PAIRS, D), bf16)],
         [((4, PAIRS, D), f32)],
-    )(summed, last, gain_merge, cots, pair, unpair)
-    first = down(row)
+    )(summed, behind, gain_merge, cots, pair, unpair)
+    last = up(row)
     band = jnp.asarray(band_selector(), bf16)
     unshift = jnp.asarray(shift_selector(WIN_LAT, COLS, SHIFT_LON).T, bf16)
     pair_unshift = jnp.asarray(shift_selector(PAIR_ROWS, PAIR_COLS, SHIFT_LON // 2).T, bf16)
-    up1, dqkv1, xst, mixt = call(
+    up0, dqkv0, xst, mixt = call(
         inner_back_kernel,
         [((BAND, D), bf16), ((BAND, 3 * D), bf16), ((D, WIDTH), bf16), ((D, WIDTH), bf16)],
         [((BAND, D), bf16)],
-    )(d_summed, qkv1, probs1, w_proj, band, xs0, xs1, mixed0, mixed1)
+    )(d_summed, qkv0, probs0, qkv1, probs1, w_proj, band, xs0, xs1, mixed0, mixed1)
     m_main, m_lat, m_lon, m_diag = call(
         merge_kernel,
         [
-            ((PAIRS - PAIR_TOP, 2 * D), bf16), ((2 * PAIR_TOP, D), bf16),
+            ((PAIRS, 2 * D), bf16), ((2 * PAIR_TOP, D), bf16),
             ((2 * (PAIR_SIDE - PAIR_CORNER), D), bf16), ((2 * PAIR_CORNER, D), bf16),
         ],
     )(merge_normed, w_merge, pair_unshift)
@@ -516,7 +517,7 @@
         outer_back_kernel,
         [((WIDTH, 3 * D), bf16), ((4, 32, 32, 128), bf16), ((4, 32, 32, 128), bf16)],
         [((WIDTH, D), bf16), ((BAND, D), bf16)],
-    )(d_summed, first, xst, mixt, after(up1, m_main), dqkv1, qkv0, probs0, qkv1, probs1, w_proj, band)
+    )(d_summed, last, xst, mixt, after(up0, m_main), dqkv0, qkv1, probs1, w_proj, band)
     main, to_lat, to_lon, to_diag = call(
         cells_back_kernel,
         [
@@ -524,7 +525,7 @@
             ((EDGE + 2 * (PAIR_SIDE - PAIR_CORNER), D), bf16), ((TURN + 2 * PAIR_CORNER, D), bf16),
         ],
         [((WIDTH, D), bf16)],
-    )(dqkv, w_qkv, cells_pick, unshift, tok, d_summed, first, gain, m_lon, m_diag)
+    )(dqkv, w_qkv, cells_pick, unshift, tok, d_summed, last, gain, m_lon, m_diag)
 
     def finish(lat, lon, diag):
         grad_tokens, merged = call(own_cells_kernel, [((TOKENS, D), bf16), ((PAIRS, 2 * D), bf16)])(

time: 84.4 us -> 80.6 us (0.955)
  starting transfers between devices: 33.3 us -> 30.9 us
  waiting for transfers between devices: 21.6 us -> 20.6 us
    ppermute x3, waiting for transfers between devices: 8.23 us -> 6.23 us  [swap(): lax.ppermute(block, ('lat', 'lon'), [(i, across(i, step)) for i in range(...]
    ppermute x10, starting transfers between devices: 22.6 us -> 21.2 us  [send(): return lax.ppermute(block, ('lat', 'lon'), route)]
    ppermute x10, waiting for transfers between devices: 13.4 us -> 14.3 us  [send(): return lax.ppermute(block, ('lat', 'lon'), route)]
  transfers between devices with their start and end apart: 15 -> 15, of which waited for: 5 -> 4; matrix products, arithmetic and copies ran while one was open for 0% -> 0% of each run, Pallas kernels for 22% -> 23%
where the time goes in v7:
time: 80.6 us; the launch traced here: 80.3 us
  starting transfers between devices  30.9 us (38%)
  Pallas kernels  25.8 us (32%)
  waiting for transfers between devices  20.6 us (26%)
  local copies, waits for them, and re-layouts  2.1 us (3%)
  between operations  0.91 us (1%)
    ppermute x10, starting transfers between devices, send(): return lax.ppermute(block, ('lat', 'lon'), route)  21.2 us
    ppermute x10, waiting for transfers between devices, send(): return lax.ppermute(block, ('lat', 'lon'), route)  14.3 us
    ppermute x3, waiting for transfers between devices, swap(): lax.ppermute(block, ('lat', 'lon'), [(i, across(i, step)) for i in range(...  6.23 us
    pallas_call x1, Pallas kernels, chain(): call(outer_back_kernel, [((WIDTH, 3 * D), bf16), ((4, 32, 32, 128), bf16)...  4.82 us
    pallas_call x1, Pallas kernels, chain(): call(inner_kernel, [(h.shape, h.dtype) for h in held] + [((TOKENS - TOP,...  4.15 us
    all_to_all x1, starting transfers between devices, reduce_rest(): lax.all_to_all(sums, ('lat', 'lon'), 0, 0, axis_index_groups=rest, tiled=...  4.09 us
    pallas_call x1, Pallas kernels, chain(): call(outer_kernel, saved(REST) + [((TOKENS, D), bf16), ((TOKENS, D), bf16...  4.04 us
    ppermute x3, starting transfers between devices, swap(): lax.ppermute(block, ('lat', 'lon'), [(i, across(i, step)) for i in range(...  3.93 us
  transfers between devices with their start and end apart: 15, of which 4 were waited for; matrix products, arithmetic and copies ran while one was open for 0% of the time, Pallas kernels for 23%

profile of v7, /device:TPU:1, one launch (start us, length us, event | category | flops | bytes accessed | tf_op | source)
XLA Modules:
  0.0 80.3 jit_solution(3704343616425378919)
XLA Ops:
  0.6 1.1 %copy-done.5 = bf16[12,48,512]{2,1,0:T(8,128)(2,1)S(1)} copy-done((bf16[12,48,512]{2,1,0:T(8,128)(2,1)S(1)}, bf16[12,48,512]{2,1,0:T(8,128)(2,1)}, u32[]{:S(2)}) %copy-start.5) | copy-done | bytes 589848
  1.7 1.0 %copy-done.7 = bf16[6,24,1024]{2,1,0:T(8,128)(2,1)S(1)} copy-done((bf16[6,24,1024]{2,1,0:T(8,128)(2,1)S(1)}, bf16[6,24,1024]{2,1,0:T(8,128)(2,1)}, u32[]{:S(2)}) %copy-start.7) | copy-done | bytes 294936
  2.7 0.0 copy-start.10
  2.7 0.0 copy-start.11
  2.7 0.0 copy-start.12
  2.7 0.0 copy-start.13
  2.7 0.0 copy-start.14
  2.7 0.0 copy-start.15
  2.7 0.2 shard_map.175
  3.0 3.3 %collective-permute-start.1 = (bf16[192,512]{1,0:T(8,128)(2,1)S(1)}, bf16[192,512]{1,0:T(8,128)(2,1)S(1)}, u32[]{:S(2)}, u32[]{:S(2)}) collective-permute-start(bf16[192,512]{1,0:T(8,128)(2,1)S(1)} %get-tuple-element.68), channel_id=1, source_target_pairs={{0,15},{1,0},{2,1},{3,2},{4,3},{5,4},{6,5},{7,6},{8,7},{9,8},{10,9... | collective-permute-start | bytes 589832 | tf_op jit(solution)/shard_map/ppermute | solution.py:547
  6.3 6.5 %collective-permute-start = (bf16[144,512]{1,0:T(8,128)(2,1)S(1)}, bf16[144,512]{1,0:T(8,128)(2,1)S(1)}, u32[]{:S(2)}, u32[]{:S(2)}) collective-permute-start(bf16[144,512]{1,0:T(8,128)(2,1)S(1)} %get-tuple-element.67), channel_id=1, source_target_pairs={{0,240},{1,241},{2,242},{3,243},{4,244},{5,245},{6,246},{7,247},{8... | collective-permute-start | bytes 442376 | tf_op jit(solution)/shard_map/ppermute | solution.py:547
  12.8 3.8 %collective-permute-start.2 = (bf16[48,512]{1,0:T(8,128)(2,1)S(1)}, bf16[48,512]{1,0:T(8,128)(2,1)S(1)}, u32[]{:S(2)}, u32[]{:S(2)}) collective-permute-start(bf16[48,512]{1,0:T(8,128)(2,1)S(1)} %get-tuple-element.69), channel_id=1, source_target_pairs={{0,255},{1,240},{2,241},{3,242},{4,243},{5,244},{6,245},{7,246},{8... | collective-permute-start | bytes 147464 | tf_op jit(solution)/shard_map/ppermute | solution.py:547
  16.6 0.7 collective-permute-start.4
  17.4 4.1 %shard_map.176 = (f32[1,512]{1,0:T(1,128)S(1)}, bf16[320,336]{1,0:T(8,128)(2,1)S(1)}, bf16[512,1536]{1,0:T(8,128)(2,1)S(1)}, bf16[512,512]{1,0:T(8,128)(2,1)S(1)...) custom-call(bf16[576,512]{1,0:T(8,128)(2,1)S(1)} %get-tuple-element., ...), custom_call_target="tpu_custom_call" | custom-call | flops 1000000000 | bytes 2000000 | tf_op jit(solution)/shard_map/pallas_call | solution.py:474
  21.5 0.0 collective-permute-done.2.diag_ref
  21.6 0.0 copy-start
  21.6 4.0 %shard_map.177 = (bf16[400,512]{1,0:T(8,128)(2,1)S(1)}, bf16[400,1536]{1,0:T(8,128)(2,1)S(1)}, bf16[400,512]{1,0:T(8,128)(2,1)S(1)}, f32[5,2,80,320]{3,2,1,0:T(8...) custom-call(bf16[576,512]{1,0:T(8,128)(2,1)S(1)} %get-tuple-element.65.tok_ref, ...), custom_call_target="tpu_custom_call" | custom-call | flops 1000000000 | bytes 2000000 | tf_op jit(solution)/shard_map/pallas_call | solution.py:482
  25.6 0.8 %collective-permute-start.3 = (bf16[48,512]{1,0:T(8,128)(2,1)S(1)}, bf16[48,512]{1,0:T(8,128)(2,1)S(1)}, u32[]{:S(2)}, u32[]{:S(2)}) collective-permute-start(bf16[48,512]{1,0:T(8,128)(2,1)S(1)} %get-tuple-element.78), channel_id=1, source_target_pairs={{0,16},{1,17},{2,18},{3,19},{4,20},{5,21},{6,22},{7,23},{8,24},{9,... | collective-permute-start | bytes 147464 | tf_op jit(solution)/shard_map/ppermute | solution.py:547
  26.5 2.0 %shard_map.178 = (f32[4,144,512]{2,1,0:T(8,128)S(1)}, bf16[2048,1024]{1,0:T(8,128)(2,1)S(1)}) custom-call(bf16[144,1024]{1,0:T(8,128)(2,1)S(1)} %get-tuple-element.81.g_ref, bf16[48,512]{1,0:T(8,128)(2,1)S(1)} %collective-permute-done.4.lat_ref, bf16[192,512]{1,0:T(8,128)(2,1)S(1)} %collective-permute-done.1.lon_ref, ...), custom_call_target="tpu_custom_call" | custom-call | flops 1000000000 | bytes 2000000 | tf_op jit(solution)/shard_map/pallas_call | solution.py:488
  28.5 3.8 %collective-permute-done.3.row_ref = bf16[48,512]{1,0:T(8,128)(2,1)S(1)} collective-permute-done((bf16[48,512]{1,0:T(8,128)(2,1)S(1)}, bf16[48,512]{1,0:T(8,128)(2,1)S(1)}, u32[]{:S(2)}, u32[]{:S(2)}) %collective-permute-start.3) | collective-permute-done | bytes 49184 | tf_op jit(solution)/shard_map/ppermute | solution.py:547
  32.3 1.2 %shard_map.179 = (bf16[576,512]{1,0:T(8,128)(2,1)S(1)}, bf16[48,512]{1,0:T(8,128)(2,1)S(1)}, bf16[4,144,512]{2,1,0:T(8,128)(2,1)S(1)}) custom-call(bf16[576,512]{1,0:T(8,128)(2,1)S(1)} %get-tuple-element.77.summed_ref, bf16[48,512]{1,0:T(8,128)(2,1)S(1)} %collective-permute-done.3.row_ref, f32[4,1,512]{2,1,0:T(1,128)S(1)} %get-tuple-element.79.gain_ref, ...), custom_call_target="tpu_custom_call" | custom-call | flops 1000000000 | bytes 2000000 | tf_op jit(solution)/shard_map/pallas_call | solution.py:494
  33.5 0.9 %collective-permute-start.5 = (bf16[48,512]{1,0:T(8,128)(2,1)S(1)}, bf16[48,512]{1,0:T(8,128)(2,1)S(1)}, u32[]{:S(2)}, u32[]{:S(2)}) collective-permute-start(bf16[48,512]{1,0:T(8,128)(2,1)S(1)} %get-tuple-element.88), channel_id=1, source_target_pairs={{0,240},{1,241},{2,242},{3,243},{4,244},{5,245},{6,246},{7,247},{8... | collective-permute-start | bytes 147464 | tf_op jit(solution)/shard_map/ppermute | solution.py:547
  34.4 1.0 %shard_map.181 = (bf16[144,1024]{1,0:T(8,128)(2,1)S(1)}, bf16[48,512]{1,0:T(8,128)(2,1)S(1)}, bf16[80,512]{1,0:T(8,128)(2,1)S(1)}, bf16[16,512]{1,0:T(8,128)(2,1)S(1)}) custom-call(bf16[4,144,512]{2,1,0:T(8,128)(2,1)S(1)} %get-tuple-element.100.normed_ref, bf16[2048,1024]{1,0:T(8,128)(2,1)S(1)} %get-tuple-element.101.wmerge_ref, bf16[192,144]{1,0:T(8,128)(2,1)S(1)} %copy-done.3), custom_call_target="tpu_custom_call" | custom-call | flops 1000000000 | bytes 2000000 | tf_op jit(solution)/shard_map/pallas_call | solution.py:508
  35.4 3.1 %shard_map.180 = (bf16[320,512]{1,0:T(8,128)(2,1)S(1)}, bf16[320,1536]{1,0:T(8,128)(2,1)S(1)}, bf16[512,640]{1,0:T(8,128)(2,1)S(1)}, bf16[512,640]{1,0:T(8,128)(2,1)S(1)}) custom-call(bf16[576,512]{1,0:T(8,128)(2,1)S(1)} %get-tuple-element.87.dsum_ref, bf16[240,1536]{1,0:T(8,128)(2,1)S(1)} %get-tuple-element.89.qkv0_ref, ...), custom_call_target="tpu_custom_call" | custom-call | flops 1000000000 | bytes 2000000 | tf_op jit(solution)/shard_map/pallas_call | solution.py:503
  38.5 0.0 collective-permute-done.5.row_ref
  38.5 0.0 copy-start.2
  38.5 4.8 %shard_map.182 = (bf16[640,1536]{1,0:T(8,128)(2,1)S(1)}, bf16[4,32,32,128]{3,2,1,0:T(8,128)(2,1)S(1)}, bf16[4,32,32,128]{3,2,1,0:T(8,128)(2,1)S(1)}) custom-call(bf16[576,512]{1,0:T(8,128)(2,1)S(1)} %get-tuple-element.87.dsum_ref, bf16[48,512]{1,0:T(8,128)(2,1)S(1)} %collective-permute-done.5.row_ref, bf16[512,640]{1,0:T(8,128)(2,1)S(1)} %get-tuple-element.97.xst_ref, ...), custom_call_target="tpu_custom_call" | custom-call | flops 1000000000 | bytes 2000000 | tf_op jit(solution)/shard_map/pallas_call | solution.py:516
  43.3 1.7 %collective-permute-start.7 = (bf16[4,32,32,128]{3,2,1,0:T(8,128)(2,1)S(1)}, bf16[4,32,32,128]{3,2,1,0:T(8,128)(2,1)S(1)}, u32[]{:S(2)}, u32[]{:S(2)}) collective-permute-start(bf16[4,32,32,128]{3,2,1,0:T(8,128)(2,1)S(1)} %get-tuple-element.112), channel_id=1, source_target_pairs={{0,1},{1,0},{2,3},{3,2},{4,5},{5,4},{6,7},{7,6},{8,9},{9,8},{10,11... | collective-permute-start | bytes 3145736 | tf_op jit(solution)/shard_map/ppermute | solution.py:574
  45.1 2.5 %shard_map.183 = (bf16[432,512]{1,0:T(8,128)(2,1)S(1)}, bf16[144,512]{1,0:T(8,128)(2,1)S(1)}, bf16[176,512]{1,0:T(8,128)(2,1)S(1)}, bf16[48,512]{1,0:T(8,128)(2,1)S(1)}) custom-call(bf16[640,1536]{1,0:T(8,128)(2,1)S(1)} %get-tuple-element.105.dqkv_ref, bf16[512,1536]{1,0:T(8,128)(2,1)S(1)} %get-tuple-element.71.wqkv_ref, ...), custom_call_target="tpu_custom_call" | custom-call | flops 1000000000 | bytes 2000000 | tf_op jit(solution)/shard_map/pallas_call | solution.py:521
  47.6 0.2 shard_map.184
  47.8 0.1 collective-permute-start.10
  47.9 0.1 collective-permute-start.8
  48.0 3.7 %collective-permute-start.9 = (bf16[32,32,128]{2,1,0:T(8,128)(2,1)S(1)}, bf16[32,32,128]{2,1,0:T(8,128)(2,1)S(1)}, u32[]{:S(2)}, u32[]{:S(2)}) collective-permute-start(bf16[32,32,128]{2,1,0:T(8,128)(2,1)S(1)} %get-tuple-element.116), channel_id=1, source_target_pairs={{0,4},{1,129},{2,6},{3,131},{4,0},{5,133},{6,2},{7,135},{8,12},{9,... | collective-permute-start | bytes 786440 | tf_op jit(solution)/shard_map/ppermute | solution.py:571
  51.8 1.2 %collective-permute-start.11 = (bf16[48,512]{1,0:T(8,128)(2,1)S(1)}, bf16[48,512]{1,0:T(8,128)(2,1)S(1)}, u32[]{:S(2)}, u32[]{:S(2)}) collective-permute-start(bf16[48,512]{1,0:T(8,128)(2,1)S(1)} %get-tuple-element.118), channel_id=1, source_target_pairs={{0,16},{1,17},{2,18},{3,19},{4,20},{5,21},{6,22},{7,23},{8,24},{9,... | collective-permute-start | bytes 147464 | tf_op jit(solution)/shard_map/ppermute | solution.py:547
  52.9 1.7 %collective-permute-done.10.d_ref = bf16[32,32,128]{2,1,0:T(8,128)(2,1)S(1)} collective-permute-done((bf16[32,32,128]{2,1,0:T(8,128)(2,1)S(1)}, bf16[32,32,128]{2,1,0:T(8,128)(2,1)S(1)}, u32[]{:S(2)}, u32[]{:S(2)}) %collective-permute-start.10) | collective-permute-done | bytes 262176 | tf_op jit(solution)/shard_map/ppermute | solution.py:571
  54.6 0.0 collective-permute-done.8.b_ref
  54.6 4.5 %collective-permute-done.9.c_ref = bf16[32,32,128]{2,1,0:T(8,128)(2,1)S(1)} collective-permute-done((bf16[32,32,128]{2,1,0:T(8,128)(2,1)S(1)}, bf16[32,32,128]{2,1,0:T(8,128)(2,1)S(1)}, u32[]{:S(2)}, u32[]{:S(2)}) %collective-permute-start.9) | collective-permute-done | bytes 262176 | tf_op jit(solution)/shard_map/ppermute | solution.py:571
  59.1 0.8 %shard_map.185 = bf16[32,32,128]{2,1,0:T(8,128)(2,1)} custom-call(bf16[32,32,128]{2,1,0:T(8,128)(2,1)S(1)} %get-tuple-element.114.a_ref, bf16[32,32,128]{2,1,0:T(8,128)(2,1)S(1)} %collective-permute-done.8.b_ref, bf16[32,32,128]{2,1,0:T(8,128)(2,1)S(1)} %collective-permute-done.9.c_ref, bf16[32,32,128]{2,1,0:T(8,128)(2,1)S(1)} %collective-permute-done.10.d_ref), custom_call_target="tpu_custom_call" | custom-call | flops 1000000000 | bytes 2000000 | tf_op jit(solution)/shard_map/pallas_call | solution.py:577
  60.0 0.0 collective-permute-done.11.m_lat_ref
  60.0 4.1 %all-to-all-start = ((bf16[32,32,128]{2,1,0:T(8,128)(2,1)}), bf16[32,32,128]{2,1,0:T(8,128)(2,1)S(1)}, u32[]{:S(2)}, u32[]{:S(2)}) async-start(bf16[32,32,128]{2,1,0:T(8,128)(2,1)} %shard_map.185), calls=%async_computation | async-start | bytes 524288 | tf_op jit(solution)/shard_map/all_to_all | solution.py:580
  64.1 1.0 %collective-permute-start.12 = (bf16[176,512]{1,0:T(8,128)(2,1)S(1)}, bf16[176,512]{1,0:T(8,128)(2,1)S(1)}, u32[]{:S(2)}, u32[]{:S(2)}) collective-permute-start(bf16[176,512]{1,0:T(8,128)(2,1)S(1)} %get-tuple-element.121), channel_id=1, source_target_pairs={{0,1},{1,2},{2,3},{3,4},{4,5},{5,6},{6,7},{7,8},{8,9},{9,10},{10,1... | collective-permute-start | bytes 540680 | tf_op jit(solution)/shard_map/ppermute | solution.py:547
  65.1 1.5 %collective-permute-start.6 = (bf16[144,512]{1,0:T(8,128)(2,1)S(1)}, bf16[144,512]{1,0:T(8,128)(2,1)S(1)}, u32[]{:S(2)}, u32[]{:S(2)}) collective-permute-start(bf16[144,512]{1,0:T(8,128)(2,1)S(1)} %get-tuple-element.110), channel_id=1, source_target_pairs={{0,16},{1,17},{2,18},{3,19},{4,20},{5,21},{6,22},{7,23},{8,24},{9,... | collective-permute-start | bytes 442376 | tf_op jit(solution)/shard_map/ppermute | solution.py:547
  66.6 1.5 %collective-permute-start.13 = (bf16[48,512]{1,0:T(8,128)(2,1)S(1)}, bf16[48,512]{1,0:T(8,128)(2,1)S(1)}, u32[]{:S(2)}, u32[]{:S(2)}) collective-permute-start(bf16[48,512]{1,0:T(8,128)(2,1)S(1)} %get-tuple-element.123), channel_id=1, source_target_pairs={{0,17},{1,18},{2,19},{3,20},{4,21},{5,22},{6,23},{7,24},{8,25},{9,... | collective-permute-start | bytes 147464 | tf_op jit(solution)/shard_map/ppermute | solution.py:547
  68.1 10.6 %collective-permute-done.13.diag_ref = bf16[48,512]{1,0:T(8,128)(2,1)S(1)} collective-permute-done((bf16[48,512]{1,0:T(8,128)(2,1)S(1)}, bf16[48,512]{1,0:T(8,128)(2,1)S(1)}, u32[]{:S(2)}, u32[]{:S(2)}) %collective-permute-start.13) | collective-permute-done | bytes 49184 | tf_op jit(solution)/shard_map/ppermute | solution.py:547
  78.6 0.0 collective-permute-done.12.lon_ref
  78.6 0.0 collective-permute-done.6.lat_ref
  78.6 1.0 %shard_map.186 = (bf16[576,512]{1,0:T(8,128)(2,1)}, bf16[144,1024]{1,0:T(8,128)(2,1)}) custom-call(bf16[432,512]{1,0:T(8,128)(2,1)S(1)} %get-tuple-element.109.main_ref, bf16[144,512]{1,0:T(8,128)(2,1)S(1)} %collective-permute-done.6.lat_ref, bf16[176,512]{1,0:T(8,128)(2,1)S(1)} %collective-permute-done.12.lon_ref, ...), custom_call_target="tpu_custom_call" | custom-call | flops 1000000000 | bytes 2000000 | tf_op jit(solution)/shard_map/pallas_call | solution.py:531
  79.6 0.7 shard_map.187
  (27 shorter events, 0.1 us)
Async XLA Ops:
  0.6 1.1 %copy-start.5 = (bf16[12,48,512]{2,1,0:T(8,128)(2,1)S(1)}, bf16[12,48,512]{2,1,0:T(8,128)(2,1)}, u32[]{:S(2)}) copy-start(bf16[12,48,512]{2,1,0:T(8,128)(2,1)} %param.16) | copy-start | bytes 1769476
  1.7 1.0 %copy-start.7 = (bf16[6,24,1024]{2,1,0:T(8,128)(2,1)S(1)}, bf16[6,24,1024]{2,1,0:T(8,128)(2,1)}, u32[]{:S(2)}) copy-start(bf16[6,24,1024]{2,1,0:T(8,128)(2,1)} %param.22) | copy-start | bytes 884740
  2.7 14.7 %copy-start.4 = (bf16[512,1536]{1,0:T(8,128)(2,1)S(1)}, bf16[512,1536]{1,0:T(8,128)(2,1)}, u32[]{:S(2)}) copy-start(bf16[512,1536]{1,0:T(8,128)(2,1)} %refs_2_.1) | copy-start | bytes 4718596
  2.7 14.7 %copy-start.6 = (bf16[512,512]{1,0:T(8,128)(2,1)S(1)}, bf16[512,512]{1,0:T(8,128)(2,1)}, u32[]{:S(2)}) copy-start(bf16[512,512]{1,0:T(8,128)(2,1)} %refs_3_.1) | copy-start | bytes 1572868
  2.7 14.7 %copy-start.8 = (f32[2048]{0:T(1024)S(1)}, f32[2048]{0:T(1024)}, u32[]{:S(2)}) copy-start(f32[2048]{0:T(1024)} %param.20) | copy-start | bytes 24580
  2.7 14.7 %copy-start.9 = (f32[512]{0:T(512)S(1)}, f32[512]{0:T(512)}, u32[]{:S(2)}) copy-start(f32[512]{0:T(512)} %param.17) | copy-start | bytes 6148
  2.7 14.7 %copy-start.10 = (bf16[320,336]{1,0:T(8,128)(2,1)S(1)}, bf16[320,336]{1,0:T(8,128)(2,1)}, u32[]{:S(2)}) copy-start(bf16[320,336]{1,0:T(8,128)(2,1)} %constant.18.clone.refs_1_) | copy-start | bytes 645124
  2.7 14.7 %copy-start.11 = (bf16[288,336]{1,0:T(8,128)(2,1)S(1)}, bf16[288,336]{1,0:T(8,128)(2,1)}, u32[]{:S(2)}) copy-start(bf16[288,336]{1,0:T(8,128)(2,1)} %constant.19.clone.refs_5_) | copy-start | bytes 580612
  2.7 14.7 %copy-start.12 = (bf16[288,320]{1,0:T(8,128)(2,1)S(1)}, bf16[288,320]{1,0:T(8,128)(2,1)}, u32[]{:S(2)}) copy-start(bf16[288,320]{1,0:T(8,128)(2,1)} %constant.20.clone.refs_6_) | copy-start | bytes 552964
  2.7 14.7 %copy-start.13 = (bf16[192,192]{1,0:T(8,128)(2,1)S(1)}, bf16[192,192]{1,0:T(8,128)(2,1)}, u32[]{:S(2)}) copy-start(bf16[192,192]{1,0:T(8,128)(2,1)} %constant.21.clone.refs_7_) | copy-start | bytes 221188
  2.7 14.6 %copy-start.14 = (bf16[192,192]{1,0:T(8,128)(2,1)S(1)}, bf16[192,192]{1,0:T(8,128)(2,1)}, u32[]{:S(2)}) copy-start(bf16[192,192]{1,0:T(8,128)(2,1)} %constant.22.clone.refs_8_) | copy-start | bytes 221188
  2.7 14.6 %copy-start.15 = (bf16[144,192]{1,0:T(8,128)(2,1)S(1)}, bf16[144,192]{1,0:T(8,128)(2,1)}, u32[]{:S(2)}) copy-start(bf16[144,192]{1,0:T(8,128)(2,1)} %constant.23.clone.refs_9_) | copy-start | bytes 165892
  3.0 18.6 %collective-permute-start.1 = (bf16[192,512]{1,0:T(8,128)(2,1)S(1)}, bf16[192,512]{1,0:T(8,128)(2,1)S(1)}, u32[]{:S(2)}, u32[]{:S(2)}) collective-permute-start(bf16[192,512]{1,0:T(8,128)(2,1)S(1)} %get-tuple-element.68), channel_id=1, source_target_pairs={{0,15},{1,0},{2,1},{3,2},{4,3},{5,4},{6,5},{7,6},{8,7},{9,8},{10,9... | collective-permute-start | bytes 589832 | tf_op jit(solution)/shard_map/ppermute | solution.py:547
  6.3 15.3 %collective-permute-start = (bf16[144,512]{1,0:T(8,128)(2,1)S(1)}, bf16[144,512]{1,0:T(8,128)(2,1)S(1)}, u32[]{:S(2)}, u32[]{:S(2)}) collective-permute-start(bf16[144,512]{1,0:T(8,128)(2,1)S(1)} %get-tuple-element.67), channel_id=1, source_target_pairs={{0,240},{1,241},{2,242},{3,243},{4,244},{5,245},{6,246},{7,247},{8... | collective-permute-start | bytes 442376 | tf_op jit(solution)/shard_map/ppermute | solution.py:547
  12.8 8.8 %collective-permute-start.2 = (bf16[48,512]{1,0:T(8,128)(2,1)S(1)}, bf16[48,512]{1,0:T(8,128)(2,1)S(1)}, u32[]{:S(2)}, u32[]{:S(2)}) collective-permute-start(bf16[48,512]{1,0:T(8,128)(2,1)S(1)} %get-tuple-element.69), channel_id=1, source_target_pairs={{0,255},{1,240},{2,241},{3,242},{4,243},{5,244},{6,245},{7,246},{8... | collective-permute-start | bytes 147464 | tf_op jit(solution)/shard_map/ppermute | solution.py:547
  16.6 9.9 %collective-permute-start.4 = (bf16[48,512]{1,0:T(8,128)(2,1)S(1)}, bf16[48,512]{1,0:T(8,128)(2,1)S(1)}, u32[]{:S(2)}, u32[]{:S(2)}) collective-permute-start(bf16[48,512]{1,0:T(8,128)(2,1)S(1)} %get-tuple-element.82), channel_id=1, source_target_pairs={{0,240},{1,241},{2,242},{3,243},{4,244},{5,245},{6,246},{7,247},{8... | collective-permute-start | bytes 147464 | tf_op jit(solution)/shard_map/ppermute | solution.py:547
  21.6 4.9 %copy-start = (bf16[2048,1024]{1,0:T(8,128)(2,1)S(1)}, bf16[2048,1024]{1,0:T(8,128)(2,1)}, u32[]{:S(2)}) copy-start(bf16[2048,1024]{1,0:T(8,128)(2,1)} %wmerge_ref.1) | copy-start | bytes 12582916
  25.6 6.6 %collective-permute-start.3 = (bf16[48,512]{1,0:T(8,128)(2,1)S(1)}, bf16[48,512]{1,0:T(8,128)(2,1)S(1)}, u32[]{:S(2)}, u32[]{:S(2)}) collective-permute-start(bf16[48,512]{1,0:T(8,128)(2,1)S(1)} %get-tuple-element.78), channel_id=1, source_target_pairs={{0,16},{1,17},{2,18},{3,19},{4,20},{5,21},{6,22},{7,23},{8,24},{9,... | collective-permute-start | bytes 147464 | tf_op jit(solution)/shard_map/ppermute | solution.py:547
  32.3 2.1 %copy-start.3 = (bf16[192,144]{1,0:T(8,128)(2,1)S(1)}, bf16[192,144]{1,0:T(8,128)(2,1)}, u32[]{:S(2)}) copy-start(bf16[192,144]{1,0:T(8,128)(2,1)} %constant.26.clone.unshift_ref) | copy-start | bytes 165892
  33.5 5.0 %collective-permute-start.5 = (bf16[48,512]{1,0:T(8,128)(2,1)S(1)}, bf16[48,512]{1,0:T(8,128)(2,1)S(1)}, u32[]{:S(2)}, u32[]{:S(2)}) collective-permute-start(bf16[48,512]{1,0:T(8,128)(2,1)S(1)} %get-tuple-element.88), channel_id=1, source_target_pairs={{0,240},{1,241},{2,242},{3,243},{4,244},{5,245},{6,246},{7,247},{8... | collective-permute-start | bytes 147464 | tf_op jit(solution)/shard_map/ppermute | solution.py:547
  34.4 1.0 %copy-start.1 = (bf16[320,288]{1,0:T(8,128)(2,1)S(1)}, bf16[320,288]{1,0:T(8,128)(2,1)}, u32[]{:S(2)}) copy-start(bf16[320,288]{1,0:T(8,128)(2,1)} %constant.24.clone.pick_ref) | copy-start | bytes 552964
  38.5 6.6 %copy-start.2 = (bf16[336,288]{1,0:T(8,128)(2,1)S(1)}, bf16[336,288]{1,0:T(8,128)(2,1)}, u32[]{:S(2)}) copy-start(bf16[336,288]{1,0:T(8,128)(2,1)} %constant.25.clone.unshift_ref) | copy-start | bytes 580612
  43.3 4.2 %collective-permute-start.7 = (bf16[4,32,32,128]{3,2,1,0:T(8,128)(2,1)S(1)}, bf16[4,32,32,128]{3,2,1,0:T(8,128)(2,1)S(1)}, u32[]{:S(2)}, u32[]{:S(2)}) collective-permute-start(bf16[4,32,32,128]{3,2,1,0:T(8,128)(2,1)S(1)} %get-tuple-element.112), channel_id=1, source_target_pairs={{0,1},{1,0},{2,3},{3,2},{4,5},{5,4},{6,7},{7,6},{8,9},{9,8},{10,11... | collective-permute-start | bytes 3145736 | tf_op jit(solution)/shard_map/ppermute | solution.py:574
  47.8 6.8 %collective-permute-start.10 = (bf16[32,32,128]{2,1,0:T(8,128)(2,1)S(1)}, bf16[32,32,128]{2,1,0:T(8,128)(2,1)S(1)}, u32[]{:S(2)}, u32[]{:S(2)}) collective-permute-start(bf16[32,32,128]{2,1,0:T(8,128)(2,1)S(1)} %get-tuple-element.117), channel_id=1, source_target_pairs={{0,6},{1,137},{2,4},{3,139},{4,2},{5,141},{6,0},{7,143},{8,14},{9,... | collective-permute-start | bytes 786440 | tf_op jit(solution)/shard_map/ppermute | solution.py:571
  47.9 6.7 %collective-permute-start.8 = (bf16[32,32,128]{2,1,0:T(8,128)(2,1)S(1)}, bf16[32,32,128]{2,1,0:T(8,128)(2,1)S(1)}, u32[]{:S(2)}, u32[]{:S(2)}) collective-permute-start(bf16[32,32,128]{2,1,0:T(8,128)(2,1)S(1)} %get-tuple-element.115), channel_id=1, source_target_pairs={{0,2},{1,9},{2,0},{3,11},{4,6},{5,13},{6,4},{7,15},{8,10},{9,1},{1... | collective-permute-start | bytes 786440 | tf_op jit(solution)/shard_map/ppermute | solution.py:571
  48.0 11.1 %collective-permute-start.9 = (bf16[32,32,128]{2,1,0:T(8,128)(2,1)S(1)}, bf16[32,32,128]{2,1,0:T(8,128)(2,1)S(1)}, u32[]{:S(2)}, u32[]{:S(2)}) collective-permute-start(bf16[32,32,128]{2,1,0:T(8,128)(2,1)S(1)} %get-tuple-element.116), channel_id=1, source_target_pairs={{0,4},{1,129},{2,6},{3,131},{4,0},{5,133},{6,2},{7,135},{8,12},{9,... | collective-permute-start | bytes 786440 | tf_op jit(solution)/shard_map/ppermute | solution.py:571
  51.8 8.2 %collective-permute-start.11 = (bf16[48,512]{1,0:T(8,128)(2,1)S(1)}, bf16[48,512]{1,0:T(8,128)(2,1)S(1)}, u32[]{:S(2)}, u32[]{:S(2)}) collective-permute-start(bf16[48,512]{1,0:T(8,128)(2,1)S(1)} %get-tuple-element.118), channel_id=1, source_target_pairs={{0,16},{1,17},{2,18},{3,19},{4,20},{5,21},{6,22},{7,23},{8,24},{9,... | collective-permute-start | bytes 147464 | tf_op jit(solution)/shard_map/ppermute | solution.py:547
  60.0 19.7 %all-to-all-start = ((bf16[32,32,128]{2,1,0:T(8,128)(2,1)}), bf16[32,32,128]{2,1,0:T(8,128)(2,1)S(1)}, u32[]{:S(2)}, u32[]{:S(2)}) async-start(bf16[32,32,128]{2,1,0:T(8,128)(2,1)} %shard_map.185), calls=%async_computation | async-start | bytes 524288 | tf_op jit(solution)/shard_map/all_to_all | solution.py:580
  64.1 14.6 %collective-permute-start.12 = (bf16[176,512]{1,0:T(8,128)(2,1)S(1)}, bf16[176,512]{1,0:T(8,128)(2,1)S(1)}, u32[]{:S(2)}, u32[]{:S(2)}) collective-permute-start(bf16[176,512]{1,0:T(8,128)(2,1)S(1)} %get-tuple-element.121), channel_id=1, source_target_pairs={{0,1},{1,2},{2,3},{3,4},{4,5},{5,6},{6,7},{7,8},{8,9},{9,10},{10,1... | collective-permute-start | bytes 540680 | tf_op jit(solution)/shard_map/ppermute | solution.py:547
  65.1 13.6 %collective-permute-start.6 = (bf16[144,512]{1,0:T(8,128)(2,1)S(1)}, bf16[144,512]{1,0:T(8,128)(2,1)S(1)}, u32[]{:S(2)}, u32[]{:S(2)}) collective-permute-start(bf16[144,512]{1,0:T(8,128)(2,1)S(1)} %get-tuple-element.110), channel_id=1, source_target_pairs={{0,16},{1,17},{2,18},{3,19},{4,20},{5,21},{6,22},{7,23},{8,24},{9,... | collective-permute-start | bytes 442376 | tf_op jit(solution)/shard_map/ppermute | solution.py:547
  66.6 12.1 %collective-permute-start.13 = (bf16[48,512]{1,0:T(8,128)(2,1)S(1)}, bf16[48,512]{1,0:T(8,128)(2,1)S(1)}, u32[]{:S(2)}, u32[]{:S(2)}) collective-permute-start(bf16[48,512]{1,0:T(8,128)(2,1)S(1)} %get-tuple-element.123), channel_id=1, source_target_pairs={{0,17},{1,18},{2,19},{3,20},{4,21},{5,22},{6,23},{7,24},{8,25},{9,... | collective-permute-start | bytes 147464 | tf_op jit(solution)/shard_map/ppermute | solution.py:547

commit v8 on v7

--- a/solution.py
+++ b/solution.py
@@ -181,23 +181,25 @@
             dqkv_ref[out, 2 * D + at : 2 * D + at + GROUP_WIDTH] = d_values.astype(bf16)
 
 
-def border_kernel(tok_ref, g_ref, own_ref, own_g_ref, top_ref, g_top_ref, edge_ref, corner_ref, sem):
-    copies = [
-        pltpu.make_async_copy(tok_ref, own_ref, sem.at[0]),
-        pltpu.make_async_copy(g_ref, own_g_ref, sem.at[1]),
-    ]
-    for copy in copies:
-        copy.start()
-    for copy in copies:
-        copy.wait()
+def border_kernel(tok_ref, own_ref, top_ref, edge_ref, sem):
+    copy = pltpu.make_async_copy(tok_ref, own_ref, sem)
+    copy.start()
+    copy.wait()
     edge = [own_ref[row * COLS : row * COLS + 16].astype(f32)[:BORDER] for row in range(ROWS)]
+    top_ref[...] = own_ref[:TOP]
+    edge_ref[...] = jnp.concatenate(edge, axis=0).astype(bf16)
+
+
+def border_pairs_kernel(g_ref, cells_ref, own_g_ref, g_top_ref, edge_ref, corner_ref, sem):
+    copy = pltpu.make_async_copy(g_ref, own_g_ref, sem)
+    copy.start()
+    edge_ref[:EDGE] = cells_ref[...]
+    corner_ref[:TURN] = cells_ref[:TURN]
+    copy.wait()
     cots = own_g_ref[...].astype(f32)
     side = [cots[row * PAIR_COLS : row * PAIR_COLS + BORDER] for row in range(PAIR_ROWS)]
-    top_ref[...] = own_ref[:TOP]
     g_top_ref[...] = halves(cots[:PAIR_TOP]).astype(bf16)
-    edge_ref[:EDGE] = jnp.concatenate(edge, axis=0).astype(bf16)
     edge_ref[EDGE:] = halves(jnp.concatenate(side, axis=0).astype(bf16))
-    corner_ref[:TURN] = jnp.concatenate(edge[:4], axis=0).astype(bf16)
     corner_ref[TURN:] = halves(side[0]).astype(bf16)
 
 
@@ -454,16 +456,21 @@
 
 
 def chain(tok, gain, w_qkv, w_proj, gain_merge, w_merge, g_merged, fetch, up, down):
-    tok, g_merged, top, g_top, edge, corner = call(
+    tok, top, edge = call(
         border_kernel,
+        [((TOKENS, D), bf16), ((TOP, D), bf16), ((EDGE, D), bf16)],
+        [pltpu.SemaphoreType.DMA],
+        [2],
+    )(tok)
+    g_merged, g_top, edge, corner = call(
+        border_pairs_kernel,
         [
-            ((TOKENS, D), bf16), ((PAIRS, 2 * D), bf16),
-            ((TOP, D), bf16), ((2 * PAIR_TOP, D), bf16),
+            ((PAIRS, 2 * D), bf16), ((2 * PAIR_TOP, D), bf16),
             ((EDGE + 2 * PAIR_SIDE, D), bf16), ((TURN + 2 * PAIR_CORNER, D), bf16),
         ],
-        [pltpu.SemaphoreType.DMA((2,))],
-        [2, 2],
-    )(tok, g_merged)
+        [pltpu.SemaphoreType.DMA],
+        [2, 0],
+    )(g_merged, edge)
     beside = fetch(top, edge, corner)
     g_lat = up(g_top)
     pair, band = pair_selector(), band_selector()

time: 80.6 us -> 80.4 us (level)
  no operation moved by 1% of the time
where the time goes in v8:
time: 80.4 us; the launch traced here: 80.1 us
  starting transfers between devices  30.9 us (38%)
  Pallas kernels  25.8 us (32%)
  waiting for transfers between devices  20.6 us (26%)
  local copies, waits for them, and re-layouts  1.95 us (2%)
  between operations  0.92 us (1%)
    ppermute x10, starting transfers between devices, send(): return lax.ppermute(block, ('lat', 'lon'), route)  21.2 us
    ppermute x10, waiting for transfers between devices, send(): return lax.ppermute(block, ('lat', 'lon'), route)  14.3 us
    ppermute x3, waiting for transfers between devices, swap(): lax.ppermute(block, ('lat', 'lon'), [(i, across(i, step)) for i in range(...  6.25 us
    pallas_call x1, Pallas kernels, chain(): call(outer_back_kernel, [((WIDTH, 3 * D), bf16), ((4, 32, 32, 128), bf16)...  4.82 us
    pallas_call x1, Pallas kernels, chain(): call(inner_kernel, [(h.shape, h.dtype) for h in held] + [((TOKENS - TOP,...  4.15 us
    all_to_all x1, starting transfers between devices, reduce_rest(): lax.all_to_all(sums, ('lat', 'lon'), 0, 0, axis_index_groups=rest, tiled=...  4.09 us
    pallas_call x1, Pallas kernels, chain(): call(outer_kernel, saved(REST) + [((TOKENS, D), bf16), ((TOKENS, D), bf16...  4.04 us
    ppermute x3, starting transfers between devices, swap(): lax.ppermute(block, ('lat', 'lon'), [(i, across(i, step)) for i in range(...  3.93 us
  transfers between devices with their start and end apart: 15, of which 4 were waited for; matrix products, arithmetic and copies ran while one was open for 0% of the time, Pallas kernels for 23%

profile of v8, /device:TPU:1, one launch (start us, length us, event | category | flops | bytes accessed | tf_op | source)
XLA Modules:
  0.0 80.1 jit_solution(17619248768417103696)
XLA Ops:
  0.6 1.1 %copy-done.5 = bf16[12,48,512]{2,1,0:T(8,128)(2,1)S(1)} copy-done((bf16[12,48,512]{2,1,0:T(8,128)(2,1)S(1)}, bf16[12,48,512]{2,1,0:T(8,128)(2,1)}, u32[]{:S(2)}) %copy-start.5) | copy-done | bytes 589848
  1.7 0.1 shard_map.175
  1.8 0.8 %copy-done.7 = bf16[6,24,1024]{2,1,0:T(8,128)(2,1)S(1)} copy-done((bf16[6,24,1024]{2,1,0:T(8,128)(2,1)S(1)}, bf16[6,24,1024]{2,1,0:T(8,128)(2,1)}, u32[]{:S(2)}) %copy-start.7) | copy-done | bytes 294936
  2.7 0.0 copy-start.10
  2.7 0.0 copy-start.11
  2.7 0.0 copy-start.12
  2.7 0.0 copy-start.13
  2.7 0.0 copy-start.14
  2.7 0.0 copy-start.15
  2.7 0.1 shard_map.177
  2.8 3.3 %collective-permute-start.1 = (bf16[192,512]{1,0:T(8,128)(2,1)S(1)}, bf16[192,512]{1,0:T(8,128)(2,1)S(1)}, u32[]{:S(2)}, u32[]{:S(2)}) collective-permute-start(bf16[192,512]{1,0:T(8,128)(2,1)S(1)} %get-tuple-element.70), channel_id=1, source_target_pairs={{0,15},{1,0},{2,1},{3,2},{4,3},{5,4},{6,5},{7,6},{8,7},{9,8},{10,9... | collective-permute-start | bytes 589832 | tf_op jit(solution)/shard_map/ppermute | solution.py:554
  6.2 6.5 %collective-permute-start = (bf16[144,512]{1,0:T(8,128)(2,1)S(1)}, bf16[144,512]{1,0:T(8,128)(2,1)S(1)}, u32[]{:S(2)}, u32[]{:S(2)}) collective-permute-start(bf16[144,512]{1,0:T(8,128)(2,1)S(1)} %get-tuple-element.68), channel_id=1, source_target_pairs={{0,240},{1,241},{2,242},{3,243},{4,244},{5,245},{6,246},{7,247},{8... | collective-permute-start | bytes 442376 | tf_op jit(solution)/shard_map/ppermute | solution.py:554
  12.6 3.8 %collective-permute-start.2 = (bf16[48,512]{1,0:T(8,128)(2,1)S(1)}, bf16[48,512]{1,0:T(8,128)(2,1)S(1)}, u32[]{:S(2)}, u32[]{:S(2)}) collective-permute-start(bf16[48,512]{1,0:T(8,128)(2,1)S(1)} %get-tuple-element.71), channel_id=1, source_target_pairs={{0,255},{1,240},{2,241},{3,242},{4,243},{5,244},{6,245},{7,246},{8... | collective-permute-start | bytes 147464 | tf_op jit(solution)/shard_map/ppermute | solution.py:554
  16.4 0.7 collective-permute-start.4
  17.2 4.1 %shard_map.176 = (f32[1,512]{1,0:T(1,128)S(1)}, bf16[320,336]{1,0:T(8,128)(2,1)S(1)}, bf16[512,1536]{1,0:T(8,128)(2,1)S(1)}, bf16[512,512]{1,0:T(8,128)(2,1)S(1)...) custom-call(bf16[576,512]{1,0:T(8,128)(2,1)S(1)} %get-tuple-element., ...), custom_call_target="tpu_custom_call" | custom-call | flops 1000000000 | bytes 2000000 | tf_op jit(solution)/shard_map/pallas_call | solution.py:481
  21.4 0.0 collective-permute-done.2.diag_ref
  21.4 0.0 collective-permute-done.lat_ref
  21.4 0.0 copy-start
  21.4 4.0 %shard_map.178 = (bf16[400,512]{1,0:T(8,128)(2,1)S(1)}, bf16[400,1536]{1,0:T(8,128)(2,1)S(1)}, bf16[400,512]{1,0:T(8,128)(2,1)S(1)}, f32[5,2,80,320]{3,2,1,0:T(8...) custom-call(bf16[576,512]{1,0:T(8,128)(2,1)S(1)} %get-tuple-element.66.tok_ref, ...), custom_call_target="tpu_custom_call" | custom-call | flops 1000000000 | bytes 2000000 | tf_op jit(solution)/shard_map/pallas_call | solution.py:489
  25.5 0.8 %collective-permute-start.3 = (bf16[48,512]{1,0:T(8,128)(2,1)S(1)}, bf16[48,512]{1,0:T(8,128)(2,1)S(1)}, u32[]{:S(2)}, u32[]{:S(2)}) collective-permute-start(bf16[48,512]{1,0:T(8,128)(2,1)S(1)} %get-tuple-element.80), channel_id=1, source_target_pairs={{0,16},{1,17},{2,18},{3,19},{4,20},{5,21},{6,22},{7,23},{8,24},{9,... | collective-permute-start | bytes 147464 | tf_op jit(solution)/shard_map/ppermute | solution.py:554
  26.3 0.0 collective-permute-done.4.lat_ref
  26.3 2.0 %shard_map.179 = (f32[4,144,512]{2,1,0:T(8,128)S(1)}, bf16[2048,1024]{1,0:T(8,128)(2,1)S(1)}) custom-call(bf16[144,1024]{1,0:T(8,128)(2,1)S(1)} %get-tuple-element.83.g_ref, bf16[48,512]{1,0:T(8,128)(2,1)S(1)} %collective-permute-done.4.lat_ref, bf16[192,512]{1,0:T(8,128)(2,1)S(1)} %collective-permute-done.1.lon_ref, ...), custom_call_target="tpu_custom_call" | custom-call | flops 1000000000 | bytes 2000000 | tf_op jit(solution)/shard_map/pallas_call | solution.py:495
  28.4 3.8 %collective-permute-done.3.row_ref = bf16[48,512]{1,0:T(8,128)(2,1)S(1)} collective-permute-done((bf16[48,512]{1,0:T(8,128)(2,1)S(1)}, bf16[48,512]{1,0:T(8,128)(2,1)S(1)}, u32[]{:S(2)}, u32[]{:S(2)}) %collective-permute-start.3) | collective-permute-done | bytes 49184 | tf_op jit(solution)/shard_map/ppermute | solution.py:554
  32.1 1.2 %shard_map.180 = (bf16[576,512]{1,0:T(8,128)(2,1)S(1)}, bf16[48,512]{1,0:T(8,128)(2,1)S(1)}, bf16[4,144,512]{2,1,0:T(8,128)(2,1)S(1)}) custom-call(bf16[576,512]{1,0:T(8,128)(2,1)S(1)} %get-tuple-element.79.summed_ref, bf16[48,512]{1,0:T(8,128)(2,1)S(1)} %collective-permute-done.3.row_ref, f32[4,1,512]{2,1,0:T(1,128)S(1)} %get-tuple-element.81.gain_ref, ...), custom_call_target="tpu_custom_call" | custom-call | flops 1000000000 | bytes 2000000 | tf_op jit(solution)/shard_map/pallas_call | solution.py:501
  33.4 0.9 %collective-permute-start.5 = (bf16[48,512]{1,0:T(8,128)(2,1)S(1)}, bf16[48,512]{1,0:T(8,128)(2,1)S(1)}, u32[]{:S(2)}, u32[]{:S(2)}) collective-permute-start(bf16[48,512]{1,0:T(8,128)(2,1)S(1)} %get-tuple-element.90), channel_id=1, source_target_pairs={{0,240},{1,241},{2,242},{3,243},{4,244},{5,245},{6,246},{7,247},{8... | collective-permute-start | bytes 147464 | tf_op jit(solution)/shard_map/ppermute | solution.py:554
  34.2 1.0 %shard_map.182 = (bf16[144,1024]{1,0:T(8,128)(2,1)S(1)}, bf16[48,512]{1,0:T(8,128)(2,1)S(1)}, bf16[80,512]{1,0:T(8,128)(2,1)S(1)}, bf16[16,512]{1,0:T(8,128)(2,1)S(1)}) custom-call(bf16[4,144,512]{2,1,0:T(8,128)(2,1)S(1)} %get-tuple-element.102.normed_ref, bf16[2048,1024]{1,0:T(8,128)(2,1)S(1)} %get-tuple-element.103.wmerge_ref, bf16[192,144]{1,0:T(8,128)(2,1)S(1)} %copy-done.3), custom_call_target="tpu_custom_call" | custom-call | flops 1000000000 | bytes 2000000 | tf_op jit(solution)/shard_map/pallas_call | solution.py:515
  35.2 3.1 %shard_map.181 = (bf16[320,512]{1,0:T(8,128)(2,1)S(1)}, bf16[320,1536]{1,0:T(8,128)(2,1)S(1)}, bf16[512,640]{1,0:T(8,128)(2,1)S(1)}, bf16[512,640]{1,0:T(8,128)(2,1)S(1)}) custom-call(bf16[576,512]{1,0:T(8,128)(2,1)S(1)} %get-tuple-element.89.dsum_ref, bf16[240,1536]{1,0:T(8,128)(2,1)S(1)} %get-tuple-element.91.qkv0_ref, ...), custom_call_target="tpu_custom_call" | custom-call | flops 1000000000 | bytes 2000000 | tf_op jit(solution)/shard_map/pallas_call | solution.py:510
  38.3 0.0 copy-start.2
  38.4 4.8 %shard_map.183 = (bf16[640,1536]{1,0:T(8,128)(2,1)S(1)}, bf16[4,32,32,128]{3,2,1,0:T(8,128)(2,1)S(1)}, bf16[4,32,32,128]{3,2,1,0:T(8,128)(2,1)S(1)}) custom-call(bf16[576,512]{1,0:T(8,128)(2,1)S(1)} %get-tuple-element.89.dsum_ref, bf16[48,512]{1,0:T(8,128)(2,1)S(1)} %collective-permute-done.5.row_ref, bf16[512,640]{1,0:T(8,128)(2,1)S(1)} %get-tuple-element.99.xst_ref, ...), custom_call_target="tpu_custom_call" | custom-call | flops 1000000000 | bytes 2000000 | tf_op jit(solution)/shard_map/pallas_call | solution.py:523
  43.2 1.7 %collective-permute-start.7 = (bf16[4,32,32,128]{3,2,1,0:T(8,128)(2,1)S(1)}, bf16[4,32,32,128]{3,2,1,0:T(8,128)(2,1)S(1)}, u32[]{:S(2)}, u32[]{:S(2)}) collective-permute-start(bf16[4,32,32,128]{3,2,1,0:T(8,128)(2,1)S(1)} %get-tuple-element.114), channel_id=1, source_target_pairs={{0,1},{1,0},{2,3},{3,2},{4,5},{5,4},{6,7},{7,6},{8,9},{9,8},{10,11... | collective-permute-start | bytes 3145736 | tf_op jit(solution)/shard_map/ppermute | solution.py:581
  44.9 2.5 %shard_map.184 = (bf16[432,512]{1,0:T(8,128)(2,1)S(1)}, bf16[144,512]{1,0:T(8,128)(2,1)S(1)}, bf16[176,512]{1,0:T(8,128)(2,1)S(1)}, bf16[48,512]{1,0:T(8,128)(2,1)S(1)}) custom-call(bf16[640,1536]{1,0:T(8,128)(2,1)S(1)} %get-tuple-element.107.dqkv_ref, bf16[512,1536]{1,0:T(8,128)(2,1)S(1)} %get-tuple-element.73.wqkv_ref, ...), custom_call_target="tpu_custom_call" | custom-call | flops 1000000000 | bytes 2000000 | tf_op jit(solution)/shard_map/pallas_call | solution.py:528
  47.4 0.2 shard_map.185
  47.7 0.1 collective-permute-start.10
  47.8 0.1 collective-permute-start.8
  47.9 3.7 %collective-permute-start.9 = (bf16[32,32,128]{2,1,0:T(8,128)(2,1)S(1)}, bf16[32,32,128]{2,1,0:T(8,128)(2,1)S(1)}, u32[]{:S(2)}, u32[]{:S(2)}) collective-permute-start(bf16[32,32,128]{2,1,0:T(8,128)(2,1)S(1)} %get-tuple-element.118), channel_id=1, source_target_pairs={{0,4},{1,129},{2,6},{3,131},{4,0},{5,133},{6,2},{7,135},{8,12},{9,... | collective-permute-start | bytes 786440 | tf_op jit(solution)/shard_map/ppermute | solution.py:578
  51.6 1.1 %collective-permute-start.11 = (bf16[48,512]{1,0:T(8,128)(2,1)S(1)}, bf16[48,512]{1,0:T(8,128)(2,1)S(1)}, u32[]{:S(2)}, u32[]{:S(2)}) collective-permute-start(bf16[48,512]{1,0:T(8,128)(2,1)S(1)} %get-tuple-element.120), channel_id=1, source_target_pairs={{0,16},{1,17},{2,18},{3,19},{4,20},{5,21},{6,22},{7,23},{8,24},{9,... | collective-permute-start | bytes 147464 | tf_op jit(solution)/shard_map/ppermute | solution.py:554
  52.8 1.7 %collective-permute-done.10.d_ref = bf16[32,32,128]{2,1,0:T(8,128)(2,1)S(1)} collective-permute-done((bf16[32,32,128]{2,1,0:T(8,128)(2,1)S(1)}, bf16[32,32,128]{2,1,0:T(8,128)(2,1)S(1)}, u32[]{:S(2)}, u32[]{:S(2)}) %collective-permute-start.10) | collective-permute-done | bytes 262176 | tf_op jit(solution)/shard_map/ppermute | solution.py:578
  54.5 0.0 collective-permute-done.8.b_ref
  54.5 4.5 %collective-permute-done.9.c_ref = bf16[32,32,128]{2,1,0:T(8,128)(2,1)S(1)} collective-permute-done((bf16[32,32,128]{2,1,0:T(8,128)(2,1)S(1)}, bf16[32,32,128]{2,1,0:T(8,128)(2,1)S(1)}, u32[]{:S(2)}, u32[]{:S(2)}) %collective-permute-start.9) | collective-permute-done | bytes 262176 | tf_op jit(solution)/shard_map/ppermute | solution.py:578
  59.0 0.8 %shard_map.186 = bf16[32,32,128]{2,1,0:T(8,128)(2,1)} custom-call(bf16[32,32,128]{2,1,0:T(8,128)(2,1)S(1)} %get-tuple-element.116.a_ref, bf16[32,32,128]{2,1,0:T(8,128)(2,1)S(1)} %collective-permute-done.8.b_ref, bf16[32,32,128]{2,1,0:T(8,128)(2,1)S(1)} %collective-permute-done.9.c_ref, bf16[32,32,128]{2,1,0:T(8,128)(2,1)S(1)} %collective-permute-done.10.d_ref), custom_call_target="tpu_custom_call" | custom-call | flops 1000000000 | bytes 2000000 | tf_op jit(solution)/shard_map/pallas_call | solution.py:584
  59.8 0.0 collective-permute-done.11.m_lat_ref
  59.8 4.1 %all-to-all-start = ((bf16[32,32,128]{2,1,0:T(8,128)(2,1)}), bf16[32,32,128]{2,1,0:T(8,128)(2,1)S(1)}, u32[]{:S(2)}, u32[]{:S(2)}) async-start(bf16[32,32,128]{2,1,0:T(8,128)(2,1)} %shard_map.186), calls=%async_computation | async-start | bytes 524288 | tf_op jit(solution)/shard_map/all_to_all | solution.py:587
  63.9 1.0 %collective-permute-start.12 = (bf16[176,512]{1,0:T(8,128)(2,1)S(1)}, bf16[176,512]{1,0:T(8,128)(2,1)S(1)}, u32[]{:S(2)}, u32[]{:S(2)}) collective-permute-start(bf16[176,512]{1,0:T(8,128)(2,1)S(1)} %get-tuple-element.123), channel_id=1, source_target_pairs={{0,1},{1,2},{2,3},{3,4},{4,5},{5,6},{6,7},{7,8},{8,9},{9,10},{10,1... | collective-permute-start | bytes 540680 | tf_op jit(solution)/shard_map/ppermute | solution.py:554
  64.9 1.5 %collective-permute-start.6 = (bf16[144,512]{1,0:T(8,128)(2,1)S(1)}, bf16[144,512]{1,0:T(8,128)(2,1)S(1)}, u32[]{:S(2)}, u32[]{:S(2)}) collective-permute-start(bf16[144,512]{1,0:T(8,128)(2,1)S(1)} %get-tuple-element.112), channel_id=1, source_target_pairs={{0,16},{1,17},{2,18},{3,19},{4,20},{5,21},{6,22},{7,23},{8,24},{9,... | collective-permute-start | bytes 442376 | tf_op jit(solution)/shard_map/ppermute | solution.py:554
  66.4 1.5 %collective-permute-start.13 = (bf16[48,512]{1,0:T(8,128)(2,1)S(1)}, bf16[48,512]{1,0:T(8,128)(2,1)S(1)}, u32[]{:S(2)}, u32[]{:S(2)}) collective-permute-start(bf16[48,512]{1,0:T(8,128)(2,1)S(1)} %get-tuple-element.125), channel_id=1, source_target_pairs={{0,17},{1,18},{2,19},{3,20},{4,21},{5,22},{6,23},{7,24},{8,25},{9,... | collective-permute-start | bytes 147464 | tf_op jit(solution)/shard_map/ppermute | solution.py:554
  67.9 10.6 %collective-permute-done.13.diag_ref = bf16[48,512]{1,0:T(8,128)(2,1)S(1)} collective-permute-done((bf16[48,512]{1,0:T(8,128)(2,1)S(1)}, bf16[48,512]{1,0:T(8,128)(2,1)S(1)}, u32[]{:S(2)}, u32[]{:S(2)}) %collective-permute-start.13) | collective-permute-done | bytes 49184 | tf_op jit(solution)/shard_map/ppermute | solution.py:554
  78.5 1.0 %shard_map.187 = (bf16[576,512]{1,0:T(8,128)(2,1)}, bf16[144,1024]{1,0:T(8,128)(2,1)}) custom-call(bf16[432,512]{1,0:T(8,128)(2,1)S(1)} %get-tuple-element.111.main_ref, bf16[144,512]{1,0:T(8,128)(2,1)S(1)} %collective-permute-done.6.lat_ref, bf16[176,512]{1,0:T(8,128)(2,1)S(1)} %collective-permute-done.12.lon_ref, ...), custom_call_target="tpu_custom_call" | custom-call | flops 1000000000 | bytes 2000000 | tf_op jit(solution)/shard_map/pallas_call | solution.py:538
  79.5 0.7 shard_map.188
  (28 shorter events, 0.1 us)
Async XLA Ops:
  0.6 1.1 %copy-start.5 = (bf16[12,48,512]{2,1,0:T(8,128)(2,1)S(1)}, bf16[12,48,512]{2,1,0:T(8,128)(2,1)}, u32[]{:S(2)}) copy-start(bf16[12,48,512]{2,1,0:T(8,128)(2,1)} %param.16) | copy-start | bytes 1769476
  1.7 1.0 %copy-start.7 = (bf16[6,24,1024]{2,1,0:T(8,128)(2,1)S(1)}, bf16[6,24,1024]{2,1,0:T(8,128)(2,1)}, u32[]{:S(2)}) copy-start(bf16[6,24,1024]{2,1,0:T(8,128)(2,1)} %param.22) | copy-start | bytes 884740
  2.7 14.5 %copy-start.4 = (bf16[512,1536]{1,0:T(8,128)(2,1)S(1)}, bf16[512,1536]{1,0:T(8,128)(2,1)}, u32[]{:S(2)}) copy-start(bf16[512,1536]{1,0:T(8,128)(2,1)} %refs_2_.1) | copy-start | bytes 4718596
  2.7 14.5 %copy-start.6 = (bf16[512,512]{1,0:T(8,128)(2,1)S(1)}, bf16[512,512]{1,0:T(8,128)(2,1)}, u32[]{:S(2)}) copy-start(bf16[512,512]{1,0:T(8,128)(2,1)} %refs_3_.1) | copy-start | bytes 1572868
  2.7 14.5 %copy-start.8 = (f32[2048]{0:T(1024)S(1)}, f32[2048]{0:T(1024)}, u32[]{:S(2)}) copy-start(f32[2048]{0:T(1024)} %param.20) | copy-start | bytes 24580
  2.7 14.5 %copy-start.9 = (f32[512]{0:T(512)S(1)}, f32[512]{0:T(512)}, u32[]{:S(2)}) copy-start(f32[512]{0:T(512)} %param.17) | copy-start | bytes 6148
  2.7 14.5 %copy-start.10 = (bf16[320,336]{1,0:T(8,128)(2,1)S(1)}, bf16[320,336]{1,0:T(8,128)(2,1)}, u32[]{:S(2)}) copy-start(bf16[320,336]{1,0:T(8,128)(2,1)} %constant.18.clone.refs_1_) | copy-start | bytes 645124
  2.7 14.5 %copy-start.11 = (bf16[288,336]{1,0:T(8,128)(2,1)S(1)}, bf16[288,336]{1,0:T(8,128)(2,1)}, u32[]{:S(2)}) copy-start(bf16[288,336]{1,0:T(8,128)(2,1)} %constant.19.clone.refs_5_) | copy-start | bytes 580612
  2.7 14.5 %copy-start.12 = (bf16[288,320]{1,0:T(8,128)(2,1)S(1)}, bf16[288,320]{1,0:T(8,128)(2,1)}, u32[]{:S(2)}) copy-start(bf16[288,320]{1,0:T(8,128)(2,1)} %constant.20.clone.refs_6_) | copy-start | bytes 552964
  2.7 14.5 %copy-start.13 = (bf16[192,192]{1,0:T(8,128)(2,1)S(1)}, bf16[192,192]{1,0:T(8,128)(2,1)}, u32[]{:S(2)}) copy-start(bf16[192,192]{1,0:T(8,128)(2,1)} %constant.21.clone.refs_7_) | copy-start | bytes 221188
  2.7 14.5 %copy-start.14 = (bf16[192,192]{1,0:T(8,128)(2,1)S(1)}, bf16[192,192]{1,0:T(8,128)(2,1)}, u32[]{:S(2)}) copy-start(bf16[192,192]{1,0:T(8,128)(2,1)} %constant.22.clone.refs_8_) | copy-start | bytes 221188
  2.7 14.5 %copy-start.15 = (bf16[144,192]{1,0:T(8,128)(2,1)S(1)}, bf16[144,192]{1,0:T(8,128)(2,1)}, u32[]{:S(2)}) copy-start(bf16[144,192]{1,0:T(8,128)(2,1)} %constant.23.clone.refs_9_) | copy-start | bytes 165892
  2.8 18.6 %collective-permute-start.1 = (bf16[192,512]{1,0:T(8,128)(2,1)S(1)}, bf16[192,512]{1,0:T(8,128)(2,1)S(1)}, u32[]{:S(2)}, u32[]{:S(2)}) collective-permute-start(bf16[192,512]{1,0:T(8,128)(2,1)S(1)} %get-tuple-element.70), channel_id=1, source_target_pairs={{0,15},{1,0},{2,1},{3,2},{4,3},{5,4},{6,5},{7,6},{8,7},{9,8},{10,9... | collective-permute-start | bytes 589832 | tf_op jit(solution)/shard_map/ppermute | solution.py:554
  6.2 15.3 %collective-permute-start = (bf16[144,512]{1,0:T(8,128)(2,1)S(1)}, bf16[144,512]{1,0:T(8,128)(2,1)S(1)}, u32[]{:S(2)}, u32[]{:S(2)}) collective-permute-start(bf16[144,512]{1,0:T(8,128)(2,1)S(1)} %get-tuple-element.68), channel_id=1, source_target_pairs={{0,240},{1,241},{2,242},{3,243},{4,244},{5,245},{6,246},{7,247},{8... | collective-permute-start | bytes 442376 | tf_op jit(solution)/shard_map/ppermute | solution.py:554
  12.6 8.8 %collective-permute-start.2 = (bf16[48,512]{1,0:T(8,128)(2,1)S(1)}, bf16[48,512]{1,0:T(8,128)(2,1)S(1)}, u32[]{:S(2)}, u32[]{:S(2)}) collective-permute-start(bf16[48,512]{1,0:T(8,128)(2,1)S(1)} %get-tuple-element.71), channel_id=1, source_target_pairs={{0,255},{1,240},{2,241},{3,242},{4,243},{5,244},{6,245},{7,246},{8... | collective-permute-start | bytes 147464 | tf_op jit(solution)/shard_map/ppermute | solution.py:554
  16.4 9.9 %collective-permute-start.4 = (bf16[48,512]{1,0:T(8,128)(2,1)S(1)}, bf16[48,512]{1,0:T(8,128)(2,1)S(1)}, u32[]{:S(2)}, u32[]{:S(2)}) collective-permute-start(bf16[48,512]{1,0:T(8,128)(2,1)S(1)} %get-tuple-element.84), channel_id=1, source_target_pairs={{0,240},{1,241},{2,242},{3,243},{4,244},{5,245},{6,246},{7,247},{8... | collective-permute-start | bytes 147464 | tf_op jit(solution)/shard_map/ppermute | solution.py:554
  21.4 4.9 %copy-start = (bf16[2048,1024]{1,0:T(8,128)(2,1)S(1)}, bf16[2048,1024]{1,0:T(8,128)(2,1)}, u32[]{:S(2)}) copy-start(bf16[2048,1024]{1,0:T(8,128)(2,1)} %wmerge_ref.1) | copy-start | bytes 12582916
  25.5 6.6 %collective-permute-start.3 = (bf16[48,512]{1,0:T(8,128)(2,1)S(1)}, bf16[48,512]{1,0:T(8,128)(2,1)S(1)}, u32[]{:S(2)}, u32[]{:S(2)}) collective-permute-start(bf16[48,512]{1,0:T(8,128)(2,1)S(1)} %get-tuple-element.80), channel_id=1, source_target_pairs={{0,16},{1,17},{2,18},{3,19},{4,20},{5,21},{6,22},{7,23},{8,24},{9,... | collective-permute-start | bytes 147464 | tf_op jit(solution)/shard_map/ppermute | solution.py:554
  32.1 2.1 %copy-start.3 = (bf16[192,144]{1,0:T(8,128)(2,1)S(1)}, bf16[192,144]{1,0:T(8,128)(2,1)}, u32[]{:S(2)}) copy-start(bf16[192,144]{1,0:T(8,128)(2,1)} %constant.26.clone.unshift_ref) | copy-start | bytes 165892
  33.4 5.0 %collective-permute-start.5 = (bf16[48,512]{1,0:T(8,128)(2,1)S(1)}, bf16[48,512]{1,0:T(8,128)(2,1)S(1)}, u32[]{:S(2)}, u32[]{:S(2)}) collective-permute-start(bf16[48,512]{1,0:T(8,128)(2,1)S(1)} %get-tuple-element.90), channel_id=1, source_target_pairs={{0,240},{1,241},{2,242},{3,243},{4,244},{5,245},{6,246},{7,247},{8... | collective-permute-start | bytes 147464 | tf_op jit(solution)/shard_map/ppermute | solution.py:554
  34.2 1.0 %copy-start.1 = (bf16[320,288]{1,0:T(8,128)(2,1)S(1)}, bf16[320,288]{1,0:T(8,128)(2,1)}, u32[]{:S(2)}) copy-start(bf16[320,288]{1,0:T(8,128)(2,1)} %constant.24.clone.pick_ref) | copy-start | bytes 552964
  38.3 6.6 %copy-start.2 = (bf16[336,288]{1,0:T(8,128)(2,1)S(1)}, bf16[336,288]{1,0:T(8,128)(2,1)}, u32[]{:S(2)}) copy-start(bf16[336,288]{1,0:T(8,128)(2,1)} %constant.25.clone.unshift_ref) | copy-start | bytes 580612
  43.2 4.2 %collective-permute-start.7 = (bf16[4,32,32,128]{3,2,1,0:T(8,128)(2,1)S(1)}, bf16[4,32,32,128]{3,2,1,0:T(8,128)(2,1)S(1)}, u32[]{:S(2)}, u32[]{:S(2)}) collective-permute-start(bf16[4,32,32,128]{3,2,1,0:T(8,128)(2,1)S(1)} %get-tuple-element.114), channel_id=1, source_target_pairs={{0,1},{1,0},{2,3},{3,2},{4,5},{5,4},{6,7},{7,6},{8,9},{9,8},{10,11... | collective-permute-start | bytes 3145736 | tf_op jit(solution)/shard_map/ppermute | solution.py:581
  47.7 6.8 %collective-permute-start.10 = (bf16[32,32,128]{2,1,0:T(8,128)(2,1)S(1)}, bf16[32,32,128]{2,1,0:T(8,128)(2,1)S(1)}, u32[]{:S(2)}, u32[]{:S(2)}) collective-permute-start(bf16[32,32,128]{2,1,0:T(8,128)(2,1)S(1)} %get-tuple-element.119), channel_id=1, source_target_pairs={{0,6},{1,137},{2,4},{3,139},{4,2},{5,141},{6,0},{7,143},{8,14},{9,... | collective-permute-start | bytes 786440 | tf_op jit(solution)/shard_map/ppermute | solution.py:578
  47.8 6.7 %collective-permute-start.8 = (bf16[32,32,128]{2,1,0:T(8,128)(2,1)S(1)}, bf16[32,32,128]{2,1,0:T(8,128)(2,1)S(1)}, u32[]{:S(2)}, u32[]{:S(2)}) collective-permute-start(bf16[32,32,128]{2,1,0:T(8,128)(2,1)S(1)} %get-tuple-element.117), channel_id=1, source_target_pairs={{0,2},{1,9},{2,0},{3,11},{4,6},{5,13},{6,4},{7,15},{8,10},{9,1},{1... | collective-permute-start | bytes 786440 | tf_op jit(solution)/shard_map/ppermute | solution.py:578
  47.9 11.1 %collective-permute-start.9 = (bf16[32,32,128]{2,1,0:T(8,128)(2,1)S(1)}, bf16[32,32,128]{2,1,0:T(8,128)(2,1)S(1)}, u32[]{:S(2)}, u32[]{:S(2)}) collective-permute-start(bf16[32,32,128]{2,1,0:T(8,128)(2,1)S(1)} %get-tuple-element.118), channel_id=1, source_target_pairs={{0,4},{1,129},{2,6},{3,131},{4,0},{5,133},{6,2},{7,135},{8,12},{9,... | collective-permute-start | bytes 786440 | tf_op jit(solution)/shard_map/ppermute | solution.py:578
  51.6 8.2 %collective-permute-start.11 = (bf16[48,512]{1,0:T(8,128)(2,1)S(1)}, bf16[48,512]{1,0:T(8,128)(2,1)S(1)}, u32[]{:S(2)}, u32[]{:S(2)}) collective-permute-start(bf16[48,512]{1,0:T(8,128)(2,1)S(1)} %get-tuple-element.120), channel_id=1, source_target_pairs={{0,16},{1,17},{2,18},{3,19},{4,20},{5,21},{6,22},{7,23},{8,24},{9,... | collective-permute-start | bytes 147464 | tf_op jit(solution)/shard_map/ppermute | solution.py:554
  59.8 19.6 %all-to-all-start = ((bf16[32,32,128]{2,1,0:T(8,128)(2,1)}), bf16[32,32,128]{2,1,0:T(8,128)(2,1)S(1)}, u32[]{:S(2)}, u32[]{:S(2)}) async-start(bf16[32,32,128]{2,1,0:T(8,128)(2,1)} %shard_map.186), calls=%async_computation | async-start | bytes 524288 | tf_op jit(solution)/shard_map/all_to_all | solution.py:587
  63.9 14.6 %collective-permute-start.12 = (bf16[176,512]{1,0:T(8,128)(2,1)S(1)}, bf16[176,512]{1,0:T(8,128)(2,1)S(1)}, u32[]{:S(2)}, u32[]{:S(2)}) collective-permute-start(bf16[176,512]{1,0:T(8,128)(2,1)S(1)} %get-tuple-element.123), channel_id=1, source_target_pairs={{0,1},{1,2},{2,3},{3,4},{4,5},{5,6},{6,7},{7,8},{8,9},{9,10},{10,1... | collective-permute-start | bytes 540680 | tf_op jit(solution)/shard_map/ppermute | solution.py:554
  64.9 13.6 %collective-permute-start.6 = (bf16[144,512]{1,0:T(8,128)(2,1)S(1)}, bf16[144,512]{1,0:T(8,128)(2,1)S(1)}, u32[]{:S(2)}, u32[]{:S(2)}) collective-permute-start(bf16[144,512]{1,0:T(8,128)(2,1)S(1)} %get-tuple-element.112), channel_id=1, source_target_pairs={{0,16},{1,17},{2,18},{3,19},{4,20},{5,21},{6,22},{7,23},{8,24},{9,... | collective-permute-start | bytes 442376 | tf_op jit(solution)/shard_map/ppermute | solution.py:554
  66.4 12.1 %collective-permute-start.13 = (bf16[48,512]{1,0:T(8,128)(2,1)S(1)}, bf16[48,512]{1,0:T(8,128)(2,1)S(1)}, u32[]{:S(2)}, u32[]{:S(2)}) collective-permute-start(bf16[48,512]{1,0:T(8,128)(2,1)S(1)} %get-tuple-element.125), channel_id=1, source_target_pairs={{0,17},{1,18},{2,19},{3,20},{4,21},{5,22},{6,23},{7,24},{8,25},{9,... | collective-permute-start | bytes 147464 | tf_op jit(solution)/shard_map/ppermute | solution.py:554

commit v9 on v7

--- a/solution.py
+++ b/solution.py
@@ -245,10 +245,13 @@
 
 
 def cotangent_kernel(
-    g_ref, lat_ref, lon_ref, diag_ref, gain_ref, shift_ref, wmerge_ref, out_ref, weights_ref, sem
+    g_ref, lat_ref, lon_ref, diag_ref, gain_ref, shift_ref, xs0_ref, xs_ref, mixed0_ref, mixed_ref, wmerge_ref,
+    out_ref, weights_ref, xst_ref, mixt_ref, sem
 ):
     copy = pltpu.make_async_copy(wmerge_ref, weights_ref, sem)
     copy.start()
+    xst_ref[...] = jnp.concatenate([xs0_ref[...], xs_ref[...]], axis=0).T
+    mixt_ref[...] = jnp.concatenate([mixed0_ref[...], mixed_ref[...]], axis=0).T
     parts = []
     for half in range(2):
         lat = lat_ref[...].astype(f32)[half * PAIR_TOP : (half + 1) * PAIR_TOP]
@@ -312,12 +315,10 @@
 
 
 def inner_back_kernel(
-    dsum_ref, qkv0_ref, probs0_ref, qkv_ref, probs_ref, wproj_ref, pick_ref, xs0_ref, xs_ref, mixed0_ref, mixed_ref,
-    up_ref, dqkv_ref, xst_ref, mixt_ref,
+    dsum_ref, qkv0_ref, probs0_ref, qkv_ref, probs_ref, wproj_ref, pick_ref,
+    up_ref, dqkv_ref,
     dmix_ref,
 ):
-    xst_ref[...] = jnp.concatenate([xs0_ref[...], xs_ref[...]], axis=0).T
-    mixt_ref[...] = jnp.concatenate([mixed0_ref[...], mixed_ref[...]], axis=0).T
     up_ref[...] = dot(pick_ref[...], dsum_ref[COLS : COLS + BAND_CELLS]).astype(bf16)
     dmix_ref[...] = dot_nt(up_ref[...], wproj_ref[...]).astype(bf16)
     windows = [(qkv0_ref, probs0_ref, win) for win in range(LOCAL)] + [(qkv_ref, probs_ref, 0)]
@@ -485,12 +486,12 @@
         [((WIDTH, D), bf16)],
     )(tok, cells, *beside, gain, w_qkv, w_proj, pick, shift, cells_pick, att0)
     behind = down(row)
-    cots, w_merge = call(
+    cots, w_merge, xst, mixt = call(
         cotangent_kernel,
-        [((4, PAIRS, D), f32), ((4 * D, 2 * D), bf16)],
+        [((4, PAIRS, D), f32), ((4 * D, 2 * D), bf16), ((D, WIDTH), bf16), ((D, WIDTH), bf16)],
         [pltpu.SemaphoreType.DMA],
-        [0] * 6 + [1],
-    )(after(g_merged, row), g_lat, *beside[1:], gain_merge, pair_shift, w_merge)
+        [0] * 10 + [1],
+    )(after(g_merged, row), g_lat, *beside[1:], gain_merge, pair_shift, xs0, xs1, mixed0, mixed1, w_merge)
     d_summed, row, merge_normed = call(
         pair_kernel,
         [((TOKENS, D), bf16), ((COLS, D), bf16), ((4, PAIRS, D), bf16)],
@@ -500,11 +501,9 @@
     band = jnp.asarray(band_selector(), bf16)
     unshift = jnp.asarray(shift_selector(WIN_LAT, COLS, SHIFT_LON).T, bf16)
     pair_unshift = jnp.asarray(shift_selector(PAIR_ROWS, PAIR_COLS, SHIFT_LON // 2).T, bf16)
-    up0, dqkv0, xst, mixt = call(
-        inner_back_kernel,
-        [((BAND, D), bf16), ((BAND, 3 * D), bf16), ((D, WIDTH), bf16), ((D, WIDTH), bf16)],
-        [((BAND, D), bf16)],
-    )(d_summed, qkv0, probs0, qkv1, probs1, w_proj, band, xs0, xs1, mixed0, mixed1)
+    up0, dqkv0 = call(
+        inner_back_kernel, [((BAND, D), bf16), ((BAND, 3 * D), bf16)], [((BAND, D), bf16)]
+    )(d_summed, qkv0, probs0, qkv1, probs1, w_proj, band)
     m_main, m_lat, m_lon, m_diag = call(
         merge_kernel,
         [

time: 80.6 us -> 81.3 us (level)
  starting transfers between devices: 30.9 us -> 31.8 us
  transfers between devices with their start and end apart: 15 -> 15, of which waited for: 4 -> 5; matrix products, arithmetic and copies ran while one was open for 0% -> 0% of each run, Pallas kernels for 23% -> 23%
where the time goes in v9:
time: 81.3 us; the launch traced here: 80.6 us
  starting transfers between devices  31.8 us (39%)
  Pallas kernels  25.9 us (32%)
  waiting for transfers between devices  19.9 us (24%)
  local copies, waits for them, and re-layouts  2.1 us (3%)
  between operations  0.91 us (1%)
    ppermute x10, starting transfers between devices, send(): return lax.ppermute(block, ('lat', 'lon'), route)  21.4 us
    ppermute x10, waiting for transfers between devices, send(): return lax.ppermute(block, ('lat', 'lon'), route)  13.8 us
    ppermute x3, waiting for transfers between devices, swap(): lax.ppermute(block, ('lat', 'lon'), [(i, across(i, step)) for i in range(...  6.06 us
    all_to_all x1, starting transfers between devices, reduce_rest(): lax.all_to_all(sums, ('lat', 'lon'), 0, 0, axis_index_groups=rest, tiled=...  4.87 us
    pallas_call x1, Pallas kernels, chain(): call(outer_back_kernel, [((WIDTH, 3 * D), bf16), ((4, 32, 32, 128), bf16)...  4.83 us
    pallas_call x1, Pallas kernels, chain(): call(inner_kernel, [(h.shape, h.dtype) for h in held] + [((TOKENS - TOP,...  4.15 us
    pallas_call x1, Pallas kernels, chain(): call(outer_kernel, saved(REST) + [((TOKENS, D), bf16), ((TOKENS, D), bf16...  4.04 us
    ppermute x3, starting transfers between devices, swap(): lax.ppermute(block, ('lat', 'lon'), [(i, across(i, step)) for i in range(...  3.94 us
  transfers between devices with their start and end apart: 15, of which 5 were waited for; matrix products, arithmetic and copies ran while one was open for 0% of the time, Pallas kernels for 23%

profile of v9, /device:TPU:1, one launch (start us, length us, event | category | flops | bytes accessed | tf_op | source)
XLA Modules:
  0.0 80.6 jit_solution(9310006883122948600)
XLA Ops:
  0.6 1.1 %copy-done.5 = bf16[12,48,512]{2,1,0:T(8,128)(2,1)S(1)} copy-done((bf16[12,48,512]{2,1,0:T(8,128)(2,1)S(1)}, bf16[12,48,512]{2,1,0:T(8,128)(2,1)}, u32[]{:S(2)}) %copy-start.5) | copy-done | bytes 589848
  1.7 1.0 %copy-done.7 = bf16[6,24,1024]{2,1,0:T(8,128)(2,1)S(1)} copy-done((bf16[6,24,1024]{2,1,0:T(8,128)(2,1)S(1)}, bf16[6,24,1024]{2,1,0:T(8,128)(2,1)}, u32[]{:S(2)}) %copy-start.7) | copy-done | bytes 294936
  2.7 0.0 copy-start.10
  2.7 0.0 copy-start.11
  2.7 0.0 copy-start.12
  2.7 0.0 copy-start.13
  2.7 0.0 copy-start.14
  2.7 0.0 copy-start.15
  2.7 0.2 shard_map.175
  3.0 3.3 %collective-permute-start.1 = (bf16[192,512]{1,0:T(8,128)(2,1)S(1)}, bf16[192,512]{1,0:T(8,128)(2,1)S(1)}, u32[]{:S(2)}, u32[]{:S(2)}) collective-permute-start(bf16[192,512]{1,0:T(8,128)(2,1)S(1)} %get-tuple-element.68), channel_id=1, source_target_pairs={{0,15},{1,0},{2,1},{3,2},{4,3},{5,4},{6,5},{7,6},{8,7},{9,8},{10,9... | collective-permute-start | bytes 589832 | tf_op jit(solution)/shard_map/ppermute | solution.py:546
  6.3 6.5 %collective-permute-start = (bf16[144,512]{1,0:T(8,128)(2,1)S(1)}, bf16[144,512]{1,0:T(8,128)(2,1)S(1)}, u32[]{:S(2)}, u32[]{:S(2)}) collective-permute-start(bf16[144,512]{1,0:T(8,128)(2,1)S(1)} %get-tuple-element.67), channel_id=1, source_target_pairs={{0,240},{1,241},{2,242},{3,243},{4,244},{5,245},{6,246},{7,247},{8... | collective-permute-start | bytes 442376 | tf_op jit(solution)/shard_map/ppermute | solution.py:546
  12.8 3.8 %collective-permute-start.2 = (bf16[48,512]{1,0:T(8,128)(2,1)S(1)}, bf16[48,512]{1,0:T(8,128)(2,1)S(1)}, u32[]{:S(2)}, u32[]{:S(2)}) collective-permute-start(bf16[48,512]{1,0:T(8,128)(2,1)S(1)} %get-tuple-element.69), channel_id=1, source_target_pairs={{0,255},{1,240},{2,241},{3,242},{4,243},{5,244},{6,245},{7,246},{8... | collective-permute-start | bytes 147464 | tf_op jit(solution)/shard_map/ppermute | solution.py:546
  16.6 0.7 collective-permute-start.4
  17.4 4.1 %shard_map.176 = (f32[1,512]{1,0:T(1,128)S(1)}, bf16[320,336]{1,0:T(8,128)(2,1)S(1)}, bf16[512,1536]{1,0:T(8,128)(2,1)S(1)}, bf16[512,512]{1,0:T(8,128)(2,1)S(1)...) custom-call(bf16[576,512]{1,0:T(8,128)(2,1)S(1)} %get-tuple-element., ...), custom_call_target="tpu_custom_call" | custom-call | flops 1000000000 | bytes 2000000 | tf_op jit(solution)/shard_map/pallas_call | solution.py:475
  21.6 0.0 collective-permute-done.lat_ref
  21.6 0.0 collective-permute-done.1.lon_ref
  21.6 0.0 copy-start
  21.6 4.0 %shard_map.177 = (bf16[400,512]{1,0:T(8,128)(2,1)S(1)}, bf16[400,1536]{1,0:T(8,128)(2,1)S(1)}, bf16[400,512]{1,0:T(8,128)(2,1)S(1)}, f32[5,2,80,320]{3,2,1,0:T(8...) custom-call(bf16[576,512]{1,0:T(8,128)(2,1)S(1)} %get-tuple-element.65.tok_ref, ...), custom_call_target="tpu_custom_call" | custom-call | flops 1000000000 | bytes 2000000 | tf_op jit(solution)/shard_map/pallas_call | solution.py:483
  25.6 0.8 %collective-permute-start.3 = (bf16[48,512]{1,0:T(8,128)(2,1)S(1)}, bf16[48,512]{1,0:T(8,128)(2,1)S(1)}, u32[]{:S(2)}, u32[]{:S(2)}) collective-permute-start(bf16[48,512]{1,0:T(8,128)(2,1)S(1)} %get-tuple-element.78), channel_id=1, source_target_pairs={{0,16},{1,17},{2,18},{3,19},{4,20},{5,21},{6,22},{7,23},{8,24},{9,... | collective-permute-start | bytes 147464 | tf_op jit(solution)/shard_map/ppermute | solution.py:546
  26.5 0.0 collective-permute-done.4.lat_ref
  26.5 2.2 %shard_map.178 = (f32[4,144,512]{2,1,0:T(8,128)S(1)}, bf16[2048,1024]{1,0:T(8,128)(2,1)S(1)}, bf16[512,640]{1,0:T(8,128)(2,1)S(1)}, bf16[512,640]{1,0:T(8,128)(2,1)S(1)}) custom-call(bf16[144,1024]{1,0:T(8,128)(2,1)S(1)} %get-tuple-element.81.g_ref, bf16[48,512]{1,0:T(8,128)(2,1)S(1)} %collective-permute-done.4.lat_ref, ...), custom_call_target="tpu_custom_call" | custom-call | flops 1000000000 | bytes 2000000 | tf_op jit(solution)/shard_map/pallas_call | solution.py:489
  28.7 3.6 %collective-permute-done.3.row_ref = bf16[48,512]{1,0:T(8,128)(2,1)S(1)} collective-permute-done((bf16[48,512]{1,0:T(8,128)(2,1)S(1)}, bf16[48,512]{1,0:T(8,128)(2,1)S(1)}, u32[]{:S(2)}, u32[]{:S(2)}) %collective-permute-start.3) | collective-permute-done | bytes 49184 | tf_op jit(solution)/shard_map/ppermute | solution.py:546
  32.3 1.2 %shard_map.179 = (bf16[576,512]{1,0:T(8,128)(2,1)S(1)}, bf16[48,512]{1,0:T(8,128)(2,1)S(1)}, bf16[4,144,512]{2,1,0:T(8,128)(2,1)S(1)}) custom-call(bf16[576,512]{1,0:T(8,128)(2,1)S(1)} %get-tuple-element.77.summed_ref, bf16[48,512]{1,0:T(8,128)(2,1)S(1)} %collective-permute-done.3.row_ref, f32[4,1,512]{2,1,0:T(1,128)S(1)} %get-tuple-element.79.gain_ref, ...), custom_call_target="tpu_custom_call" | custom-call | flops 1000000000 | bytes 2000000 | tf_op jit(solution)/shard_map/pallas_call | solution.py:495
  33.5 1.1 %collective-permute-start.5 = (bf16[48,512]{1,0:T(8,128)(2,1)S(1)}, bf16[48,512]{1,0:T(8,128)(2,1)S(1)}, u32[]{:S(2)}, u32[]{:S(2)}) collective-permute-start(bf16[48,512]{1,0:T(8,128)(2,1)S(1)} %get-tuple-element.92), channel_id=1, source_target_pairs={{0,240},{1,241},{2,242},{3,243},{4,244},{5,245},{6,246},{7,247},{8... | collective-permute-start | bytes 147464 | tf_op jit(solution)/shard_map/ppermute | solution.py:546
  34.6 1.0 %shard_map.181 = (bf16[144,1024]{1,0:T(8,128)(2,1)S(1)}, bf16[48,512]{1,0:T(8,128)(2,1)S(1)}, bf16[80,512]{1,0:T(8,128)(2,1)S(1)}, bf16[16,512]{1,0:T(8,128)(2,1)S(1)}) custom-call(bf16[4,144,512]{2,1,0:T(8,128)(2,1)S(1)} %get-tuple-element.100.normed_ref, bf16[2048,1024]{1,0:T(8,128)(2,1)S(1)} %get-tuple-element.101.wmerge_ref, bf16[192,144]{1,0:T(8,128)(2,1)S(1)} %copy-done.3), custom_call_target="tpu_custom_call" | custom-call | flops 1000000000 | bytes 2000000 | tf_op jit(solution)/shard_map/pallas_call | solution.py:507
  35.6 0.0 copy-done.1
  35.6 3.1 %shard_map.180 = (bf16[320,512]{1,0:T(8,128)(2,1)S(1)}, bf16[320,1536]{1,0:T(8,128)(2,1)S(1)}) custom-call(bf16[576,512]{1,0:T(8,128)(2,1)S(1)} %get-tuple-element.91.dsum_ref, bf16[240,1536]{1,0:T(8,128)(2,1)S(1)} %get-tuple-element.95.qkv0_ref, f32[3,2,80,320]{3,2,1,0:T(8,128)S(1)} %get-tuple-element.96.probs0_ref, ...), custom_call_target="tpu_custom_call" | custom-call | flops 1000000000 | bytes 2000000 | tf_op jit(solution)/shard_map/pallas_call | solution.py:504
  38.6 0.0 collective-permute-done.5.row_ref
  38.6 0.0 copy-start.2
  38.7 4.8 %shard_map.182 = (bf16[640,1536]{1,0:T(8,128)(2,1)S(1)}, bf16[4,32,32,128]{3,2,1,0:T(8,128)(2,1)S(1)}, bf16[4,32,32,128]{3,2,1,0:T(8,128)(2,1)S(1)}) custom-call(bf16[576,512]{1,0:T(8,128)(2,1)S(1)} %get-tuple-element.91.dsum_ref, bf16[48,512]{1,0:T(8,128)(2,1)S(1)} %collective-permute-done.5.row_ref, bf16[512,640]{1,0:T(8,128)(2,1)S(1)} %get-tuple-element.93.xst_ref, ...), custom_call_target="tpu_custom_call" | custom-call | flops 1000000000 | bytes 2000000 | tf_op jit(solution)/shard_map/pallas_call | solution.py:515
  43.5 1.5 %collective-permute-start.7 = (bf16[4,32,32,128]{3,2,1,0:T(8,128)(2,1)S(1)}, bf16[4,32,32,128]{3,2,1,0:T(8,128)(2,1)S(1)}, u32[]{:S(2)}, u32[]{:S(2)}) collective-permute-start(bf16[4,32,32,128]{3,2,1,0:T(8,128)(2,1)S(1)} %get-tuple-element.112), channel_id=1, source_target_pairs={{0,1},{1,0},{2,3},{3,2},{4,5},{5,4},{6,7},{7,6},{8,9},{9,8},{10,11... | collective-permute-start | bytes 3145736 | tf_op jit(solution)/shard_map/ppermute | solution.py:573
  45.0 2.5 %shard_map.183 = (bf16[432,512]{1,0:T(8,128)(2,1)S(1)}, bf16[144,512]{1,0:T(8,128)(2,1)S(1)}, bf16[176,512]{1,0:T(8,128)(2,1)S(1)}, bf16[48,512]{1,0:T(8,128)(2,1)S(1)}) custom-call(bf16[640,1536]{1,0:T(8,128)(2,1)S(1)} %get-tuple-element.105.dqkv_ref, bf16[512,1536]{1,0:T(8,128)(2,1)S(1)} %get-tuple-element.71.wqkv_ref, ...), custom_call_target="tpu_custom_call" | custom-call | flops 1000000000 | bytes 2000000 | tf_op jit(solution)/shard_map/pallas_call | solution.py:520
  47.5 0.2 shard_map.184
  47.8 0.1 collective-permute-start.8
  47.9 0.9 %collective-permute-start.9 = (bf16[32,32,128]{2,1,0:T(8,128)(2,1)S(1)}, bf16[32,32,128]{2,1,0:T(8,128)(2,1)S(1)}, u32[]{:S(2)}, u32[]{:S(2)}) collective-permute-start(bf16[32,32,128]{2,1,0:T(8,128)(2,1)S(1)} %get-tuple-element.116), channel_id=1, source_target_pairs={{0,4},{1,129},{2,6},{3,131},{4,0},{5,133},{6,2},{7,135},{8,12},{9,... | collective-permute-start | bytes 786440 | tf_op jit(solution)/shard_map/ppermute | solution.py:570
  48.8 3.0 %collective-permute-start.10 = (bf16[32,32,128]{2,1,0:T(8,128)(2,1)S(1)}, bf16[32,32,128]{2,1,0:T(8,128)(2,1)S(1)}, u32[]{:S(2)}, u32[]{:S(2)}) collective-permute-start(bf16[32,32,128]{2,1,0:T(8,128)(2,1)S(1)} %get-tuple-element.117), channel_id=1, source_target_pairs={{0,6},{1,137},{2,4},{3,139},{4,2},{5,141},{6,0},{7,143},{8,14},{9,... | collective-permute-start | bytes 786440 | tf_op jit(solution)/shard_map/ppermute | solution.py:570
  51.7 1.2 %collective-permute-start.11 = (bf16[48,512]{1,0:T(8,128)(2,1)S(1)}, bf16[48,512]{1,0:T(8,128)(2,1)S(1)}, u32[]{:S(2)}, u32[]{:S(2)}) collective-permute-start(bf16[48,512]{1,0:T(8,128)(2,1)S(1)} %get-tuple-element.118), channel_id=1, source_target_pairs={{0,16},{1,17},{2,18},{3,19},{4,20},{5,21},{6,22},{7,23},{8,24},{9,... | collective-permute-start | bytes 147464 | tf_op jit(solution)/shard_map/ppermute | solution.py:546
  52.9 0.5 collective-permute-done.8.b_ref
  53.4 2.3 %collective-permute-done.9.c_ref = bf16[32,32,128]{2,1,0:T(8,128)(2,1)S(1)} collective-permute-done((bf16[32,32,128]{2,1,0:T(8,128)(2,1)S(1)}, bf16[32,32,128]{2,1,0:T(8,128)(2,1)S(1)}, u32[]{:S(2)}, u32[]{:S(2)}) %collective-permute-start.9) | collective-permute-done | bytes 262176 | tf_op jit(solution)/shard_map/ppermute | solution.py:570
  55.7 3.3 %collective-permute-done.10.d_ref = bf16[32,32,128]{2,1,0:T(8,128)(2,1)S(1)} collective-permute-done((bf16[32,32,128]{2,1,0:T(8,128)(2,1)S(1)}, bf16[32,32,128]{2,1,0:T(8,128)(2,1)S(1)}, u32[]{:S(2)}, u32[]{:S(2)}) %collective-permute-start.10) | collective-permute-done | bytes 262176 | tf_op jit(solution)/shard_map/ppermute | solution.py:570
  58.9 0.8 %shard_map.185 = bf16[32,32,128]{2,1,0:T(8,128)(2,1)} custom-call(bf16[32,32,128]{2,1,0:T(8,128)(2,1)S(1)} %get-tuple-element.114.a_ref, bf16[32,32,128]{2,1,0:T(8,128)(2,1)S(1)} %collective-permute-done.8.b_ref, bf16[32,32,128]{2,1,0:T(8,128)(2,1)S(1)} %collective-permute-done.9.c_ref, bf16[32,32,128]{2,1,0:T(8,128)(2,1)S(1)} %collective-permute-done.10.d_ref), custom_call_target="tpu_custom_call" | custom-call | flops 1000000000 | bytes 2000000 | tf_op jit(solution)/shard_map/pallas_call | solution.py:576
  59.8 4.9 %all-to-all-start = ((bf16[32,32,128]{2,1,0:T(8,128)(2,1)}), bf16[32,32,128]{2,1,0:T(8,128)(2,1)S(1)}, u32[]{:S(2)}, u32[]{:S(2)}) async-start(bf16[32,32,128]{2,1,0:T(8,128)(2,1)} %shard_map.185), calls=%async_computation | async-start | bytes 524288 | tf_op jit(solution)/shard_map/all_to_all | solution.py:579
  64.7 0.4 collective-permute-start.12
  65.0 1.5 %collective-permute-start.6 = (bf16[144,512]{1,0:T(8,128)(2,1)S(1)}, bf16[144,512]{1,0:T(8,128)(2,1)S(1)}, u32[]{:S(2)}, u32[]{:S(2)}) collective-permute-start(bf16[144,512]{1,0:T(8,128)(2,1)S(1)} %get-tuple-element.110), channel_id=1, source_target_pairs={{0,16},{1,17},{2,18},{3,19},{4,20},{5,21},{6,22},{7,23},{8,24},{9,... | collective-permute-start | bytes 442376 | tf_op jit(solution)/shard_map/ppermute | solution.py:546
  66.6 2.2 %collective-permute-start.13 = (bf16[48,512]{1,0:T(8,128)(2,1)S(1)}, bf16[48,512]{1,0:T(8,128)(2,1)S(1)}, u32[]{:S(2)}, u32[]{:S(2)}) collective-permute-start(bf16[48,512]{1,0:T(8,128)(2,1)S(1)} %get-tuple-element.123), channel_id=1, source_target_pairs={{0,17},{1,18},{2,19},{3,20},{4,21},{5,22},{6,23},{7,24},{8,25},{9,... | collective-permute-start | bytes 147464 | tf_op jit(solution)/shard_map/ppermute | solution.py:546
  68.7 10.3 %collective-permute-done.13.diag_ref = bf16[48,512]{1,0:T(8,128)(2,1)S(1)} collective-permute-done((bf16[48,512]{1,0:T(8,128)(2,1)S(1)}, bf16[48,512]{1,0:T(8,128)(2,1)S(1)}, u32[]{:S(2)}, u32[]{:S(2)}) %collective-permute-start.13) | collective-permute-done | bytes 49184 | tf_op jit(solution)/shard_map/ppermute | solution.py:546
  79.0 1.0 %shard_map.186 = (bf16[576,512]{1,0:T(8,128)(2,1)}, bf16[144,1024]{1,0:T(8,128)(2,1)}) custom-call(bf16[432,512]{1,0:T(8,128)(2,1)S(1)} %get-tuple-element.109.main_ref, bf16[144,512]{1,0:T(8,128)(2,1)S(1)} %collective-permute-done.6.lat_ref, bf16[176,512]{1,0:T(8,128)(2,1)S(1)} %collective-permute-done.12.lon_ref, ...), custom_call_target="tpu_custom_call" | custom-call | flops 1000000000 | bytes 2000000 | tf_op jit(solution)/shard_map/pallas_call | solution.py:530
  80.0 0.7 shard_map.187
  (27 shorter events, 0.1 us)
Async XLA Ops:
  0.6 1.1 %copy-start.5 = (bf16[12,48,512]{2,1,0:T(8,128)(2,1)S(1)}, bf16[12,48,512]{2,1,0:T(8,128)(2,1)}, u32[]{:S(2)}) copy-start(bf16[12,48,512]{2,1,0:T(8,128)(2,1)} %param.16) | copy-start | bytes 1769476
  1.7 1.0 %copy-start.7 = (bf16[6,24,1024]{2,1,0:T(8,128)(2,1)S(1)}, bf16[6,24,1024]{2,1,0:T(8,128)(2,1)}, u32[]{:S(2)}) copy-start(bf16[6,24,1024]{2,1,0:T(8,128)(2,1)} %param.22) | copy-start | bytes 884740
  2.7 14.7 %copy-start.4 = (bf16[512,1536]{1,0:T(8,128)(2,1)S(1)}, bf16[512,1536]{1,0:T(8,128)(2,1)}, u32[]{:S(2)}) copy-start(bf16[512,1536]{1,0:T(8,128)(2,1)} %refs_2_.1) | copy-start | bytes 4718596
  2.7 14.7 %copy-start.6 = (bf16[512,512]{1,0:T(8,128)(2,1)S(1)}, bf16[512,512]{1,0:T(8,128)(2,1)}, u32[]{:S(2)}) copy-start(bf16[512,512]{1,0:T(8,128)(2,1)} %refs_3_.1) | copy-start | bytes 1572868
  2.7 14.7 %copy-start.8 = (f32[2048]{0:T(1024)S(1)}, f32[2048]{0:T(1024)}, u32[]{:S(2)}) copy-start(f32[2048]{0:T(1024)} %param.20) | copy-start | bytes 24580
  2.7 14.7 %copy-start.9 = (f32[512]{0:T(512)S(1)}, f32[512]{0:T(512)}, u32[]{:S(2)}) copy-start(f32[512]{0:T(512)} %param.17) | copy-start | bytes 6148
  2.7 14.7 %copy-start.10 = (bf16[320,336]{1,0:T(8,128)(2,1)S(1)}, bf16[320,336]{1,0:T(8,128)(2,1)}, u32[]{:S(2)}) copy-start(bf16[320,336]{1,0:T(8,128)(2,1)} %constant.18.clone.refs_1_) | copy-start | bytes 645124
  2.7 14.7 %copy-start.11 = (bf16[288,320]{1,0:T(8,128)(2,1)S(1)}, bf16[288,320]{1,0:T(8,128)(2,1)}, u32[]{:S(2)}) copy-start(bf16[288,320]{1,0:T(8,128)(2,1)} %constant.20.clone.refs_6_) | copy-start | bytes 552964
  2.7 14.7 %copy-start.12 = (bf16[288,336]{1,0:T(8,128)(2,1)S(1)}, bf16[288,336]{1,0:T(8,128)(2,1)}, u32[]{:S(2)}) copy-start(bf16[288,336]{1,0:T(8,128)(2,1)} %constant.19.clone.refs_5_) | copy-start | bytes 580612
  2.7 14.7 %copy-start.13 = (bf16[192,192]{1,0:T(8,128)(2,1)S(1)}, bf16[192,192]{1,0:T(8,128)(2,1)}, u32[]{:S(2)}) copy-start(bf16[192,192]{1,0:T(8,128)(2,1)} %constant.22.clone.refs_8_) | copy-start | bytes 221188
  2.7 14.6 %copy-start.14 = (bf16[192,192]{1,0:T(8,128)(2,1)S(1)}, bf16[192,192]{1,0:T(8,128)(2,1)}, u32[]{:S(2)}) copy-start(bf16[192,192]{1,0:T(8,128)(2,1)} %constant.21.clone.refs_7_) | copy-start | bytes 221188
  2.7 14.6 %copy-start.15 = (bf16[144,192]{1,0:T(8,128)(2,1)S(1)}, bf16[144,192]{1,0:T(8,128)(2,1)}, u32[]{:S(2)}) copy-start(bf16[144,192]{1,0:T(8,128)(2,1)} %constant.23.clone.refs_9_) | copy-start | bytes 165892
  3.0 18.6 %collective-permute-start.1 = (bf16[192,512]{1,0:T(8,128)(2,1)S(1)}, bf16[192,512]{1,0:T(8,128)(2,1)S(1)}, u32[]{:S(2)}, u32[]{:S(2)}) collective-permute-start(bf16[192,512]{1,0:T(8,128)(2,1)S(1)} %get-tuple-element.68), channel_id=1, source_target_pairs={{0,15},{1,0},{2,1},{3,2},{4,3},{5,4},{6,5},{7,6},{8,7},{9,8},{10,9... | collective-permute-start | bytes 589832 | tf_op jit(solution)/shard_map/ppermute | solution.py:546
  6.3 15.3 %collective-permute-start = (bf16[144,512]{1,0:T(8,128)(2,1)S(1)}, bf16[144,512]{1,0:T(8,128)(2,1)S(1)}, u32[]{:S(2)}, u32[]{:S(2)}) collective-permute-start(bf16[144,512]{1,0:T(8,128)(2,1)S(1)} %get-tuple-element.67), channel_id=1, source_target_pairs={{0,240},{1,241},{2,242},{3,243},{4,244},{5,245},{6,246},{7,247},{8... | collective-permute-start | bytes 442376 | tf_op jit(solution)/shard_map/ppermute | solution.py:546
  12.8 8.8 %collective-permute-start.2 = (bf16[48,512]{1,0:T(8,128)(2,1)S(1)}, bf16[48,512]{1,0:T(8,128)(2,1)S(1)}, u32[]{:S(2)}, u32[]{:S(2)}) collective-permute-start(bf16[48,512]{1,0:T(8,128)(2,1)S(1)} %get-tuple-element.69), channel_id=1, source_target_pairs={{0,255},{1,240},{2,241},{3,242},{4,243},{5,244},{6,245},{7,246},{8... | collective-permute-start | bytes 147464 | tf_op jit(solution)/shard_map/ppermute | solution.py:546
  16.6 9.9 %collective-permute-start.4 = (bf16[48,512]{1,0:T(8,128)(2,1)S(1)}, bf16[48,512]{1,0:T(8,128)(2,1)S(1)}, u32[]{:S(2)}, u32[]{:S(2)}) collective-permute-start(bf16[48,512]{1,0:T(8,128)(2,1)S(1)} %get-tuple-element.82), channel_id=1, source_target_pairs={{0,240},{1,241},{2,242},{3,243},{4,244},{5,245},{6,246},{7,247},{8... | collective-permute-start | bytes 147464 | tf_op jit(solution)/shard_map/ppermute | solution.py:546
  21.6 4.9 %copy-start = (bf16[2048,1024]{1,0:T(8,128)(2,1)S(1)}, bf16[2048,1024]{1,0:T(8,128)(2,1)}, u32[]{:S(2)}) copy-start(bf16[2048,1024]{1,0:T(8,128)(2,1)} %wmerge_ref.1) | copy-start | bytes 12582916
  25.6 6.6 %collective-permute-start.3 = (bf16[48,512]{1,0:T(8,128)(2,1)S(1)}, bf16[48,512]{1,0:T(8,128)(2,1)S(1)}, u32[]{:S(2)}, u32[]{:S(2)}) collective-permute-start(bf16[48,512]{1,0:T(8,128)(2,1)S(1)} %get-tuple-element.78), channel_id=1, source_target_pairs={{0,16},{1,17},{2,18},{3,19},{4,20},{5,21},{6,22},{7,23},{8,24},{9,... | collective-permute-start | bytes 147464 | tf_op jit(solution)/shard_map/ppermute | solution.py:546
  32.3 2.3 %copy-start.3 = (bf16[192,144]{1,0:T(8,128)(2,1)S(1)}, bf16[192,144]{1,0:T(8,128)(2,1)}, u32[]{:S(2)}) copy-start(bf16[192,144]{1,0:T(8,128)(2,1)} %constant.26.clone.unshift_ref) | copy-start | bytes 165892
  33.5 5.1 %collective-permute-start.5 = (bf16[48,512]{1,0:T(8,128)(2,1)S(1)}, bf16[48,512]{1,0:T(8,128)(2,1)S(1)}, u32[]{:S(2)}, u32[]{:S(2)}) collective-permute-start(bf16[48,512]{1,0:T(8,128)(2,1)S(1)} %get-tuple-element.92), channel_id=1, source_target_pairs={{0,240},{1,241},{2,242},{3,243},{4,244},{5,245},{6,246},{7,247},{8... | collective-permute-start | bytes 147464 | tf_op jit(solution)/shard_map/ppermute | solution.py:546
  34.6 1.0 %copy-start.1 = (bf16[320,288]{1,0:T(8,128)(2,1)S(1)}, bf16[320,288]{1,0:T(8,128)(2,1)}, u32[]{:S(2)}) copy-start(bf16[320,288]{1,0:T(8,128)(2,1)} %constant.24.clone.pick_ref) | copy-start | bytes 552964
  38.6 6.4 %copy-start.2 = (bf16[336,288]{1,0:T(8,128)(2,1)S(1)}, bf16[336,288]{1,0:T(8,128)(2,1)}, u32[]{:S(2)}) copy-start(bf16[336,288]{1,0:T(8,128)(2,1)} %constant.25.clone.unshift_ref) | copy-start | bytes 580612
  43.5 4.0 %collective-permute-start.7 = (bf16[4,32,32,128]{3,2,1,0:T(8,128)(2,1)S(1)}, bf16[4,32,32,128]{3,2,1,0:T(8,128)(2,1)S(1)}, u32[]{:S(2)}, u32[]{:S(2)}) collective-permute-start(bf16[4,32,32,128]{3,2,1,0:T(8,128)(2,1)S(1)} %get-tuple-element.112), channel_id=1, source_target_pairs={{0,1},{1,0},{2,3},{3,2},{4,5},{5,4},{6,7},{7,6},{8,9},{9,8},{10,11... | collective-permute-start | bytes 3145736 | tf_op jit(solution)/shard_map/ppermute | solution.py:573
  47.8 5.6 %collective-permute-start.8 = (bf16[32,32,128]{2,1,0:T(8,128)(2,1)S(1)}, bf16[32,32,128]{2,1,0:T(8,128)(2,1)S(1)}, u32[]{:S(2)}, u32[]{:S(2)}) collective-permute-start(bf16[32,32,128]{2,1,0:T(8,128)(2,1)S(1)} %get-tuple-element.115), channel_id=1, source_target_pairs={{0,2},{1,9},{2,0},{3,11},{4,6},{5,13},{6,4},{7,15},{8,10},{9,1},{1... | collective-permute-start | bytes 786440 | tf_op jit(solution)/shard_map/ppermute | solution.py:570
  47.9 7.8 %collective-permute-start.9 = (bf16[32,32,128]{2,1,0:T(8,128)(2,1)S(1)}, bf16[32,32,128]{2,1,0:T(8,128)(2,1)S(1)}, u32[]{:S(2)}, u32[]{:S(2)}) collective-permute-start(bf16[32,32,128]{2,1,0:T(8,128)(2,1)S(1)} %get-tuple-element.116), channel_id=1, source_target_pairs={{0,4},{1,129},{2,6},{3,131},{4,0},{5,133},{6,2},{7,135},{8,12},{9,... | collective-permute-start | bytes 786440 | tf_op jit(solution)/shard_map/ppermute | solution.py:570
  48.8 10.2 %collective-permute-start.10 = (bf16[32,32,128]{2,1,0:T(8,128)(2,1)S(1)}, bf16[32,32,128]{2,1,0:T(8,128)(2,1)S(1)}, u32[]{:S(2)}, u32[]{:S(2)}) collective-permute-start(bf16[32,32,128]{2,1,0:T(8,128)(2,1)S(1)} %get-tuple-element.117), channel_id=1, source_target_pairs={{0,6},{1,137},{2,4},{3,139},{4,2},{5,141},{6,0},{7,143},{8,14},{9,... | collective-permute-start | bytes 786440 | tf_op jit(solution)/shard_map/ppermute | solution.py:570
  51.7 8.1 %collective-permute-start.11 = (bf16[48,512]{1,0:T(8,128)(2,1)S(1)}, bf16[48,512]{1,0:T(8,128)(2,1)S(1)}, u32[]{:S(2)}, u32[]{:S(2)}) collective-permute-start(bf16[48,512]{1,0:T(8,128)(2,1)S(1)} %get-tuple-element.118), channel_id=1, source_target_pairs={{0,16},{1,17},{2,18},{3,19},{4,20},{5,21},{6,22},{7,23},{8,24},{9,... | collective-permute-start | bytes 147464 | tf_op jit(solution)/shard_map/ppermute | solution.py:546
  59.8 20.2 %all-to-all-start = ((bf16[32,32,128]{2,1,0:T(8,128)(2,1)}), bf16[32,32,128]{2,1,0:T(8,128)(2,1)S(1)}, u32[]{:S(2)}, u32[]{:S(2)}) async-start(bf16[32,32,128]{2,1,0:T(8,128)(2,1)} %shard_map.185), calls=%async_computation | async-start | bytes 524288 | tf_op jit(solution)/shard_map/all_to_all | solution.py:579
  64.7 14.3 %collective-permute-start.12 = (bf16[176,512]{1,0:T(8,128)(2,1)S(1)}, bf16[176,512]{1,0:T(8,128)(2,1)S(1)}, u32[]{:S(2)}, u32[]{:S(2)}) collective-permute-start(bf16[176,512]{1,0:T(8,128)(2,1)S(1)} %get-tuple-element.121), channel_id=1, source_target_pairs={{0,1},{1,2},{2,3},{3,4},{4,5},{5,6},{6,7},{7,8},{8,9},{9,10},{10,1... | collective-permute-start | bytes 540680 | tf_op jit(solution)/shard_map/ppermute | solution.py:546
  65.0 14.0 %collective-permute-start.6 = (bf16[144,512]{1,0:T(8,128)(2,1)S(1)}, bf16[144,512]{1,0:T(8,128)(2,1)S(1)}, u32[]{:S(2)}, u32[]{:S(2)}) collective-permute-start(bf16[144,512]{1,0:T(8,128)(2,1)S(1)} %get-tuple-element.110), channel_id=1, source_target_pairs={{0,16},{1,17},{2,18},{3,19},{4,20},{5,21},{6,22},{7,23},{8,24},{9,... | collective-permute-start | bytes 442376 | tf_op jit(solution)/shard_map/ppermute | solution.py:546
  66.6 12.4 %collective-permute-start.13 = (bf16[48,512]{1,0:T(8,128)(2,1)S(1)}, bf16[48,512]{1,0:T(8,128)(2,1)S(1)}, u32[]{:S(2)}, u32[]{:S(2)}) collective-permute-start(bf16[48,512]{1,0:T(8,128)(2,1)S(1)} %get-tuple-element.123), channel_id=1, source_target_pairs={{0,17},{1,18},{2,19},{3,20},{4,21},{5,22},{6,23},{7,24},{8,25},{9,... | collective-permute-start | bytes 147464 | tf_op jit(solution)/shard_map/ppermute | solution.py:546

commit v10 on v7

--- a/solution.py
+++ b/solution.py
@@ -300,15 +300,19 @@
     out_row_ref[...] = dsum_ref[:COLS]
 
 
-def merge_kernel(normed_ref, wmerge_ref, unshift_ref, main_ref, lat_ref, lon_ref, diag_ref):
+def merge_kernel(
+    normed_ref, wmerge_ref, unshift_ref, cells_lon_ref, cells_diag_ref, main_ref, lat_ref, lon_ref, diag_ref
+):
     total = dot(normed_ref[0], wmerge_ref[:D])
     for k in range(1, 4):
         total = total + dot(normed_ref[k], wmerge_ref[k * D : (k + 1) * D])
     pairs = dot(unshift_ref[...], total.astype(bf16))
     main_ref[...] = pairs[:PAIRS].astype(bf16)
     lat_ref[...] = halves(pairs[PAIRS - PAIR_TOP : PAIRS]).astype(bf16)
-    lon_ref[...] = halves(pairs[PAIRS : PAIRS + PAIR_SIDE - PAIR_CORNER]).astype(bf16)
-    diag_ref[...] = halves(pairs[PAIRS + PAIR_SIDE - PAIR_CORNER :]).astype(bf16)
+    lon_ref[:EDGE] = cells_lon_ref[...]
+    lon_ref[EDGE:] = halves(pairs[PAIRS : PAIRS + PAIR_SIDE - PAIR_CORNER]).astype(bf16)
+    diag_ref[:TURN] = cells_diag_ref[...]
+    diag_ref[TURN:] = halves(pairs[PAIRS + PAIR_SIDE - PAIR_CORNER :]).astype(bf16)
 
 
 def inner_back_kernel(
@@ -363,7 +367,7 @@
 
 
 def cells_back_kernel(
-    dqkv_ref, wqkv_ref, cells_pick_ref, unshift_ref, tok_ref, dsum_ref, row_ref, gain_ref, m_lon_ref, m_diag_ref,
+    dqkv_ref, wqkv_ref, cells_pick_ref, unshift_ref, tok_ref, dsum_ref, row_ref, gain_ref,
     main_ref, lat_ref, lon_ref, diag_ref,
     dx_ref,
 ):
@@ -384,10 +388,8 @@
         else:
             main_ref[BAND_CELLS:] = cells[: BAND_CELLS - TOP]
             lat_ref[...] = cells[BAND_CELLS - TOP : BAND_CELLS]
-            diag_ref[:TURN] = cells[BAND_CELLS + SIDE - TURN :]
+            diag_ref[...] = cells[BAND_CELLS + SIDE - TURN :]
         lon_ref[band * SIDE : (band + 1) * SIDE] = cells[BAND_CELLS:]
-    lon_ref[EDGE:] = m_lon_ref[...]
-    diag_ref[TURN:] = m_diag_ref[...]
 
 
 def fill_edge(field, side, rows, cols):
@@ -505,35 +507,34 @@
         [((BAND, D), bf16), ((BAND, 3 * D), bf16), ((D, WIDTH), bf16), ((D, WIDTH), bf16)],
         [((BAND, D), bf16)],
     )(d_summed, qkv0, probs0, qkv1, probs1, w_proj, band, xs0, xs1, mixed0, mixed1)
-    m_main, m_lat, m_lon, m_diag = call(
-        merge_kernel,
-        [
-            ((PAIRS, 2 * D), bf16), ((2 * PAIR_TOP, D), bf16),
-            ((2 * (PAIR_SIDE - PAIR_CORNER), D), bf16), ((2 * PAIR_CORNER, D), bf16),
-        ],
-    )(merge_normed, w_merge, pair_unshift)
-    m_lat = down(m_lat)
     dqkv, keep, sent = call(
         outer_back_kernel,
         [((WIDTH, 3 * D), bf16), ((4, 32, 32, 128), bf16), ((4, 32, 32, 128), bf16)],
         [((WIDTH, D), bf16), ((BAND, D), bf16)],
-    )(d_summed, last, xst, mixt, after(up0, m_main), dqkv0, qkv1, probs1, w_proj, band)
+    )(d_summed, last, xst, mixt, up0, dqkv0, qkv1, probs1, w_proj, band)
     main, to_lat, to_lon, to_diag = call(
         cells_back_kernel,
-        [
-            ((TOKENS - TOP, D), bf16), ((TOP, D), bf16),
-            ((EDGE + 2 * (PAIR_SIDE - PAIR_CORNER), D), bf16), ((TURN + 2 * PAIR_CORNER, D), bf16),
-        ],
+        [((TOKENS - TOP, D), bf16), ((TOP, D), bf16), ((EDGE, D), bf16), ((TURN, D), bf16)],
         [((WIDTH, D), bf16)],
-    )(dqkv, w_qkv, cells_pick, unshift, tok, d_summed, last, gain, m_lon, m_diag)
-
-    def finish(lat, lon, diag):
+    )(dqkv, w_qkv, cells_pick, unshift, tok, d_summed, last, gain)
+
+    def merge(ready):
+        m_main, m_lat, lon, diag = call(
+            merge_kernel,
+            [
+                ((PAIRS, 2 * D), bf16), ((2 * PAIR_TOP, D), bf16),
+                ((EDGE + 2 * (PAIR_SIDE - PAIR_CORNER), D), bf16), ((TURN + 2 * PAIR_CORNER, D), bf16),
+            ],
+        )(after(merge_normed, ready), w_merge, pair_unshift, to_lon, to_diag)
+        return m_main, down(m_lat), to_lat, lon, diag
+
+    def finish(lat, lon, diag, m_main, m_lat):
         grad_tokens, merged = call(own_cells_kernel, [((TOKENS, D), bf16), ((PAIRS, 2 * D), bf16)])(
             main, lat, lon, diag, m_main, m_lat
         )
         return merged, grad_tokens
 
-    return finish, keep, sent, (to_lat, to_lon, to_diag), m_lat
+    return merge, finish, keep, sent, to_lat
 
 
 def solution(mesh):
@@ -570,27 +571,29 @@
     def swap(block, step):
         return lax.ppermute(block, ("lat", "lon"), [(i, across(i, step)) for i in range(count)])
 
-    def reduce_across(keep, sent, to_lat):
+    def reduce_across(keep, sent, to_lat, merge):
         other = lax.ppermute(sent, ("lat", "lon"), [(i, i ^ 1) for i in range(count)])
         own, *others = call(add_kernel, [((32, 32, 128), bf16)] * 4)(keep, after(other, to_lat))
         got = [swap(block, step) for step, block in enumerate(others, 1)]
-        return call(join_kernel, [((32, 32, 128), bf16)])(own, *got)[0]
+        m_main, m_lat, *pieces = merge(own)
+        sums = call(join_kernel, [((32, 32, 128), bf16)])(after(own, m_main), *got)[0]
+        return sums, m_main, m_lat, pieces
 
     def reduce_rest(sums):
         parts = lax.all_to_all(sums, ("lat", "lon"), 0, 0, axis_index_groups=rest, tiled=True)
         return call(sum_kernel, [((32, 128), f32)])(parts)[0]
 
     def body(tokens, gain_attn, w_qkv, w_proj, gain_merge, w_merge, g_merged):
-        finish, keep, sent, pieces, m_lat = chain(
+        merge, finish, keep, sent, to_lat = chain(
             tokens.reshape(TOKENS, D), gain_attn.reshape(1, D), w_qkv, w_proj, gain_merge.reshape(4, 1, D),
             w_merge, g_merged.reshape(PAIRS, 2 * D), fetch,
             lambda row: send(row, -1, 0), lambda row: send(row, 1, 0),
         )
-        sums = after(reduce_across(keep, sent, pieces[0]), m_lat)
+        sums, m_main, m_lat, (to_lat, to_lon, to_diag) = reduce_across(keep, sent, to_lat, merge)
+        sums = after(sums, m_lat)
         grad_weights = reduce_rest(sums)
-        to_lat, to_lon, to_diag = pieces
         beside = send(to_lat, 1, 0), send(to_lon, 0, 1), send(to_diag, 1, 1)
-        merged, grad_tokens = finish(*(after(piece, sums) for piece in beside))
+        merged, grad_tokens = finish(*(after(piece, sums) for piece in beside), m_main, m_lat)
         return (
             merged.reshape(ROWS // 2, COLS // 2, 2 * D),
             grad_tokens.reshape(ROWS, COLS, D),

time: 80.6 us -> 81.3 us (level)
  starting transfers between devices: 30.9 us -> 32.5 us
  waiting for transfers between devices: 20.6 us -> 19.3 us
    all_to_all x1, starting transfers between devices: 4.09 us -> 5.54 us  [reduce_rest(): lax.all_to_all(sums, ('lat', 'lon'), 0, 0, axis_index_groups=rest, tiled=...]
    ppermute x3, waiting for transfers between devices: 6.23 us -> 5.32 us  [swap(): lax.ppermute(block, ('lat', 'lon'), [(i, across(i, step)) for i in range(...]
where the time goes in v10:
time: 81.3 us; the launch traced here: 80.6 us
  starting transfers between devices  32.5 us (40%)
  Pallas kernels  25.8 us (32%)
  waiting for transfers between devices  19.3 us (24%)
  local copies, waits for them, and re-layouts  2.1 us (3%)
  between operations  0.91 us (1%)
    ppermute x10, starting transfers between devices, send(): return lax.ppermute(block, ('lat', 'lon'), route)  21 us
    ppermute x10, waiting for transfers between devices, send(): return lax.ppermute(block, ('lat', 'lon'), route)  14 us
    all_to_all x1, starting transfers between devices, reduce_rest(): lax.all_to_all(sums, ('lat', 'lon'), 0, 0, axis_index_groups=rest, tiled=...  5.54 us
    ppermute x3, waiting for transfers between devices, swap(): lax.ppermute(block, ('lat', 'lon'), [(i, across(i, step)) for i in range(...  5.32 us
    pallas_call x1, Pallas kernels, chain(): call(outer_back_kernel, [((WIDTH, 3 * D), bf16), ((4, 32, 32, 128), bf16)...  4.82 us
    pallas_call x1, Pallas kernels, chain(): call(inner_kernel, [(h.shape, h.dtype) for h in held] + [((TOKENS - TOP,...  4.15 us
    pallas_call x1, Pallas kernels, chain(): call(outer_kernel, saved(REST) + [((TOKENS, D), bf16), ((TOKENS, D), bf16...  4.05 us
    ppermute x3, starting transfers between devices, swap(): lax.ppermute(block, ('lat', 'lon'), [(i, across(i, step)) for i in range(...  3.94 us
  transfers between devices with their start and end apart: 15, of which 4 were waited for; matrix products, arithmetic and copies ran while one was open for 0% of the time, Pallas kernels for 23%

profile of v10, /device:TPU:1, one launch (start us, length us, event | category | flops | bytes accessed | tf_op | source)
XLA Modules:
  0.0 80.6 jit_solution(3894289502722047181)
XLA Ops:
  0.6 1.1 %copy-done.5 = bf16[12,48,512]{2,1,0:T(8,128)(2,1)S(1)} copy-done((bf16[12,48,512]{2,1,0:T(8,128)(2,1)S(1)}, bf16[12,48,512]{2,1,0:T(8,128)(2,1)}, u32[]{:S(2)}) %copy-start.5) | copy-done | bytes 589848
  1.7 1.0 %copy-done.7 = bf16[6,24,1024]{2,1,0:T(8,128)(2,1)S(1)} copy-done((bf16[6,24,1024]{2,1,0:T(8,128)(2,1)S(1)}, bf16[6,24,1024]{2,1,0:T(8,128)(2,1)}, u32[]{:S(2)}) %copy-start.7) | copy-done | bytes 294936
  2.7 0.0 copy-start.10
  2.7 0.0 copy-start.11
  2.7 0.0 copy-start.12
  2.7 0.0 copy-start.13
  2.7 0.0 copy-start.14
  2.7 0.0 copy-start.15
  2.7 0.2 shard_map.175
  3.0 3.3 %collective-permute-start.1 = (bf16[192,512]{1,0:T(8,128)(2,1)S(1)}, bf16[192,512]{1,0:T(8,128)(2,1)S(1)}, u32[]{:S(2)}, u32[]{:S(2)}) collective-permute-start(bf16[192,512]{1,0:T(8,128)(2,1)S(1)} %get-tuple-element.69), channel_id=1, source_target_pairs={{0,15},{1,0},{2,1},{3,2},{4,3},{5,4},{6,5},{7,6},{8,7},{9,8},{10,9... | collective-permute-start | bytes 589832 | tf_op jit(solution)/shard_map/ppermute | solution.py:548
  6.3 6.5 %collective-permute-start = (bf16[144,512]{1,0:T(8,128)(2,1)S(1)}, bf16[144,512]{1,0:T(8,128)(2,1)S(1)}, u32[]{:S(2)}, u32[]{:S(2)}) collective-permute-start(bf16[144,512]{1,0:T(8,128)(2,1)S(1)} %get-tuple-element.68), channel_id=1, source_target_pairs={{0,240},{1,241},{2,242},{3,243},{4,244},{5,245},{6,246},{7,247},{8... | collective-permute-start | bytes 442376 | tf_op jit(solution)/shard_map/ppermute | solution.py:548
  12.8 3.8 %collective-permute-start.2 = (bf16[48,512]{1,0:T(8,128)(2,1)S(1)}, bf16[48,512]{1,0:T(8,128)(2,1)S(1)}, u32[]{:S(2)}, u32[]{:S(2)}) collective-permute-start(bf16[48,512]{1,0:T(8,128)(2,1)S(1)} %get-tuple-element.70), channel_id=1, source_target_pairs={{0,255},{1,240},{2,241},{3,242},{4,243},{5,244},{6,245},{7,246},{8... | collective-permute-start | bytes 147464 | tf_op jit(solution)/shard_map/ppermute | solution.py:548
  16.6 0.7 collective-permute-start.4
  17.4 4.1 %shard_map.176 = (f32[1,512]{1,0:T(1,128)S(1)}, bf16[320,336]{1,0:T(8,128)(2,1)S(1)}, bf16[512,1536]{1,0:T(8,128)(2,1)S(1)}, bf16[512,512]{1,0:T(8,128)(2,1)S(1)...) custom-call(bf16[576,512]{1,0:T(8,128)(2,1)S(1)} %get-tuple-element., ...), custom_call_target="tpu_custom_call" | custom-call | flops 1000000000 | bytes 2000000 | tf_op jit(solution)/shard_map/pallas_call | solution.py:476
  21.6 0.0 collective-permute-done.lat_ref
  21.6 0.0 collective-permute-done.1.lon_ref
  21.6 0.0 copy-start
  21.6 4.0 %shard_map.177 = (bf16[400,512]{1,0:T(8,128)(2,1)S(1)}, bf16[400,1536]{1,0:T(8,128)(2,1)S(1)}, bf16[400,512]{1,0:T(8,128)(2,1)S(1)}, f32[5,2,80,320]{3,2,1,0:T(8...) custom-call(bf16[576,512]{1,0:T(8,128)(2,1)S(1)} %get-tuple-element.66.tok_ref, ...), custom_call_target="tpu_custom_call" | custom-call | flops 1000000000 | bytes 2000000 | tf_op jit(solution)/shard_map/pallas_call | solution.py:484
  25.6 0.8 %collective-permute-start.3 = (bf16[48,512]{1,0:T(8,128)(2,1)S(1)}, bf16[48,512]{1,0:T(8,128)(2,1)S(1)}, u32[]{:S(2)}, u32[]{:S(2)}) collective-permute-start(bf16[48,512]{1,0:T(8,128)(2,1)S(1)} %get-tuple-element.79), channel_id=1, source_target_pairs={{0,16},{1,17},{2,18},{3,19},{4,20},{5,21},{6,22},{7,23},{8,24},{9,... | collective-permute-start | bytes 147464 | tf_op jit(solution)/shard_map/ppermute | solution.py:548
  26.5 0.0 collective-permute-done.4.lat_ref
  26.5 2.0 %shard_map.178 = (f32[4,144,512]{2,1,0:T(8,128)S(1)}, bf16[2048,1024]{1,0:T(8,128)(2,1)S(1)}) custom-call(bf16[144,1024]{1,0:T(8,128)(2,1)S(1)} %get-tuple-element.82.g_ref, bf16[48,512]{1,0:T(8,128)(2,1)S(1)} %collective-permute-done.4.lat_ref, bf16[192,512]{1,0:T(8,128)(2,1)S(1)} %collective-permute-done.1.lon_ref, ...), custom_call_target="tpu_custom_call" | custom-call | flops 1000000000 | bytes 2000000 | tf_op jit(solution)/shard_map/pallas_call | solution.py:490
  28.5 3.8 %collective-permute-done.3.row_ref = bf16[48,512]{1,0:T(8,128)(2,1)S(1)} collective-permute-done((bf16[48,512]{1,0:T(8,128)(2,1)S(1)}, bf16[48,512]{1,0:T(8,128)(2,1)S(1)}, u32[]{:S(2)}, u32[]{:S(2)}) %collective-permute-start.3) | collective-permute-done | bytes 49184 | tf_op jit(solution)/shard_map/ppermute | solution.py:548
  32.3 1.2 %shard_map.179 = (bf16[576,512]{1,0:T(8,128)(2,1)S(1)}, bf16[48,512]{1,0:T(8,128)(2,1)S(1)}, bf16[4,144,512]{2,1,0:T(8,128)(2,1)S(1)}) custom-call(bf16[576,512]{1,0:T(8,128)(2,1)S(1)} %get-tuple-element.78.summed_ref, bf16[48,512]{1,0:T(8,128)(2,1)S(1)} %collective-permute-done.3.row_ref, f32[4,1,512]{2,1,0:T(1,128)S(1)} %get-tuple-element.80.gain_ref, ...), custom_call_target="tpu_custom_call" | custom-call | flops 1000000000 | bytes 2000000 | tf_op jit(solution)/shard_map/pallas_call | solution.py:496
  33.5 0.9 %collective-permute-start.5 = (bf16[48,512]{1,0:T(8,128)(2,1)S(1)}, bf16[48,512]{1,0:T(8,128)(2,1)S(1)}, u32[]{:S(2)}, u32[]{:S(2)}) collective-permute-start(bf16[48,512]{1,0:T(8,128)(2,1)S(1)} %get-tuple-element.89), channel_id=1, source_target_pairs={{0,240},{1,241},{2,242},{3,243},{4,244},{5,245},{6,246},{7,247},{8... | collective-permute-start | bytes 147464 | tf_op jit(solution)/shard_map/ppermute | solution.py:548
  34.4 3.1 %shard_map.180 = (bf16[320,512]{1,0:T(8,128)(2,1)S(1)}, bf16[320,1536]{1,0:T(8,128)(2,1)S(1)}, bf16[512,640]{1,0:T(8,128)(2,1)S(1)}, bf16[512,640]{1,0:T(8,128)(2,1)S(1)}) custom-call(bf16[576,512]{1,0:T(8,128)(2,1)S(1)} %get-tuple-element.88.dsum_ref, bf16[240,1536]{1,0:T(8,128)(2,1)S(1)} %get-tuple-element.90.qkv0_ref, ...), custom_call_target="tpu_custom_call" | custom-call | flops 1000000000 | bytes 2000000 | tf_op jit(solution)/shard_map/pallas_call | solution.py:505
  37.5 0.0 collective-permute-done.5.row_ref
  37.5 0.0 copy-start.2
  37.5 4.8 %shard_map.181 = (bf16[640,1536]{1,0:T(8,128)(2,1)S(1)}, bf16[4,32,32,128]{3,2,1,0:T(8,128)(2,1)S(1)}, bf16[4,32,32,128]{3,2,1,0:T(8,128)(2,1)S(1)}) custom-call(bf16[576,512]{1,0:T(8,128)(2,1)S(1)} %get-tuple-element.88.dsum_ref, bf16[48,512]{1,0:T(8,128)(2,1)S(1)} %collective-permute-done.5.row_ref, bf16[512,640]{1,0:T(8,128)(2,1)S(1)} %get-tuple-element.98.xst_ref, ...), custom_call_target="tpu_custom_call" | custom-call | flops 1000000000 | bytes 2000000 | tf_op jit(solution)/shard_map/pallas_call | solution.py:510
  42.3 2.1 %collective-permute-start.7 = (bf16[4,32,32,128]{3,2,1,0:T(8,128)(2,1)S(1)}, bf16[4,32,32,128]{3,2,1,0:T(8,128)(2,1)S(1)}, u32[]{:S(2)}, u32[]{:S(2)}) collective-permute-start(bf16[4,32,32,128]{3,2,1,0:T(8,128)(2,1)S(1)} %get-tuple-element.107), channel_id=1, source_target_pairs={{0,1},{1,0},{2,3},{3,2},{4,5},{5,4},{6,7},{7,6},{8,9},{9,8},{10,11... | collective-permute-start | bytes 3145736 | tf_op jit(solution)/shard_map/ppermute | solution.py:575
  44.4 2.5 %shard_map.182 = (bf16[432,512]{1,0:T(8,128)(2,1)S(1)}, bf16[144,512]{1,0:T(8,128)(2,1)S(1)}, bf16[96,512]{1,0:T(8,128)(2,1)S(1)}, bf16[32,512]{1,0:T(8,128)(2,1)S(1)}) custom-call(bf16[640,1536]{1,0:T(8,128)(2,1)S(1)} %get-tuple-element.102.dqkv_ref, bf16[512,1536]{1,0:T(8,128)(2,1)S(1)} %get-tuple-element.72.wqkv_ref, ...), custom_call_target="tpu_custom_call" | custom-call | flops 1000000000 | bytes 2000000 | tf_op jit(solution)/shard_map/pallas_call | solution.py:515
  46.9 0.0 collective-permute-done.7.b_ref
  46.9 0.0 copy-start.3
  46.9 0.2 shard_map.183
  47.2 0.1 collective-permute-start.8
  47.3 1.1 %collective-permute-start.9 = (bf16[32,32,128]{2,1,0:T(8,128)(2,1)S(1)}, bf16[32,32,128]{2,1,0:T(8,128)(2,1)S(1)}, u32[]{:S(2)}, u32[]{:S(2)}) collective-permute-start(bf16[32,32,128]{2,1,0:T(8,128)(2,1)S(1)} %get-tuple-element.118), channel_id=1, source_target_pairs={{0,4},{1,129},{2,6},{3,131},{4,0},{5,133},{6,2},{7,135},{8,12},{9,... | collective-permute-start | bytes 786440 | tf_op jit(solution)/shard_map/ppermute | solution.py:572
  48.4 2.7 %collective-permute-start.10 = (bf16[32,32,128]{2,1,0:T(8,128)(2,1)S(1)}, bf16[32,32,128]{2,1,0:T(8,128)(2,1)S(1)}, u32[]{:S(2)}, u32[]{:S(2)}) collective-permute-start(bf16[32,32,128]{2,1,0:T(8,128)(2,1)S(1)} %get-tuple-element.119), channel_id=1, source_target_pairs={{0,6},{1,137},{2,4},{3,139},{4,2},{5,141},{6,0},{7,143},{8,14},{9,... | collective-permute-start | bytes 786440 | tf_op jit(solution)/shard_map/ppermute | solution.py:572
  51.1 1.0 %shard_map.184 = (bf16[144,1024]{1,0:T(8,128)(2,1)S(1)}, bf16[48,512]{1,0:T(8,128)(2,1)S(1)}, bf16[176,512]{1,0:T(8,128)(2,1)S(1)}, bf16[48,512]{1,0:T(8,128)(2,1)S(1)}) custom-call(bf16[4,144,512]{2,1,0:T(8,128)(2,1)S(1)} %get-tuple-element.111.normed_ref, bf16[2048,1024]{1,0:T(8,128)(2,1)S(1)} %get-tuple-element.112.wmerge_ref, ...), custom_call_target="tpu_custom_call" | custom-call | flops 1000000000 | bytes 2000000 | tf_op jit(solution)/shard_map/pallas_call | solution.py:522
  52.1 0.9 %collective-permute-start.11 = (bf16[48,512]{1,0:T(8,128)(2,1)S(1)}, bf16[48,512]{1,0:T(8,128)(2,1)S(1)}, u32[]{:S(2)}, u32[]{:S(2)}) collective-permute-start(bf16[48,512]{1,0:T(8,128)(2,1)S(1)} %get-tuple-element.120), channel_id=1, source_target_pairs={{0,16},{1,17},{2,18},{3,19},{4,20},{5,21},{6,22},{7,23},{8,24},{9,... | collective-permute-start | bytes 147464 | tf_op jit(solution)/shard_map/ppermute | solution.py:548
  53.0 2.3 %collective-permute-done.9.c_ref = bf16[32,32,128]{2,1,0:T(8,128)(2,1)S(1)} collective-permute-done((bf16[32,32,128]{2,1,0:T(8,128)(2,1)S(1)}, bf16[32,32,128]{2,1,0:T(8,128)(2,1)S(1)}, u32[]{:S(2)}, u32[]{:S(2)}) %collective-permute-start.9) | collective-permute-done | bytes 262176 | tf_op jit(solution)/shard_map/ppermute | solution.py:572
  55.3 3.0 %collective-permute-done.10.d_ref = bf16[32,32,128]{2,1,0:T(8,128)(2,1)S(1)} collective-permute-done((bf16[32,32,128]{2,1,0:T(8,128)(2,1)S(1)}, bf16[32,32,128]{2,1,0:T(8,128)(2,1)S(1)}, u32[]{:S(2)}, u32[]{:S(2)}) %collective-permute-start.10) | collective-permute-done | bytes 262176 | tf_op jit(solution)/shard_map/ppermute | solution.py:572
  58.3 0.8 %shard_map.185 = bf16[32,32,128]{2,1,0:T(8,128)(2,1)} custom-call(bf16[32,32,128]{2,1,0:T(8,128)(2,1)S(1)} %get-tuple-element.116.a_ref, bf16[32,32,128]{2,1,0:T(8,128)(2,1)S(1)} %collective-permute-done.8.b_ref, bf16[32,32,128]{2,1,0:T(8,128)(2,1)S(1)} %collective-permute-done.9.c_ref, bf16[32,32,128]{2,1,0:T(8,128)(2,1)S(1)} %collective-permute-done.10.d_ref), custom_call_target="tpu_custom_call" | custom-call | flops 1000000000 | bytes 2000000 | tf_op jit(solution)/shard_map/pallas_call | solution.py:579
  59.1 5.5 %all-to-all-start = ((bf16[32,32,128]{2,1,0:T(8,128)(2,1)}), bf16[32,32,128]{2,1,0:T(8,128)(2,1)S(1)}, u32[]{:S(2)}, u32[]{:S(2)}) async-start(bf16[32,32,128]{2,1,0:T(8,128)(2,1)} %shard_map.185), calls=%async_computation | async-start | bytes 524288 | tf_op jit(solution)/shard_map/all_to_all | solution.py:583
  64.7 0.3 collective-permute-start.12
  65.0 1.5 %collective-permute-start.6 = (bf16[144,512]{1,0:T(8,128)(2,1)S(1)}, bf16[144,512]{1,0:T(8,128)(2,1)S(1)}, u32[]{:S(2)}, u32[]{:S(2)}) collective-permute-start(bf16[144,512]{1,0:T(8,128)(2,1)S(1)} %get-tuple-element.105), channel_id=1, source_target_pairs={{0,16},{1,17},{2,18},{3,19},{4,20},{5,21},{6,22},{7,23},{8,24},{9,... | collective-permute-start | bytes 442376 | tf_op jit(solution)/shard_map/ppermute | solution.py:548
  66.5 2.2 %collective-permute-start.13 = (bf16[48,512]{1,0:T(8,128)(2,1)S(1)}, bf16[48,512]{1,0:T(8,128)(2,1)S(1)}, u32[]{:S(2)}, u32[]{:S(2)}) collective-permute-start(bf16[48,512]{1,0:T(8,128)(2,1)S(1)} %get-tuple-element.125), channel_id=1, source_target_pairs={{0,17},{1,18},{2,19},{3,20},{4,21},{5,22},{6,23},{7,24},{8,25},{9,... | collective-permute-start | bytes 147464 | tf_op jit(solution)/shard_map/ppermute | solution.py:548
  68.8 10.2 %collective-permute-done.13.diag_ref = bf16[48,512]{1,0:T(8,128)(2,1)S(1)} collective-permute-done((bf16[48,512]{1,0:T(8,128)(2,1)S(1)}, bf16[48,512]{1,0:T(8,128)(2,1)S(1)}, u32[]{:S(2)}, u32[]{:S(2)}) %collective-permute-start.13) | collective-permute-done | bytes 49184 | tf_op jit(solution)/shard_map/ppermute | solution.py:548
  79.0 1.0 %shard_map.186 = (bf16[576,512]{1,0:T(8,128)(2,1)}, bf16[144,1024]{1,0:T(8,128)(2,1)}) custom-call(bf16[432,512]{1,0:T(8,128)(2,1)S(1)} %get-tuple-element.104.main_ref, bf16[144,512]{1,0:T(8,128)(2,1)S(1)} %collective-permute-done.6.lat_ref, bf16[176,512]{1,0:T(8,128)(2,1)S(1)} %collective-permute-done.12.lon_ref, ...), custom_call_target="tpu_custom_call" | custom-call | flops 1000000000 | bytes 2000000 | tf_op jit(solution)/shard_map/pallas_call | solution.py:532
  79.9 0.7 shard_map.187
  (27 shorter events, 0.1 us)
Async XLA Ops:
  0.6 1.1 %copy-start.5 = (bf16[12,48,512]{2,1,0:T(8,128)(2,1)S(1)}, bf16[12,48,512]{2,1,0:T(8,128)(2,1)}, u32[]{:S(2)}) copy-start(bf16[12,48,512]{2,1,0:T(8,128)(2,1)} %param.16) | copy-start | bytes 1769476
  1.7 1.0 %copy-start.7 = (bf16[6,24,1024]{2,1,0:T(8,128)(2,1)S(1)}, bf16[6,24,1024]{2,1,0:T(8,128)(2,1)}, u32[]{:S(2)}) copy-start(bf16[6,24,1024]{2,1,0:T(8,128)(2,1)} %param.22) | copy-start | bytes 884740
  2.7 14.7 %copy-start.4 = (bf16[512,1536]{1,0:T(8,128)(2,1)S(1)}, bf16[512,1536]{1,0:T(8,128)(2,1)}, u32[]{:S(2)}) copy-start(bf16[512,1536]{1,0:T(8,128)(2,1)} %refs_2_.1) | copy-start | bytes 4718596
  2.7 14.7 %copy-start.6 = (bf16[512,512]{1,0:T(8,128)(2,1)S(1)}, bf16[512,512]{1,0:T(8,128)(2,1)}, u32[]{:S(2)}) copy-start(bf16[512,512]{1,0:T(8,128)(2,1)} %refs_3_.1) | copy-start | bytes 1572868
  2.7 14.7 %copy-start.8 = (f32[2048]{0:T(1024)S(1)}, f32[2048]{0:T(1024)}, u32[]{:S(2)}) copy-start(f32[2048]{0:T(1024)} %param.20) | copy-start | bytes 24580
  2.7 14.7 %copy-start.9 = (f32[512]{0:T(512)S(1)}, f32[512]{0:T(512)}, u32[]{:S(2)}) copy-start(f32[512]{0:T(512)} %param.17) | copy-start | bytes 6148
  2.7 14.7 %copy-start.10 = (bf16[320,336]{1,0:T(8,128)(2,1)S(1)}, bf16[320,336]{1,0:T(8,128)(2,1)}, u32[]{:S(2)}) copy-start(bf16[320,336]{1,0:T(8,128)(2,1)} %constant.18.clone.refs_1_) | copy-start | bytes 645124
  2.7 14.7 %copy-start.11 = (bf16[288,320]{1,0:T(8,128)(2,1)S(1)}, bf16[288,320]{1,0:T(8,128)(2,1)}, u32[]{:S(2)}) copy-start(bf16[288,320]{1,0:T(8,128)(2,1)} %constant.20.clone.refs_6_) | copy-start | bytes 552964
  2.7 14.7 %copy-start.12 = (bf16[288,336]{1,0:T(8,128)(2,1)S(1)}, bf16[288,336]{1,0:T(8,128)(2,1)}, u32[]{:S(2)}) copy-start(bf16[288,336]{1,0:T(8,128)(2,1)} %constant.19.clone.refs_5_) | copy-start | bytes 580612
  2.7 14.7 %copy-start.13 = (bf16[192,192]{1,0:T(8,128)(2,1)S(1)}, bf16[192,192]{1,0:T(8,128)(2,1)}, u32[]{:S(2)}) copy-start(bf16[192,192]{1,0:T(8,128)(2,1)} %constant.22.clone.refs_8_) | copy-start | bytes 221188
  2.7 14.6 %copy-start.14 = (bf16[192,192]{1,0:T(8,128)(2,1)S(1)}, bf16[192,192]{1,0:T(8,128)(2,1)}, u32[]{:S(2)}) copy-start(bf16[192,192]{1,0:T(8,128)(2,1)} %constant.21.clone.refs_7_) | copy-start | bytes 221188
  2.7 14.6 %copy-start.15 = (bf16[144,192]{1,0:T(8,128)(2,1)S(1)}, bf16[144,192]{1,0:T(8,128)(2,1)}, u32[]{:S(2)}) copy-start(bf16[144,192]{1,0:T(8,128)(2,1)} %constant.23.clone.refs_9_) | copy-start | bytes 165892
  3.0 18.6 %collective-permute-start.1 = (bf16[192,512]{1,0:T(8,128)(2,1)S(1)}, bf16[192,512]{1,0:T(8,128)(2,1)S(1)}, u32[]{:S(2)}, u32[]{:S(2)}) collective-permute-start(bf16[192,512]{1,0:T(8,128)(2,1)S(1)} %get-tuple-element.69), channel_id=1, source_target_pairs={{0,15},{1,0},{2,1},{3,2},{4,3},{5,4},{6,5},{7,6},{8,7},{9,8},{10,9... | collective-permute-start | bytes 589832 | tf_op jit(solution)/shard_map/ppermute | solution.py:548
  6.3 15.3 %collective-permute-start = (bf16[144,512]{1,0:T(8,128)(2,1)S(1)}, bf16[144,512]{1,0:T(8,128)(2,1)S(1)}, u32[]{:S(2)}, u32[]{:S(2)}) collective-permute-start(bf16[144,512]{1,0:T(8,128)(2,1)S(1)} %get-tuple-element.68), channel_id=1, source_target_pairs={{0,240},{1,241},{2,242},{3,243},{4,244},{5,245},{6,246},{7,247},{8... | collective-permute-start | bytes 442376 | tf_op jit(solution)/shard_map/ppermute | solution.py:548
  12.8 8.8 %collective-permute-start.2 = (bf16[48,512]{1,0:T(8,128)(2,1)S(1)}, bf16[48,512]{1,0:T(8,128)(2,1)S(1)}, u32[]{:S(2)}, u32[]{:S(2)}) collective-permute-start(bf16[48,512]{1,0:T(8,128)(2,1)S(1)} %get-tuple-element.70), channel_id=1, source_target_pairs={{0,255},{1,240},{2,241},{3,242},{4,243},{5,244},{6,245},{7,246},{8... | collective-permute-start | bytes 147464 | tf_op jit(solution)/shard_map/ppermute | solution.py:548
  16.6 9.9 %collective-permute-start.4 = (bf16[48,512]{1,0:T(8,128)(2,1)S(1)}, bf16[48,512]{1,0:T(8,128)(2,1)S(1)}, u32[]{:S(2)}, u32[]{:S(2)}) collective-permute-start(bf16[48,512]{1,0:T(8,128)(2,1)S(1)} %get-tuple-element.83), channel_id=1, source_target_pairs={{0,240},{1,241},{2,242},{3,243},{4,244},{5,245},{6,246},{7,247},{8... | collective-permute-start | bytes 147464 | tf_op jit(solution)/shard_map/ppermute | solution.py:548
  21.6 4.9 %copy-start = (bf16[2048,1024]{1,0:T(8,128)(2,1)S(1)}, bf16[2048,1024]{1,0:T(8,128)(2,1)}, u32[]{:S(2)}) copy-start(bf16[2048,1024]{1,0:T(8,128)(2,1)} %wmerge_ref.1) | copy-start | bytes 12582916
  25.6 6.6 %collective-permute-start.3 = (bf16[48,512]{1,0:T(8,128)(2,1)S(1)}, bf16[48,512]{1,0:T(8,128)(2,1)S(1)}, u32[]{:S(2)}, u32[]{:S(2)}) collective-permute-start(bf16[48,512]{1,0:T(8,128)(2,1)S(1)} %get-tuple-element.79), channel_id=1, source_target_pairs={{0,16},{1,17},{2,18},{3,19},{4,20},{5,21},{6,22},{7,23},{8,24},{9,... | collective-permute-start | bytes 147464 | tf_op jit(solution)/shard_map/ppermute | solution.py:548
  32.3 2.1 %copy-start.1 = (bf16[320,288]{1,0:T(8,128)(2,1)S(1)}, bf16[320,288]{1,0:T(8,128)(2,1)}, u32[]{:S(2)}) copy-start(bf16[320,288]{1,0:T(8,128)(2,1)} %constant.24.clone.pick_ref) | copy-start | bytes 552964
  33.5 4.0 %collective-permute-start.5 = (bf16[48,512]{1,0:T(8,128)(2,1)S(1)}, bf16[48,512]{1,0:T(8,128)(2,1)S(1)}, u32[]{:S(2)}, u32[]{:S(2)}) collective-permute-start(bf16[48,512]{1,0:T(8,128)(2,1)S(1)} %get-tuple-element.89), channel_id=1, source_target_pairs={{0,240},{1,241},{2,242},{3,243},{4,244},{5,245},{6,246},{7,247},{8... | collective-permute-start | bytes 147464 | tf_op jit(solution)/shard_map/ppermute | solution.py:548
  37.5 6.9 %copy-start.2 = (bf16[336,288]{1,0:T(8,128)(2,1)S(1)}, bf16[336,288]{1,0:T(8,128)(2,1)}, u32[]{:S(2)}) copy-start(bf16[336,288]{1,0:T(8,128)(2,1)} %constant.25.clone.unshift_ref) | copy-start | bytes 580612
  42.3 4.6 %collective-permute-start.7 = (bf16[4,32,32,128]{3,2,1,0:T(8,128)(2,1)S(1)}, bf16[4,32,32,128]{3,2,1,0:T(8,128)(2,1)S(1)}, u32[]{:S(2)}, u32[]{:S(2)}) collective-permute-start(bf16[4,32,32,128]{3,2,1,0:T(8,128)(2,1)S(1)} %get-tuple-element.107), channel_id=1, source_target_pairs={{0,1},{1,0},{2,3},{3,2},{4,5},{5,4},{6,7},{7,6},{8,9},{9,8},{10,11... | collective-permute-start | bytes 3145736 | tf_op jit(solution)/shard_map/ppermute | solution.py:575
  46.9 4.2 %copy-start.3 = (bf16[192,144]{1,0:T(8,128)(2,1)S(1)}, bf16[192,144]{1,0:T(8,128)(2,1)}, u32[]{:S(2)}) copy-start(bf16[192,144]{1,0:T(8,128)(2,1)} %constant.26.clone.unshift_ref) | copy-start | bytes 165892
  47.2 5.8 %collective-permute-start.8 = (bf16[32,32,128]{2,1,0:T(8,128)(2,1)S(1)}, bf16[32,32,128]{2,1,0:T(8,128)(2,1)S(1)}, u32[]{:S(2)}, u32[]{:S(2)}) collective-permute-start(bf16[32,32,128]{2,1,0:T(8,128)(2,1)S(1)} %get-tuple-element.117), channel_id=1, source_target_pairs={{0,2},{1,9},{2,0},{3,11},{4,6},{5,13},{6,4},{7,15},{8,10},{9,1},{1... | collective-permute-start | bytes 786440 | tf_op jit(solution)/shard_map/ppermute | solution.py:572
  47.3 8.0 %collective-permute-start.9 = (bf16[32,32,128]{2,1,0:T(8,128)(2,1)S(1)}, bf16[32,32,128]{2,1,0:T(8,128)(2,1)S(1)}, u32[]{:S(2)}, u32[]{:S(2)}) collective-permute-start(bf16[32,32,128]{2,1,0:T(8,128)(2,1)S(1)} %get-tuple-element.118), channel_id=1, source_target_pairs={{0,4},{1,129},{2,6},{3,131},{4,0},{5,133},{6,2},{7,135},{8,12},{9,... | collective-permute-start | bytes 786440 | tf_op jit(solution)/shard_map/ppermute | solution.py:572
  48.4 9.9 %collective-permute-start.10 = (bf16[32,32,128]{2,1,0:T(8,128)(2,1)S(1)}, bf16[32,32,128]{2,1,0:T(8,128)(2,1)S(1)}, u32[]{:S(2)}, u32[]{:S(2)}) collective-permute-start(bf16[32,32,128]{2,1,0:T(8,128)(2,1)S(1)} %get-tuple-element.119), channel_id=1, source_target_pairs={{0,6},{1,137},{2,4},{3,139},{4,2},{5,141},{6,0},{7,143},{8,14},{9,... | collective-permute-start | bytes 786440 | tf_op jit(solution)/shard_map/ppermute | solution.py:572
  52.1 7.0 %collective-permute-start.11 = (bf16[48,512]{1,0:T(8,128)(2,1)S(1)}, bf16[48,512]{1,0:T(8,128)(2,1)S(1)}, u32[]{:S(2)}, u32[]{:S(2)}) collective-permute-start(bf16[48,512]{1,0:T(8,128)(2,1)S(1)} %get-tuple-element.120), channel_id=1, source_target_pairs={{0,16},{1,17},{2,18},{3,19},{4,20},{5,21},{6,22},{7,23},{8,24},{9,... | collective-permute-start | bytes 147464 | tf_op jit(solution)/shard_map/ppermute | solution.py:548
  59.1 20.8 %all-to-all-start = ((bf16[32,32,128]{2,1,0:T(8,128)(2,1)}), bf16[32,32,128]{2,1,0:T(8,128)(2,1)S(1)}, u32[]{:S(2)}, u32[]{:S(2)}) async-start(bf16[32,32,128]{2,1,0:T(8,128)(2,1)} %shard_map.185), calls=%async_computation | async-start | bytes 524288 | tf_op jit(solution)/shard_map/all_to_all | solution.py:583
  64.7 14.3 %collective-permute-start.12 = (bf16[176,512]{1,0:T(8,128)(2,1)S(1)}, bf16[176,512]{1,0:T(8,128)(2,1)S(1)}, u32[]{:S(2)}, u32[]{:S(2)}) collective-permute-start(bf16[176,512]{1,0:T(8,128)(2,1)S(1)} %get-tuple-element.123), channel_id=1, source_target_pairs={{0,1},{1,2},{2,3},{3,4},{4,5},{5,6},{6,7},{7,8},{8,9},{9,10},{10,1... | collective-permute-start | bytes 540680 | tf_op jit(solution)/shard_map/ppermute | solution.py:548
  65.0 13.9 %collective-permute-start.6 = (bf16[144,512]{1,0:T(8,128)(2,1)S(1)}, bf16[144,512]{1,0:T(8,128)(2,1)S(1)}, u32[]{:S(2)}, u32[]{:S(2)}) collective-permute-start(bf16[144,512]{1,0:T(8,128)(2,1)S(1)} %get-tuple-element.105), channel_id=1, source_target_pairs={{0,16},{1,17},{2,18},{3,19},{4,20},{5,21},{6,22},{7,23},{8,24},{9,... | collective-permute-start | bytes 442376 | tf_op jit(solution)/shard_map/ppermute | solution.py:548
  66.5 12.4 %collective-permute-start.13 = (bf16[48,512]{1,0:T(8,128)(2,1)S(1)}, bf16[48,512]{1,0:T(8,128)(2,1)S(1)}, u32[]{:S(2)}, u32[]{:S(2)}) collective-permute-start(bf16[48,512]{1,0:T(8,128)(2,1)S(1)} %get-tuple-element.125), channel_id=1, source_target_pairs={{0,17},{1,18},{2,19},{3,20},{4,21},{5,22},{6,23},{7,24},{8,25},{9,... | collective-permute-start | bytes 147464 | tf_op jit(solution)/shard_map/ppermute | solution.py:548
